TPU v7x, 512 devices: a whole 4x8x8 slice. The times are simulated.
512 devices in a mesh: dp: 32 (over y, x), expert: 16 (over z, core).
Axes of the slice: x: 4, y: 8, z: 8, core: 2. Of those that a mesh axis runs over, the one named last changes fastest.
Arguments:
- tokens: bfloat16 [65536, 1024], P(('dp', 'expert')), may hold values from -6 to 6
- cotangent: bfloat16 [65536, 1024], P(('dp', 'expert')), may hold values from -6 to 6
- routing: int32 [65536, 10], P(('dp', 'expert')), may hold values from 0 to 15, all different within a row; in each aligned block of 128 rows (0 to 127, 128 to 255, ...) at most 96 rows name the same one
- gates: bfloat16 [65536, 10], P(('dp', 'expert')), may hold values from 0.049804688 to 1
- gate_weight: bfloat16 [16, 1024, 256], P('expert'), may hold values from -0.1875 to 0.1875
- up_weight: bfloat16 [16, 1024, 256], P('expert'), may hold values from -0.1875 to 0.1875
- down_weight: bfloat16 [16, 256, 1024], P('expert'), may hold values from -0.375 to 0.375
Outputs:
- token_grad: bfloat16 [65536, 1024], P(('dp', 'expert'))
- gate_grad: bfloat16 [65536, 10], P(('dp', 'expert'))
- grad_gate: float32 [16, 1024, 256], P('expert', 'dp')
- grad_up: float32 [16, 1024, 256], P('expert', 'dp')
- grad_down: float32 [16, 256, 1024], P('expert', 'dp')
Inputs may be any that keep to these rules, and one draw needn't show every extreme that they name: `routing`: each row names 10 different experts; among the rows of one device no expert is named by more than 96 rows, a bound that some block reaches.
All inputs are finite; a program needn't handle non-finite values.
Results may differ from a plain program's by a relative error of at most 0.02.
Values may be sent and summed in bfloat16 or wider, within the bound.
No kernel may reach another device: no remote copies, remote signals or barrier semaphores. Data moves between devices by JAX's collectives and lax.ppermute only.
A program may use at most 64 MiB of HBM per device.

v0:
```python
import jax
import jax.numpy as jnp
from jax import lax
from jax.sharding import PartitionSpec as P

CAP = 96


def forward_part(recv_x, gate_weight, up_weight, down_weight):
    pre_gate = jnp.einsum("spcd,pdf->spcf", recv_x, gate_weight, preferred_element_type=jnp.float32)
    pre_up = jnp.einsum("spcd,pdf->spcf", recv_x, up_weight, preferred_element_type=jnp.float32)
    sigmoid_gate = jax.nn.sigmoid(pre_gate)
    silu_gate = pre_gate * sigmoid_gate
    activated = (silu_gate * pre_up).astype(jnp.bfloat16)
    expert_out = jnp.einsum(
        "spcf,pfd->spcd", activated, down_weight, preferred_element_type=jnp.float32
    )
    return (pre_gate, pre_up, sigmoid_gate, silu_gate, activated, expert_out)


def on_device(tokens, cotangent, routing, gates, gate_weight, up_weight, down_weight):
    groups = lax.axis_size("expert")
    local_experts = gate_weight.shape[0]
    token_rows = tokens.shape[0]
    top_count = routing.shape[1]
    feature_width = tokens.shape[1]
    total_experts = groups * local_experts
    capacity = CAP
    flat_routes = routing.reshape(-1)
    onehot = (flat_routes[:, None] == jnp.arange(total_experts, dtype=jnp.int32)[None, :]).astype(
        jnp.int32
    )
    slot_index = jnp.sum((jnp.cumsum(onehot, axis=0) - 1) * onehot, axis=1)
    position = flat_routes * capacity + slot_index
    copy_total = flat_routes.shape[0]
    source_copy = (
        jnp.zeros((total_experts * capacity,), jnp.int32)
        .at[position]
        .set(jnp.arange(copy_total, dtype=jnp.int32) + 1)
        - 1
    )
    filled = source_copy >= 0
    copy_pick = jnp.maximum(source_copy, 0)
    token_index = copy_pick // top_count
    buffer_shape = (groups, local_experts, capacity, feature_width)
    send_x = jnp.where(filled[:, None], tokens[token_index], 0).reshape(buffer_shape)
    send_dy = jnp.where(filled[:, None], cotangent[token_index], 0).reshape(buffer_shape)
    send_g = jnp.where(filled, gates.reshape(-1)[copy_pick], 0).reshape(
        groups, local_experts, capacity
    )
    recv_x, recv_dy, recv_g = (
        lax.all_to_all(send_x, "expert", split_axis=0, concat_axis=0, tiled=True),
        lax.all_to_all(send_dy, "expert", split_axis=0, concat_axis=0, tiled=True),
        lax.all_to_all(send_g, "expert", split_axis=0, concat_axis=0, tiled=True),
    )
    pre_gate, pre_up, sigmoid_gate, silu_gate, activated, expert_out = forward_part(
        recv_x, gate_weight, up_weight, down_weight
    )
    gate_terms = jnp.sum(recv_dy.astype(jnp.float32) * expert_out, axis=-1).astype(jnp.bfloat16)
    out_grad = (recv_g.astype(jnp.float32)[..., None] * recv_dy.astype(jnp.float32)).astype(
        jnp.bfloat16
    )
    act_grad = jnp.einsum(
        "spcd,pfd->spcf", out_grad, down_weight, preferred_element_type=jnp.float32
    )
    gate_pre_grad = (
        act_grad * pre_up * sigmoid_gate * (1.0 + pre_gate * (1.0 - sigmoid_gate))
    ).astype(jnp.bfloat16)
    up_pre_grad = (act_grad * silu_gate).astype(jnp.bfloat16)
    input_grad = (
        jnp.einsum("spcf,pdf->spcd", gate_pre_grad, gate_weight, preferred_element_type=jnp.float32)
        + jnp.einsum("spcf,pdf->spcd", up_pre_grad, up_weight, preferred_element_type=jnp.float32)
    ).astype(jnp.bfloat16)
    back_grad, back_terms = (
        lax.all_to_all(input_grad, "expert", split_axis=0, concat_axis=0, tiled=True),
        lax.all_to_all(gate_terms, "expert", split_axis=0, concat_axis=0, tiled=True),
    )
    gate_term = jnp.einsum(
        "spcd,spcf->pdf", recv_x, gate_pre_grad, preferred_element_type=jnp.float32
    ).astype(jnp.bfloat16)
    up_term = jnp.einsum(
        "spcd,spcf->pdf", recv_x, up_pre_grad, preferred_element_type=jnp.float32
    ).astype(jnp.bfloat16)
    down_term = jnp.einsum(
        "spcf,spcd->pfd", activated, out_grad, preferred_element_type=jnp.float32
    ).astype(jnp.bfloat16)
    sum_gate, sum_up, sum_down = (
        lax.psum_scatter(gate_term, "dp", scatter_dimension=1, tiled=True).astype(jnp.float32),
        lax.psum_scatter(up_term, "dp", scatter_dimension=1, tiled=True).astype(jnp.float32),
        lax.psum_scatter(down_term, "dp", scatter_dimension=1, tiled=True).astype(jnp.float32),
    )
    copy_grads = back_grad.reshape(total_experts * capacity, feature_width)[position]
    token_grad = jnp.sum(
        copy_grads.reshape(token_rows, top_count, feature_width).astype(jnp.float32), axis=1
    ).astype(jnp.bfloat16)
    gate_grad = back_terms.reshape(-1)[position].reshape(token_rows, top_count)
    return (token_grad, gate_grad, sum_gate, sum_up, sum_down)


def solution(mesh):
    in_specs = (
        P(("dp", "expert"), None),
        P(("dp", "expert"), None),
        P(("dp", "expert"), None),
        P(("dp", "expert"), None),
        P("expert", None, None),
        P("expert", None, None),
        P("expert", None, None),
    )
    out_specs = (
        P(("dp", "expert"), None),
        P(("dp", "expert"), None),
        P("expert", "dp", None),
        P("expert", "dp", None),
        P("expert", "dp", None),
    )
    return jax.shard_map(
        on_device, mesh=mesh, in_specs=in_specs, out_specs=out_specs, check_vma=False
    )
```

profile of v0, /device:TPU:1, one launch (start us, length us, event | category | flops | bytes accessed | tf_op | source)
XLA Modules:
  0.0 928.5 jit_solution(106443880734862499)
XLA Ops:
  10.3 4.5 reduce-window.6
  15.6 5.2 scatter_custom_fusion
  20.9 9.5 %gather_fusion = bf16[1536]{0:T(1024)(128)(2,1)S(1)} fusion(bf16[1280]{0:T(1024)(128)(2,1)S(1)} %reshape.175, s32[2048]{0:T(1024)S(1)} %get-tuple-element.30), kind=kCustom, calls=%fused_computation | custom fusion | bytes 12288 | tf_op jit(solution)/shard_map/gather | solution.py:48
  31.1 11.8 %all-to-all-start = ((bf16[16,1,96]{2,1,0:T(2,128)(2,1)}), bf16[16,1,96]{2,1,0:T(2,128)(2,1)S(1)}, u32[]{:S(2)}, u32[]{:S(2)}) async-start(bf16[16,1,96]{2,1,0:T(2,128)(2,1)} %reshape.247), calls=%async_computation | async-start | bytes 16384 | tf_op jit(solution)/shard_map/all_to_all | solution.py:54
  43.0 5.8 gather_fusion.2
  48.8 5.9 gather_fusion.1
  54.7 4.8 broadcast_select_fusion.1
  59.6 80.8 %all_to_all.25 = bf16[16,1,96,1024]{3,2,1,0:T(8,128)(2,1)} all-to-all(bf16[16,1,96,1024]{3,2,1,0:T(8,128)(2,1)} %get-tuple-element.28), channel_id=1, replica_groups=mesh['dp'=32,'expert'=16] {'expert'}, dimensions={0} | all-to-all | bytes 6291456 | tf_op jit(solution)/shard_map/all_to_all | solution.py:52
  140.4 4.5 all-to-all-start.1
  147.9 66.9 %all-to-all-done.1 = bf16[16,1,96,1024]{3,2,1,0:T(8,128)(2,1)} async-done(((bf16[16,1,96,1024]{3,2,1,0:T(8,128)(2,1)}), bf16[16,1,96,1024]{3,2,1,0:T(8,128)(2,1)}, u32[]{:S(2)}, u32[]{:S(2)}) %all-to-all-start.1) | async-done | bytes 3145760 | tf_op jit(solution)/shard_map/all_to_all | solution.py:53
  214.7 3.1 fusion.14
  220.3 3.3 fusion.1
  224.2 5.4 all-to-all-start.4
  233.5 3.1 all-to-all-done.4
  236.6 5.0 all-to-all-start.3
  241.6 4.0 fusion.43
  245.8 3.7 fusion.46
  249.6 3.7 fusion.49
  253.4 8.0 gather_fusion.4
  262.2 198.7 %reduce-scatter.8.cloned.1.call-done = bf16[1,8,1024]{2,1,0:T(8,128)(2,1)} async-done(((bf16[1,256,1024]{2,1,0:T(8,128)(2,1)}), bf16[1,8,1024]{2,1,0:T(8,128)(2,1)}) %reduce-scatter.8.cloned.1.call-update) | async-done | bytes 16400 | tf_op jit(solution)/shard_map/reduce_scatter | solution.py:90
  462.3 220.6 %reduce-scatter.4.cloned.1.call-done = bf16[1,32,256]{2,1,0:T(8,128)(2,1)} async-done(((bf16[1,1024,256]{2,1,0:T(8,128)(2,1)}), bf16[1,32,256]{2,1,0:T(8,128)(2,1)}) %reduce-scatter.4.cloned.1.call-update) | async-done | bytes 16400 | tf_op jit(solution)/shard_map/reduce_scatter | solution.py:88
  684.2 220.3 %reduce-scatter.6.cloned.1.call-done = bf16[1,32,256]{2,1,0:T(8,128)(2,1)} async-done(((bf16[1,1024,256]{2,1,0:T(8,128)(2,1)}), bf16[1,32,256]{2,1,0:T(8,128)(2,1)}) %reduce-scatter.6.cloned.1.call-update) | async-done | bytes 16400 | tf_op jit(solution)/shard_map/reduce_scatter | solution.py:89
  905.9 8.3 gather_fusion.3
  917.0 5.0 reduce_sum.34
  (61 shorter events, 22.4 us)
Async XLA Ops:
  7.2 210.7 %copy-start = (bf16[1,1024,256]{2,1,0:T(8,128)(2,1)S(1)}, bf16[1,1024,256]{2,1,0:T(8,128)(2,1)}, u32[]{:S(2)}) copy-start(bf16[1,1024,256]{2,1,0:T(8,128)(2,1)} %param.12) | copy-start | bytes 1572868
  7.2 35.8 %copy-start.1 = (bf16[128,1024]{1,0:T(8,128)(2,1)S(1)}, bf16[128,1024]{1,0:T(8,128)(2,1)}, u32[]{:S(2)}) copy-start(bf16[128,1024]{1,0:T(8,128)(2,1)} %param.7) | copy-start | bytes 786436
  31.1 28.5 %all-to-all-start = ((bf16[16,1,96]{2,1,0:T(2,128)(2,1)}), bf16[16,1,96]{2,1,0:T(2,128)(2,1)S(1)}, u32[]{:S(2)}, u32[]{:S(2)}) async-start(bf16[16,1,96]{2,1,0:T(2,128)(2,1)} %reshape.247), calls=%async_computation | async-start | bytes 16384 | tf_op jit(solution)/shard_map/all_to_all | solution.py:54
  43.0 5.8 copy-start.2
  140.4 4.5 copy-start.4
  140.4 74.3 %all-to-all-start.1 = ((bf16[16,1,96,1024]{3,2,1,0:T(8,128)(2,1)}), bf16[16,1,96,1024]{3,2,1,0:T(8,128)(2,1)}, u32[]{:S(2)}, u32[]{:S(2)}) async-start(bf16[16,1,96,1024]{3,2,1,0:T(8,128)(2,1)} %get-tuple-element.27), calls=%async_computation.1 | async-start | bytes 6291456 | tf_op jit(solution)/shard_map/all_to_all | solution.py:53
  144.9 69.8 %copy-start.6 = (bf16[1,256,1024]{2,1,0:T(8,128)(2,1)S(1)}, bf16[1,256,1024]{2,1,0:T(8,128)(2,1)}, u32[]{:S(2)}) copy-start(bf16[1,256,1024]{2,1,0:T(8,128)(2,1)} %param.13) | copy-start | bytes 1572868
  214.7 3.1 copy-start.3
  217.8 2.5 copy-start.7
  220.3 3.3 copy-start.8
  224.2 12.3 %all-to-all-start.4 = ((bf16[16,1,96]{2,1,0:T(2,128)(2,1)}), bf16[16,1,96]{2,1,0:T(2,128)(2,1)S(1)}, u32[]{:S(2)}, u32[]{:S(2)}) async-start(bf16[16,1,96]{2,1,0:T(2,128)(2,1)} %copy.35), calls=%async_computation.4 | async-start | bytes 16384 | tf_op jit(solution)/shard_map/all_to_all | solution.py:76
  229.6 1.1 copy-start.5
  236.6 669.3 %all-to-all-start.3 = ((bf16[16,1,96,1024]{3,2,1,0:T(8,128)(2,1)}), bf16[16,1,96,1024]{3,2,1,0:T(8,128)(2,1)}, u32[]{:S(2)}, u32[]{:S(2)}) async-start(bf16[16,1,96,1024]{3,2,1,0:T(8,128)(2,1)} %fusion.2), calls=%async_computation.3 | async-start | bytes 6291456 | tf_op jit(solution)/shard_map/all_to_all | solution.py:75
  241.6 219.3 %reduce-scatter.8.cloned.1.call-start = ((), (), s32[]{:S(2)}) async-start(), calls=%async_computation.10 | async-start | bytes 540672 | tf_op jit(solution)/shard_map/reduce_scatter | solution.py:90
  245.7 437.2 %reduce-scatter.4.cloned.1.call-start = ((), (), s32[]{:S(2)}) async-start(), calls=%async_computation.8 | async-start | bytes 540672 | tf_op jit(solution)/shard_map/reduce_scatter | solution.py:88
  249.5 655.0 %reduce-scatter.6.cloned.1.call-start = ((), (), s32[]{:S(2)}) async-start(), calls=%async_computation.9 | async-start | bytes 540672 | tf_op jit(solution)/shard_map/reduce_scatter | solution.py:89
Sparse Core Ops, SparseCore 0:
  246.8 214.0 reduce-scatter.7
  465.9 216.9 reduce-scatter.3
  687.3 217.2 reduce-scatter.5
where the time goes:
time: 933 us; the launch traced here: 928 us
  waiting for transfers between devices  710 us (76%)
  blocking collectives  80.8 us (9%)
  local copies, waits for them, and re-layouts  50.6 us (5%)
  matrix products  27 us (3%)
  starting transfers between devices  26.9 us (3%)
  other arithmetic  19.6 us (2%)
  between operations  14 us (2%)
    reduce_scatter x1, waiting for transfers between devices, on_device(): lax.psum_scatter(gate_term, 'dp', scatter_dimension=1, tiled=True)  221 us
    reduce_scatter x1, waiting for transfers between devices, on_device(): lax.psum_scatter(up_term, 'dp', scatter_dimension=1, tiled=True)  220 us
    reduce_scatter x1, waiting for transfers between devices, on_device(): lax.psum_scatter(down_term, 'dp', scatter_dimension=1, tiled=True)  199 us
    all_to_all x1, blocking collectives, on_device(): lax.all_to_all(send_x, 'expert', split_axis=0, concat_axis=0, tiled=True)  80.8 us
    all_to_all x1, waiting for transfers between devices, on_device(): lax.all_to_all(send_dy, 'expert', split_axis=0, concat_axis=0, tiled=True)  66.9 us
  transfers between devices with their start and end apart: 7, of which 5 were waited for; matrix products, arithmetic and copies ran while one was open for 5% of the time, Pallas kernels for 0%

commit v1 on v0

v1 whole, which is shorter than its diff:
```python
import jax
import jax.numpy as jnp
from jax import lax
from jax.sharding import PartitionSpec as P

BF = jnp.bfloat16
F32 = jnp.float32


def matmul(a, b, dims):
    return lax.dot_general(a, b, (dims, ((), ())), preferred_element_type=F32)


def on_device(tokens, cotangent, routing, gates, gate_weight, up_weight, down_weight):
    groups = lax.axis_size("expert")
    replicas = lax.axis_size("dp")
    rows, width = tokens.shape
    w_gate, w_up, w_down = gate_weight[0], up_weight[0], down_weight[0]
    hidden = w_gate.shape[1]

    chosen = routing[:, :, None] == jnp.arange(groups, dtype=jnp.int32)
    dense_gates = jnp.sum(jnp.where(chosen, gates[:, :, None].astype(F32), 0.0), axis=1).T.astype(BF)

    all_x = lax.all_gather(tokens, "expert", axis=0, tiled=True)
    all_dy = lax.all_gather(cotangent, "expert", axis=0, tiled=True)
    own_gates = lax.all_to_all(dense_gates, "expert", split_axis=0, concat_axis=0, tiled=True)
    g = own_gates.reshape(-1, 1).astype(F32)

    pre_gate = matmul(all_x, w_gate, ((1,), (0,)))
    pre_up = matmul(all_x, w_up, ((1,), (0,)))
    back = matmul(all_dy, w_down, ((1,), (1,)))
    sig = jax.nn.sigmoid(pre_gate)
    silu = pre_gate * sig
    act = silu * pre_up
    terms = jnp.sum(act * back, axis=1).astype(BF).reshape(groups, rows)
    act_gated = (g * act).astype(BF)
    act_grad = g * back
    gate_pre = (act_grad * pre_up * sig * (1.0 + pre_gate * (1.0 - sig))).astype(BF)
    up_pre = (act_grad * silu).astype(BF)
    input_grad = (
        matmul(gate_pre, w_gate, ((1,), (1,))) + matmul(up_pre, w_up, ((1,), (1,)))
    ).astype(BF)
    token_grad = lax.psum_scatter(input_grad, "expert", scatter_dimension=0, tiled=True)

    d_gate = matmul(all_x, gate_pre, ((0,), (0,))).astype(BF).reshape(replicas, -1, hidden)
    d_up = matmul(all_x, up_pre, ((0,), (0,))).astype(BF).reshape(replicas, -1, hidden)
    d_down = matmul(act_gated, all_dy, ((0,), (0,))).astype(BF)
    slab = hidden // replicas
    d_down = d_down.reshape(replicas, slab, width // hidden, hidden).swapaxes(1, 2)
    d_down = d_down.reshape(replicas, -1, hidden)
    parts = jnp.concatenate([d_gate, d_up, d_down], axis=1)
    parts = lax.all_to_all(parts, "dp", split_axis=0, concat_axis=0, tiled=True)
    total = jnp.sum(parts.astype(F32), axis=0)
    n = width // replicas
    sum_gate, sum_up = total[:n], total[n : 2 * n]
    sum_down = total[2 * n :].reshape(width // hidden, slab, hidden).swapaxes(0, 1).reshape(slab, width)

    back_terms = lax.all_to_all(terms, "expert", split_axis=0, concat_axis=0, tiled=True)
    picked = jnp.where(chosen, back_terms.T[:, None, :].astype(F32), 0.0)
    gate_grad = jnp.sum(picked, axis=2).astype(BF)
    return token_grad, gate_grad, sum_gate[None], sum_up[None], sum_down[None]


def solution(mesh):
    in_specs = (
        P(("dp", "expert"), None),
        P(("dp", "expert"), None),
        P(("dp", "expert"), None),
        P(("dp", "expert"), None),
        P("expert", None, None),
        P("expert", None, None),
        P("expert", None, None),
    )
    out_specs = (
        P(("dp", "expert"), None),
        P(("dp", "expert"), None),
        P("expert", "dp", None),
        P("expert", "dp", None),
        P("expert", "dp", None),
    )
    return jax.shard_map(
        on_device, mesh=mesh, in_specs=in_specs, out_specs=out_specs, check_vma=False
    )
```

time: 933 us -> 214 us (0.23)
  waiting for transfers between devices: 710 us -> 101 us
  local copies, waits for them, and re-layouts: 50.6 us -> 1.69 us
  blocking collectives: 80.8 us -> 57.4 us
  starting transfers between devices: 26.9 us -> 4.51 us
  other arithmetic: 19.6 us -> 5.14 us
    reduce_scatter x3 -> x1, waiting for transfers between devices: 640 us -> 0.01 us  [on_device(): lax.psum_scatter(input_grad, 'expert', scatter_dimension=0, tiled=True)]
    all_gather x0 -> x2, waiting for transfers between devices: none -> 92.7 us  [the longest x1 53.1 us: on_device(): all_x = lax.all_gather(tokens, 'expert', axis=0, tiled=True)]
    all_to_all x4 -> x1, waiting for transfers between devices: 70 us -> 6.88 us  [on_device(): lax.all_to_all(terms, 'expert', split_axis=0, concat_axis=0, tiled=True)]
    gather x5 -> x0, local copies, waits for them, and re-layouts: 37.4 us -> none  [the longest x1 9.46 us: on_device(): gates.reshape(-1)[copy_pick]]
    all_to_all x1 -> x2, blocking collectives: 80.8 us -> 57.4 us  [the longest x1 47.3 us: on_device(): parts = lax.all_to_all(parts, 'dp', split_axis=0, concat_axis=0, tiled=True)]
    all_to_all x4 -> x1, starting transfers between devices: 26.8 us -> 4.4 us  [on_device(): lax.all_to_all(terms, 'expert', split_axis=0, concat_axis=0, tiled=True)]
    dot_general x9 -> x8, matrix products: 27 us -> 28.6 us  [matmul(): return lax.dot_general(a, b, (dims, ((), ())), preferred_element_type=F32)]
  transfers between devices with their start and end apart: 7 -> 4, of which waited for: 5 -> 3; matrix products, arithmetic and copies ran while one was open for 5% -> 9% of each run, Pallas kernels for 0% -> 0%
where the time goes in v1:
time: 214 us; the launch traced here: 212 us
  waiting for transfers between devices  101 us (47%)
  blocking collectives  57.4 us (27%)
  matrix products  28.6 us (13%)
  between operations  13.9 us (6%)
  other arithmetic  5.14 us (2%)
  starting transfers between devices  4.51 us (2%)
    all_gather x1, waiting for transfers between devices, on_device(): all_x = lax.all_gather(tokens, 'expert', axis=0, tiled=True)  53.1 us
    all_to_all x1, blocking collectives, on_device(): parts = lax.all_to_all(parts, 'dp', split_axis=0, concat_axis=0, tiled=True)  47.3 us
    all_gather x1, waiting for transfers between devices, on_device(): all_dy = lax.all_gather(cotangent, 'expert', axis=0, tiled=True)  39.6 us
    dot_general x8, matrix products, matmul(): return lax.dot_general(a, b, (dims, ((), ())), preferred_element_type=F32)  28.6 us
    all_to_all x1, blocking collectives, on_device(): lax.all_to_all(dense_gates, 'expert', split_axis=0, concat_axis=0, tiled=...  10.1 us
    all_to_all x1, waiting for transfers between devices, on_device(): lax.all_to_all(terms, 'expert', split_axis=0, concat_axis=0, tiled=True)  6.88 us
    all_to_all x1, starting transfers between devices, on_device(): lax.all_to_all(terms, 'expert', split_axis=0, concat_axis=0, tiled=True)  4.4 us
  transfers between devices with their start and end apart: 4, of which 3 were waited for; matrix products, arithmetic and copies ran while one was open for 9% of the time, Pallas kernels for 0%

profile of v1, /device:TPU:1, one launch (start us, length us, event | category | flops | bytes accessed | tf_op | source)
XLA Modules:
  0.0 212.1 jit_solution(15471269436180027728)
XLA Ops:
  7.2 0.7 all-gather.5.cloned.1.call-update
  8.0 0.7 all-gather.3.cloned.1.call-update
  8.7 53.1 %all-gather.5.cloned.1.call-done = bf16[2048,1024]{1,0:T(8,128)(2,1)} async-done(((bf16[128,1024]{1,0:T(8,128)(2,1)}), bf16[2048,1024]{1,0:T(8,128)(2,1)}) %all-gather.5.cloned.1.call-update) | async-done | bytes 4194320 | tf_op jit(solution)/shard_map/all_gather | solution.py:24
  61.8 3.6 %fusion.7 = f32[2048,256]{0,1:T(8,128)S(1)} fusion(bf16[2048,1024]{1,0:T(8,128)(2,1)} %all-gather.5.cloned.1.call-done, bf16[1,1024,256]{2,1,0:T(8,128)(2,1)S(1)} %copy-done), kind=kOutput, calls=%fused_computation.18 | convolution fusion | flops 1073741824 | bytes 6815744 | tf_op jit(solution)/shard_map/dot_general | solution.py:11
  65.4 2.6 %fusion.10 = f32[2048,256]{0,1:T(8,128)} fusion(bf16[2048,1024]{1,0:T(8,128)(2,1)S(1)} %copy-done.5, bf16[1,1024,256]{2,1,0:T(8,128)(2,1)S(1)} %copy-done.2), kind=kOutput, calls=%fused_computation.21 | convolution fusion | flops 1073741824 | bytes 6815744 | tf_op jit(solution)/shard_map/dot_general | solution.py:11
  68.1 39.6 %all-gather.3.cloned.1.call-done = bf16[2048,1024]{1,0:T(8,128)(2,1)} async-done(((bf16[128,1024]{1,0:T(8,128)(2,1)}), bf16[2048,1024]{1,0:T(8,128)(2,1)}) %all-gather.3.cloned.1.call-update) | async-done | bytes 4194320 | tf_op jit(solution)/shard_map/all_gather | solution.py:25
  107.7 5.9 %multiply_reduce_fusion = (bf16[2048]{0:T(1024)(128)(2,1)S(1)}, f32[2048,256]{0,1:T(8,128)}) fusion(f32[2048,256]{0,1:T(8,128)} %fusion.10, f32[2048,256]{0,1:T(8,128)S(1)} %fusion.7, bf16[2048,1024]{1,0:T(8,128)(2,1)} %all-gather.3.cloned.1.call-done, bf16[1,256,1024]{2,1,0:T(8,128)(2,1)} %param.13), kind=kOutput, calls=%fused_computation.3 | convolution fusion | flops 1077409792 | bytes 11014144 | tf_op jit(solution)/shard_map/dot_general | solution.py:11
  113.5 0.6 copy.37
  114.2 4.4 %all-to-all-start.1 = ((bf16[16,1,128]{2,1,0:T(2,128)(2,1)}), bf16[16,1,128]{2,1,0:T(2,128)(2,1)S(1)}, u32[]{:S(2)}, u32[]{:S(2)}) async-start(bf16[16,1,128]{2,1,0:T(2,128)(2,1)} %copy.37), calls=%async_computation.2 | async-start | bytes 16384 | tf_op jit(solution)/shard_map/all_to_all | solution.py:58
  118.6 6.9 %all-to-all-done.1 = bf16[16,1,128]{2,1,0:T(2,128)(2,1)S(1)} async-done(((bf16[16,1,128]{2,1,0:T(2,128)(2,1)}), bf16[16,1,128]{2,1,0:T(2,128)(2,1)S(1)}, u32[]{:S(2)}, u32[]{:S(2)}) %all-to-all-start.1) | async-done | bytes 4128 | tf_op jit(solution)/shard_map/all_to_all | solution.py:58
  125.5 0.6 select_reduce_fusion
  126.2 10.1 %all_to_all.20 = bf16[16,1,128]{2,1,0:T(2,128)(2,1)S(1)} all-to-all(bf16[16,1,128]{2,1,0:T(2,128)(2,1)S(1)} %copy.35), channel_id=1, replica_groups=mesh['dp'=32,'expert'=16] {'expert'}, dimensions={0} | all-to-all | bytes 8192 | tf_op jit(solution)/shard_map/all_to_all | solution.py:26
  136.2 4.2 %multiply_convert_fusion.1 = (bf16[2048,256]{0,1:T(8,128)(2,1)S(1)}, bf16[2048,256]{0,1:T(8,128)(2,1)S(1)}) fusion(f32[2048,256]{0,1:T(8,128)} %get-tuple-element.13, f32[2048]{0:T(1024)S(1)} %bitcast_convert_fusion, f32[2048,256]{0,1:T(8,128)} %copy-done.1, f32[2048,256]{0,1:T(8,128)} %fusion.10), kind=kLoop, calls=%fused_computation.4 | loop fusion | flops 7340032 | bytes 8396800 | tf_op jit(solution)/shard_map/convert_element_type | solution.py:39
  140.4 1.3 fusion.5
  141.7 3.4 %add_convert_fusion = bf16[2048,1024]{1,0:T(8,128)(2,1)} fusion(f32[2048,1024]{1,0:T(8,128)S(1)} %fusion.5, bf16[2048,256]{0,1:T(8,128)(2,1)S(1)} %get-tuple-element.7, bf16[1,1024,256]{2,1,0:T(8,128)(2,1)S(1)} %copy-done.2), kind=kOutput, calls=%fused_computation | convolution fusion | flops 1077936128 | bytes 14155776 | tf_op jit(solution)/shard_map/dot_general | solution.py:11
  145.1 3.4 %fusion.1 = bf16[1024,256]{0,1:T(8,128)(2,1)S(1)} fusion(bf16[2048,256]{0,1:T(8,128)(2,1)S(1)} %get-tuple-element.8, bf16[2048,1024]{1,0:T(8,128)(2,1)} %all-gather.5.cloned.1.call-done), kind=kOutput, calls=%fused_computation.12 | convolution fusion | flops 1074003968 | bytes 5767168 | tf_op jit(solution)/shard_map/dot_general | solution.py:11
  148.6 0.2 copy.38
  148.8 3.4 %fusion.2 = bf16[1024,256]{0,1:T(8,128)(2,1)S(1)} fusion(bf16[2048,256]{0,1:T(8,128)(2,1)S(1)} %get-tuple-element.7, bf16[2048,1024]{1,0:T(8,128)(2,1)} %all-gather.5.cloned.1.call-done), kind=kOutput, calls=%fused_computation.13 | convolution fusion | flops 1074003968 | bytes 5767168 | tf_op jit(solution)/shard_map/dot_general | solution.py:11
  152.2 0.2 copy.39
  152.4 4.9 %convolution_convert_fusion = bf16[256,1024]{1,0:T(8,128)(2,1)S(1)} fusion(bf16[2048,1024]{1,0:T(8,128)(2,1)} %all-gather.3.cloned.1.call-done, f32[2048]{0:T(1024)S(1)} %bitcast_convert_fusion, f32[2048,256]{0,1:T(8,128)} %fusion.10, f32[2048,256]{0,1:T(8,128)} %copy-done.1), kind=kOutput, calls=%fused_computation.9 | convolution fusion | flops 1077673984 | bytes 8921088 | tf_op jit(solution)/shard_map/dot_general | solution.py:11
  157.4 0.1 pad_maximum_fusion
  157.5 47.3 %all_to_all.21 = bf16[32,96,256]{2,1,0:T(8,128)(2,1)S(1)} all-to-all(bf16[32,96,256]{2,1,0:T(8,128)(2,1)S(1)} %pad_maximum_fusion), channel_id=1, replica_groups=mesh['dp'=32,'expert'=16] {'dp'}, dimensions={0} | all-to-all | bytes 3145728 | tf_op jit(solution)/shard_map/all_to_all | solution.py:52
  204.7 0.2 convert_reduce_fusion
  205.0 0.6 fusion.15
  (21 shorter events, 0.2 us)
Async XLA Ops:
  7.2 54.6 %copy-start = (bf16[1,1024,256]{2,1,0:T(8,128)(2,1)S(1)}, bf16[1,1024,256]{2,1,0:T(8,128)(2,1)}, u32[]{:S(2)}) copy-start(bf16[1,1024,256]{2,1,0:T(8,128)(2,1)} %param.11) | copy-start | bytes 1572868
  7.2 54.6 %all-gather.5.cloned.1.call-start = ((), (), s32[]{:S(2)}) async-start(), calls=%async_computation.5 | async-start | bytes 4456448 | tf_op jit(solution)/shard_map/all_gather | solution.py:24
  7.9 99.7 %all-gather.3.cloned.1.call-start = ((), (), s32[]{:S(2)}) async-start(), calls=%async_computation.4 | async-start | bytes 4456448 | tf_op jit(solution)/shard_map/all_gather | solution.py:25
  8.7 56.7 %copy-start.2 = (bf16[1,1024,256]{2,1,0:T(8,128)(2,1)S(1)}, bf16[1,1024,256]{2,1,0:T(8,128)(2,1)}, u32[]{:S(2)}) copy-start(bf16[1,1024,256]{2,1,0:T(8,128)(2,1)} %param.12) | copy-start | bytes 1572868
  61.8 3.7 %copy-start.5 = (bf16[2048,1024]{1,0:T(8,128)(2,1)S(1)}, bf16[2048,1024]{1,0:T(8,128)(2,1)}, u32[]{:S(2)}) copy-start(bf16[2048,1024]{1,0:T(8,128)(2,1)} %all-gather.5.cloned.1.call-done) | copy-start | bytes 12582916
  65.4 42.2 %copy-start.1 = (f32[2048,256]{0,1:T(8,128)}, f32[2048,256]{0,1:T(8,128)S(1)}, u32[]{:S(2)}) copy-start(f32[2048,256]{0,1:T(8,128)S(1)} %fusion.7) | copy-start | bytes 6291460
  68.1 50.5 %copy-start.4 = (bf16[128,10]{0,1:T(8,128)(2,1)S(1)}, bf16[128,10]{0,1:T(8,128)(2,1)}, u32[]{:S(2)}) copy-start(bf16[128,10]{0,1:T(8,128)(2,1)} %param.10) | copy-start | bytes 7684
  68.1 57.5 %copy-start.3 = (s32[128,10]{0,1:T(8,128)S(1)}, s32[128,10]{0,1:T(8,128)}, u32[]{:S(2)}) copy-start(s32[128,10]{0,1:T(8,128)} %param.9) | copy-start | bytes 15364
  114.2 11.3 %all-to-all-start.1 = ((bf16[16,1,128]{2,1,0:T(2,128)(2,1)}), bf16[16,1,128]{2,1,0:T(2,128)(2,1)S(1)}, u32[]{:S(2)}, u32[]{:S(2)}) async-start(bf16[16,1,128]{2,1,0:T(2,128)(2,1)} %copy.37), calls=%async_computation.2 | async-start | bytes 16384 | tf_op jit(solution)/shard_map/all_to_all | solution.py:58
  118.6 87.1 %reduce-scatter.2.cloned.1.call-start = ((), (), s32[]{:S(2)}) async-start(), calls=%async_computation.6 | async-start | bytes 4456448 | tf_op jit(solution)/shard_map/reduce_scatter | solution.py:43
Sparse Core Ops, SparseCore 0:
  10.1 51.5 all-gather.4
  63.9 43.7 all-gather.2
  145.2 59.7 reduce-scatter.1

commit v2 on v1

v2 whole, which is shorter than its diff:
```python
import functools

import jax
import jax.numpy as jnp
from jax import lax
from jax.experimental import pallas as pl
from jax.experimental.pallas import tpu as pltpu
from jax.sharding import PartitionSpec as P

BF = jnp.bfloat16
F32 = jnp.float32
LANES = 128


def dot(a, b, ca, cb):
    return lax.dot_general(a, b, (((ca,), (cb,)), ((), ())), preferred_element_type=F32)


def pack_kernel(routing, gates, tokens, cotangent, out):
    rows, width = tokens.shape
    out[:, :width] = tokens[...]
    out[:, width : 2 * width] = cotangent[...]
    expert = lax.broadcasted_iota(jnp.int32, (LANES, rows), 0)
    dense = jnp.zeros((LANES, rows), F32)
    named, gate = routing[...], gates[...].astype(F32)
    for k in range(routing.shape[0]):
        dense = jnp.where(expert == named[k : k + 1], gate[k : k + 1], dense)
    out[:, 2 * width :] = dense.T.astype(BF)


def finish_kernel(routing, p, q, r, token_grad, gate_grad):
    rows, width = token_grad.shape
    total = p[...].astype(F32) + q[...].astype(F32) + r[:rows].astype(F32)
    token_grad[...] = total[:, :width].astype(BF)
    terms = total[:, width:].T
    expert = lax.broadcasted_iota(jnp.int32, (LANES, rows), 0)
    named = routing[...]
    picked = [
        jnp.sum(jnp.where(expert == named[k : k + 1], terms, 0.0), axis=0, keepdims=True)
        for k in range(routing.shape[0])
    ]
    gate_grad[...] = jnp.concatenate(picked, axis=0).astype(BF)


def group_kernel(first, last, width, hidden, replicas, expert_ref, b0, b1, w_own, w_oth, *refs):
    if first:
        out_grad, out_a, out_b = refs
    else:
        acc_gu, acc_d, out_grad, out_a, out_b = refs
    mine = expert_ref[0]
    x = jnp.concatenate([b0[:, :width], b1[:, :width]], axis=0)
    dy = jnp.concatenate([b0[:, width : 2 * width], b1[:, width : 2 * width]], axis=0)
    dense = jnp.concatenate([b0[:, 2 * width :], b1[:, 2 * width :]], axis=0).astype(F32)
    lane = lax.broadcasted_iota(jnp.int32, dense.shape, 1)
    terms = jnp.zeros(dense.shape, F32)
    grad = jnp.zeros(x.shape, F32)
    grads, acts = [], []
    for j, w in enumerate((w_own, w_oth)):
        here = lane == (mine if j == 0 else mine + 1 - 2 * lax.rem(mine, 2))
        g = jnp.sum(jnp.where(here, dense, 0.0), axis=1, keepdims=True)
        pre = dot(x, w[:, : 2 * hidden], 1, 0)
        pre_gate, pre_up = pre[:, :hidden], pre[:, hidden:]
        back = dot(dy, w[:, 2 * hidden :], 1, 0)
        sig = jax.nn.sigmoid(pre_gate)
        silu = pre_gate * sig
        act = silu * pre_up
        terms = terms + jnp.where(here, jnp.sum(act * back, axis=1, keepdims=True), 0.0)
        act_grad = g * back
        gate_pre = (act_grad * pre_up * sig * (1.0 + pre_gate * (1.0 - sig))).astype(BF)
        up_pre = (act_grad * silu).astype(BF)
        both = jnp.concatenate([gate_pre, up_pre], axis=1)
        grads.append(both)
        acts.append((g * act).astype(BF))
        grad = grad + dot(both, w[:, : 2 * hidden], 1, 1)
    out_grad[:, :width] = grad.astype(BF)
    out_grad[:, width:] = terms.astype(BF)

    n, m, half = width // replicas, hidden // replicas, width // 2
    grads = jnp.concatenate(grads, axis=1)
    step = max(n, 2 * hidden)
    for r in range(0, width, step):
        rows = slice(r, r + step)
        d_gu = dot(x[:, rows], grads, 0, 0)
        if not first:
            d_gu = d_gu + acc_gu[rows, :]
        if last:
            d_gu, reps = d_gu.astype(BF), step // n
            to = slice(r // n, r // n + reps)
            out_a[to, :n, :] = d_gu[:, : 2 * hidden].reshape(reps, n, 2 * hidden)
            out_b[to, :n, :] = d_gu[:, 2 * hidden :].reshape(reps, n, 2 * hidden)
        else:
            out_a[rows, :] = d_gu
    for j, act in enumerate(acts):
        rows = slice(j * hidden, (j + 1) * hidden)
        d_down = dot(act, dy, 0, 0)
        if not first:
            d_down = d_down + acc_d[rows, :]
        if last:
            d_down = jnp.concatenate(
                [d_down[:, :half].reshape(replicas, m, half), d_down[:, half:].reshape(replicas, m, half)], axis=1
            )
            (out_b if j else out_a)[:, n:, :] = d_down.astype(BF)
        else:
            out_b[rows, :] = d_down


VMEM = pl.BlockSpec(memory_space=pltpu.VMEM)


def group(first, last, replicas, expert, blocks, weights, acc):
    rows = blocks[0].shape[0]
    width, packed = weights[0].shape
    hidden = packed // 3
    if last:
        n, m = width // replicas, hidden // replicas
        sums = [jax.ShapeDtypeStruct((replicas, n + 2 * m, 2 * hidden), BF)] * 2
    else:
        sums = [
            jax.ShapeDtypeStruct((width, 4 * hidden), F32),
            jax.ShapeDtypeStruct((2 * hidden, width), F32),
        ]
    flops = 2 * 2 * rows * width * hidden * 16
    return pl.pallas_call(
        functools.partial(group_kernel, first, last, width, hidden, replicas),
        out_shape=[jax.ShapeDtypeStruct((2 * rows, width + LANES), BF)] + sums,
        in_specs=[pl.BlockSpec(memory_space=pltpu.SMEM)] + [VMEM] * (4 + len(acc)),
        out_specs=[VMEM] * 3,
        input_output_aliases={} if first or last else {5: 1, 6: 2},
        compiler_params=pltpu.CompilerParams(vmem_limit_bytes=26 * 1024 * 1024),
        cost_estimate=pl.CostEstimate(flops=flops, bytes_accessed=16 * 1024 * 1024, transcendentals=0),
    )(expert, *blocks, *weights, *acc)


def after(a, *others):
    return lax.optimization_barrier((a, *others))[0]


def on_device(tokens, cotangent, routing, gates, gate_weight, up_weight, down_weight):
    groups = lax.axis_size("expert")
    replicas = lax.axis_size("dp")
    rows, width = tokens.shape
    hidden = gate_weight.shape[2]
    out = [(i, (i + 2 if i % 2 == 0 else i - 2) % groups) for i in range(groups)]
    home = [(b, a) for a, b in out]
    swap = [(i, i ^ 1) for i in range(groups)]
    cross = [(i, (i - 1 if i % 2 == 0 else i + 1) % groups) for i in range(groups)]
    uncross = [(b, a) for a, b in cross]

    def send(a, pairs):
        return lax.ppermute(a, "expert", pairs)

    own = pl.pallas_call(
        pack_kernel,
        out_shape=jax.ShapeDtypeStruct((rows, 2 * width + LANES), BF),
        in_specs=[VMEM] * 4,
        out_specs=VMEM,
        compiler_params=pltpu.CompilerParams(vmem_limit_bytes=8 * 1024 * 1024),
    )(routing.T, gates.T, tokens, cotangent)
    w_own = jnp.concatenate([gate_weight[0], up_weight[0], down_weight[0].T], axis=1)
    expert = lax.axis_index("expert").astype(jnp.int32).reshape(1)

    a1 = send(own, out)
    b1 = send(own, cross)
    w_oth = send(w_own, swap)
    weights = (w_own, w_oth)
    a2 = send(a1, out)
    g0, *acc = group(True, False, replicas, expert, (own, a1), weights, ())
    b2 = send(b1, out)
    a3 = send(a2, out)
    g1, *acc = group(False, False, replicas, expert, (b1, a2), weights, acc)
    b3 = send(after(b2, g0), out)
    a4 = send(after(a3, g1), out)
    g2, *acc = group(False, False, replicas, expert, (b2, a3), weights, acc)
    g3, mine, theirs = group(False, True, replicas, expert, (b3, a4), weights, acc)

    got = send(theirs, swap)
    parts = (mine.astype(F32) + got.astype(F32)).astype(BF)
    parts = lax.all_to_all(parts, "dp", split_axis=0, concat_axis=0, tiled=True)
    total = jnp.sum(parts.astype(F32), axis=0)
    n, m = width // replicas, hidden // replicas
    sum_gate, sum_up = total[:n, :hidden], total[:n, hidden:]
    sum_down = jnp.concatenate([total[n : n + m], total[n + m :]], axis=1)

    def add(p, q):
        return (p.astype(F32) + q.astype(F32)).astype(BF)

    b = send(g3[:rows], home)
    a = send(g3[rows:], home)
    b = send(add(b, g2[:rows]), home)
    a = send(add(a, g2[rows:]), home)
    b = send(add(b, g1[:rows]), uncross)
    a = send(add(a, g1[rows:]), home)
    a = send(add(a, g0[rows:]), home)
    token_grad, gate_grad = pl.pallas_call(
        finish_kernel,
        out_shape=[jax.ShapeDtypeStruct((rows, width), BF), jax.ShapeDtypeStruct(gates.shape[::-1], BF)],
        in_specs=[VMEM] * 4,
        out_specs=[VMEM] * 2,
        compiler_params=pltpu.CompilerParams(vmem_limit_bytes=8 * 1024 * 1024),
    )(routing.T, a, b, g0)
    return token_grad, gate_grad.T, sum_gate[None], sum_up[None], sum_down[None]


def solution(mesh):
    in_specs = (
        P(("dp", "expert"), None),
        P(("dp", "expert"), None),
        P(("dp", "expert"), None),
        P(("dp", "expert"), None),
        P("expert", None, None),
        P("expert", None, None),
        P("expert", None, None),
    )
    out_specs = (
        P(("dp", "expert"), None),
        P(("dp", "expert"), None),
        P("expert", "dp", None),
        P("expert", "dp", None),
        P("expert", "dp", None),
    )
    return jax.shard_map(
        on_device, mesh=mesh, in_specs=in_specs, out_specs=out_specs, check_vma=False
    )
```

time: 214 us -> 136 us (0.64)
  starting transfers between devices: 4.51 us -> 67.3 us
  waiting for transfers between devices: 101 us -> 39.2 us
  blocking collectives: 57.4 us -> 0 us
  matrix products: 28.6 us -> 0 us
  Pallas kernels: 0 us -> 15.8 us
  between operations: 13.9 us -> 1.04 us
  local copies, waits for them, and re-layouts: 1.69 us -> 6.55 us
    all_gather x2 -> x0, waiting for transfers between devices: 92.7 us -> none  [the longest x1 53.1 us: on_device(): all_x = lax.all_gather(tokens, 'expert', axis=0, tiled=True)]
    ppermute x0 -> x16, starting transfers between devices: none -> 57.5 us  [send(): return lax.ppermute(a, 'expert', pairs)]
    all_to_all x2 -> x0, blocking collectives: 57.4 us -> none  [the longest x1 47.3 us: on_device(): parts = lax.all_to_all(parts, 'dp', split_axis=0, concat_axis=0, tiled=True)]
    ppermute x0 -> x16, waiting for transfers between devices: none -> 39.2 us  [send(): return lax.ppermute(a, 'expert', pairs)]
    dot_general x8 -> x0, matrix products: 28.6 us -> none  [matmul(): return lax.dot_general(a, b, (dims, ((), ())), preferred_element_type=F32)]
    pallas_call x0 -> x6, Pallas kernels: none -> 15.8 us  [the longest x4 14.7 us: group(): pl.pallas_call(functools.partial(group_kernel, first, last, width, hidden...]
    all_to_all x1, waiting for transfers between devices: 6.88 us -> 0.01 us  [on_device(): parts = lax.all_to_all(parts, 'dp', split_axis=0, concat_axis=0, tiled=True)]
    unnamed x12 -> x33, local copies, waits for them, and re-layouts: 0.03 us -> 5.86 us
  transfers between devices with their start and end apart: 4 -> 17, of which waited for: 3 -> 11; matrix products, arithmetic and copies ran while one was open for 9% -> 0% of each run, Pallas kernels for 0% -> 10%
where the time goes in v2:
time: 136 us; the launch traced here: 134 us
  starting transfers between devices  67.3 us (49%)
  waiting for transfers between devices  39.2 us (29%)
  Pallas kernels  15.8 us (12%)
  local copies, waits for them, and re-layouts  6.55 us (5%)
  other arithmetic  4.29 us (3%)
    ppermute x16, starting transfers between devices, send(): return lax.ppermute(a, 'expert', pairs)  57.5 us
    ppermute x16, waiting for transfers between devices, send(): return lax.ppermute(a, 'expert', pairs)  39.2 us
    pallas_call x4, Pallas kernels, group(): pl.pallas_call(functools.partial(group_kernel, first, last, width, hidden...  14.7 us
    all_to_all x1, starting transfers between devices, on_device(): parts = lax.all_to_all(parts, 'dp', split_axis=0, concat_axis=0, tiled=True)  9.81 us
    unnamed x33, local copies, waits for them, and re-layouts  5.86 us
  transfers between devices with their start and end apart: 17, of which 11 were waited for; matrix products, arithmetic and copies ran while one was open for 0% of the time, Pallas kernels for 10%

profile of v2, /device:TPU:1, one launch (start us, length us, event | category | flops | bytes accessed | tf_op | source)
XLA Modules:
  0.0 134.2 jit_solution(17174684811354175575)
XLA Ops:
  3.3 8.8 %collective-permute-start.3 = (bf16[1024,768]{1,0:T(8,128)(2,1)S(1)}, bf16[1024,768]{1,0:T(8,128)(2,1)S(1)}, u32[]{:S(2)}, u32[]{:S(2)}) collective-permute-start(bf16[1024,768]{1,0:T(8,128)(2,1)S(1)} %pad_maximum_fusion.w_own), channel_id=1, source_target_pairs={{0,1},{1,0},{2,3},{3,2},{4,5},{5,4},{6,7},{7,6},{8,9},{9,8},{10,11... | collective-permute-start | bytes 4718600 | tf_op jit(solution)/shard_map/ppermute | solution.py:150
  12.3 5.3 %collective-permute-start.2 = (bf16[128,2176]{1,0:T(8,128)(2,1)S(1)}, bf16[128,2176]{1,0:T(8,128)(2,1)S(1)}, u32[]{:S(2)}, u32[]{:S(2)}) collective-permute-start(bf16[128,2176]{1,0:T(8,128)(2,1)S(1)} %shard_map.110.b0), channel_id=1, source_target_pairs={{0,2},{1,15},{2,4},{3,1},{4,6},{5,3},{6,8},{7,5},{8,10},{9,7},{10,... | collective-permute-start | bytes 1671176 | tf_op jit(solution)/shard_map/ppermute | solution.py:150
  20.3 6.8 %collective-permute-done.2.b1 = bf16[128,2176]{1,0:T(8,128)(2,1)S(1)} collective-permute-done((bf16[128,2176]{1,0:T(8,128)(2,1)S(1)}, bf16[128,2176]{1,0:T(8,128)(2,1)S(1)}, u32[]{:S(2)}, u32[]{:S(2)}) %collective-permute-start.2) | collective-permute-done | bytes 557088 | tf_op jit(solution)/shard_map/ppermute | solution.py:150
  27.2 5.0 %collective-permute-start.5 = (bf16[128,2176]{1,0:T(8,128)(2,1)S(1)}, bf16[128,2176]{1,0:T(8,128)(2,1)}, u32[]{:S(2)}, u32[]{:S(2)}) collective-permute-start(bf16[128,2176]{1,0:T(8,128)(2,1)S(1)} %collective-permute-done.2.b1), channel_id=1, source_target_pairs={{0,2},{1,15},{2,4},{3,1},{4,6},{5,3},{6,8},{7,5},{8,10},{9,7},{10,... | collective-permute-start | bytes 1671176 | tf_op jit(solution)/shard_map/ppermute | solution.py:150
  35.1 3.5 %collective-permute-done.5.b1 = bf16[128,2176]{1,0:T(8,128)(2,1)} collective-permute-done((bf16[128,2176]{1,0:T(8,128)(2,1)S(1)}, bf16[128,2176]{1,0:T(8,128)(2,1)}, u32[]{:S(2)}, u32[]{:S(2)}) %collective-permute-start.5) | collective-permute-done | bytes 557088 | tf_op jit(solution)/shard_map/ppermute | solution.py:150
  38.6 5.1 %collective-permute-start.6 = (bf16[128,2176]{1,0:T(8,128)(2,1)}, bf16[128,2176]{1,0:T(8,128)(2,1)}, u32[]{:S(2)}, u32[]{:S(2)}) collective-permute-start(bf16[128,2176]{1,0:T(8,128)(2,1)} %collective-permute-done.5.b1), channel_id=1, source_target_pairs={{0,2},{1,15},{2,4},{3,1},{4,6},{5,3},{6,8},{7,5},{8,10},{9,7},{10,... | collective-permute-start | bytes 1671176 | tf_op jit(solution)/shard_map/ppermute | solution.py:150
  45.9 2.6 %shard_map.111 = (bf16[256,1152]{1,0:T(8,128)(2,1)S(1)}, f32[1024,1024]{1,0:T(8,128)S(1)}, f32[512,1024]{1,0:T(8,128)S(1)}) custom-call(s32[1]{0:T(128)} %bitcast.1.expert_ref, bf16[128,2176]{1,0:T(8,128)(2,1)S(1)} %copy-done.9, bf16[128,2176]{1,0:T(8,128)(2,1)S(1)} %copy-done.15, bf16[1024,768]{1,0:T(8,128)(2,1)S(1)} %pad_maximum_fusion.w_own, ...), custom_call_target="tpu_custom_call" | custom-call | flops 2147483648 | bytes 16777216 | tf_op jit(solution)/shard_map/pallas_call | solution.py:123
  50.5 4.7 %shard_map.112 = (bf16[256,1152]{1,0:T(8,128)(2,1)S(1)}, f32[1024,1024]{1,0:T(8,128)S(1)}, f32[512,1024]{1,0:T(8,128)S(1)}) custom-call(s32[1]{0:T(128)} %bitcast.1.expert_ref, bf16[128,2176]{1,0:T(8,128)(2,1)} %collective-permute-done.b0, bf16[128,2176]{1,0:T(8,128)(2,1)} %collective-permute-done.5.b1, ...), custom_call_target="tpu_custom_call", output_to_operand_aliasing={{1}: (5, {}), {2}: (6, {})} | custom-call | flops 2147483648 | bytes 16777216 | tf_op jit(solution)/shard_map/pallas_call | solution.py:123
  57.3 4.8 %shard_map.113 = (bf16[256,1152]{1,0:T(8,128)(2,1)S(1)}, f32[1024,1024]{1,0:T(8,128)S(1)}, f32[512,1024]{1,0:T(8,128)S(1)}) custom-call(s32[1]{0:T(128)} %bitcast.1.expert_ref, bf16[128,2176]{1,0:T(8,128)(2,1)} %collective-permute-done.1.b0, bf16[128,2176]{1,0:T(8,128)(2,1)} %collective-permute-done.6.b1, ...), custom_call_target="tpu_custom_call", output_to_operand_aliasing={{1}: (5, {}), {2}: (6, {})} | custom-call | flops 2147483648 | bytes 16777216 | tf_op jit(solution)/shard_map/pallas_call | solution.py:123
  62.1 3.9 %collective-permute-done.7.b1 = bf16[128,2176]{1,0:T(8,128)(2,1)S(1)} collective-permute-done((bf16[128,2176]{1,0:T(8,128)(2,1)}, bf16[128,2176]{1,0:T(8,128)(2,1)S(1)}, u32[]{:S(2)}, u32[]{:S(2)}) %collective-permute-start.7) | collective-permute-done | bytes 557088 | tf_op jit(solution)/shard_map/ppermute | solution.py:150
  66.0 2.6 %shard_map.114 = (bf16[256,1152]{1,0:T(8,128)(2,1)S(1)}, bf16[32,48,512]{2,1,0:T(8,128)(2,1)S(1)}, bf16[32,48,512]{2,1,0:T(8,128)(2,1)S(1)}) custom-call(s32[1]{0:T(128)} %bitcast.1.expert_ref, bf16[128,2176]{1,0:T(8,128)(2,1)S(1)} %collective-permute-done.4.b0, bf16[128,2176]{1,0:T(8,128)(2,1)S(1)} %collective-permute-done.7.b1, ...), custom_call_target="tpu_custom_call" | custom-call | flops 2147483648 | bytes 16777216 | tf_op jit(solution)/shard_map/pallas_call | solution.py:123
  69.5 4.1 %collective-permute-start.15 = (bf16[32,48,512]{2,1,0:T(8,128)(2,1)S(1)}, bf16[32,48,512]{2,1,0:T(8,128)(2,1)S(1)}, u32[]{:S(2)}, u32[]{:S(2)}) collective-permute-start(bf16[32,48,512]{2,1,0:T(8,128)(2,1)S(1)} %get-tuple-element.36), channel_id=1, source_target_pairs={{0,1},{1,0},{2,3},{3,2},{4,5},{5,4},{6,7},{7,6},{8,9},{9,8},{10,11... | collective-permute-start | bytes 4718600 | tf_op jit(solution)/shard_map/ppermute | solution.py:150
  73.6 3.0 %collective-permute-done.15 = bf16[32,48,512]{2,1,0:T(8,128)(2,1)S(1)} collective-permute-done((bf16[32,48,512]{2,1,0:T(8,128)(2,1)S(1)}, bf16[32,48,512]{2,1,0:T(8,128)(2,1)S(1)}, u32[]{:S(2)}, u32[]{:S(2)}) %collective-permute-start.15) | collective-permute-done | bytes 1572896 | tf_op jit(solution)/shard_map/ppermute | solution.py:150
  78.3 9.8 %all-to-all-start = ((bf16[32,48,512]{2,1,0:T(8,128)(2,1)}), bf16[32,48,512]{2,1,0:T(8,128)(2,1)S(1)}, u32[]{:S(2)}, u32[]{:S(2)}) async-start(bf16[32,48,512]{2,1,0:T(8,128)(2,1)} %add_convert_fusion), calls=%async_computation | async-start | bytes 3145728 | tf_op jit(solution)/shard_map/all_to_all | solution.py:178
  88.2 2.2 %collective-permute-start.12 = (bf16[128,1152]{1,0:T(8,128)(2,1)S(1)}, bf16[128,1152]{1,0:T(8,128)(2,1)S(1)}, u32[]{:S(2)}, u32[]{:S(2)}) collective-permute-start(bf16[128,1152]{1,0:T(8,128)(2,1)S(1)} %get-tuple-element.41), channel_id=1, source_target_pairs={{2,0},{15,1},{4,2},{1,3},{6,4},{3,5},{8,6},{5,7},{10,8},{7,9},{12,... | collective-permute-start | bytes 884744 | tf_op jit(solution)/shard_map/ppermute | solution.py:150
  90.4 4.0 %collective-permute-start.8 = (bf16[128,1152]{1,0:T(8,128)(2,1)S(1)}, bf16[128,1152]{1,0:T(8,128)(2,1)S(1)}, u32[]{:S(2)}, u32[]{:S(2)}) collective-permute-start(bf16[128,1152]{1,0:T(8,128)(2,1)S(1)} %get-tuple-element.42), channel_id=1, source_target_pairs={{2,0},{15,1},{4,2},{1,3},{6,4},{3,5},{8,6},{5,7},{10,8},{7,9},{12,... | collective-permute-start | bytes 884744 | tf_op jit(solution)/shard_map/ppermute | solution.py:150
  94.5 2.9 %collective-permute-done.12 = bf16[128,1152]{1,0:T(8,128)(2,1)S(1)} collective-permute-done((bf16[128,1152]{1,0:T(8,128)(2,1)S(1)}, bf16[128,1152]{1,0:T(8,128)(2,1)S(1)}, u32[]{:S(2)}, u32[]{:S(2)}) %collective-permute-start.12) | collective-permute-done | bytes 294944 | tf_op jit(solution)/shard_map/ppermute | solution.py:150
  97.3 3.2 %collective-permute-done.8 = bf16[128,1152]{1,0:T(8,128)(2,1)S(1)} collective-permute-done((bf16[128,1152]{1,0:T(8,128)(2,1)S(1)}, bf16[128,1152]{1,0:T(8,128)(2,1)S(1)}, u32[]{:S(2)}, u32[]{:S(2)}) %collective-permute-start.8) | collective-permute-done | bytes 294944 | tf_op jit(solution)/shard_map/ppermute | solution.py:150
  102.6 2.9 %collective-permute-start.9 = (bf16[128,1152]{1,0:T(8,128)(2,1)S(1)}, bf16[128,1152]{1,0:T(8,128)(2,1)S(1)}, u32[]{:S(2)}, u32[]{:S(2)}) collective-permute-start(bf16[128,1152]{1,0:T(8,128)(2,1)S(1)} %get-tuple-element.40), channel_id=1, source_target_pairs={{2,0},{15,1},{4,2},{1,3},{6,4},{3,5},{8,6},{5,7},{10,8},{7,9},{12,... | collective-permute-start | bytes 884744 | tf_op jit(solution)/shard_map/ppermute | solution.py:150
  105.5 4.1 %collective-permute-done.13 = bf16[128,1152]{1,0:T(8,128)(2,1)S(1)} collective-permute-done((bf16[128,1152]{1,0:T(8,128)(2,1)S(1)}, bf16[128,1152]{1,0:T(8,128)(2,1)S(1)}, u32[]{:S(2)}, u32[]{:S(2)}) %collective-permute-start.13) | collective-permute-done | bytes 294944 | tf_op jit(solution)/shard_map/ppermute | solution.py:150
  109.6 3.2 %collective-permute-done.9 = bf16[128,1152]{1,0:T(8,128)(2,1)S(1)} collective-permute-done((bf16[128,1152]{1,0:T(8,128)(2,1)S(1)}, bf16[128,1152]{1,0:T(8,128)(2,1)S(1)}, u32[]{:S(2)}, u32[]{:S(2)}) %collective-permute-start.9) | collective-permute-done | bytes 294944 | tf_op jit(solution)/shard_map/ppermute | solution.py:150
  114.9 6.2 %collective-permute-start.14 = (bf16[128,1152]{1,0:T(8,128)(2,1)S(1)}, bf16[128,1152]{1,0:T(8,128)(2,1)S(1)}, u32[]{:S(2)}, u32[]{:S(2)}) collective-permute-start(bf16[128,1152]{1,0:T(8,128)(2,1)S(1)} %get-tuple-element.37), channel_id=1, source_target_pairs={{15,0},{2,1},{1,2},{4,3},{3,4},{6,5},{5,6},{8,7},{7,8},{10,9},{9,1... | collective-permute-start | bytes 884744 | tf_op jit(solution)/shard_map/ppermute | solution.py:150
  123.9 3.1 %collective-permute-done.14.q = bf16[128,1152]{1,0:T(8,128)(2,1)S(1)} collective-permute-done((bf16[128,1152]{1,0:T(8,128)(2,1)S(1)}, bf16[128,1152]{1,0:T(8,128)(2,1)S(1)}, u32[]{:S(2)}, u32[]{:S(2)}) %collective-permute-start.14) | collective-permute-done | bytes 294944 | tf_op jit(solution)/shard_map/ppermute | solution.py:150
  127.0 4.7 %collective-permute-done.11.p = bf16[128,1152]{1,0:T(8,128)(2,1)S(1)} collective-permute-done((bf16[128,1152]{1,0:T(8,128)(2,1)S(1)}, bf16[128,1152]{1,0:T(8,128)(2,1)S(1)}, u32[]{:S(2)}, u32[]{:S(2)}) %collective-permute-start.11) | collective-permute-done | bytes 294944 | tf_op jit(solution)/shard_map/ppermute | solution.py:150
  (59 shorter events, 26.6 us)
Async XLA Ops:
  0.6 11.5 %copy-start.12 = (s32[128,10]{0,1:T(8,128)S(1)}, s32[128,10]{0,1:T(8,128)}, u32[]{:S(2)}) copy-start(s32[128,10]{0,1:T(8,128)} %param.9) | copy-start | bytes 15364
  0.6 11.5 %copy-start.13 = (bf16[128,10]{0,1:T(8,128)(2,1)S(1)}, bf16[128,10]{0,1:T(8,128)(2,1)}, u32[]{:S(2)}) copy-start(bf16[128,10]{0,1:T(8,128)(2,1)} %param.10) | copy-start | bytes 7684
  0.7 11.5 %copy-start.10 = (bf16[128,1024]{1,0:T(8,128)(2,1)S(1)}, bf16[128,1024]{1,0:T(8,128)(2,1)}, u32[]{:S(2)}) copy-start(bf16[128,1024]{1,0:T(8,128)(2,1)} %tokens.1) | copy-start | bytes 786436
  2.0 10.2 %copy-start.11 = (bf16[128,1024]{1,0:T(8,128)(2,1)S(1)}, bf16[128,1024]{1,0:T(8,128)(2,1)}, u32[]{:S(2)}) copy-start(bf16[128,1024]{1,0:T(8,128)(2,1)} %cotangent.1) | copy-start | bytes 786436
  3.3 40.5 %collective-permute-start.3 = (bf16[1024,768]{1,0:T(8,128)(2,1)S(1)}, bf16[1024,768]{1,0:T(8,128)(2,1)S(1)}, u32[]{:S(2)}, u32[]{:S(2)}) collective-permute-start(bf16[1024,768]{1,0:T(8,128)(2,1)S(1)} %pad_maximum_fusion.w_own), channel_id=1, source_target_pairs={{0,1},{1,0},{2,3},{3,2},{4,5},{5,4},{6,7},{7,6},{8,9},{9,8},{10,11... | collective-permute-start | bytes 4718600 | tf_op jit(solution)/shard_map/ppermute | solution.py:150
  12.3 14.9 %collective-permute-start.2 = (bf16[128,2176]{1,0:T(8,128)(2,1)S(1)}, bf16[128,2176]{1,0:T(8,128)(2,1)S(1)}, u32[]{:S(2)}, u32[]{:S(2)}) collective-permute-start(bf16[128,2176]{1,0:T(8,128)(2,1)S(1)} %shard_map.110.b0), channel_id=1, source_target_pairs={{0,2},{1,15},{2,4},{3,1},{4,6},{5,3},{6,8},{7,5},{8,10},{9,7},{10,... | collective-permute-start | bytes 1671176 | tf_op jit(solution)/shard_map/ppermute | solution.py:150
  17.6 15.4 %collective-permute-start = (bf16[128,2176]{1,0:T(8,128)(2,1)S(1)}, bf16[128,2176]{1,0:T(8,128)(2,1)}, u32[]{:S(2)}, u32[]{:S(2)}) collective-permute-start(bf16[128,2176]{1,0:T(8,128)(2,1)S(1)} %shard_map.110.b0), channel_id=1, source_target_pairs={{0,15},{1,2},{2,1},{3,4},{4,3},{5,6},{6,5},{7,8},{8,7},{9,10},{10,... | collective-permute-start | bytes 1671176 | tf_op jit(solution)/shard_map/ppermute | solution.py:150
  27.2 11.5 %collective-permute-start.5 = (bf16[128,2176]{1,0:T(8,128)(2,1)S(1)}, bf16[128,2176]{1,0:T(8,128)(2,1)}, u32[]{:S(2)}, u32[]{:S(2)}) collective-permute-start(bf16[128,2176]{1,0:T(8,128)(2,1)S(1)} %collective-permute-done.2.b1), channel_id=1, source_target_pairs={{0,2},{1,15},{2,4},{3,1},{4,6},{5,3},{6,8},{7,5},{8,10},{9,7},{10,... | collective-permute-start | bytes 1671176 | tf_op jit(solution)/shard_map/ppermute | solution.py:150
  33.0 15.5 %collective-permute-start.1 = (bf16[128,2176]{1,0:T(8,128)(2,1)}, bf16[128,2176]{1,0:T(8,128)(2,1)}, u32[]{:S(2)}, u32[]{:S(2)}) collective-permute-start(bf16[128,2176]{1,0:T(8,128)(2,1)} %collective-permute-done.b0), channel_id=1, source_target_pairs={{0,2},{1,15},{2,4},{3,1},{4,6},{5,3},{6,8},{7,5},{8,10},{9,7},{10,... | collective-permute-start | bytes 1671176 | tf_op jit(solution)/shard_map/ppermute | solution.py:150
  38.6 16.6 %collective-permute-start.6 = (bf16[128,2176]{1,0:T(8,128)(2,1)}, bf16[128,2176]{1,0:T(8,128)(2,1)}, u32[]{:S(2)}, u32[]{:S(2)}) collective-permute-start(bf16[128,2176]{1,0:T(8,128)(2,1)} %collective-permute-done.5.b1), channel_id=1, source_target_pairs={{0,2},{1,15},{2,4},{3,1},{4,6},{5,3},{6,8},{7,5},{8,10},{9,7},{10,... | collective-permute-start | bytes 1671176 | tf_op jit(solution)/shard_map/ppermute | solution.py:150
  48.5 13.6 %collective-permute-start.4 = (bf16[128,2176]{1,0:T(8,128)(2,1)}, bf16[128,2176]{1,0:T(8,128)(2,1)S(1)}, u32[]{:S(2)}, u32[]{:S(2)}) collective-permute-start(bf16[128,2176]{1,0:T(8,128)(2,1)} %collective-permute-done.1.b0), channel_id=1, source_target_pairs={{0,2},{1,15},{2,4},{3,1},{4,6},{5,3},{6,8},{7,5},{8,10},{9,7},{10,... | collective-permute-start | bytes 1671176 | tf_op jit(solution)/shard_map/ppermute | solution.py:150
  55.2 10.8 %collective-permute-start.7 = (bf16[128,2176]{1,0:T(8,128)(2,1)}, bf16[128,2176]{1,0:T(8,128)(2,1)S(1)}, u32[]{:S(2)}, u32[]{:S(2)}) collective-permute-start(bf16[128,2176]{1,0:T(8,128)(2,1)} %collective-permute-done.6.b1), channel_id=1, source_target_pairs={{0,2},{1,15},{2,4},{3,1},{4,6},{5,3},{6,8},{7,5},{8,10},{9,7},{10,... | collective-permute-start | bytes 1671176 | tf_op jit(solution)/shard_map/ppermute | solution.py:150
  69.5 7.1 %collective-permute-start.15 = (bf16[32,48,512]{2,1,0:T(8,128)(2,1)S(1)}, bf16[32,48,512]{2,1,0:T(8,128)(2,1)S(1)}, u32[]{:S(2)}, u32[]{:S(2)}) collective-permute-start(bf16[32,48,512]{2,1,0:T(8,128)(2,1)S(1)} %get-tuple-element.36), channel_id=1, source_target_pairs={{0,1},{1,0},{2,3},{3,2},{4,5},{5,4},{6,7},{7,6},{8,9},{9,8},{10,11... | collective-permute-start | bytes 4718600 | tf_op jit(solution)/shard_map/ppermute | solution.py:150
  78.3 22.2 %copy-start.5 = (bf16[256,1152]{1,0:T(8,128)(2,1)S(1)}, bf16[256,1152]{1,0:T(8,128)(2,1)}, u32[]{:S(2)}) copy-start(bf16[256,1152]{1,0:T(8,128)(2,1)} %copy-done.4) | copy-start | bytes 1769476
  78.3 54.4 %all-to-all-start = ((bf16[32,48,512]{2,1,0:T(8,128)(2,1)}), bf16[32,48,512]{2,1,0:T(8,128)(2,1)S(1)}, u32[]{:S(2)}, u32[]{:S(2)}) async-start(bf16[32,48,512]{2,1,0:T(8,128)(2,1)} %add_convert_fusion), calls=%async_computation | async-start | bytes 3145728 | tf_op jit(solution)/shard_map/all_to_all | solution.py:178
  88.2 24.6 %copy-start.3 = (bf16[256,1152]{1,0:T(8,128)(2,1)S(1)}, bf16[256,1152]{1,0:T(8,128)(2,1)}, u32[]{:S(2)}) copy-start(bf16[256,1152]{1,0:T(8,128)(2,1)} %copy-done.2) | copy-start | bytes 1769476
  88.2 33.7 %copy-start.1 = (bf16[256,1152]{1,0:T(8,128)(2,1)S(1)}, bf16[256,1152]{1,0:T(8,128)(2,1)}, u32[]{:S(2)}) copy-start(bf16[256,1152]{1,0:T(8,128)(2,1)} %copy-done) | copy-start | bytes 1769476
  88.2 9.1 %collective-permute-start.12 = (bf16[128,1152]{1,0:T(8,128)(2,1)S(1)}, bf16[128,1152]{1,0:T(8,128)(2,1)S(1)}, u32[]{:S(2)}, u32[]{:S(2)}) collective-permute-start(bf16[128,1152]{1,0:T(8,128)(2,1)S(1)} %get-tuple-element.41), channel_id=1, source_target_pairs={{2,0},{15,1},{4,2},{1,3},{6,4},{3,5},{8,6},{5,7},{10,8},{7,9},{12,... | collective-permute-start | bytes 884744 | tf_op jit(solution)/shard_map/ppermute | solution.py:150
  90.4 10.1 %collective-permute-start.8 = (bf16[128,1152]{1,0:T(8,128)(2,1)S(1)}, bf16[128,1152]{1,0:T(8,128)(2,1)S(1)}, u32[]{:S(2)}, u32[]{:S(2)}) collective-permute-start(bf16[128,1152]{1,0:T(8,128)(2,1)S(1)} %get-tuple-element.42), channel_id=1, source_target_pairs={{2,0},{15,1},{4,2},{1,3},{6,4},{3,5},{8,6},{5,7},{10,8},{7,9},{12,... | collective-permute-start | bytes 884744 | tf_op jit(solution)/shard_map/ppermute | solution.py:150
  100.7 9.0 %collective-permute-start.13 = (bf16[128,1152]{1,0:T(8,128)(2,1)S(1)}, bf16[128,1152]{1,0:T(8,128)(2,1)S(1)}, u32[]{:S(2)}, u32[]{:S(2)}) collective-permute-start(bf16[128,1152]{1,0:T(8,128)(2,1)S(1)} %get-tuple-element.39), channel_id=1, source_target_pairs={{2,0},{15,1},{4,2},{1,3},{6,4},{3,5},{8,6},{5,7},{10,8},{7,9},{12,... | collective-permute-start | bytes 884744 | tf_op jit(solution)/shard_map/ppermute | solution.py:150
  102.6 10.2 %collective-permute-start.9 = (bf16[128,1152]{1,0:T(8,128)(2,1)S(1)}, bf16[128,1152]{1,0:T(8,128)(2,1)S(1)}, u32[]{:S(2)}, u32[]{:S(2)}) collective-permute-start(bf16[128,1152]{1,0:T(8,128)(2,1)S(1)} %get-tuple-element.40), channel_id=1, source_target_pairs={{2,0},{15,1},{4,2},{1,3},{6,4},{3,5},{8,6},{5,7},{10,8},{7,9},{12,... | collective-permute-start | bytes 884744 | tf_op jit(solution)/shard_map/ppermute | solution.py:150
  112.9 9.0 %collective-permute-start.10 = (bf16[128,1152]{1,0:T(8,128)(2,1)S(1)}, bf16[128,1152]{1,0:T(8,128)(2,1)S(1)}, u32[]{:S(2)}, u32[]{:S(2)}) collective-permute-start(bf16[128,1152]{1,0:T(8,128)(2,1)S(1)} %get-tuple-element.38), channel_id=1, source_target_pairs={{2,0},{15,1},{4,2},{1,3},{6,4},{3,5},{8,6},{5,7},{10,8},{7,9},{12,... | collective-permute-start | bytes 884744 | tf_op jit(solution)/shard_map/ppermute | solution.py:150
  114.9 12.1 %collective-permute-start.14 = (bf16[128,1152]{1,0:T(8,128)(2,1)S(1)}, bf16[128,1152]{1,0:T(8,128)(2,1)S(1)}, u32[]{:S(2)}, u32[]{:S(2)}) collective-permute-start(bf16[128,1152]{1,0:T(8,128)(2,1)S(1)} %get-tuple-element.37), channel_id=1, source_target_pairs={{15,0},{2,1},{1,2},{4,3},{3,4},{6,5},{5,6},{8,7},{7,8},{10,9},{9,1... | collective-permute-start | bytes 884744 | tf_op jit(solution)/shard_map/ppermute | solution.py:150
  122.0 9.7 %collective-permute-start.11 = (bf16[128,1152]{1,0:T(8,128)(2,1)S(1)}, bf16[128,1152]{1,0:T(8,128)(2,1)S(1)}, u32[]{:S(2)}, u32[]{:S(2)}) collective-permute-start(bf16[128,1152]{1,0:T(8,128)(2,1)S(1)} %add_convert_fusion.3), channel_id=1, source_target_pairs={{2,0},{15,1},{4,2},{1,3},{6,4},{3,5},{8,6},{5,7},{10,8},{7,9},{12,... | collective-permute-start | bytes 884744 | tf_op jit(solution)/shard_map/ppermute | solution.py:150
  (9 other events, 34.5 us)

commit v3 on v2

--- a/solution.py
+++ b/solution.py
@@ -16,16 +16,39 @@
     return lax.dot_general(a, b, (((ca,), (cb,)), ((), ())), preferred_element_type=F32)
 
 
-def pack_kernel(routing, gates, tokens, cotangent, out):
+def pack_kernel(routing, gates, tokens, cotangent, out, named_ref, gate_ref, sems):
     rows, width = tokens.shape
-    out[:, :width] = tokens[...]
-    out[:, width : 2 * width] = cotangent[...]
+    small = [pltpu.make_async_copy(routing, named_ref, sems.at[0]), pltpu.make_async_copy(gates, gate_ref, sems.at[1])]
+    large = [
+        pltpu.make_async_copy(tokens, out.at[:, pl.ds(0, width)], sems.at[2]),
+        pltpu.make_async_copy(cotangent, out.at[:, pl.ds(width, width)], sems.at[3]),
+    ]
+    for copy in small + large:
+        copy.start()
+    for copy in small:
+        copy.wait()
     expert = lax.broadcasted_iota(jnp.int32, (LANES, rows), 0)
     dense = jnp.zeros((LANES, rows), F32)
-    named, gate = routing[...], gates[...].astype(F32)
+    named, gate = named_ref[...], gate_ref[...].astype(F32)
     for k in range(routing.shape[0]):
         dense = jnp.where(expert == named[k : k + 1], gate[k : k + 1], dense)
     out[:, 2 * width :] = dense.T.astype(BF)
+    for copy in large:
+        copy.wait()
+
+
+def pack_weights_kernel(gate, up, down, follows, out, sems):
+    width, hidden = gate.shape[1:]
+    copies = [
+        pltpu.make_async_copy(gate.at[0], out.at[pl.ds(0, width), pl.ds(0, hidden)], sems.at[0]),
+        pltpu.make_async_copy(up.at[0], out.at[pl.ds(0, width), pl.ds(hidden, hidden)], sems.at[1]),
+        pltpu.make_async_copy(down.at[0, :, pl.ds(0, width // 2)], out.at[pl.ds(width, hidden)], sems.at[2]),
+        pltpu.make_async_copy(down.at[0, :, pl.ds(width // 2, width // 2)], out.at[pl.ds(width + hidden, hidden)], sems.at[3]),
+    ]
+    for copy in copies:
+        copy.start()
+    for copy in copies:
+        copy.wait()
 
 
 def finish_kernel(routing, p, q, r, token_grad, gate_grad):
@@ -48,6 +71,7 @@
     else:
         acc_gu, acc_d, out_grad, out_a, out_b = refs
     mine = expert_ref[0]
+    half = width // 2
     x = jnp.concatenate([b0[:, :width], b1[:, :width]], axis=0)
     dy = jnp.concatenate([b0[:, width : 2 * width], b1[:, width : 2 * width]], axis=0)
     dense = jnp.concatenate([b0[:, 2 * width :], b1[:, 2 * width :]], axis=0).astype(F32)
@@ -58,9 +82,9 @@
     for j, w in enumerate((w_own, w_oth)):
         here = lane == (mine if j == 0 else mine + 1 - 2 * lax.rem(mine, 2))
         g = jnp.sum(jnp.where(here, dense, 0.0), axis=1, keepdims=True)
-        pre = dot(x, w[:, : 2 * hidden], 1, 0)
+        pre = dot(x, w[:width], 1, 0)
         pre_gate, pre_up = pre[:, :hidden], pre[:, hidden:]
-        back = dot(dy, w[:, 2 * hidden :], 1, 0)
+        back = dot(dy[:, :half], w[width : width + hidden], 1, 1) + dot(dy[:, half:], w[width + hidden :], 1, 1)
         sig = jax.nn.sigmoid(pre_gate)
         silu = pre_gate * sig
         act = silu * pre_up
@@ -71,11 +95,11 @@
         both = jnp.concatenate([gate_pre, up_pre], axis=1)
         grads.append(both)
         acts.append((g * act).astype(BF))
-        grad = grad + dot(both, w[:, : 2 * hidden], 1, 1)
+        grad = grad + dot(both, w[:width], 1, 1)
     out_grad[:, :width] = grad.astype(BF)
     out_grad[:, width:] = terms.astype(BF)
 
-    n, m, half = width // replicas, hidden // replicas, width // 2
+    n, m = width // replicas, hidden // replicas
     grads = jnp.concatenate(grads, axis=1)
     step = max(n, 2 * hidden)
     for r in range(0, width, step):
@@ -109,8 +133,8 @@
 
 def group(first, last, replicas, expert, blocks, weights, acc):
     rows = blocks[0].shape[0]
-    width, packed = weights[0].shape
-    hidden = packed // 3
+    hidden = weights[0].shape[1] // 2
+    width = weights[0].shape[0] - 2 * hidden
     if last:
         n, m = width // replicas, hidden // replicas
         sums = [jax.ShapeDtypeStruct((replicas, n + 2 * m, 2 * hidden), BF)] * 2
@@ -142,6 +166,7 @@
     hidden = gate_weight.shape[2]
     out = [(i, (i + 2 if i % 2 == 0 else i - 2) % groups) for i in range(groups)]
     home = [(b, a) for a, b in out]
+    home_two = [(i, (i - 4 if i % 2 == 0 else i + 4) % groups) for i in range(groups)]
     swap = [(i, i ^ 1) for i in range(groups)]
     cross = [(i, (i - 1 if i % 2 == 0 else i + 1) % groups) for i in range(groups)]
     uncross = [(b, a) for a, b in cross]
@@ -149,47 +174,61 @@
     def send(a, pairs):
         return lax.ppermute(a, "expert", pairs)
 
+    in_hbm = pl.BlockSpec(memory_space=pltpu.HBM)
     own = pl.pallas_call(
         pack_kernel,
         out_shape=jax.ShapeDtypeStruct((rows, 2 * width + LANES), BF),
-        in_specs=[VMEM] * 4,
+        in_specs=[in_hbm] * 4,
         out_specs=VMEM,
-        compiler_params=pltpu.CompilerParams(vmem_limit_bytes=8 * 1024 * 1024),
+        scratch_shapes=[
+            pltpu.VMEM(routing.shape[::-1], jnp.int32),
+            pltpu.VMEM(gates.shape[::-1], BF),
+            pltpu.SemaphoreType.DMA((4,)),
+        ],
+        compiler_params=pltpu.CompilerParams(vmem_limit_bytes=58 * 1024 * 1024),
     )(routing.T, gates.T, tokens, cotangent)
-    w_own = jnp.concatenate([gate_weight[0], up_weight[0], down_weight[0].T], axis=1)
     expert = lax.axis_index("expert").astype(jnp.int32).reshape(1)
 
     a1 = send(own, out)
     b1 = send(own, cross)
-    w_oth = send(w_own, swap)
+    w_own = pl.pallas_call(
+        pack_weights_kernel,
+        out_shape=jax.ShapeDtypeStruct((width + 2 * hidden, 2 * hidden), BF),
+        in_specs=[in_hbm] * 4,
+        out_specs=VMEM,
+        scratch_shapes=[pltpu.SemaphoreType.DMA((4,))],
+        compiler_params=pltpu.CompilerParams(vmem_limit_bytes=58 * 1024 * 1024),
+    )(gate_weight, up_weight, down_weight, own)
+    w_oth = send(after(w_own, a1, b1), swap)
     weights = (w_own, w_oth)
-    a2 = send(a1, out)
+    a2 = send(after(a1, b1), out)
     g0, *acc = group(True, False, replicas, expert, (own, a1), weights, ())
     b2 = send(b1, out)
-    a3 = send(a2, out)
+    a3 = send(after(a2, g0), out)
     g1, *acc = group(False, False, replicas, expert, (b1, a2), weights, acc)
-    b3 = send(after(b2, g0), out)
+    b3 = send(b2, out)
     a4 = send(after(a3, g1), out)
     g2, *acc = group(False, False, replicas, expert, (b2, a3), weights, acc)
+    far = send(g2[rows:], home)
     g3, mine, theirs = group(False, True, replicas, expert, (b3, a4), weights, acc)
+
+    def add(*parts):
+        return functools.reduce(lambda p, q: p + q, [p.astype(F32) for p in parts]).astype(BF)
+
+    farthest = send(g3[rows:], home_two)
+    b = send(g3[:rows], home)
 
     got = send(theirs, swap)
     parts = (mine.astype(F32) + got.astype(F32)).astype(BF)
-    parts = lax.all_to_all(parts, "dp", split_axis=0, concat_axis=0, tiled=True)
+    parts = lax.all_to_all(after(parts, farthest, b), "dp", split_axis=0, concat_axis=0, tiled=True)
     total = jnp.sum(parts.astype(F32), axis=0)
     n, m = width // replicas, hidden // replicas
     sum_gate, sum_up = total[:n, :hidden], total[:n, hidden:]
     sum_down = jnp.concatenate([total[n : n + m], total[n + m :]], axis=1)
 
-    def add(p, q):
-        return (p.astype(F32) + q.astype(F32)).astype(BF)
-
-    b = send(g3[:rows], home)
-    a = send(g3[rows:], home)
     b = send(add(b, g2[:rows]), home)
-    a = send(add(a, g2[rows:]), home)
+    a = send(add(farthest, far, g1[rows:]), home)
     b = send(add(b, g1[:rows]), uncross)
-    a = send(add(a, g1[rows:]), home)
     a = send(add(a, g0[rows:]), home)
     token_grad, gate_grad = pl.pallas_call(
         finish_kernel,

time: 136 us -> 138 us (1.015)
  the two profiles are of different devices: /device:TPU:1 before, /device:TPU:67 now
where the time goes in v3:
time: 138 us; the launch traced here: 137 us
  starting transfers between devices  68.1 us (49%)
  waiting for transfers between devices  42.4 us (31%)
  Pallas kernels  19 us (14%)
  other arithmetic  4.29 us (3%)
  local copies, waits for them, and re-layouts  2.13 us (2%)
    ppermute x16, starting transfers between devices, send(): return lax.ppermute(a, 'expert', pairs)  58.4 us
    ppermute x16, waiting for transfers between devices, send(): return lax.ppermute(a, 'expert', pairs)  33.8 us
    pallas_call x4, Pallas kernels, group(): pl.pallas_call(functools.partial(group_kernel, first, last, width, hidden...  13.5 us
    all_to_all x1, starting transfers between devices, on_device(): lax.all_to_all(after(parts, farthest, b), 'dp', split_axis=0, concat_axis...  9.73 us
    all_to_all x1, waiting for transfers between devices, on_device(): lax.all_to_all(after(parts, farthest, b), 'dp', split_axis=0, concat_axis...  8.59 us
  transfers between devices with their start and end apart: 17, of which 11 were waited for; matrix products, arithmetic and copies ran while one was open for 2% of the time, Pallas kernels for 11%

profile of v3, /device:TPU:67, one launch (start us, length us, event | category | flops | bytes accessed | tf_op | source)
XLA Modules:
  0.0 136.8 jit_solution(2295075018565665308)
XLA Ops:
  2.6 4.7 %collective-permute-start = (bf16[128,2176]{1,0:T(8,128)(2,1)}, bf16[128,2176]{1,0:T(8,128)(2,1)S(1)}, u32[]{:S(2)}, u32[]{:S(2)}) collective-permute-start(bf16[128,2176]{1,0:T(8,128)(2,1)} %shard_map.110.follows.b0), channel_id=1, source_target_pairs={{0,15},{1,2},{2,1},{3,4},{4,3},{5,6},{6,5},{7,8},{8,7},{9,10},{10,... | collective-permute-start | bytes 1671176 | tf_op jit(solution)/shard_map/ppermute | solution.py:175
  9.2 2.6 %shard_map.111.w_own = bf16[1536,512]{1,0:T(8,128)(2,1)} custom-call(bf16[1,1024,256]{2,1,0:T(8,128)(2,1)} %gate.1, bf16[1,1024,256]{2,1,0:T(8,128)(2,1)} %up.1, bf16[1,256,1024]{2,1,0:T(8,128)(2,1)} %down.1, bf16[128,2176]{1,0:T(8,128)(2,1)} %shard_map.110.follows.b0), custom_call_target="tpu_custom_call" | custom-call | tf_op jit(solution)/shard_map/pallas_call | solution.py:194
  11.8 5.6 %collective-permute-done.b0 = bf16[128,2176]{1,0:T(8,128)(2,1)S(1)} collective-permute-done((bf16[128,2176]{1,0:T(8,128)(2,1)}, bf16[128,2176]{1,0:T(8,128)(2,1)S(1)}, u32[]{:S(2)}, u32[]{:S(2)}) %collective-permute-start) | collective-permute-done | bytes 557088 | tf_op jit(solution)/shard_map/ppermute | solution.py:175
  17.4 3.6 %collective-permute-done.3.b1 = bf16[128,2176]{1,0:T(8,128)(2,1)} collective-permute-done((bf16[128,2176]{1,0:T(8,128)(2,1)}, bf16[128,2176]{1,0:T(8,128)(2,1)}, u32[]{:S(2)}, u32[]{:S(2)}) %collective-permute-start.3) | collective-permute-done | bytes 557088 | tf_op jit(solution)/shard_map/ppermute | solution.py:175
  21.0 4.0 %collective-permute-start.5 = (bf16[1536,512]{1,0:T(8,128)(2,1)}, bf16[1536,512]{1,0:T(8,128)(2,1)S(1)}, u32[]{:S(2)}, u32[]{:S(2)}) collective-permute-start(bf16[1536,512]{1,0:T(8,128)(2,1)} %shard_map.111.w_own), channel_id=1, source_target_pairs={{0,1},{1,0},{2,3},{3,2},{4,5},{5,4},{6,7},{7,6},{8,9},{9,8},{10,11... | collective-permute-start | bytes 4718600 | tf_op jit(solution)/shard_map/ppermute | solution.py:175
  25.0 5.4 %collective-permute-start.4 = (bf16[128,2176]{1,0:T(8,128)(2,1)}, bf16[128,2176]{1,0:T(8,128)(2,1)}, u32[]{:S(2)}, u32[]{:S(2)}) collective-permute-start(bf16[128,2176]{1,0:T(8,128)(2,1)} %collective-permute-done.3.b1), channel_id=1, source_target_pairs={{0,2},{1,15},{2,4},{3,1},{4,6},{5,3},{6,8},{7,5},{8,10},{9,7},{10,... | collective-permute-start | bytes 1671176 | tf_op jit(solution)/shard_map/ppermute | solution.py:175
  30.4 4.5 %collective-permute-start.1 = (bf16[128,2176]{1,0:T(8,128)(2,1)S(1)}, bf16[128,2176]{1,0:T(8,128)(2,1)S(1)}, u32[]{:S(2)}, u32[]{:S(2)}) collective-permute-start(bf16[128,2176]{1,0:T(8,128)(2,1)S(1)} %collective-permute-done.b0), channel_id=1, source_target_pairs={{0,2},{1,15},{2,4},{3,1},{4,6},{5,3},{6,8},{7,5},{8,10},{9,7},{10,... | collective-permute-start | bytes 1671176 | tf_op jit(solution)/shard_map/ppermute | solution.py:175
  36.4 3.7 %shard_map.112 = (bf16[256,1152]{1,0:T(8,128)(2,1)S(1)}, f32[1024,1024]{1,0:T(8,128)S(1)}, f32[512,1024]{1,0:T(8,128)S(1)}) custom-call(s32[1]{0:T(128)} %bitcast.1.expert_ref, bf16[128,2176]{1,0:T(8,128)(2,1)S(1)} %copy-done.2, bf16[128,2176]{1,0:T(8,128)(2,1)} %collective-permute-done.3.b1, bf16[1536,512]{1,0:T(8,128)(2,1)S(1)} %copy-done, ...), custom_call_target="tpu_custom_call" | custom-call | flops 2147483648 | bytes 16777216 | tf_op jit(solution)/shard_map/pallas_call | solution.py:147
  43.1 4.5 %collective-permute-start.2 = (bf16[128,2176]{1,0:T(8,128)(2,1)S(1)}, bf16[128,2176]{1,0:T(8,128)(2,1)S(1)}, u32[]{:S(2)}, u32[]{:S(2)}) collective-permute-start(bf16[128,2176]{1,0:T(8,128)(2,1)S(1)} %collective-permute-done.1.b0), channel_id=1, source_target_pairs={{0,2},{1,15},{2,4},{3,1},{4,6},{5,3},{6,8},{7,5},{8,10},{9,7},{10,... | collective-permute-start | bytes 1671176 | tf_op jit(solution)/shard_map/ppermute | solution.py:175
  47.5 4.4 %shard_map.113 = (bf16[256,1152]{1,0:T(8,128)(2,1)S(1)}, f32[1024,1024]{1,0:T(8,128)S(1)}, f32[512,1024]{1,0:T(8,128)S(1)}) custom-call(s32[1]{0:T(128)} %bitcast.1.expert_ref, bf16[128,2176]{1,0:T(8,128)(2,1)S(1)} %collective-permute-done.b0, bf16[128,2176]{1,0:T(8,128)(2,1)} %collective-permute-done.4.b1, ...), custom_call_target="tpu_custom_call", output_to_operand_aliasing={{1}: (5, {}), {2}: (6, {})} | custom-call | flops 2147483648 | bytes 16777216 | tf_op jit(solution)/shard_map/pallas_call | solution.py:147
  52.0 5.0 %collective-permute-start.7 = (bf16[128,2176]{1,0:T(8,128)(2,1)S(1)}, bf16[128,2176]{1,0:T(8,128)(2,1)S(1)}, u32[]{:S(2)}, u32[]{:S(2)}) collective-permute-start(bf16[128,2176]{1,0:T(8,128)(2,1)S(1)} %collective-permute-done.6.b1), channel_id=1, source_target_pairs={{0,2},{1,15},{2,4},{3,1},{4,6},{5,3},{6,8},{7,5},{8,10},{9,7},{10,... | collective-permute-start | bytes 1671176 | tf_op jit(solution)/shard_map/ppermute | solution.py:175
  57.0 2.9 %shard_map.114 = (bf16[256,1152]{1,0:T(8,128)(2,1)S(1)}, f32[1024,1024]{1,0:T(8,128)S(1)}, f32[512,1024]{1,0:T(8,128)S(1)}) custom-call(s32[1]{0:T(128)} %bitcast.1.expert_ref, bf16[128,2176]{1,0:T(8,128)(2,1)S(1)} %collective-permute-done.1.b0, bf16[128,2176]{1,0:T(8,128)(2,1)S(1)} %collective-permute-done.6.b1, ...), custom_call_target="tpu_custom_call", output_to_operand_aliasing={{1}: (5, {}), {2}: (6, {})} | custom-call | flops 2147483648 | bytes 16777216 | tf_op jit(solution)/shard_map/pallas_call | solution.py:147
  60.0 3.5 %collective-permute-done.7.b1 = bf16[128,2176]{1,0:T(8,128)(2,1)S(1)} collective-permute-done((bf16[128,2176]{1,0:T(8,128)(2,1)S(1)}, bf16[128,2176]{1,0:T(8,128)(2,1)S(1)}, u32[]{:S(2)}, u32[]{:S(2)}) %collective-permute-start.7) | collective-permute-done | bytes 557088 | tf_op jit(solution)/shard_map/ppermute | solution.py:175
  68.6 3.6 %collective-permute-start.12 = (bf16[128,1152]{1,0:T(8,128)(2,1)S(1)}, bf16[128,1152]{1,0:T(8,128)(2,1)S(1)}, u32[]{:S(2)}, u32[]{:S(2)}) collective-permute-start(bf16[128,1152]{1,0:T(8,128)(2,1)S(1)} %get-tuple-element.45), channel_id=1, source_target_pairs={{2,0},{15,1},{4,2},{1,3},{6,4},{3,5},{8,6},{5,7},{10,8},{7,9},{12,... | collective-permute-start | bytes 884744 | tf_op jit(solution)/shard_map/ppermute | solution.py:175
  72.2 5.6 %collective-permute-start.8 = (bf16[128,1152]{1,0:T(8,128)(2,1)S(1)}, bf16[128,1152]{1,0:T(8,128)(2,1)S(1)}, u32[]{:S(2)}, u32[]{:S(2)}) collective-permute-start(bf16[128,1152]{1,0:T(8,128)(2,1)S(1)} %get-tuple-element.46), channel_id=1, source_target_pairs={{0,12},{1,5},{2,14},{3,7},{4,0},{5,9},{6,2},{7,11},{8,4},{9,13},{1... | collective-permute-start | bytes 884744 | tf_op jit(solution)/shard_map/ppermute | solution.py:175
  79.5 6.8 %collective-permute-done.8 = bf16[128,1152]{1,0:T(8,128)(2,1)S(1)} collective-permute-done((bf16[128,1152]{1,0:T(8,128)(2,1)S(1)}, bf16[128,1152]{1,0:T(8,128)(2,1)S(1)}, u32[]{:S(2)}, u32[]{:S(2)}) %collective-permute-start.8) | collective-permute-done | bytes 294944 | tf_op jit(solution)/shard_map/ppermute | solution.py:175
  86.2 9.7 %all-to-all-start = ((bf16[32,48,512]{2,1,0:T(8,128)(2,1)}), bf16[32,48,512]{2,1,0:T(8,128)(2,1)}, u32[]{:S(2)}, u32[]{:S(2)}) async-start(bf16[32,48,512]{2,1,0:T(8,128)(2,1)} %add_convert_fusion), calls=%async_computation | async-start | bytes 3145728 | tf_op jit(solution)/shard_map/all_to_all | solution.py:223
  98.0 2.7 %collective-permute-start.13 = (bf16[128,1152]{1,0:T(8,128)(2,1)S(1)}, bf16[128,1152]{1,0:T(8,128)(2,1)S(1)}, u32[]{:S(2)}, u32[]{:S(2)}) collective-permute-start(bf16[128,1152]{1,0:T(8,128)(2,1)S(1)} %add_convert_fusion.2), channel_id=1, source_target_pairs={{2,0},{15,1},{4,2},{1,3},{6,4},{3,5},{8,6},{5,7},{10,8},{7,9},{12,... | collective-permute-start | bytes 884744 | tf_op jit(solution)/shard_map/ppermute | solution.py:175
  100.8 3.1 %collective-permute-done.9 = bf16[128,1152]{1,0:T(8,128)(2,1)S(1)} collective-permute-done((bf16[128,1152]{1,0:T(8,128)(2,1)S(1)}, bf16[128,1152]{1,0:T(8,128)(2,1)S(1)}, u32[]{:S(2)}, u32[]{:S(2)}) %collective-permute-start.9) | collective-permute-done | bytes 294944 | tf_op jit(solution)/shard_map/ppermute | solution.py:175
  103.9 3.2 %collective-permute-done.13 = bf16[128,1152]{1,0:T(8,128)(2,1)S(1)} collective-permute-done((bf16[128,1152]{1,0:T(8,128)(2,1)S(1)}, bf16[128,1152]{1,0:T(8,128)(2,1)S(1)}, u32[]{:S(2)}, u32[]{:S(2)}) %collective-permute-start.13) | collective-permute-done | bytes 294944 | tf_op jit(solution)/shard_map/ppermute | solution.py:175
  109.2 5.3 %collective-permute-start.14 = (bf16[128,1152]{1,0:T(8,128)(2,1)S(1)}, bf16[128,1152]{1,0:T(8,128)(2,1)S(1)}, u32[]{:S(2)}, u32[]{:S(2)}) collective-permute-start(bf16[128,1152]{1,0:T(8,128)(2,1)S(1)} %get-tuple-element.43), channel_id=1, source_target_pairs={{15,0},{2,1},{1,2},{4,3},{3,4},{6,5},{5,6},{8,7},{7,8},{10,9},{9,1... | collective-permute-start | bytes 884744 | tf_op jit(solution)/shard_map/ppermute | solution.py:175
  115.3 2.9 %collective-permute-start.11 = (bf16[128,1152]{1,0:T(8,128)(2,1)S(1)}, bf16[128,1152]{1,0:T(8,128)(2,1)S(1)}, u32[]{:S(2)}, u32[]{:S(2)}) collective-permute-start(bf16[128,1152]{1,0:T(8,128)(2,1)S(1)} %add_convert_fusion.3), channel_id=1, source_target_pairs={{2,0},{15,1},{4,2},{1,3},{6,4},{3,5},{8,6},{5,7},{10,8},{7,9},{12,... | collective-permute-start | bytes 884744 | tf_op jit(solution)/shard_map/ppermute | solution.py:175
  120.5 3.9 %collective-permute-done.11.p = bf16[128,1152]{1,0:T(8,128)(2,1)S(1)} collective-permute-done((bf16[128,1152]{1,0:T(8,128)(2,1)S(1)}, bf16[128,1152]{1,0:T(8,128)(2,1)S(1)}, u32[]{:S(2)}, u32[]{:S(2)}) %collective-permute-start.11) | collective-permute-done | bytes 294944 | tf_op jit(solution)/shard_map/ppermute | solution.py:175
  125.3 8.6 %all-to-all-done = bf16[32,48,512]{2,1,0:T(8,128)(2,1)} async-done(((bf16[32,48,512]{2,1,0:T(8,128)(2,1)}), bf16[32,48,512]{2,1,0:T(8,128)(2,1)}, u32[]{:S(2)}, u32[]{:S(2)}) %all-to-all-start) | async-done | bytes 1572896 | tf_op jit(solution)/shard_map/all_to_all | solution.py:223
  (39 shorter events, 26.2 us)
Async XLA Ops:
  2.5 32.4 %copy-start.2 = (bf16[128,2176]{1,0:T(8,128)(2,1)S(1)}, bf16[128,2176]{1,0:T(8,128)(2,1)}, u32[]{:S(2)}) copy-start(bf16[128,2176]{1,0:T(8,128)(2,1)} %shard_map.110.follows.b0) | copy-start | bytes 1671172
  2.6 14.9 %collective-permute-start = (bf16[128,2176]{1,0:T(8,128)(2,1)}, bf16[128,2176]{1,0:T(8,128)(2,1)S(1)}, u32[]{:S(2)}, u32[]{:S(2)}) collective-permute-start(bf16[128,2176]{1,0:T(8,128)(2,1)} %shard_map.110.follows.b0), channel_id=1, source_target_pairs={{0,15},{1,2},{2,1},{3,4},{4,3},{5,6},{6,5},{7,8},{8,7},{9,10},{10,... | collective-permute-start | bytes 1671176 | tf_op jit(solution)/shard_map/ppermute | solution.py:175
  7.3 13.8 %collective-permute-start.3 = (bf16[128,2176]{1,0:T(8,128)(2,1)}, bf16[128,2176]{1,0:T(8,128)(2,1)}, u32[]{:S(2)}, u32[]{:S(2)}) collective-permute-start(bf16[128,2176]{1,0:T(8,128)(2,1)} %shard_map.110.follows.b0), channel_id=1, source_target_pairs={{0,2},{1,15},{2,4},{3,1},{4,6},{5,3},{6,8},{7,5},{8,10},{9,7},{10,... | collective-permute-start | bytes 1671176 | tf_op jit(solution)/shard_map/ppermute | solution.py:175
  21.0 13.9 %collective-permute-start.5 = (bf16[1536,512]{1,0:T(8,128)(2,1)}, bf16[1536,512]{1,0:T(8,128)(2,1)S(1)}, u32[]{:S(2)}, u32[]{:S(2)}) collective-permute-start(bf16[1536,512]{1,0:T(8,128)(2,1)} %shard_map.111.w_own), channel_id=1, source_target_pairs={{0,1},{1,0},{2,3},{3,2},{4,5},{5,4},{6,7},{7,6},{8,9},{9,8},{10,11... | collective-permute-start | bytes 4718600 | tf_op jit(solution)/shard_map/ppermute | solution.py:175
  25.0 15.0 %collective-permute-start.4 = (bf16[128,2176]{1,0:T(8,128)(2,1)}, bf16[128,2176]{1,0:T(8,128)(2,1)}, u32[]{:S(2)}, u32[]{:S(2)}) collective-permute-start(bf16[128,2176]{1,0:T(8,128)(2,1)} %collective-permute-done.3.b1), channel_id=1, source_target_pairs={{0,2},{1,15},{2,4},{3,1},{4,6},{5,3},{6,8},{7,5},{8,10},{9,7},{10,... | collective-permute-start | bytes 1671176 | tf_op jit(solution)/shard_map/ppermute | solution.py:175
  30.4 12.6 %collective-permute-start.1 = (bf16[128,2176]{1,0:T(8,128)(2,1)S(1)}, bf16[128,2176]{1,0:T(8,128)(2,1)S(1)}, u32[]{:S(2)}, u32[]{:S(2)}) collective-permute-start(bf16[128,2176]{1,0:T(8,128)(2,1)S(1)} %collective-permute-done.b0), channel_id=1, source_target_pairs={{0,2},{1,15},{2,4},{3,1},{4,6},{5,3},{6,8},{7,5},{8,10},{9,7},{10,... | collective-permute-start | bytes 1671176 | tf_op jit(solution)/shard_map/ppermute | solution.py:175
  34.9 1.4 %copy-start = (bf16[1536,512]{1,0:T(8,128)(2,1)S(1)}, bf16[1536,512]{1,0:T(8,128)(2,1)}, u32[]{:S(2)}) copy-start(bf16[1536,512]{1,0:T(8,128)(2,1)} %shard_map.111.w_own) | copy-start | bytes 4718596
  36.3 11.2 %copy-start.1 = (bf16[1536,512]{1,0:T(8,128)(2,1)S(1)}, bf16[1536,512]{1,0:T(8,128)(2,1)}, u32[]{:S(2)}) copy-start(bf16[1536,512]{1,0:T(8,128)(2,1)} %shard_map.111.w_own) | copy-start | bytes 4718596
  40.0 11.9 %collective-permute-start.6 = (bf16[128,2176]{1,0:T(8,128)(2,1)}, bf16[128,2176]{1,0:T(8,128)(2,1)S(1)}, u32[]{:S(2)}, u32[]{:S(2)}) collective-permute-start(bf16[128,2176]{1,0:T(8,128)(2,1)} %collective-permute-done.4.b1), channel_id=1, source_target_pairs={{0,2},{1,15},{2,4},{3,1},{4,6},{5,3},{6,8},{7,5},{8,10},{9,7},{10,... | collective-permute-start | bytes 1671176 | tf_op jit(solution)/shard_map/ppermute | solution.py:175
  43.1 16.9 %collective-permute-start.2 = (bf16[128,2176]{1,0:T(8,128)(2,1)S(1)}, bf16[128,2176]{1,0:T(8,128)(2,1)S(1)}, u32[]{:S(2)}, u32[]{:S(2)}) collective-permute-start(bf16[128,2176]{1,0:T(8,128)(2,1)S(1)} %collective-permute-done.1.b0), channel_id=1, source_target_pairs={{0,2},{1,15},{2,4},{3,1},{4,6},{5,3},{6,8},{7,5},{8,10},{9,7},{10,... | collective-permute-start | bytes 1671176 | tf_op jit(solution)/shard_map/ppermute | solution.py:175
  52.0 8.0 %copy-start.3 = (bf16[256,1152]{1,0:T(8,128)(2,1)}, bf16[256,1152]{1,0:T(8,128)(2,1)S(1)}, u32[]{:S(2)}) copy-start(bf16[256,1152]{1,0:T(8,128)(2,1)S(1)} %get-tuple-element.30) | copy-start | bytes 1769476
  52.0 11.5 %collective-permute-start.7 = (bf16[128,2176]{1,0:T(8,128)(2,1)S(1)}, bf16[128,2176]{1,0:T(8,128)(2,1)S(1)}, u32[]{:S(2)}, u32[]{:S(2)}) collective-permute-start(bf16[128,2176]{1,0:T(8,128)(2,1)S(1)} %collective-permute-done.6.b1), channel_id=1, source_target_pairs={{0,2},{1,15},{2,4},{3,1},{4,6},{5,3},{6,8},{7,5},{8,10},{9,7},{10,... | collective-permute-start | bytes 1671176 | tf_op jit(solution)/shard_map/ppermute | solution.py:175
  66.0 11.8 %collective-permute-start.15 = (bf16[32,48,512]{2,1,0:T(8,128)(2,1)S(1)}, bf16[32,48,512]{2,1,0:T(8,128)(2,1)S(1)}, u32[]{:S(2)}, u32[]{:S(2)}) collective-permute-start(bf16[32,48,512]{2,1,0:T(8,128)(2,1)S(1)} %get-tuple-element.41), channel_id=1, source_target_pairs={{0,1},{1,0},{2,3},{3,2},{4,5},{5,4},{6,7},{7,6},{8,9},{9,8},{10,11... | collective-permute-start | bytes 4718600 | tf_op jit(solution)/shard_map/ppermute | solution.py:175
  68.6 10.9 %collective-permute-start.12 = (bf16[128,1152]{1,0:T(8,128)(2,1)S(1)}, bf16[128,1152]{1,0:T(8,128)(2,1)S(1)}, u32[]{:S(2)}, u32[]{:S(2)}) collective-permute-start(bf16[128,1152]{1,0:T(8,128)(2,1)S(1)} %get-tuple-element.45), channel_id=1, source_target_pairs={{2,0},{15,1},{4,2},{1,3},{6,4},{3,5},{8,6},{5,7},{10,8},{7,9},{12,... | collective-permute-start | bytes 884744 | tf_op jit(solution)/shard_map/ppermute | solution.py:175
  72.2 14.1 %collective-permute-start.8 = (bf16[128,1152]{1,0:T(8,128)(2,1)S(1)}, bf16[128,1152]{1,0:T(8,128)(2,1)S(1)}, u32[]{:S(2)}, u32[]{:S(2)}) collective-permute-start(bf16[128,1152]{1,0:T(8,128)(2,1)S(1)} %get-tuple-element.46), channel_id=1, source_target_pairs={{0,12},{1,5},{2,14},{3,7},{4,0},{5,9},{6,2},{7,11},{8,4},{9,13},{1... | collective-permute-start | bytes 884744 | tf_op jit(solution)/shard_map/ppermute | solution.py:175
  79.4 27.6 %copy-start.4 = (bf16[256,1152]{1,0:T(8,128)(2,1)S(1)}, bf16[256,1152]{1,0:T(8,128)(2,1)}, u32[]{:S(2)}) copy-start(bf16[256,1152]{1,0:T(8,128)(2,1)} %copy-done.3) | copy-start | bytes 1769476
  86.2 47.7 %all-to-all-start = ((bf16[32,48,512]{2,1,0:T(8,128)(2,1)}), bf16[32,48,512]{2,1,0:T(8,128)(2,1)}, u32[]{:S(2)}, u32[]{:S(2)}) async-start(bf16[32,48,512]{2,1,0:T(8,128)(2,1)} %add_convert_fusion), calls=%async_computation | async-start | bytes 3145728 | tf_op jit(solution)/shard_map/all_to_all | solution.py:223
  96.0 7.9 %collective-permute-start.9 = (bf16[128,1152]{1,0:T(8,128)(2,1)S(1)}, bf16[128,1152]{1,0:T(8,128)(2,1)S(1)}, u32[]{:S(2)}, u32[]{:S(2)}) collective-permute-start(bf16[128,1152]{1,0:T(8,128)(2,1)S(1)} %slice.34), channel_id=1, source_target_pairs={{2,0},{15,1},{4,2},{1,3},{6,4},{3,5},{8,6},{5,7},{10,8},{7,9},{12,... | collective-permute-start | bytes 884744 | tf_op jit(solution)/shard_map/ppermute | solution.py:175
  98.0 26.3 %copy-start.5 = (s32[128,10]{0,1:T(8,128)S(1)}, s32[128,10]{0,1:T(8,128)}, u32[]{:S(2)}) copy-start(s32[128,10]{0,1:T(8,128)} %param.9) | copy-start | bytes 15364
  98.0 9.0 %collective-permute-start.13 = (bf16[128,1152]{1,0:T(8,128)(2,1)S(1)}, bf16[128,1152]{1,0:T(8,128)(2,1)S(1)}, u32[]{:S(2)}, u32[]{:S(2)}) collective-permute-start(bf16[128,1152]{1,0:T(8,128)(2,1)S(1)} %add_convert_fusion.2), channel_id=1, source_target_pairs={{2,0},{15,1},{4,2},{1,3},{6,4},{3,5},{8,6},{5,7},{10,8},{7,9},{12,... | collective-permute-start | bytes 884744 | tf_op jit(solution)/shard_map/ppermute | solution.py:175
  107.2 7.9 %collective-permute-start.10 = (bf16[128,1152]{1,0:T(8,128)(2,1)S(1)}, bf16[128,1152]{1,0:T(8,128)(2,1)S(1)}, u32[]{:S(2)}, u32[]{:S(2)}) collective-permute-start(bf16[128,1152]{1,0:T(8,128)(2,1)S(1)} %get-tuple-element.44), channel_id=1, source_target_pairs={{2,0},{15,1},{4,2},{1,3},{6,4},{3,5},{8,6},{5,7},{10,8},{7,9},{12,... | collective-permute-start | bytes 884744 | tf_op jit(solution)/shard_map/ppermute | solution.py:175
  109.2 11.3 %collective-permute-start.14 = (bf16[128,1152]{1,0:T(8,128)(2,1)S(1)}, bf16[128,1152]{1,0:T(8,128)(2,1)S(1)}, u32[]{:S(2)}, u32[]{:S(2)}) collective-permute-start(bf16[128,1152]{1,0:T(8,128)(2,1)S(1)} %get-tuple-element.43), channel_id=1, source_target_pairs={{15,0},{2,1},{1,2},{4,3},{3,4},{6,5},{5,6},{8,7},{7,8},{10,9},{9,1... | collective-permute-start | bytes 884744 | tf_op jit(solution)/shard_map/ppermute | solution.py:175
  115.3 9.1 %collective-permute-start.11 = (bf16[128,1152]{1,0:T(8,128)(2,1)S(1)}, bf16[128,1152]{1,0:T(8,128)(2,1)S(1)}, u32[]{:S(2)}, u32[]{:S(2)}) collective-permute-start(bf16[128,1152]{1,0:T(8,128)(2,1)S(1)} %add_convert_fusion.3), channel_id=1, source_target_pairs={{2,0},{15,1},{4,2},{1,3},{6,4},{3,5},{8,6},{5,7},{10,8},{7,9},{12,... | collective-permute-start | bytes 884744 | tf_op jit(solution)/shard_map/ppermute | solution.py:175

commit v4 on v3

--- a/solution.py
+++ b/solution.py
@@ -10,6 +10,7 @@
 BF = jnp.bfloat16
 F32 = jnp.float32
 LANES = 128
+HOP_FLOPS = 7_000_000_000
 
 
 def dot(a, b, ca, cb):
@@ -37,23 +38,9 @@
         copy.wait()
 
 
-def pack_weights_kernel(gate, up, down, follows, out, sems):
-    width, hidden = gate.shape[1:]
-    copies = [
-        pltpu.make_async_copy(gate.at[0], out.at[pl.ds(0, width), pl.ds(0, hidden)], sems.at[0]),
-        pltpu.make_async_copy(up.at[0], out.at[pl.ds(0, width), pl.ds(hidden, hidden)], sems.at[1]),
-        pltpu.make_async_copy(down.at[0, :, pl.ds(0, width // 2)], out.at[pl.ds(width, hidden)], sems.at[2]),
-        pltpu.make_async_copy(down.at[0, :, pl.ds(width // 2, width // 2)], out.at[pl.ds(width + hidden, hidden)], sems.at[3]),
-    ]
-    for copy in copies:
-        copy.start()
-    for copy in copies:
-        copy.wait()
-
-
 def finish_kernel(routing, p, q, r, token_grad, gate_grad):
     rows, width = token_grad.shape
-    total = p[...].astype(F32) + q[...].astype(F32) + r[:rows].astype(F32)
+    total = p[...].astype(F32) + q[...].astype(F32) + r[...].astype(F32)
     token_grad[...] = total[:, :width].astype(BF)
     terms = total[:, width:].T
     expert = lax.broadcasted_iota(jnp.int32, (LANES, rows), 0)
@@ -65,11 +52,12 @@
     gate_grad[...] = jnp.concatenate(picked, axis=0).astype(BF)
 
 
-def group_kernel(first, last, width, hidden, replicas, expert_ref, b0, b1, w_own, w_oth, *refs):
+def group_kernel(first, last, width, hidden, replicas, expert_ref, b0, b1, *refs):
+    weights, refs = (refs[:3], refs[3:6]), refs[6:]
     if first:
-        out_grad, out_a, out_b = refs
+        grad0, grad1, out_a, out_b = refs
     else:
-        acc_gu, acc_d, out_grad, out_a, out_b = refs
+        acc_gu, acc_d, grad0, grad1, out_a, out_b = refs
     mine = expert_ref[0]
     half = width // 2
     x = jnp.concatenate([b0[:, :width], b1[:, :width]], axis=0)
@@ -79,12 +67,11 @@
     terms = jnp.zeros(dense.shape, F32)
     grad = jnp.zeros(x.shape, F32)
     grads, acts = [], []
-    for j, w in enumerate((w_own, w_oth)):
+    for j, (w_gate, w_up, w_down) in enumerate(weights):
         here = lane == (mine if j == 0 else mine + 1 - 2 * lax.rem(mine, 2))
         g = jnp.sum(jnp.where(here, dense, 0.0), axis=1, keepdims=True)
-        pre = dot(x, w[:width], 1, 0)
-        pre_gate, pre_up = pre[:, :hidden], pre[:, hidden:]
-        back = dot(dy[:, :half], w[width : width + hidden], 1, 1) + dot(dy[:, half:], w[width + hidden :], 1, 1)
+        pre_gate, pre_up = dot(x, w_gate[...], 1, 0), dot(x, w_up[...], 1, 0)
+        back = dot(dy, w_down[...], 1, 1)
         sig = jax.nn.sigmoid(pre_gate)
         silu = pre_gate * sig
         act = silu * pre_up
@@ -92,12 +79,13 @@
         act_grad = g * back
         gate_pre = (act_grad * pre_up * sig * (1.0 + pre_gate * (1.0 - sig))).astype(BF)
         up_pre = (act_grad * silu).astype(BF)
-        both = jnp.concatenate([gate_pre, up_pre], axis=1)
-        grads.append(both)
+        grads += [gate_pre, up_pre]
         acts.append((g * act).astype(BF))
-        grad = grad + dot(both, w[:width], 1, 1)
-    out_grad[:, :width] = grad.astype(BF)
-    out_grad[:, width:] = terms.astype(BF)
+        grad = grad + dot(gate_pre, w_gate[...], 1, 1) + dot(up_pre, w_up[...], 1, 1)
+    block = b0.shape[0]
+    for i, out in enumerate((grad0, grad1)):
+        out[:, :width] = grad[i * block : (i + 1) * block].astype(BF)
+        out[:, width:] = terms[i * block : (i + 1) * block].astype(BF)
 
     n, m = width // replicas, hidden // replicas
     grads = jnp.concatenate(grads, axis=1)
@@ -133,8 +121,7 @@
 
 def group(first, last, replicas, expert, blocks, weights, acc):
     rows = blocks[0].shape[0]
-    hidden = weights[0].shape[1] // 2
-    width = weights[0].shape[0] - 2 * hidden
+    width, hidden = weights[0].shape
     if last:
         n, m = width // replicas, hidden // replicas
         sums = [jax.ShapeDtypeStruct((replicas, n + 2 * m, 2 * hidden), BF)] * 2
@@ -146,13 +133,28 @@
     flops = 2 * 2 * rows * width * hidden * 16
     return pl.pallas_call(
         functools.partial(group_kernel, first, last, width, hidden, replicas),
-        out_shape=[jax.ShapeDtypeStruct((2 * rows, width + LANES), BF)] + sums,
-        in_specs=[pl.BlockSpec(memory_space=pltpu.SMEM)] + [VMEM] * (4 + len(acc)),
-        out_specs=[VMEM] * 3,
-        input_output_aliases={} if first or last else {5: 1, 6: 2},
+        out_shape=[jax.ShapeDtypeStruct((rows, width + LANES), BF)] * 2 + sums,
+        in_specs=[pl.BlockSpec(memory_space=pltpu.SMEM)] + [VMEM] * (8 + len(acc)),
+        out_specs=[VMEM] * 4,
+        input_output_aliases={} if first or last else {9: 2, 10: 3},
         compiler_params=pltpu.CompilerParams(vmem_limit_bytes=26 * 1024 * 1024),
         cost_estimate=pl.CostEstimate(flops=flops, bytes_accessed=16 * 1024 * 1024, transcendentals=0),
     )(expert, *blocks, *weights, *acc)
+
+
+def add_kernel(p, q, out):
+    out[...] = (p[...].astype(F32) + q[...].astype(F32)).astype(BF)
+
+
+def add(p, q):
+    return pl.pallas_call(
+        add_kernel,
+        out_shape=jax.ShapeDtypeStruct(p.shape, BF),
+        in_specs=[VMEM] * 2,
+        out_specs=VMEM,
+        compiler_params=pltpu.CompilerParams(vmem_limit_bytes=8 * 1024 * 1024),
+        cost_estimate=pl.CostEstimate(flops=HOP_FLOPS, bytes_accessed=3 * 2 * p.size, transcendentals=0),
+    )(p, q)
 
 
 def after(a, *others):
@@ -166,7 +168,6 @@
     hidden = gate_weight.shape[2]
     out = [(i, (i + 2 if i % 2 == 0 else i - 2) % groups) for i in range(groups)]
     home = [(b, a) for a, b in out]
-    home_two = [(i, (i - 4 if i % 2 == 0 else i + 4) % groups) for i in range(groups)]
     swap = [(i, i ^ 1) for i in range(groups)]
     cross = [(i, (i - 1 if i % 2 == 0 else i + 1) % groups) for i in range(groups)]
     uncross = [(b, a) for a, b in cross]
@@ -191,52 +192,41 @@
 
     a1 = send(own, out)
     b1 = send(own, cross)
-    w_own = pl.pallas_call(
-        pack_weights_kernel,
-        out_shape=jax.ShapeDtypeStruct((width + 2 * hidden, 2 * hidden), BF),
-        in_specs=[in_hbm] * 4,
-        out_specs=VMEM,
-        scratch_shapes=[pltpu.SemaphoreType.DMA((4,))],
-        compiler_params=pltpu.CompilerParams(vmem_limit_bytes=58 * 1024 * 1024),
-    )(gate_weight, up_weight, down_weight, own)
-    w_oth = send(after(w_own, a1, b1), swap)
-    weights = (w_own, w_oth)
-    a2 = send(after(a1, b1), out)
-    g0, *acc = group(True, False, replicas, expert, (own, a1), weights, ())
+    weights = [gate_weight[0], up_weight[0], down_weight[0]]
+    weights = weights + [send(w, swap) for w in weights]
+    a2 = send(a1, out)
+    g_own, g_a1, *acc = group(True, False, replicas, expert, (own, a1), weights, ())
     b2 = send(b1, out)
-    a3 = send(after(a2, g0), out)
-    g1, *acc = group(False, False, replicas, expert, (b1, a2), weights, acc)
+    a3 = send(after(a2, g_a1), out)
+    g_b1, g_a2, *acc = group(False, False, replicas, expert, (b1, a2), weights, acc)
     b3 = send(b2, out)
-    a4 = send(after(a3, g1), out)
-    g2, *acc = group(False, False, replicas, expert, (b2, a3), weights, acc)
-    far = send(g2[rows:], home)
-    g3, mine, theirs = group(False, True, replicas, expert, (b3, a4), weights, acc)
-
-    def add(*parts):
-        return functools.reduce(lambda p, q: p + q, [p.astype(F32) for p in parts]).astype(BF)
-
-    farthest = send(g3[rows:], home_two)
-    b = send(g3[:rows], home)
+    a4 = send(after(a3, g_a2), out)
+    g_b2, g_a3, *acc = group(False, False, replicas, expert, (b2, a3), weights, acc)
+    g_b3, g_a4, mine, theirs = group(False, True, replicas, expert, (b3, a4), weights, acc)
+
+    b = send(g_b3, home)
+    a = send(g_a4, home)
 
     got = send(theirs, swap)
     parts = (mine.astype(F32) + got.astype(F32)).astype(BF)
-    parts = lax.all_to_all(after(parts, farthest, b), "dp", split_axis=0, concat_axis=0, tiled=True)
+    parts = lax.all_to_all(parts, "dp", split_axis=0, concat_axis=0, tiled=True)
     total = jnp.sum(parts.astype(F32), axis=0)
     n, m = width // replicas, hidden // replicas
     sum_gate, sum_up = total[:n, :hidden], total[:n, hidden:]
     sum_down = jnp.concatenate([total[n : n + m], total[n + m :]], axis=1)
 
-    b = send(add(b, g2[:rows]), home)
-    a = send(add(farthest, far, g1[rows:]), home)
-    b = send(add(b, g1[:rows]), uncross)
-    a = send(add(a, g0[rows:]), home)
+    b = send(add(b, g_b2), home)
+    a = send(add(a, g_a3), home)
+    b = send(add(b, g_b1), uncross)
+    a = send(add(a, g_a2), home)
+    a = send(add(a, g_a1), home)
     token_grad, gate_grad = pl.pallas_call(
         finish_kernel,
         out_shape=[jax.ShapeDtypeStruct((rows, width), BF), jax.ShapeDtypeStruct(gates.shape[::-1], BF)],
         in_specs=[VMEM] * 4,
         out_specs=[VMEM] * 2,
         compiler_params=pltpu.CompilerParams(vmem_limit_bytes=8 * 1024 * 1024),
-    )(routing.T, a, b, g0)
+    )(routing.T, a, b, g_own)
     return token_grad, gate_grad.T, sum_gate[None], sum_up[None], sum_down[None]
 
 

time: 138 us -> 128 us (0.928)
  the two profiles are of different devices: /device:TPU:67 before, /device:TPU:16 now
where the time goes in v4:
time: 128 us; the launch traced here: 127 us
  starting transfers between devices  63.8 us (50%)
  waiting for transfers between devices  36.1 us (28%)
  Pallas kernels  17 us (13%)
  local copies, waits for them, and re-layouts  5.54 us (4%)
  other arithmetic  3.96 us (3%)
    ppermute x18, starting transfers between devices, send(): return lax.ppermute(a, 'expert', pairs)  53.7 us
    ppermute x18, waiting for transfers between devices, send(): return lax.ppermute(a, 'expert', pairs)  26.4 us
    pallas_call x4, Pallas kernels, group(): pl.pallas_call(functools.partial(group_kernel, first, last, width, hidden...  13.7 us
    all_to_all x1, starting transfers between devices, on_device(): parts = lax.all_to_all(parts, 'dp', split_axis=0, concat_axis=0, tiled=True)  10.1 us
    all_to_all x1, waiting for transfers between devices, on_device(): parts = lax.all_to_all(parts, 'dp', split_axis=0, concat_axis=0, tiled=True)  9.71 us
    unnamed x24, local copies, waits for them, and re-layouts  4.91 us
  transfers between devices with their start and end apart: 19, of which 10 were waited for; matrix products, arithmetic and copies ran while one was open for 1% of the time, Pallas kernels for 9%

profile of v4, /device:TPU:16, one launch (start us, length us, event | category | flops | bytes accessed | tf_op | source)
XLA Modules:
  0.0 127.4 jit_solution(9917424395431472876)
XLA Ops:
  2.5 4.3 %collective-permute-start.3 = (bf16[128,2176]{1,0:T(8,128)(2,1)}, bf16[128,2176]{1,0:T(8,128)(2,1)S(1)}, u32[]{:S(2)}, u32[]{:S(2)}) collective-permute-start(bf16[128,2176]{1,0:T(8,128)(2,1)} %shard_map.110.b0), channel_id=1, source_target_pairs={{0,2},{1,15},{2,4},{3,1},{4,6},{5,3},{6,8},{7,5},{8,10},{9,7},{10,... | collective-permute-start | bytes 1671176 | tf_op jit(solution)/shard_map/ppermute | solution.py:176
  6.8 8.3 %collective-permute-start = (bf16[128,2176]{1,0:T(8,128)(2,1)}, bf16[128,2176]{1,0:T(8,128)(2,1)S(1)}, u32[]{:S(2)}, u32[]{:S(2)}) collective-permute-start(bf16[128,2176]{1,0:T(8,128)(2,1)} %shard_map.110.b0), channel_id=1, source_target_pairs={{0,15},{1,2},{2,1},{3,4},{4,3},{5,6},{6,5},{7,8},{8,7},{9,10},{10,... | collective-permute-start | bytes 1671176 | tf_op jit(solution)/shard_map/ppermute | solution.py:176
  15.1 1.9 %collective-permute-start.5 = (bf16[1024,256]{1,0:T(8,128)(2,1)}, bf16[1024,256]{1,0:T(8,128)(2,1)S(1)}, u32[]{:S(2)}, u32[]{:S(2)}) collective-permute-start(bf16[1024,256]{1,0:T(8,128)(2,1)} %bitcast.13), channel_id=1, source_target_pairs={{0,1},{1,0},{2,3},{3,2},{4,5},{5,4},{6,7},{7,6},{8,9},{9,8},{10,11... | collective-permute-start | bytes 1572872 | tf_op jit(solution)/shard_map/ppermute | solution.py:176
  17.1 2.4 %collective-permute-start.6 = (bf16[1024,256]{1,0:T(8,128)(2,1)}, bf16[1024,256]{1,0:T(8,128)(2,1)S(1)}, u32[]{:S(2)}, u32[]{:S(2)}) collective-permute-start(bf16[1024,256]{1,0:T(8,128)(2,1)} %bitcast.18), channel_id=1, source_target_pairs={{0,1},{1,0},{2,3},{3,2},{4,5},{5,4},{6,7},{7,6},{8,9},{9,8},{10,11... | collective-permute-start | bytes 1572872 | tf_op jit(solution)/shard_map/ppermute | solution.py:176
  19.5 1.9 %collective-permute-start.7 = (bf16[256,1024]{1,0:T(8,128)(2,1)}, bf16[256,1024]{1,0:T(8,128)(2,1)S(1)}, u32[]{:S(2)}, u32[]{:S(2)}) collective-permute-start(bf16[256,1024]{1,0:T(8,128)(2,1)} %bitcast.23), channel_id=1, source_target_pairs={{0,1},{1,0},{2,3},{3,2},{4,5},{5,4},{6,7},{7,6},{8,9},{9,8},{10,11... | collective-permute-start | bytes 1572872 | tf_op jit(solution)/shard_map/ppermute | solution.py:176
  21.4 4.4 %collective-permute-done.3.b1 = bf16[128,2176]{1,0:T(8,128)(2,1)S(1)} collective-permute-done((bf16[128,2176]{1,0:T(8,128)(2,1)}, bf16[128,2176]{1,0:T(8,128)(2,1)S(1)}, u32[]{:S(2)}, u32[]{:S(2)}) %collective-permute-start.3) | collective-permute-done | bytes 557088 | tf_op jit(solution)/shard_map/ppermute | solution.py:176
  33.9 2.8 %shard_map.111 = (bf16[128,1152]{1,0:T(8,128)(2,1)S(1)}, bf16[128,1152]{1,0:T(8,128)(2,1)S(1)}, f32[1024,1024]{1,0:T(8,128)S(1)}, f32[512,1024]{1,0:T(8,128)S(1)}) custom-call(s32[1]{0:T(128)} %bitcast.1.expert_ref, bf16[128,2176]{1,0:T(8,128)(2,1)S(1)} %copy-done.6, bf16[128,2176]{1,0:T(8,128)(2,1)S(1)} %collective-permute-done.3.b1, ...), custom_call_target="tpu_custom_call" | custom-call | flops 2147483648 | bytes 16777216 | tf_op jit(solution)/shard_map/pallas_call | solution.py:134
  40.3 4.1 %collective-permute-done.1.b0 = bf16[128,2176]{1,0:T(8,128)(2,1)S(1)} collective-permute-done((bf16[128,2176]{1,0:T(8,128)(2,1)S(1)}, bf16[128,2176]{1,0:T(8,128)(2,1)S(1)}, u32[]{:S(2)}, u32[]{:S(2)}) %collective-permute-start.1) | collective-permute-done | bytes 557088 | tf_op jit(solution)/shard_map/ppermute | solution.py:176
  46.3 3.8 %shard_map.112 = (bf16[128,1152]{1,0:T(8,128)(2,1)S(1)}, bf16[128,1152]{1,0:T(8,128)(2,1)S(1)}, f32[1024,1024]{1,0:T(8,128)S(1)}, f32[512,1024]{1,0:T(8,128)S(1)}) custom-call(s32[1]{0:T(128)} %bitcast.1.expert_ref, bf16[128,2176]{1,0:T(8,128)(2,1)S(1)} %collective-permute-done.b0, ...), custom_call_target="tpu_custom_call", output_to_operand_aliasing={{2}: (9, {}), {3}: (10, {})} | custom-call | flops 2147483648 | bytes 16777216 | tf_op jit(solution)/shard_map/pallas_call | solution.py:134
  51.0 2.1 %collective-permute-start.9 = (bf16[128,2176]{1,0:T(8,128)(2,1)S(1)}, bf16[128,2176]{1,0:T(8,128)(2,1)S(1)}, u32[]{:S(2)}, u32[]{:S(2)}) collective-permute-start(bf16[128,2176]{1,0:T(8,128)(2,1)S(1)} %collective-permute-done.8.b1), channel_id=1, source_target_pairs={{0,2},{1,15},{2,4},{3,1},{4,6},{5,3},{6,8},{7,5},{8,10},{9,7},{10,... | collective-permute-start | bytes 1671176 | tf_op jit(solution)/shard_map/ppermute | solution.py:176
  53.1 3.8 %shard_map.113 = (bf16[128,1152]{1,0:T(8,128)(2,1)S(1)}, bf16[128,1152]{1,0:T(8,128)(2,1)S(1)}, f32[1024,1024]{1,0:T(8,128)S(1)}, f32[512,1024]{1,0:T(8,128)S(1)}) custom-call(s32[1]{0:T(128)} %bitcast.1.expert_ref, bf16[128,2176]{1,0:T(8,128)(2,1)S(1)} %collective-permute-done.1.b0, ...), custom_call_target="tpu_custom_call", output_to_operand_aliasing={{2}: (9, {}), {3}: (10, {})} | custom-call | flops 2147483648 | bytes 16777216 | tf_op jit(solution)/shard_map/pallas_call | solution.py:134
  57.0 6.7 %collective-permute-done.9.b1 = bf16[128,2176]{1,0:T(8,128)(2,1)S(1)} collective-permute-done((bf16[128,2176]{1,0:T(8,128)(2,1)S(1)}, bf16[128,2176]{1,0:T(8,128)(2,1)S(1)}, u32[]{:S(2)}, u32[]{:S(2)}) %collective-permute-start.9) | collective-permute-done | bytes 557088 | tf_op jit(solution)/shard_map/ppermute | solution.py:176
  63.7 3.4 %shard_map.114 = (bf16[128,1152]{1,0:T(8,128)(2,1)S(1)}, bf16[128,1152]{1,0:T(8,128)(2,1)}, bf16[32,48,512]{2,1,0:T(8,128)(2,1)S(1)}, bf16[32,48,512]{2,1,0:T(8,128)(2,1)S(1)}) custom-call(s32[1]{0:T(128)} %bitcast.1.expert_ref, bf16[128,2176]{1,0:T(8,128)(2,1)S(1)} %collective-permute-done.2.b0, bf16[128,2176]{1,0:T(8,128)(2,1)S(1)} %collective-permute-done.9.b1, ...), custom_call_target="tpu_custom_call" | custom-call | flops 2147483648 | bytes 16777216 | tf_op jit(solution)/shard_map/pallas_call | solution.py:134
  69.0 3.0 %collective-permute-start.14 = (bf16[128,1152]{1,0:T(8,128)(2,1)S(1)}, bf16[128,1152]{1,0:T(8,128)(2,1)S(1)}, u32[]{:S(2)}, u32[]{:S(2)}) collective-permute-start(bf16[128,1152]{1,0:T(8,128)(2,1)S(1)} %get-tuple-element.37), channel_id=1, source_target_pairs={{2,0},{15,1},{4,2},{1,3},{6,4},{3,5},{8,6},{5,7},{10,8},{7,9},{12,... | collective-permute-start | bytes 884744 | tf_op jit(solution)/shard_map/ppermute | solution.py:176
  72.0 3.1 %collective-permute-start.10 = (bf16[128,1152]{1,0:T(8,128)(2,1)}, bf16[128,1152]{1,0:T(8,128)(2,1)S(1)}, u32[]{:S(2)}, u32[]{:S(2)}) collective-permute-start(bf16[128,1152]{1,0:T(8,128)(2,1)} %get-tuple-element.35), channel_id=1, source_target_pairs={{2,0},{15,1},{4,2},{1,3},{6,4},{3,5},{8,6},{5,7},{10,8},{7,9},{12,... | collective-permute-start | bytes 884744 | tf_op jit(solution)/shard_map/ppermute | solution.py:176
  76.8 10.1 %all-to-all-start = ((bf16[32,48,512]{2,1,0:T(8,128)(2,1)}), bf16[32,48,512]{2,1,0:T(8,128)(2,1)}, u32[]{:S(2)}, u32[]{:S(2)}) async-start(bf16[32,48,512]{2,1,0:T(8,128)(2,1)} %add_convert_fusion), calls=%async_computation | async-start | bytes 3145728 | tf_op jit(solution)/shard_map/all_to_all | solution.py:212
  87.0 2.7 %collective-permute-start.11 = (bf16[128,1152]{1,0:T(8,128)(2,1)S(1)}, bf16[128,1152]{1,0:T(8,128)(2,1)S(1)}, u32[]{:S(2)}, u32[]{:S(2)}) collective-permute-start(bf16[128,1152]{1,0:T(8,128)(2,1)S(1)} %shard_map.115), channel_id=1, source_target_pairs={{2,0},{15,1},{4,2},{1,3},{6,4},{3,5},{8,6},{5,7},{10,8},{7,9},{12,... | collective-permute-start | bytes 884744 | tf_op jit(solution)/shard_map/ppermute | solution.py:176
  89.8 3.4 %collective-permute-start.15 = (bf16[128,1152]{1,0:T(8,128)(2,1)S(1)}, bf16[128,1152]{1,0:T(8,128)(2,1)S(1)}, u32[]{:S(2)}, u32[]{:S(2)}) collective-permute-start(bf16[128,1152]{1,0:T(8,128)(2,1)S(1)} %shard_map.118), channel_id=1, source_target_pairs={{2,0},{15,1},{4,2},{1,3},{6,4},{3,5},{8,6},{5,7},{10,8},{7,9},{12,... | collective-permute-start | bytes 884744 | tf_op jit(solution)/shard_map/ppermute | solution.py:176
  93.3 2.4 %collective-permute-done.11.p = bf16[128,1152]{1,0:T(8,128)(2,1)S(1)} collective-permute-done((bf16[128,1152]{1,0:T(8,128)(2,1)S(1)}, bf16[128,1152]{1,0:T(8,128)(2,1)S(1)}, u32[]{:S(2)}, u32[]{:S(2)}) %collective-permute-start.11) | collective-permute-done | bytes 294944 | tf_op jit(solution)/shard_map/ppermute | solution.py:176
  95.7 3.9 %collective-permute-start.12 = (bf16[128,1152]{1,0:T(8,128)(2,1)S(1)}, bf16[128,1152]{1,0:T(8,128)(2,1)S(1)}, u32[]{:S(2)}, u32[]{:S(2)}) collective-permute-start(bf16[128,1152]{1,0:T(8,128)(2,1)S(1)} %shard_map.116), channel_id=1, source_target_pairs={{2,0},{15,1},{4,2},{1,3},{6,4},{3,5},{8,6},{5,7},{10,8},{7,9},{12,... | collective-permute-start | bytes 884744 | tf_op jit(solution)/shard_map/ppermute | solution.py:176
  101.7 2.7 %collective-permute-done.12.p = bf16[128,1152]{1,0:T(8,128)(2,1)S(1)} collective-permute-done((bf16[128,1152]{1,0:T(8,128)(2,1)S(1)}, bf16[128,1152]{1,0:T(8,128)(2,1)S(1)}, u32[]{:S(2)}, u32[]{:S(2)}) %collective-permute-start.12) | collective-permute-done | bytes 294944 | tf_op jit(solution)/shard_map/ppermute | solution.py:176
  104.4 5.1 %collective-permute-start.13 = (bf16[128,1152]{1,0:T(8,128)(2,1)S(1)}, bf16[128,1152]{1,0:T(8,128)(2,1)S(1)}, u32[]{:S(2)}, u32[]{:S(2)}) collective-permute-start(bf16[128,1152]{1,0:T(8,128)(2,1)S(1)} %shard_map.117), channel_id=1, source_target_pairs={{2,0},{15,1},{4,2},{1,3},{6,4},{3,5},{8,6},{5,7},{10,8},{7,9},{12,... | collective-permute-start | bytes 884744 | tf_op jit(solution)/shard_map/ppermute | solution.py:176
  109.6 4.2 %collective-permute-done.13.p = bf16[128,1152]{1,0:T(8,128)(2,1)S(1)} collective-permute-done((bf16[128,1152]{1,0:T(8,128)(2,1)S(1)}, bf16[128,1152]{1,0:T(8,128)(2,1)S(1)}, u32[]{:S(2)}, u32[]{:S(2)}) %collective-permute-start.13) | collective-permute-done | bytes 294944 | tf_op jit(solution)/shard_map/ppermute | solution.py:176
  114.8 9.7 %all-to-all-done = bf16[32,48,512]{2,1,0:T(8,128)(2,1)} async-done(((bf16[32,48,512]{2,1,0:T(8,128)(2,1)}), bf16[32,48,512]{2,1,0:T(8,128)(2,1)}, u32[]{:S(2)}, u32[]{:S(2)}) %all-to-all-start) | async-done | bytes 1572896 | tf_op jit(solution)/shard_map/all_to_all | solution.py:212
  (54 shorter events, 26.3 us)
Async XLA Ops:
  2.5 23.2 %collective-permute-start.3 = (bf16[128,2176]{1,0:T(8,128)(2,1)}, bf16[128,2176]{1,0:T(8,128)(2,1)S(1)}, u32[]{:S(2)}, u32[]{:S(2)}) collective-permute-start(bf16[128,2176]{1,0:T(8,128)(2,1)} %shard_map.110.b0), channel_id=1, source_target_pairs={{0,2},{1,15},{2,4},{3,1},{4,6},{5,3},{6,8},{7,5},{8,10},{9,7},{10,... | collective-permute-start | bytes 1671176 | tf_op jit(solution)/shard_map/ppermute | solution.py:176
  6.8 20.9 %collective-permute-start = (bf16[128,2176]{1,0:T(8,128)(2,1)}, bf16[128,2176]{1,0:T(8,128)(2,1)S(1)}, u32[]{:S(2)}, u32[]{:S(2)}) collective-permute-start(bf16[128,2176]{1,0:T(8,128)(2,1)} %shard_map.110.b0), channel_id=1, source_target_pairs={{0,15},{1,2},{2,1},{3,4},{4,3},{5,6},{6,5},{7,8},{8,7},{9,10},{10,... | collective-permute-start | bytes 1671176 | tf_op jit(solution)/shard_map/ppermute | solution.py:176
  15.1 14.5 %collective-permute-start.5 = (bf16[1024,256]{1,0:T(8,128)(2,1)}, bf16[1024,256]{1,0:T(8,128)(2,1)S(1)}, u32[]{:S(2)}, u32[]{:S(2)}) collective-permute-start(bf16[1024,256]{1,0:T(8,128)(2,1)} %bitcast.13), channel_id=1, source_target_pairs={{0,1},{1,0},{2,3},{3,2},{4,5},{5,4},{6,7},{7,6},{8,9},{9,8},{10,11... | collective-permute-start | bytes 1572872 | tf_op jit(solution)/shard_map/ppermute | solution.py:176
  17.1 12.6 %collective-permute-start.6 = (bf16[1024,256]{1,0:T(8,128)(2,1)}, bf16[1024,256]{1,0:T(8,128)(2,1)S(1)}, u32[]{:S(2)}, u32[]{:S(2)}) collective-permute-start(bf16[1024,256]{1,0:T(8,128)(2,1)} %bitcast.18), channel_id=1, source_target_pairs={{0,1},{1,0},{2,3},{3,2},{4,5},{5,4},{6,7},{7,6},{8,9},{9,8},{10,11... | collective-permute-start | bytes 1572872 | tf_op jit(solution)/shard_map/ppermute | solution.py:176
  19.5 10.2 %collective-permute-start.7 = (bf16[256,1024]{1,0:T(8,128)(2,1)}, bf16[256,1024]{1,0:T(8,128)(2,1)S(1)}, u32[]{:S(2)}, u32[]{:S(2)}) collective-permute-start(bf16[256,1024]{1,0:T(8,128)(2,1)} %bitcast.23), channel_id=1, source_target_pairs={{0,1},{1,0},{2,3},{3,2},{4,5},{5,4},{6,7},{7,6},{8,9},{9,8},{10,11... | collective-permute-start | bytes 1572872 | tf_op jit(solution)/shard_map/ppermute | solution.py:176
  25.8 12.6 %collective-permute-start.4 = (bf16[128,2176]{1,0:T(8,128)(2,1)S(1)}, bf16[128,2176]{1,0:T(8,128)(2,1)S(1)}, u32[]{:S(2)}, u32[]{:S(2)}) collective-permute-start(bf16[128,2176]{1,0:T(8,128)(2,1)S(1)} %collective-permute-done.3.b1), channel_id=1, source_target_pairs={{0,2},{1,15},{2,4},{3,1},{4,6},{5,3},{6,8},{7,5},{8,10},{9,7},{10,... | collective-permute-start | bytes 1671176 | tf_op jit(solution)/shard_map/ppermute | solution.py:176
  27.7 16.7 %collective-permute-start.1 = (bf16[128,2176]{1,0:T(8,128)(2,1)S(1)}, bf16[128,2176]{1,0:T(8,128)(2,1)S(1)}, u32[]{:S(2)}, u32[]{:S(2)}) collective-permute-start(bf16[128,2176]{1,0:T(8,128)(2,1)S(1)} %collective-permute-done.b0), channel_id=1, source_target_pairs={{0,2},{1,15},{2,4},{3,1},{4,6},{5,3},{6,8},{7,5},{8,10},{9,7},{10,... | collective-permute-start | bytes 1671176 | tf_op jit(solution)/shard_map/ppermute | solution.py:176
  33.9 12.4 %copy-start.1 = (bf16[1,1024,256]{2,1,0:T(8,128)(2,1)S(1)}, bf16[1,1024,256]{2,1,0:T(8,128)(2,1)}, u32[]{:S(2)}) copy-start(bf16[1,1024,256]{2,1,0:T(8,128)(2,1)} %param.11) | copy-start | bytes 1572868
  33.9 12.4 %copy-start.3 = (bf16[1,1024,256]{2,1,0:T(8,128)(2,1)S(1)}, bf16[1,1024,256]{2,1,0:T(8,128)(2,1)}, u32[]{:S(2)}) copy-start(bf16[1,1024,256]{2,1,0:T(8,128)(2,1)} %param.12) | copy-start | bytes 1572868
  33.9 12.5 %copy-start.5 = (bf16[1,256,1024]{2,1,0:T(8,128)(2,1)S(1)}, bf16[1,256,1024]{2,1,0:T(8,128)(2,1)}, u32[]{:S(2)}) copy-start(bf16[1,256,1024]{2,1,0:T(8,128)(2,1)} %param.13) | copy-start | bytes 1572868
  38.4 12.6 %collective-permute-start.8 = (bf16[128,2176]{1,0:T(8,128)(2,1)S(1)}, bf16[128,2176]{1,0:T(8,128)(2,1)S(1)}, u32[]{:S(2)}, u32[]{:S(2)}) collective-permute-start(bf16[128,2176]{1,0:T(8,128)(2,1)S(1)} %collective-permute-done.4.b1), channel_id=1, source_target_pairs={{0,2},{1,15},{2,4},{3,1},{4,6},{5,3},{6,8},{7,5},{8,10},{9,7},{10,... | collective-permute-start | bytes 1671176 | tf_op jit(solution)/shard_map/ppermute | solution.py:176
  44.4 12.6 %collective-permute-start.2 = (bf16[128,2176]{1,0:T(8,128)(2,1)S(1)}, bf16[128,2176]{1,0:T(8,128)(2,1)S(1)}, u32[]{:S(2)}, u32[]{:S(2)}) collective-permute-start(bf16[128,2176]{1,0:T(8,128)(2,1)S(1)} %collective-permute-done.1.b0), channel_id=1, source_target_pairs={{0,2},{1,15},{2,4},{3,1},{4,6},{5,3},{6,8},{7,5},{8,10},{9,7},{10,... | collective-permute-start | bytes 1671176 | tf_op jit(solution)/shard_map/ppermute | solution.py:176
  50.1 6.8 %copy-start.8 = (bf16[128,1152]{1,0:T(8,128)(2,1)}, bf16[128,1152]{1,0:T(8,128)(2,1)S(1)}, u32[]{:S(2)}) copy-start(bf16[128,1152]{1,0:T(8,128)(2,1)S(1)} %get-tuple-element.29.q) | copy-start | bytes 884740
  51.0 12.6 %collective-permute-start.9 = (bf16[128,2176]{1,0:T(8,128)(2,1)S(1)}, bf16[128,2176]{1,0:T(8,128)(2,1)S(1)}, u32[]{:S(2)}, u32[]{:S(2)}) collective-permute-start(bf16[128,2176]{1,0:T(8,128)(2,1)S(1)} %collective-permute-done.8.b1), channel_id=1, source_target_pairs={{0,2},{1,15},{2,4},{3,1},{4,6},{5,3},{6,8},{7,5},{8,10},{9,7},{10,... | collective-permute-start | bytes 1671176 | tf_op jit(solution)/shard_map/ppermute | solution.py:176
  67.1 8.1 %collective-permute-start.17 = (bf16[32,48,512]{2,1,0:T(8,128)(2,1)S(1)}, bf16[32,48,512]{2,1,0:T(8,128)(2,1)S(1)}, u32[]{:S(2)}, u32[]{:S(2)}) collective-permute-start(bf16[32,48,512]{2,1,0:T(8,128)(2,1)S(1)} %get-tuple-element.44), channel_id=1, source_target_pairs={{0,1},{1,0},{2,3},{3,2},{4,5},{5,4},{6,7},{7,6},{8,9},{9,8},{10,11... | collective-permute-start | bytes 4718600 | tf_op jit(solution)/shard_map/ppermute | solution.py:176
  69.0 20.8 %collective-permute-start.14 = (bf16[128,1152]{1,0:T(8,128)(2,1)S(1)}, bf16[128,1152]{1,0:T(8,128)(2,1)S(1)}, u32[]{:S(2)}, u32[]{:S(2)}) collective-permute-start(bf16[128,1152]{1,0:T(8,128)(2,1)S(1)} %get-tuple-element.37), channel_id=1, source_target_pairs={{2,0},{15,1},{4,2},{1,3},{6,4},{3,5},{8,6},{5,7},{10,8},{7,9},{12,... | collective-permute-start | bytes 884744 | tf_op jit(solution)/shard_map/ppermute | solution.py:176
  72.0 15.0 %collective-permute-start.10 = (bf16[128,1152]{1,0:T(8,128)(2,1)}, bf16[128,1152]{1,0:T(8,128)(2,1)S(1)}, u32[]{:S(2)}, u32[]{:S(2)}) collective-permute-start(bf16[128,1152]{1,0:T(8,128)(2,1)} %get-tuple-element.35), channel_id=1, source_target_pairs={{2,0},{15,1},{4,2},{1,3},{6,4},{3,5},{8,6},{5,7},{10,8},{7,9},{12,... | collective-permute-start | bytes 884744 | tf_op jit(solution)/shard_map/ppermute | solution.py:176
  76.8 47.7 %all-to-all-start = ((bf16[32,48,512]{2,1,0:T(8,128)(2,1)}), bf16[32,48,512]{2,1,0:T(8,128)(2,1)}, u32[]{:S(2)}, u32[]{:S(2)}) async-start(bf16[32,48,512]{2,1,0:T(8,128)(2,1)} %add_convert_fusion), calls=%async_computation | async-start | bytes 3145728 | tf_op jit(solution)/shard_map/all_to_all | solution.py:212
  87.0 8.6 %collective-permute-start.11 = (bf16[128,1152]{1,0:T(8,128)(2,1)S(1)}, bf16[128,1152]{1,0:T(8,128)(2,1)S(1)}, u32[]{:S(2)}, u32[]{:S(2)}) collective-permute-start(bf16[128,1152]{1,0:T(8,128)(2,1)S(1)} %shard_map.115), channel_id=1, source_target_pairs={{2,0},{15,1},{4,2},{1,3},{6,4},{3,5},{8,6},{5,7},{10,8},{7,9},{12,... | collective-permute-start | bytes 884744 | tf_op jit(solution)/shard_map/ppermute | solution.py:176
  89.8 9.8 %collective-permute-start.15 = (bf16[128,1152]{1,0:T(8,128)(2,1)S(1)}, bf16[128,1152]{1,0:T(8,128)(2,1)S(1)}, u32[]{:S(2)}, u32[]{:S(2)}) collective-permute-start(bf16[128,1152]{1,0:T(8,128)(2,1)S(1)} %shard_map.118), channel_id=1, source_target_pairs={{2,0},{15,1},{4,2},{1,3},{6,4},{3,5},{8,6},{5,7},{10,8},{7,9},{12,... | collective-permute-start | bytes 884744 | tf_op jit(solution)/shard_map/ppermute | solution.py:176
  95.7 8.6 %collective-permute-start.12 = (bf16[128,1152]{1,0:T(8,128)(2,1)S(1)}, bf16[128,1152]{1,0:T(8,128)(2,1)S(1)}, u32[]{:S(2)}, u32[]{:S(2)}) collective-permute-start(bf16[128,1152]{1,0:T(8,128)(2,1)S(1)} %shard_map.116), channel_id=1, source_target_pairs={{2,0},{15,1},{4,2},{1,3},{6,4},{3,5},{8,6},{5,7},{10,8},{7,9},{12,... | collective-permute-start | bytes 884744 | tf_op jit(solution)/shard_map/ppermute | solution.py:176
  99.8 14.0 %copy-start.7 = (s32[128,10]{0,1:T(8,128)S(1)}, s32[128,10]{0,1:T(8,128)}, u32[]{:S(2)}) copy-start(s32[128,10]{0,1:T(8,128)} %param.9) | copy-start | bytes 15364
  99.8 9.8 %collective-permute-start.16 = (bf16[128,1152]{1,0:T(8,128)(2,1)S(1)}, bf16[128,1152]{1,0:T(8,128)(2,1)S(1)}, u32[]{:S(2)}, u32[]{:S(2)}) collective-permute-start(bf16[128,1152]{1,0:T(8,128)(2,1)S(1)} %shard_map.119), channel_id=1, source_target_pairs={{15,0},{2,1},{1,2},{4,3},{3,4},{6,5},{5,6},{8,7},{7,8},{10,9},{9,1... | collective-permute-start | bytes 884744 | tf_op jit(solution)/shard_map/ppermute | solution.py:176
  104.4 9.3 %collective-permute-start.13 = (bf16[128,1152]{1,0:T(8,128)(2,1)S(1)}, bf16[128,1152]{1,0:T(8,128)(2,1)S(1)}, u32[]{:S(2)}, u32[]{:S(2)}) collective-permute-start(bf16[128,1152]{1,0:T(8,128)(2,1)S(1)} %shard_map.117), channel_id=1, source_target_pairs={{2,0},{15,1},{4,2},{1,3},{6,4},{3,5},{8,6},{5,7},{10,8},{7,9},{12,... | collective-permute-start | bytes 884744 | tf_op jit(solution)/shard_map/ppermute | solution.py:176
  (7 other events, 15.5 us)

commit v5 on v4

--- a/solution.py
+++ b/solution.py
@@ -52,17 +52,17 @@
     gate_grad[...] = jnp.concatenate(picked, axis=0).astype(BF)
 
 
-def group_kernel(first, last, width, hidden, replicas, expert_ref, b0, b1, *refs):
+def group_kernel(first, last, width, hidden, replicas, n_blocks, expert_ref, *refs):
+    blocks, refs = refs[:n_blocks], refs[n_blocks:]
     weights, refs = (refs[:3], refs[3:6]), refs[6:]
-    if first:
-        grad0, grad1, out_a, out_b = refs
-    else:
-        acc_gu, acc_d, grad0, grad1, out_a, out_b = refs
+    if not first:
+        (acc_gu, acc_d), refs = refs[:2], refs[2:]
+    out_grads, (out_a, out_b) = refs[:n_blocks], refs[n_blocks:]
     mine = expert_ref[0]
     half = width // 2
-    x = jnp.concatenate([b0[:, :width], b1[:, :width]], axis=0)
-    dy = jnp.concatenate([b0[:, width : 2 * width], b1[:, width : 2 * width]], axis=0)
-    dense = jnp.concatenate([b0[:, 2 * width :], b1[:, 2 * width :]], axis=0).astype(F32)
+    x = jnp.concatenate([b[:, :width] for b in blocks], axis=0)
+    dy = jnp.concatenate([b[:, width : 2 * width] for b in blocks], axis=0)
+    dense = jnp.concatenate([b[:, 2 * width :] for b in blocks], axis=0).astype(F32)
     lane = lax.broadcasted_iota(jnp.int32, dense.shape, 1)
     terms = jnp.zeros(dense.shape, F32)
     grad = jnp.zeros(x.shape, F32)
@@ -82,8 +82,8 @@
         grads += [gate_pre, up_pre]
         acts.append((g * act).astype(BF))
         grad = grad + dot(gate_pre, w_gate[...], 1, 1) + dot(up_pre, w_up[...], 1, 1)
-    block = b0.shape[0]
-    for i, out in enumerate((grad0, grad1)):
+    block = blocks[0].shape[0]
+    for i, out in enumerate(out_grads):
         out[:, :width] = grad[i * block : (i + 1) * block].astype(BF)
         out[:, width:] = terms[i * block : (i + 1) * block].astype(BF)
 
@@ -116,6 +116,14 @@
             out_b[rows, :] = d_down
 
 
+def sum_kernel(parts, gate, up, down):
+    n, hidden = gate.shape[1:]
+    m = down.shape[1]
+    total = jnp.sum(parts[...].astype(F32), axis=0)
+    gate[0], up[0] = total[:n, :hidden], total[:n, hidden:]
+    down[0] = jnp.concatenate([total[n : n + m], total[n + m :]], axis=1)
+
+
 VMEM = pl.BlockSpec(memory_space=pltpu.VMEM)
 
 
@@ -130,13 +138,13 @@
             jax.ShapeDtypeStruct((width, 4 * hidden), F32),
             jax.ShapeDtypeStruct((2 * hidden, width), F32),
         ]
-    flops = 2 * 2 * rows * width * hidden * 16
+    flops = 2 * len(blocks) * rows * width * hidden * 16
     return pl.pallas_call(
-        functools.partial(group_kernel, first, last, width, hidden, replicas),
-        out_shape=[jax.ShapeDtypeStruct((rows, width + LANES), BF)] * 2 + sums,
-        in_specs=[pl.BlockSpec(memory_space=pltpu.SMEM)] + [VMEM] * (8 + len(acc)),
-        out_specs=[VMEM] * 4,
-        input_output_aliases={} if first or last else {9: 2, 10: 3},
+        functools.partial(group_kernel, first, last, width, hidden, replicas, len(blocks)),
+        out_shape=[jax.ShapeDtypeStruct((rows, width + LANES), BF)] * len(blocks) + sums,
+        in_specs=[pl.BlockSpec(memory_space=pltpu.SMEM)] + [VMEM] * (6 + len(blocks) + len(acc)),
+        out_specs=[VMEM] * (2 + len(blocks)),
+        input_output_aliases={} if first or last else {7 + len(blocks): len(blocks), 8 + len(blocks): len(blocks) + 1},
         compiler_params=pltpu.CompilerParams(vmem_limit_bytes=26 * 1024 * 1024),
         cost_estimate=pl.CostEstimate(flops=flops, bytes_accessed=16 * 1024 * 1024, transcendentals=0),
     )(expert, *blocks, *weights, *acc)
@@ -146,14 +154,14 @@
     out[...] = (p[...].astype(F32) + q[...].astype(F32)).astype(BF)
 
 
-def add(p, q):
+def add(p, q, flops=HOP_FLOPS):
     return pl.pallas_call(
         add_kernel,
         out_shape=jax.ShapeDtypeStruct(p.shape, BF),
         in_specs=[VMEM] * 2,
         out_specs=VMEM,
         compiler_params=pltpu.CompilerParams(vmem_limit_bytes=8 * 1024 * 1024),
-        cost_estimate=pl.CostEstimate(flops=HOP_FLOPS, bytes_accessed=3 * 2 * p.size, transcendentals=0),
+        cost_estimate=pl.CostEstimate(flops=flops, bytes_accessed=3 * 2 * p.size, transcendentals=0),
     )(p, q)
 
 
@@ -202,7 +210,8 @@
     b3 = send(b2, out)
     a4 = send(after(a3, g_a2), out)
     g_b2, g_a3, *acc = group(False, False, replicas, expert, (b2, a3), weights, acc)
-    g_b3, g_a4, mine, theirs = group(False, True, replicas, expert, (b3, a4), weights, acc)
+    g_b3, *acc = group(False, False, replicas, expert, (b3,), weights, acc)
+    g_a4, mine, theirs = group(False, True, replicas, expert, (a4,), weights, acc)
 
     b = send(g_b3, home)
     a = send(g_a4, home)
@@ -210,14 +219,18 @@
     got = send(theirs, swap)
     parts = (mine.astype(F32) + got.astype(F32)).astype(BF)
     parts = lax.all_to_all(parts, "dp", split_axis=0, concat_axis=0, tiled=True)
-    total = jnp.sum(parts.astype(F32), axis=0)
-    n, m = width // replicas, hidden // replicas
-    sum_gate, sum_up = total[:n, :hidden], total[:n, hidden:]
-    sum_down = jnp.concatenate([total[n : n + m], total[n + m :]], axis=1)
-
-    b = send(add(b, g_b2), home)
+    slab = jax.ShapeDtypeStruct((1, width // replicas, hidden), F32)
+    sums = pl.pallas_call(
+        sum_kernel,
+        out_shape=[slab, slab, jax.ShapeDtypeStruct((1, hidden // replicas, width), F32)],
+        in_specs=[VMEM],
+        out_specs=[VMEM] * 3,
+        compiler_params=pltpu.CompilerParams(vmem_limit_bytes=8 * 1024 * 1024),
+    )(parts)
+
+    b = send(add(b, g_b2, HOP_FLOPS // 2), home)
     a = send(add(a, g_a3), home)
-    b = send(add(b, g_b1), uncross)
+    b = send(add(b, g_b1, HOP_FLOPS // 2), uncross)
     a = send(add(a, g_a2), home)
     a = send(add(a, g_a1), home)
     token_grad, gate_grad = pl.pallas_call(
@@ -227,7 +240,7 @@
         out_specs=[VMEM] * 2,
         compiler_params=pltpu.CompilerParams(vmem_limit_bytes=8 * 1024 * 1024),
     )(routing.T, a, b, g_own)
-    return token_grad, gate_grad.T, sum_gate[None], sum_up[None], sum_down[None]
+    return token_grad, gate_grad.T, *sums
 
 
 def solution(mesh):

time: 128 us -> 125 us (0.977)
  the two profiles are of different devices: /device:TPU:16 before, /device:TPU:1 now
where the time goes in v5:
time: 125 us; the launch traced here: 123 us
  starting transfers between devices  65.6 us (52%)
  waiting for transfers between devices  27.5 us (22%)
  Pallas kernels  21.3 us (17%)
  local copies, waits for them, and re-layouts  5.61 us (4%)
  other arithmetic  1.76 us (1%)
    ppermute x18, starting transfers between devices, send(): return lax.ppermute(a, 'expert', pairs)  55.9 us
    ppermute x18, waiting for transfers between devices, send(): return lax.ppermute(a, 'expert', pairs)  21.4 us
    pallas_call x5, Pallas kernels, group(): pl.pallas_call(functools.partial(group_kernel, first, last, width, hidden...  16.3 us
    all_to_all x1, starting transfers between devices, on_device(): parts = lax.all_to_all(parts, 'dp', split_axis=0, concat_axis=0, tiled=True)  9.66 us
    all_to_all x1, waiting for transfers between devices, on_device(): parts = lax.all_to_all(parts, 'dp', split_axis=0, concat_axis=0, tiled=True)  6.11 us
    unnamed x24, local copies, waits for them, and re-layouts  5.61 us
  transfers between devices with their start and end apart: 19, of which 10 were waited for; matrix products, arithmetic and copies ran while one was open for 1% of the time, Pallas kernels for 13%

profile of v5, /device:TPU:1, one launch (start us, length us, event | category | flops | bytes accessed | tf_op | source)
XLA Modules:
  0.0 122.7 jit_solution(11148426986859722364)
XLA Ops:
  2.5 11.5 %collective-permute-start = (bf16[128,2176]{1,0:T(8,128)(2,1)}, bf16[128,2176]{1,0:T(8,128)(2,1)S(1)}, u32[]{:S(2)}, u32[]{:S(2)}) collective-permute-start(bf16[128,2176]{1,0:T(8,128)(2,1)} %shard_map.110.refs_0_), channel_id=1, source_target_pairs={{0,2},{1,15},{2,4},{3,1},{4,6},{5,3},{6,8},{7,5},{8,10},{9,7},{10,... | collective-permute-start | bytes 1671176 | tf_op jit(solution)/shard_map/ppermute | solution.py:184
  16.0 2.6 %collective-permute-start.2 = (bf16[1024,256]{1,0:T(8,128)(2,1)}, bf16[1024,256]{1,0:T(8,128)(2,1)S(1)}, u32[]{:S(2)}, u32[]{:S(2)}) collective-permute-start(bf16[1024,256]{1,0:T(8,128)(2,1)} %bitcast.7), channel_id=1, source_target_pairs={{0,1},{1,0},{2,3},{3,2},{4,5},{5,4},{6,7},{7,6},{8,9},{9,8},{10,11... | collective-permute-start | bytes 1572872 | tf_op jit(solution)/shard_map/ppermute | solution.py:184
  18.5 1.9 %collective-permute-start.3 = (bf16[1024,256]{1,0:T(8,128)(2,1)}, bf16[1024,256]{1,0:T(8,128)(2,1)S(1)}, u32[]{:S(2)}, u32[]{:S(2)}) collective-permute-start(bf16[1024,256]{1,0:T(8,128)(2,1)} %bitcast.13), channel_id=1, source_target_pairs={{0,1},{1,0},{2,3},{3,2},{4,5},{5,4},{6,7},{7,6},{8,9},{9,8},{10,11... | collective-permute-start | bytes 1572872 | tf_op jit(solution)/shard_map/ppermute | solution.py:184
  20.5 2.4 %collective-permute-start.4 = (bf16[256,1024]{1,0:T(8,128)(2,1)}, bf16[256,1024]{1,0:T(8,128)(2,1)S(1)}, u32[]{:S(2)}, u32[]{:S(2)}) collective-permute-start(bf16[256,1024]{1,0:T(8,128)(2,1)} %bitcast.19), channel_id=1, source_target_pairs={{0,1},{1,0},{2,3},{3,2},{4,5},{5,4},{6,7},{7,6},{8,9},{9,8},{10,11... | collective-permute-start | bytes 1572872 | tf_op jit(solution)/shard_map/ppermute | solution.py:184
  24.0 4.9 %collective-permute-start.1 = (bf16[128,2176]{1,0:T(8,128)(2,1)S(1)}, bf16[128,2176]{1,0:T(8,128)(2,1)S(1)}, u32[]{:S(2)}, u32[]{:S(2)}) collective-permute-start(bf16[128,2176]{1,0:T(8,128)(2,1)S(1)} %collective-permute-done.refs_1_), channel_id=1, source_target_pairs={{0,2},{1,15},{2,4},{3,1},{4,6},{5,3},{6,8},{7,5},{8,10},{9,7},{10,... | collective-permute-start | bytes 1671176 | tf_op jit(solution)/shard_map/ppermute | solution.py:184
  28.9 2.8 %collective-permute-start.8 = (bf16[128,2176]{1,0:T(8,128)(2,1)S(1)}, bf16[128,2176]{1,0:T(8,128)(2,1)S(1)}, u32[]{:S(2)}, u32[]{:S(2)}) collective-permute-start(bf16[128,2176]{1,0:T(8,128)(2,1)S(1)} %collective-permute-done.6.refs_0_), channel_id=1, source_target_pairs={{0,2},{1,15},{2,4},{3,1},{4,6},{5,3},{6,8},{7,5},{8,10},{9,7},{10,... | collective-permute-start | bytes 1671176 | tf_op jit(solution)/shard_map/ppermute | solution.py:184
  35.9 2.8 %shard_map.111 = (bf16[128,1152]{1,0:T(8,128)(2,1)S(1)}, bf16[128,1152]{1,0:T(8,128)(2,1)S(1)}, f32[1024,1024]{1,0:T(8,128)S(1)}, f32[512,1024]{1,0:T(8,128)S(1)}) custom-call(s32[1]{0:T(128)} %bitcast.1.expert_ref, bf16[128,2176]{1,0:T(8,128)(2,1)S(1)} %copy-done.6, bf16[128,2176]{1,0:T(8,128)(2,1)S(1)} %collective-permute-done.refs_1_, ...), custom_call_target="tpu_custom_call" | custom-call | flops 2147483648 | bytes 16777216 | tf_op jit(solution)/shard_map/pallas_call | solution.py:142
  41.4 4.9 %collective-permute-start.9 = (bf16[128,2176]{1,0:T(8,128)(2,1)S(1)}, bf16[128,2176]{1,0:T(8,128)(2,1)S(1)}, u32[]{:S(2)}, u32[]{:S(2)}) collective-permute-start(bf16[128,2176]{1,0:T(8,128)(2,1)S(1)} %collective-permute-done.8.refs_0_), channel_id=1, source_target_pairs={{0,2},{1,15},{2,4},{3,1},{4,6},{5,3},{6,8},{7,5},{8,10},{9,7},{10,... | collective-permute-start | bytes 1671176 | tf_op jit(solution)/shard_map/ppermute | solution.py:184
  46.3 3.8 %shard_map.112 = (bf16[128,1152]{1,0:T(8,128)(2,1)S(1)}, bf16[128,1152]{1,0:T(8,128)(2,1)S(1)}, f32[1024,1024]{1,0:T(8,128)S(1)}, f32[512,1024]{1,0:T(8,128)S(1)}) custom-call(s32[1]{0:T(128)} %bitcast.1.expert_ref, bf16[128,2176]{1,0:T(8,128)(2,1)S(1)} %collective-permute-done.6.refs_0_, ...), custom_call_target="tpu_custom_call", output_to_operand_aliasing={{2}: (9, {}), {3}: (10, {})} | custom-call | flops 2147483648 | bytes 16777216 | tf_op jit(solution)/shard_map/pallas_call | solution.py:142
  50.8 2.2 %collective-permute-start.7 = (bf16[128,2176]{1,0:T(8,128)(2,1)S(1)}, bf16[128,2176]{1,0:T(8,128)(2,1)S(1)}, u32[]{:S(2)}, u32[]{:S(2)}) collective-permute-start(bf16[128,2176]{1,0:T(8,128)(2,1)S(1)} %collective-permute-done.5.refs_1_), channel_id=1, source_target_pairs={{0,2},{1,15},{2,4},{3,1},{4,6},{5,3},{6,8},{7,5},{8,10},{9,7},{10,... | collective-permute-start | bytes 1671176 | tf_op jit(solution)/shard_map/ppermute | solution.py:184
  53.0 3.8 %shard_map.113 = (bf16[128,1152]{1,0:T(8,128)(2,1)S(1)}, bf16[128,1152]{1,0:T(8,128)(2,1)S(1)}, f32[1024,1024]{1,0:T(8,128)S(1)}, f32[512,1024]{1,0:T(8,128)S(1)}) custom-call(s32[1]{0:T(128)} %bitcast.1.expert_ref, bf16[128,2176]{1,0:T(8,128)(2,1)S(1)} %collective-permute-done.8.refs_0_, ...), custom_call_target="tpu_custom_call", output_to_operand_aliasing={{2}: (9, {}), {3}: (10, {})} | custom-call | flops 2147483648 | bytes 16777216 | tf_op jit(solution)/shard_map/pallas_call | solution.py:142
  56.8 3.4 %shard_map.114 = (bf16[128,1152]{1,0:T(8,128)(2,1)S(1)}, f32[1024,1024]{1,0:T(8,128)S(1)}, f32[512,1024]{1,0:T(8,128)S(1)}) custom-call(s32[1]{0:T(128)} %bitcast.1.expert_ref, bf16[128,2176]{1,0:T(8,128)(2,1)S(1)} %collective-permute-done.9.refs_0_, bf16[1024,256]{1,0:T(8,128)(2,1)S(1)} %bitcast.11, ...), custom_call_target="tpu_custom_call", output_to_operand_aliasing={{1}: (8, {}), {2}: (9, {})} | custom-call | flops 1073741824 | bytes 16777216 | tf_op jit(solution)/shard_map/pallas_call | solution.py:142
  61.9 2.5 %shard_map.115 = (bf16[128,1152]{1,0:T(8,128)(2,1)}, bf16[32,48,512]{2,1,0:T(8,128)(2,1)S(1)}, bf16[32,48,512]{2,1,0:T(8,128)(2,1)S(1)}) custom-call(s32[1]{0:T(128)} %bitcast.1.expert_ref, bf16[128,2176]{1,0:T(8,128)(2,1)S(1)} %collective-permute-done.7.refs_0_, bf16[1024,256]{1,0:T(8,128)(2,1)S(1)} %bitcast.12, bf16[1024,256]{1,0:T(8,128)(2,1)S(1)} %bitcast.18, ...), custom_call_target="tpu_custom_call" | custom-call | flops 1073741824 | bytes 16777216 | tf_op jit(solution)/shard_map/pallas_call | solution.py:142
  64.4 5.1 %collective-permute-start.17 = (bf16[32,48,512]{2,1,0:T(8,128)(2,1)S(1)}, bf16[32,48,512]{2,1,0:T(8,128)(2,1)S(1)}, u32[]{:S(2)}, u32[]{:S(2)}) collective-permute-start(bf16[32,48,512]{2,1,0:T(8,128)(2,1)S(1)} %get-tuple-element.51), channel_id=1, source_target_pairs={{0,1},{1,0},{2,3},{3,2},{4,5},{5,4},{6,7},{7,6},{8,9},{9,8},{10,11... | collective-permute-start | bytes 4718600 | tf_op jit(solution)/shard_map/ppermute | solution.py:184
  69.6 1.9 %collective-permute-start.10 = (bf16[128,1152]{1,0:T(8,128)(2,1)}, bf16[128,1152]{1,0:T(8,128)(2,1)}, u32[]{:S(2)}, u32[]{:S(2)}) collective-permute-start(bf16[128,1152]{1,0:T(8,128)(2,1)} %get-tuple-element.42), channel_id=1, source_target_pairs={{2,0},{15,1},{4,2},{1,3},{6,4},{3,5},{8,6},{5,7},{10,8},{7,9},{12,... | collective-permute-start | bytes 884744 | tf_op jit(solution)/shard_map/ppermute | solution.py:184
  74.4 9.7 %all-to-all-start = ((bf16[32,48,512]{2,1,0:T(8,128)(2,1)}), bf16[32,48,512]{2,1,0:T(8,128)(2,1)S(1)}, u32[]{:S(2)}, u32[]{:S(2)}) async-start(bf16[32,48,512]{2,1,0:T(8,128)(2,1)} %add_convert_fusion), calls=%async_computation | async-start | bytes 3145728 | tf_op jit(solution)/shard_map/all_to_all | solution.py:221
  84.0 1.9 %collective-permute-start.14 = (bf16[128,1152]{1,0:T(8,128)(2,1)S(1)}, bf16[128,1152]{1,0:T(8,128)(2,1)S(1)}, u32[]{:S(2)}, u32[]{:S(2)}) collective-permute-start(bf16[128,1152]{1,0:T(8,128)(2,1)S(1)} %get-tuple-element.44), channel_id=1, source_target_pairs={{2,0},{15,1},{4,2},{1,3},{6,4},{3,5},{8,6},{5,7},{10,8},{7,9},{12,... | collective-permute-start | bytes 884744 | tf_op jit(solution)/shard_map/ppermute | solution.py:184
  87.0 1.9 %collective-permute-start.11 = (bf16[128,1152]{1,0:T(8,128)(2,1)S(1)}, bf16[128,1152]{1,0:T(8,128)(2,1)S(1)}, u32[]{:S(2)}, u32[]{:S(2)}) collective-permute-start(bf16[128,1152]{1,0:T(8,128)(2,1)S(1)} %shard_map.116), channel_id=1, source_target_pairs={{2,0},{15,1},{4,2},{1,3},{6,4},{3,5},{8,6},{5,7},{10,8},{7,9},{12,... | collective-permute-start | bytes 884744 | tf_op jit(solution)/shard_map/ppermute | solution.py:184
  89.0 4.1 %collective-permute-done.14.p = bf16[128,1152]{1,0:T(8,128)(2,1)S(1)} collective-permute-done((bf16[128,1152]{1,0:T(8,128)(2,1)S(1)}, bf16[128,1152]{1,0:T(8,128)(2,1)S(1)}, u32[]{:S(2)}, u32[]{:S(2)}) %collective-permute-start.14) | collective-permute-done | bytes 294944 | tf_op jit(solution)/shard_map/ppermute | solution.py:184
  98.2 3.9 %collective-permute-done.15.p = bf16[128,1152]{1,0:T(8,128)(2,1)S(1)} collective-permute-done((bf16[128,1152]{1,0:T(8,128)(2,1)S(1)}, bf16[128,1152]{1,0:T(8,128)(2,1)S(1)}, u32[]{:S(2)}, u32[]{:S(2)}) %collective-permute-start.15) | collective-permute-done | bytes 294944 | tf_op jit(solution)/shard_map/ppermute | solution.py:184
  102.2 2.2 %collective-permute-start.16 = (bf16[128,1152]{1,0:T(8,128)(2,1)S(1)}, bf16[128,1152]{1,0:T(8,128)(2,1)S(1)}, u32[]{:S(2)}, u32[]{:S(2)}) collective-permute-start(bf16[128,1152]{1,0:T(8,128)(2,1)S(1)} %shard_map.120), channel_id=1, source_target_pairs={{15,0},{2,1},{1,2},{4,3},{3,4},{6,5},{5,6},{8,7},{7,8},{10,9},{9,1... | collective-permute-start | bytes 884744 | tf_op jit(solution)/shard_map/ppermute | solution.py:184
  107.2 3.4 %collective-permute-done.16.q = bf16[128,1152]{1,0:T(8,128)(2,1)S(1)} collective-permute-done((bf16[128,1152]{1,0:T(8,128)(2,1)S(1)}, bf16[128,1152]{1,0:T(8,128)(2,1)S(1)}, u32[]{:S(2)}, u32[]{:S(2)}) %collective-permute-start.16) | collective-permute-done | bytes 294944 | tf_op jit(solution)/shard_map/ppermute | solution.py:184
  110.6 4.1 %collective-permute-done.13.p = bf16[128,1152]{1,0:T(8,128)(2,1)S(1)} collective-permute-done((bf16[128,1152]{1,0:T(8,128)(2,1)S(1)}, bf16[128,1152]{1,0:T(8,128)(2,1)S(1)}, u32[]{:S(2)}, u32[]{:S(2)}) %collective-permute-start.13) | collective-permute-done | bytes 294944 | tf_op jit(solution)/shard_map/ppermute | solution.py:184
  115.8 6.1 %all-to-all-done.parts = bf16[32,48,512]{2,1,0:T(8,128)(2,1)S(1)} async-done(((bf16[32,48,512]{2,1,0:T(8,128)(2,1)}), bf16[32,48,512]{2,1,0:T(8,128)(2,1)S(1)}, u32[]{:S(2)}, u32[]{:S(2)}) %all-to-all-start) | async-done | bytes 1572896 | tf_op jit(solution)/shard_map/all_to_all | solution.py:221
  (52 shorter events, 27.9 us)
Async XLA Ops:
  2.5 21.4 %collective-permute-start = (bf16[128,2176]{1,0:T(8,128)(2,1)}, bf16[128,2176]{1,0:T(8,128)(2,1)S(1)}, u32[]{:S(2)}, u32[]{:S(2)}) collective-permute-start(bf16[128,2176]{1,0:T(8,128)(2,1)} %shard_map.110.refs_0_), channel_id=1, source_target_pairs={{0,2},{1,15},{2,4},{3,1},{4,6},{5,3},{6,8},{7,5},{8,10},{9,7},{10,... | collective-permute-start | bytes 1671176 | tf_op jit(solution)/shard_map/ppermute | solution.py:184
  14.0 14.8 %collective-permute-start.6 = (bf16[128,2176]{1,0:T(8,128)(2,1)}, bf16[128,2176]{1,0:T(8,128)(2,1)S(1)}, u32[]{:S(2)}, u32[]{:S(2)}) collective-permute-start(bf16[128,2176]{1,0:T(8,128)(2,1)} %shard_map.110.refs_0_), channel_id=1, source_target_pairs={{0,15},{1,2},{2,1},{3,4},{4,3},{5,6},{6,5},{7,8},{8,7},{9,10},{10,... | collective-permute-start | bytes 1671176 | tf_op jit(solution)/shard_map/ppermute | solution.py:184
  16.0 15.7 %collective-permute-start.2 = (bf16[1024,256]{1,0:T(8,128)(2,1)}, bf16[1024,256]{1,0:T(8,128)(2,1)S(1)}, u32[]{:S(2)}, u32[]{:S(2)}) collective-permute-start(bf16[1024,256]{1,0:T(8,128)(2,1)} %bitcast.7), channel_id=1, source_target_pairs={{0,1},{1,0},{2,3},{3,2},{4,5},{5,4},{6,7},{7,6},{8,9},{9,8},{10,11... | collective-permute-start | bytes 1572872 | tf_op jit(solution)/shard_map/ppermute | solution.py:184
  18.5 13.2 %collective-permute-start.3 = (bf16[1024,256]{1,0:T(8,128)(2,1)}, bf16[1024,256]{1,0:T(8,128)(2,1)S(1)}, u32[]{:S(2)}, u32[]{:S(2)}) collective-permute-start(bf16[1024,256]{1,0:T(8,128)(2,1)} %bitcast.13), channel_id=1, source_target_pairs={{0,1},{1,0},{2,3},{3,2},{4,5},{5,4},{6,7},{7,6},{8,9},{9,8},{10,11... | collective-permute-start | bytes 1572872 | tf_op jit(solution)/shard_map/ppermute | solution.py:184
  20.5 11.2 %collective-permute-start.4 = (bf16[256,1024]{1,0:T(8,128)(2,1)}, bf16[256,1024]{1,0:T(8,128)(2,1)S(1)}, u32[]{:S(2)}, u32[]{:S(2)}) collective-permute-start(bf16[256,1024]{1,0:T(8,128)(2,1)} %bitcast.19), channel_id=1, source_target_pairs={{0,1},{1,0},{2,3},{3,2},{4,5},{5,4},{6,7},{7,6},{8,9},{9,8},{10,11... | collective-permute-start | bytes 1572872 | tf_op jit(solution)/shard_map/ppermute | solution.py:184
  24.0 15.5 %collective-permute-start.1 = (bf16[128,2176]{1,0:T(8,128)(2,1)S(1)}, bf16[128,2176]{1,0:T(8,128)(2,1)S(1)}, u32[]{:S(2)}, u32[]{:S(2)}) collective-permute-start(bf16[128,2176]{1,0:T(8,128)(2,1)S(1)} %collective-permute-done.refs_1_), channel_id=1, source_target_pairs={{0,2},{1,15},{2,4},{3,1},{4,6},{5,3},{6,8},{7,5},{8,10},{9,7},{10,... | collective-permute-start | bytes 1671176 | tf_op jit(solution)/shard_map/ppermute | solution.py:184
  28.9 12.5 %collective-permute-start.8 = (bf16[128,2176]{1,0:T(8,128)(2,1)S(1)}, bf16[128,2176]{1,0:T(8,128)(2,1)S(1)}, u32[]{:S(2)}, u32[]{:S(2)}) collective-permute-start(bf16[128,2176]{1,0:T(8,128)(2,1)S(1)} %collective-permute-done.6.refs_0_), channel_id=1, source_target_pairs={{0,2},{1,15},{2,4},{3,1},{4,6},{5,3},{6,8},{7,5},{8,10},{9,7},{10,... | collective-permute-start | bytes 1671176 | tf_op jit(solution)/shard_map/ppermute | solution.py:184
  35.9 10.4 %copy-start.1 = (bf16[1,1024,256]{2,1,0:T(8,128)(2,1)S(1)}, bf16[1,1024,256]{2,1,0:T(8,128)(2,1)}, u32[]{:S(2)}) copy-start(bf16[1,1024,256]{2,1,0:T(8,128)(2,1)} %param.11) | copy-start | bytes 1572868
  35.9 10.4 %copy-start.3 = (bf16[1,1024,256]{2,1,0:T(8,128)(2,1)S(1)}, bf16[1,1024,256]{2,1,0:T(8,128)(2,1)}, u32[]{:S(2)}) copy-start(bf16[1,1024,256]{2,1,0:T(8,128)(2,1)} %param.12) | copy-start | bytes 1572868
  35.9 10.4 %copy-start.5 = (bf16[1,256,1024]{2,1,0:T(8,128)(2,1)S(1)}, bf16[1,256,1024]{2,1,0:T(8,128)(2,1)}, u32[]{:S(2)}) copy-start(bf16[1,256,1024]{2,1,0:T(8,128)(2,1)} %param.13) | copy-start | bytes 1572868
  39.4 11.4 %collective-permute-start.5 = (bf16[128,2176]{1,0:T(8,128)(2,1)S(1)}, bf16[128,2176]{1,0:T(8,128)(2,1)S(1)}, u32[]{:S(2)}, u32[]{:S(2)}) collective-permute-start(bf16[128,2176]{1,0:T(8,128)(2,1)S(1)} %collective-permute-done.1.refs_1_), channel_id=1, source_target_pairs={{0,2},{1,15},{2,4},{3,1},{4,6},{5,3},{6,8},{7,5},{8,10},{9,7},{10,... | collective-permute-start | bytes 1671176 | tf_op jit(solution)/shard_map/ppermute | solution.py:184
  41.4 15.5 %collective-permute-start.9 = (bf16[128,2176]{1,0:T(8,128)(2,1)S(1)}, bf16[128,2176]{1,0:T(8,128)(2,1)S(1)}, u32[]{:S(2)}, u32[]{:S(2)}) collective-permute-start(bf16[128,2176]{1,0:T(8,128)(2,1)S(1)} %collective-permute-done.8.refs_0_), channel_id=1, source_target_pairs={{0,2},{1,15},{2,4},{3,1},{4,6},{5,3},{6,8},{7,5},{8,10},{9,7},{10,... | collective-permute-start | bytes 1671176 | tf_op jit(solution)/shard_map/ppermute | solution.py:184
  50.8 11.1 %collective-permute-start.7 = (bf16[128,2176]{1,0:T(8,128)(2,1)S(1)}, bf16[128,2176]{1,0:T(8,128)(2,1)S(1)}, u32[]{:S(2)}, u32[]{:S(2)}) collective-permute-start(bf16[128,2176]{1,0:T(8,128)(2,1)S(1)} %collective-permute-done.5.refs_1_), channel_id=1, source_target_pairs={{0,2},{1,15},{2,4},{3,1},{4,6},{5,3},{6,8},{7,5},{8,10},{9,7},{10,... | collective-permute-start | bytes 1671176 | tf_op jit(solution)/shard_map/ppermute | solution.py:184
  64.4 8.2 %collective-permute-start.17 = (bf16[32,48,512]{2,1,0:T(8,128)(2,1)S(1)}, bf16[32,48,512]{2,1,0:T(8,128)(2,1)S(1)}, u32[]{:S(2)}, u32[]{:S(2)}) collective-permute-start(bf16[32,48,512]{2,1,0:T(8,128)(2,1)S(1)} %get-tuple-element.51), channel_id=1, source_target_pairs={{0,1},{1,0},{2,3},{3,2},{4,5},{5,4},{6,7},{7,6},{8,9},{9,8},{10,11... | collective-permute-start | bytes 4718600 | tf_op jit(solution)/shard_map/ppermute | solution.py:184
  69.6 16.4 %collective-permute-start.10 = (bf16[128,1152]{1,0:T(8,128)(2,1)}, bf16[128,1152]{1,0:T(8,128)(2,1)}, u32[]{:S(2)}, u32[]{:S(2)}) collective-permute-start(bf16[128,1152]{1,0:T(8,128)(2,1)} %get-tuple-element.42), channel_id=1, source_target_pairs={{2,0},{15,1},{4,2},{1,3},{6,4},{3,5},{8,6},{5,7},{10,8},{7,9},{12,... | collective-permute-start | bytes 884744 | tf_op jit(solution)/shard_map/ppermute | solution.py:184
  74.4 47.5 %all-to-all-start = ((bf16[32,48,512]{2,1,0:T(8,128)(2,1)}), bf16[32,48,512]{2,1,0:T(8,128)(2,1)S(1)}, u32[]{:S(2)}, u32[]{:S(2)}) async-start(bf16[32,48,512]{2,1,0:T(8,128)(2,1)} %add_convert_fusion), calls=%async_computation | async-start | bytes 3145728 | tf_op jit(solution)/shard_map/all_to_all | solution.py:221
  84.0 9.0 %collective-permute-start.14 = (bf16[128,1152]{1,0:T(8,128)(2,1)S(1)}, bf16[128,1152]{1,0:T(8,128)(2,1)S(1)}, u32[]{:S(2)}, u32[]{:S(2)}) collective-permute-start(bf16[128,1152]{1,0:T(8,128)(2,1)S(1)} %get-tuple-element.44), channel_id=1, source_target_pairs={{2,0},{15,1},{4,2},{1,3},{6,4},{3,5},{8,6},{5,7},{10,8},{7,9},{12,... | collective-permute-start | bytes 884744 | tf_op jit(solution)/shard_map/ppermute | solution.py:184
  87.0 9.2 %collective-permute-start.11 = (bf16[128,1152]{1,0:T(8,128)(2,1)S(1)}, bf16[128,1152]{1,0:T(8,128)(2,1)S(1)}, u32[]{:S(2)}, u32[]{:S(2)}) collective-permute-start(bf16[128,1152]{1,0:T(8,128)(2,1)S(1)} %shard_map.116), channel_id=1, source_target_pairs={{2,0},{15,1},{4,2},{1,3},{6,4},{3,5},{8,6},{5,7},{10,8},{7,9},{12,... | collective-permute-start | bytes 884744 | tf_op jit(solution)/shard_map/ppermute | solution.py:184
  93.1 9.0 %collective-permute-start.15 = (bf16[128,1152]{1,0:T(8,128)(2,1)S(1)}, bf16[128,1152]{1,0:T(8,128)(2,1)S(1)}, u32[]{:S(2)}, u32[]{:S(2)}) collective-permute-start(bf16[128,1152]{1,0:T(8,128)(2,1)S(1)} %shard_map.119), channel_id=1, source_target_pairs={{2,0},{15,1},{4,2},{1,3},{6,4},{3,5},{8,6},{5,7},{10,8},{7,9},{12,... | collective-permute-start | bytes 884744 | tf_op jit(solution)/shard_map/ppermute | solution.py:184
  96.3 9.0 %collective-permute-start.12 = (bf16[128,1152]{1,0:T(8,128)(2,1)S(1)}, bf16[128,1152]{1,0:T(8,128)(2,1)S(1)}, u32[]{:S(2)}, u32[]{:S(2)}) collective-permute-start(bf16[128,1152]{1,0:T(8,128)(2,1)S(1)} %shard_map.117), channel_id=1, source_target_pairs={{2,0},{15,1},{4,2},{1,3},{6,4},{3,5},{8,6},{5,7},{10,8},{7,9},{12,... | collective-permute-start | bytes 884744 | tf_op jit(solution)/shard_map/ppermute | solution.py:184
  102.1 3.2 %copy-start.11 = (bf16[128,1152]{1,0:T(8,128)(2,1)S(1)}, bf16[128,1152]{1,0:T(8,128)(2,1)}, u32[]{:S(2)}) copy-start(bf16[128,1152]{1,0:T(8,128)(2,1)} %copy-done.10) | copy-start | bytes 884740
  102.1 12.6 %copy-start.7 = (s32[128,10]{0,1:T(8,128)S(1)}, s32[128,10]{0,1:T(8,128)}, u32[]{:S(2)}) copy-start(s32[128,10]{0,1:T(8,128)} %param.9) | copy-start | bytes 15364
  102.2 8.5 %collective-permute-start.16 = (bf16[128,1152]{1,0:T(8,128)(2,1)S(1)}, bf16[128,1152]{1,0:T(8,128)(2,1)S(1)}, u32[]{:S(2)}, u32[]{:S(2)}) collective-permute-start(bf16[128,1152]{1,0:T(8,128)(2,1)S(1)} %shard_map.120), channel_id=1, source_target_pairs={{15,0},{2,1},{1,2},{4,3},{3,4},{6,5},{5,6},{8,7},{7,8},{10,9},{9,1... | collective-permute-start | bytes 884744 | tf_op jit(solution)/shard_map/ppermute | solution.py:184
  105.3 9.5 %collective-permute-start.13 = (bf16[128,1152]{1,0:T(8,128)(2,1)S(1)}, bf16[128,1152]{1,0:T(8,128)(2,1)S(1)}, u32[]{:S(2)}, u32[]{:S(2)}) collective-permute-start(bf16[128,1152]{1,0:T(8,128)(2,1)S(1)} %shard_map.118), channel_id=1, source_target_pairs={{2,0},{15,1},{4,2},{1,3},{6,4},{3,5},{8,6},{5,7},{10,8},{7,9},{12,... | collective-permute-start | bytes 884744 | tf_op jit(solution)/shard_map/ppermute | solution.py:184
  (7 other events, 8.8 us)

commit v6 on v5

--- a/solution.py
+++ b/solution.py
@@ -10,7 +10,8 @@
 BF = jnp.bfloat16
 F32 = jnp.float32
 LANES = 128
-HOP_FLOPS = 7_000_000_000
+HOP_FLOPS = 5_000_000_000
+SIDE_FLOPS = 2_500_000_000
 
 
 def dot(a, b, ca, cb):
@@ -52,17 +53,28 @@
     gate_grad[...] = jnp.concatenate(picked, axis=0).astype(BF)
 
 
-def group_kernel(first, last, width, hidden, replicas, n_blocks, expert_ref, *refs):
-    blocks, refs = refs[:n_blocks], refs[n_blocks:]
-    weights, refs = (refs[:3], refs[3:6]), refs[6:]
-    if not first:
-        (acc_gu, acc_d), refs = refs[:2], refs[2:]
-    out_grads, (out_a, out_b) = refs[:n_blocks], refs[n_blocks:]
-    mine = expert_ref[0]
-    half = width // 2
+def split(blocks, width):
     x = jnp.concatenate([b[:, :width] for b in blocks], axis=0)
     dy = jnp.concatenate([b[:, width : 2 * width] for b in blocks], axis=0)
     dense = jnp.concatenate([b[:, 2 * width :] for b in blocks], axis=0).astype(F32)
+    return x, dy, dense
+
+
+def one_expert(x, dy, g, w_gate, w_up, w_down):
+    pre_gate, pre_up = dot(x, w_gate[...], 1, 0), dot(x, w_up[...], 1, 0)
+    back = dot(dy, w_down[...], 1, 1)
+    sig = jax.nn.sigmoid(pre_gate)
+    silu = pre_gate * sig
+    act = silu * pre_up
+    act_grad = g * back
+    gate_pre = (act_grad * pre_up * sig * (1.0 + pre_gate * (1.0 - sig))).astype(BF)
+    up_pre = (act_grad * silu).astype(BF)
+    return gate_pre, up_pre, (g * act).astype(BF), jnp.sum(act * back, axis=1, keepdims=True)
+
+
+def both_experts(blocks, weights, mine, out_grads):
+    width = weights[0][0].shape[0]
+    x, dy, dense = split(blocks, width)
     lane = lax.broadcasted_iota(jnp.int32, dense.shape, 1)
     terms = jnp.zeros(dense.shape, F32)
     grad = jnp.zeros(x.shape, F32)
@@ -70,50 +82,92 @@
     for j, (w_gate, w_up, w_down) in enumerate(weights):
         here = lane == (mine if j == 0 else mine + 1 - 2 * lax.rem(mine, 2))
         g = jnp.sum(jnp.where(here, dense, 0.0), axis=1, keepdims=True)
-        pre_gate, pre_up = dot(x, w_gate[...], 1, 0), dot(x, w_up[...], 1, 0)
-        back = dot(dy, w_down[...], 1, 1)
-        sig = jax.nn.sigmoid(pre_gate)
-        silu = pre_gate * sig
-        act = silu * pre_up
-        terms = terms + jnp.where(here, jnp.sum(act * back, axis=1, keepdims=True), 0.0)
-        act_grad = g * back
-        gate_pre = (act_grad * pre_up * sig * (1.0 + pre_gate * (1.0 - sig))).astype(BF)
-        up_pre = (act_grad * silu).astype(BF)
+        gate_pre, up_pre, act, term = one_expert(x, dy, g, w_gate, w_up, w_down)
+        terms = terms + jnp.where(here, term, 0.0)
         grads += [gate_pre, up_pre]
-        acts.append((g * act).astype(BF))
+        acts.append(act)
         grad = grad + dot(gate_pre, w_gate[...], 1, 1) + dot(up_pre, w_up[...], 1, 1)
-    block = blocks[0].shape[0]
+    rows = blocks[0].shape[0]
     for i, out in enumerate(out_grads):
-        out[:, :width] = grad[i * block : (i + 1) * block].astype(BF)
-        out[:, width:] = terms[i * block : (i + 1) * block].astype(BF)
-
-    n, m = width // replicas, hidden // replicas
+        out[:, :width] = grad[i * rows : (i + 1) * rows].astype(BF)
+        out[:, width:] = terms[i * rows : (i + 1) * rows].astype(BF)
+    return x, dy, grads, acts
+
+
+def to_parts(out, d_gu, first_row):
+    replicas, rows, wide = out.shape
+    n = rows * 2 // 3
+    reps = d_gu.shape[0] // n
+    out[first_row // n : first_row // n + reps, :n, :] = d_gu.astype(BF).reshape(reps, n, wide)
+
+
+def down_to_parts(out, d_down):
+    replicas, rows, half = out.shape
+    m = rows // 3 // 2
+    pieces = [d_down[:, :half].reshape(replicas, m, half), d_down[:, half:].reshape(replicas, m, half)]
+    out[:, rows - 2 * m :, :] = jnp.concatenate(pieces, axis=1).astype(BF)
+
+
+def group_kernel(first, swap, n_blocks, expert_ref, *refs):
+    blocks, refs = refs[:n_blocks], refs[n_blocks:]
+    weights, refs = (refs[:3], refs[3:6]), refs[6:]
+    if not first:
+        (acc_gu, acc_d), refs = refs[:2], refs[2:]
+    out_grads, outs = refs[:n_blocks], refs[n_blocks:]
+    width, hidden = weights[0][0].shape
+    x, dy, grads, acts = both_experts(blocks, weights, expert_ref[0], out_grads)
     grads = jnp.concatenate(grads, axis=1)
-    step = max(n, 2 * hidden)
-    for r in range(0, width, step):
-        rows = slice(r, r + step)
+    for rows in steps(outs, swap, width, hidden):
         d_gu = dot(x[:, rows], grads, 0, 0)
         if not first:
             d_gu = d_gu + acc_gu[rows, :]
-        if last:
-            d_gu, reps = d_gu.astype(BF), step // n
-            to = slice(r // n, r // n + reps)
-            out_a[to, :n, :] = d_gu[:, : 2 * hidden].reshape(reps, n, 2 * hidden)
-            out_b[to, :n, :] = d_gu[:, 2 * hidden :].reshape(reps, n, 2 * hidden)
+        if swap:
+            outs[0][rows, :] = d_gu[:, : 2 * hidden]
+            to_parts(outs[2], d_gu[:, 2 * hidden :], rows.start)
         else:
-            out_a[rows, :] = d_gu
+            outs[0][rows, :] = d_gu
     for j, act in enumerate(acts):
         rows = slice(j * hidden, (j + 1) * hidden)
         d_down = dot(act, dy, 0, 0)
         if not first:
             d_down = d_down + acc_d[rows, :]
-        if last:
-            d_down = jnp.concatenate(
-                [d_down[:, :half].reshape(replicas, m, half), d_down[:, half:].reshape(replicas, m, half)], axis=1
-            )
-            (out_b if j else out_a)[:, n:, :] = d_down.astype(BF)
+        if swap and j == 1:
+            down_to_parts(outs[2], d_down)
         else:
-            out_b[rows, :] = d_down
+            outs[1][rows, :] = d_down
+
+
+def steps(outs, swap, width, hidden):
+    step = max(width // outs[2].shape[0], 2 * hidden) if swap else 2 * hidden
+    return [slice(r, r + step) for r in range(0, width, step)]
+
+
+def far_kernel(expert_ref, block, *refs):
+    weights, (out_grad, out_pre, out_act) = (refs[:3], refs[3:6]), refs[6:]
+    _, _, grads, acts = both_experts([block], weights, expert_ref[0], [out_grad])
+    out_pre[...] = jnp.concatenate(grads[:2], axis=1)
+    out_act[...] = acts[0]
+
+
+def last_kernel(expert_ref, block, pre, act, theirs, w_gate, w_up, w_down, acc_gu, acc_d, early, out):
+    width, hidden = w_gate.shape
+    x, dy, dense = split([theirs], width)
+    here = lax.broadcasted_iota(jnp.int32, dense.shape, 1) == expert_ref[0]
+    g = jnp.sum(jnp.where(here, dense, 0.0), axis=1, keepdims=True)
+    gate_pre, up_pre, gated, _ = one_expert(x, dy, g, w_gate, w_up, w_down)
+    x = jnp.concatenate([block[:, :width], x], axis=0)
+    dy = jnp.concatenate([block[:, width : 2 * width], dy], axis=0)
+    grads = jnp.concatenate([pre[...], jnp.concatenate([gate_pre, up_pre], axis=1)], axis=0)
+    gated = jnp.concatenate([act[...], gated], axis=0)
+    replicas, rows, wide = out.shape
+    n, m = width // replicas, hidden // replicas
+    step = max(n, 2 * hidden)
+    for r in range(0, width, step):
+        partner = early[r // n : (r + step) // n, :n, :].reshape(step, wide).astype(F32)
+        d_gu = dot(x[:, r : r + step], grads, 0, 0) + acc_gu[r : r + step, :] + partner
+        to_parts(out, d_gu, r)
+    down_to_parts(out, dot(gated, dy, 0, 0) + acc_d[...])
+    out[:, n:, :] = (out[:, n:, :].astype(F32) + early[:, n:, :].astype(F32)).astype(BF)
 
 
 def sum_kernel(parts, gate, up, down):
@@ -127,27 +181,37 @@
 VMEM = pl.BlockSpec(memory_space=pltpu.VMEM)
 
 
-def group(first, last, replicas, expert, blocks, weights, acc):
+def call(kernel, out_shape, expert, operands, aliases, flops):
+    return pl.pallas_call(
+        kernel,
+        out_shape=out_shape,
+        in_specs=[pl.BlockSpec(memory_space=pltpu.SMEM)] + [VMEM] * len(operands),
+        out_specs=[VMEM] * len(out_shape),
+        input_output_aliases=aliases,
+        compiler_params=pltpu.CompilerParams(vmem_limit_bytes=26 * 1024 * 1024),
+        cost_estimate=pl.CostEstimate(flops=flops, bytes_accessed=16 * 1024 * 1024, transcendentals=0),
+    )(expert, *operands)
+
+
+def group(expert, blocks, weights, acc, replicas=0):
     rows = blocks[0].shape[0]
     width, hidden = weights[0].shape
-    if last:
-        n, m = width // replicas, hidden // replicas
-        sums = [jax.ShapeDtypeStruct((replicas, n + 2 * m, 2 * hidden), BF)] * 2
-    else:
-        sums = [
-            jax.ShapeDtypeStruct((width, 4 * hidden), F32),
-            jax.ShapeDtypeStruct((2 * hidden, width), F32),
-        ]
-    flops = 2 * len(blocks) * rows * width * hidden * 16
-    return pl.pallas_call(
-        functools.partial(group_kernel, first, last, width, hidden, replicas, len(blocks)),
-        out_shape=[jax.ShapeDtypeStruct((rows, width + LANES), BF)] * len(blocks) + sums,
-        in_specs=[pl.BlockSpec(memory_space=pltpu.SMEM)] + [VMEM] * (6 + len(blocks) + len(acc)),
-        out_specs=[VMEM] * (2 + len(blocks)),
-        input_output_aliases={} if first or last else {7 + len(blocks): len(blocks), 8 + len(blocks): len(blocks) + 1},
-        compiler_params=pltpu.CompilerParams(vmem_limit_bytes=26 * 1024 * 1024),
-        cost_estimate=pl.CostEstimate(flops=flops, bytes_accessed=16 * 1024 * 1024, transcendentals=0),
-    )(expert, *blocks, *weights, *acc)
+    own = 2 * hidden if replicas else 4 * hidden
+    shapes = [jax.ShapeDtypeStruct((rows, width + LANES), BF)] * len(blocks) + [
+        jax.ShapeDtypeStruct((width, own), F32),
+        jax.ShapeDtypeStruct((own // 2, width), F32),
+    ]
+    if replicas:
+        shapes.append(jax.ShapeDtypeStruct((replicas, (width + 2 * hidden) // replicas, 2 * hidden), BF))
+    n = len(blocks)
+    return call(
+        functools.partial(group_kernel, not acc, bool(replicas), n),
+        shapes,
+        expert,
+        (*blocks, *weights, *acc),
+        {7 + n: n, 8 + n: n + 1} if acc and not replicas else {},
+        2 * n * rows * width * hidden * 16,
+    )
 
 
 def add_kernel(p, q, out):
@@ -203,21 +267,40 @@
     weights = [gate_weight[0], up_weight[0], down_weight[0]]
     weights = weights + [send(w, swap) for w in weights]
     a2 = send(a1, out)
-    g_own, g_a1, *acc = group(True, False, replicas, expert, (own, a1), weights, ())
+    g_own, g_a1, *acc = group(expert, (own, a1), weights, ())
     b2 = send(b1, out)
     a3 = send(after(a2, g_a1), out)
-    g_b1, g_a2, *acc = group(False, False, replicas, expert, (b1, a2), weights, acc)
+    g_b1, g_a2, *acc = group(expert, (b1, a2), weights, acc)
     b3 = send(b2, out)
     a4 = send(after(a3, g_a2), out)
-    g_b2, g_a3, *acc = group(False, False, replicas, expert, (b2, a3), weights, acc)
-    g_b3, *acc = group(False, False, replicas, expert, (b3,), weights, acc)
-    g_a4, mine, theirs = group(False, True, replicas, expert, (a4,), weights, acc)
+    g_b2, g_a3, *acc = group(expert, (b2, a3), weights, acc)
+    g_b3, *acc, early = group(expert, (b3,), weights, acc, replicas)
+    early = send(after(early, a4), swap)
+    theirs = send(a4, swap)
+    g_a4, pre, act = call(
+        far_kernel,
+        [
+            jax.ShapeDtypeStruct((rows, width + LANES), BF),
+            jax.ShapeDtypeStruct((rows, 2 * hidden), BF),
+            jax.ShapeDtypeStruct((rows, hidden), BF),
+        ],
+        expert,
+        (a4, *weights),
+        {},
+        2 * rows * width * hidden * 10,
+    )
+    (parts,) = call(
+        last_kernel,
+        [jax.ShapeDtypeStruct(early.shape, BF)],
+        expert,
+        (a4, pre, act, theirs, *weights[:3], *acc, early),
+        {},
+        2 * rows * width * hidden * 9,
+    )
 
     b = send(g_b3, home)
     a = send(g_a4, home)
 
-    got = send(theirs, swap)
-    parts = (mine.astype(F32) + got.astype(F32)).astype(BF)
     parts = lax.all_to_all(parts, "dp", split_axis=0, concat_axis=0, tiled=True)
     slab = jax.ShapeDtypeStruct((1, width // replicas, hidden), F32)
     sums = pl.pallas_call(
@@ -228,9 +311,9 @@
         compiler_params=pltpu.CompilerParams(vmem_limit_bytes=8 * 1024 * 1024),
     )(parts)
 
-    b = send(add(b, g_b2, HOP_FLOPS // 2), home)
+    b = send(add(b, g_b2, SIDE_FLOPS), home)
     a = send(add(a, g_a3), home)
-    b = send(add(b, g_b1, HOP_FLOPS // 2), uncross)
+    b = send(add(b, g_b1, SIDE_FLOPS), uncross)
     a = send(add(a, g_a2), home)
     a = send(add(a, g_a1), home)
     token_grad, gate_grad = pl.pallas_call(

time: 125 us -> 125 us (level)
  starting transfers between devices: 65.6 us -> 68.4 us
  waiting for transfers between devices: 27.5 us -> 25.2 us
  other arithmetic: 1.76 us -> 0 us
    all_to_all x1, waiting for transfers between devices: 6.11 us -> 0.01 us  [on_device(): parts = lax.all_to_all(parts, 'dp', split_axis=0, concat_axis=0, tiled=True)]
    ppermute x18 -> x19, waiting for transfers between devices: 21.4 us -> 25.2 us  [send(): return lax.ppermute(a, 'expert', pairs)]
    ppermute x18 -> x19, starting transfers between devices: 55.9 us -> 58.7 us  [send(): return lax.ppermute(a, 'expert', pairs)]
    convert_element_type x1 -> x0, other arithmetic: 1.76 us -> none  [on_device(): parts = (mine.astype(F32) + got.astype(F32)).astype(BF)]
    pallas_call x5 -> x6, Pallas kernels: 16.3 us -> 17.3 us  [call(): pl.pallas_call(kernel, out_shape=out_shape, in_specs=[pl.BlockSpec(memory...]
    unnamed x24 -> x26, local copies, waits for them, and re-layouts: 5.61 us -> 6.3 us
  transfers between devices with their start and end apart: 19 -> 20, of which waited for: 10 -> 9; matrix products, arithmetic and copies ran while one was open for 1% -> 0% of each run, Pallas kernels for 13% -> 13%
where the time goes in v6:
time: 125 us; the launch traced here: 122 us
  starting transfers between devices  68.4 us (55%)
  waiting for transfers between devices  25.2 us (20%)
  Pallas kernels  21.4 us (17%)
  local copies, waits for them, and re-layouts  6.3 us (5%)
    ppermute x19, starting transfers between devices, send(): return lax.ppermute(a, 'expert', pairs)  58.7 us
    ppermute x19, waiting for transfers between devices, send(): return lax.ppermute(a, 'expert', pairs)  25.2 us
    pallas_call x6, Pallas kernels, call(): pl.pallas_call(kernel, out_shape=out_shape, in_specs=[pl.BlockSpec(memory...  17.3 us
    all_to_all x1, starting transfers between devices, on_device(): parts = lax.all_to_all(parts, 'dp', split_axis=0, concat_axis=0, tiled=True)  9.67 us
    unnamed x26, local copies, waits for them, and re-layouts  6.3 us
  transfers between devices with their start and end apart: 20, of which 9 were waited for; matrix products, arithmetic and copies ran while one was open for 0% of the time, Pallas kernels for 13%

profile of v6, /device:TPU:1, one launch (start us, length us, event | category | flops | bytes accessed | tf_op | source)
XLA Modules:
  0.0 122.4 jit_solution(8588116647812191935)
XLA Ops:
  2.5 11.5 %collective-permute-start = (bf16[128,2176]{1,0:T(8,128)(2,1)}, bf16[128,2176]{1,0:T(8,128)(2,1)S(1)}, u32[]{:S(2)}, u32[]{:S(2)}) collective-permute-start(bf16[128,2176]{1,0:T(8,128)(2,1)} %shard_map.110.refs_0_), channel_id=1, source_target_pairs={{0,2},{1,15},{2,4},{3,1},{4,6},{5,3},{6,8},{7,5},{8,10},{9,7},{10,... | collective-permute-start | bytes 1671176 | tf_op jit(solution)/shard_map/ppermute | solution.py:248
  16.0 2.6 %collective-permute-start.2 = (bf16[1024,256]{1,0:T(8,128)(2,1)}, bf16[1024,256]{1,0:T(8,128)(2,1)S(1)}, u32[]{:S(2)}, u32[]{:S(2)}) collective-permute-start(bf16[1024,256]{1,0:T(8,128)(2,1)} %bitcast.7), channel_id=1, source_target_pairs={{0,1},{1,0},{2,3},{3,2},{4,5},{5,4},{6,7},{7,6},{8,9},{9,8},{10,11... | collective-permute-start | bytes 1572872 | tf_op jit(solution)/shard_map/ppermute | solution.py:248
  18.5 1.9 %collective-permute-start.3 = (bf16[1024,256]{1,0:T(8,128)(2,1)}, bf16[1024,256]{1,0:T(8,128)(2,1)S(1)}, u32[]{:S(2)}, u32[]{:S(2)}) collective-permute-start(bf16[1024,256]{1,0:T(8,128)(2,1)} %bitcast.14), channel_id=1, source_target_pairs={{0,1},{1,0},{2,3},{3,2},{4,5},{5,4},{6,7},{7,6},{8,9},{9,8},{10,11... | collective-permute-start | bytes 1572872 | tf_op jit(solution)/shard_map/ppermute | solution.py:248
  20.5 2.4 %collective-permute-start.4 = (bf16[256,1024]{1,0:T(8,128)(2,1)}, bf16[256,1024]{1,0:T(8,128)(2,1)S(1)}, u32[]{:S(2)}, u32[]{:S(2)}) collective-permute-start(bf16[256,1024]{1,0:T(8,128)(2,1)} %bitcast.21), channel_id=1, source_target_pairs={{0,1},{1,0},{2,3},{3,2},{4,5},{5,4},{6,7},{7,6},{8,9},{9,8},{10,11... | collective-permute-start | bytes 1572872 | tf_op jit(solution)/shard_map/ppermute | solution.py:248
  23.9 4.9 %collective-permute-start.1 = (bf16[128,2176]{1,0:T(8,128)(2,1)S(1)}, bf16[128,2176]{1,0:T(8,128)(2,1)S(1)}, u32[]{:S(2)}, u32[]{:S(2)}) collective-permute-start(bf16[128,2176]{1,0:T(8,128)(2,1)S(1)} %collective-permute-done.refs_1_), channel_id=1, source_target_pairs={{0,2},{1,15},{2,4},{3,1},{4,6},{5,3},{6,8},{7,5},{8,10},{9,7},{10,... | collective-permute-start | bytes 1671176 | tf_op jit(solution)/shard_map/ppermute | solution.py:248
  28.9 2.8 %collective-permute-start.9 = (bf16[128,2176]{1,0:T(8,128)(2,1)S(1)}, bf16[128,2176]{1,0:T(8,128)(2,1)S(1)}, u32[]{:S(2)}, u32[]{:S(2)}) collective-permute-start(bf16[128,2176]{1,0:T(8,128)(2,1)S(1)} %collective-permute-done.6.refs_0_), channel_id=1, source_target_pairs={{0,2},{1,15},{2,4},{3,1},{4,6},{5,3},{6,8},{7,5},{8,10},{9,7},{10,... | collective-permute-start | bytes 1671176 | tf_op jit(solution)/shard_map/ppermute | solution.py:248
  35.9 2.8 %shard_map.111 = (bf16[128,1152]{1,0:T(8,128)(2,1)S(1)}, bf16[128,1152]{1,0:T(8,128)(2,1)S(1)}, f32[1024,1024]{1,0:T(8,128)S(1)}, f32[512,1024]{1,0:T(8,128)S(1)}) custom-call(s32[1]{0:T(128)} %bitcast.1.expert_ref, bf16[128,2176]{1,0:T(8,128)(2,1)S(1)} %copy-done.6, bf16[128,2176]{1,0:T(8,128)(2,1)S(1)} %collective-permute-done.refs_1_, ...), custom_call_target="tpu_custom_call" | custom-call | flops 2147483648 | bytes 16777216 | tf_op jit(solution)/shard_map/pallas_call | solution.py:185
  41.4 4.9 %collective-permute-start.13 = (bf16[128,2176]{1,0:T(8,128)(2,1)S(1)}, bf16[128,2176]{1,0:T(8,128)(2,1)S(1)}, u32[]{:S(2)}, u32[]{:S(2)}) collective-permute-start(bf16[128,2176]{1,0:T(8,128)(2,1)S(1)} %collective-permute-done.9.refs_0_), channel_id=1, source_target_pairs={{0,2},{1,15},{2,4},{3,1},{4,6},{5,3},{6,8},{7,5},{8,10},{9,7},{10,... | collective-permute-start | bytes 1671176 | tf_op jit(solution)/shard_map/ppermute | solution.py:248
  46.3 3.8 %shard_map.112 = (bf16[128,1152]{1,0:T(8,128)(2,1)S(1)}, bf16[128,1152]{1,0:T(8,128)(2,1)S(1)}, f32[1024,1024]{1,0:T(8,128)S(1)}, f32[512,1024]{1,0:T(8,128)S(1)}) custom-call(s32[1]{0:T(128)} %bitcast.1.expert_ref, bf16[128,2176]{1,0:T(8,128)(2,1)S(1)} %collective-permute-done.6.refs_0_, ...), custom_call_target="tpu_custom_call", output_to_operand_aliasing={{2}: (9, {}), {3}: (10, {})} | custom-call | flops 2147483648 | bytes 16777216 | tf_op jit(solution)/shard_map/pallas_call | solution.py:185
  50.8 2.2 %collective-permute-start.7 = (bf16[128,2176]{1,0:T(8,128)(2,1)S(1)}, bf16[128,2176]{1,0:T(8,128)(2,1)S(1)}, u32[]{:S(2)}, u32[]{:S(2)}) collective-permute-start(bf16[128,2176]{1,0:T(8,128)(2,1)S(1)} %collective-permute-done.5.refs_1_), channel_id=1, source_target_pairs={{0,2},{1,15},{2,4},{3,1},{4,6},{5,3},{6,8},{7,5},{8,10},{9,7},{10,... | collective-permute-start | bytes 1671176 | tf_op jit(solution)/shard_map/ppermute | solution.py:248
  53.0 3.8 %shard_map.114 = (bf16[128,1152]{1,0:T(8,128)(2,1)S(1)}, bf16[128,1152]{1,0:T(8,128)(2,1)S(1)}, f32[1024,1024]{1,0:T(8,128)S(1)}, f32[512,1024]{1,0:T(8,128)S(1)}) custom-call(s32[1]{0:T(128)} %bitcast.1.expert_ref, bf16[128,2176]{1,0:T(8,128)(2,1)S(1)} %collective-permute-done.9.refs_0_, ...), custom_call_target="tpu_custom_call", output_to_operand_aliasing={{2}: (9, {}), {3}: (10, {})} | custom-call | flops 2147483648 | bytes 16777216 | tf_op jit(solution)/shard_map/pallas_call | solution.py:185
  56.9 2.5 %shard_map.118 = (bf16[128,1152]{1,0:T(8,128)(2,1)S(1)}, f32[1024,512]{1,0:T(8,128)S(1)}, f32[256,1024]{1,0:T(8,128)S(1)}, bf16[32,48,512]{2,1,0:T(8,128)(2,1)S(1)}) custom-call(s32[1]{0:T(128)} %bitcast.1.expert_ref, bf16[128,2176]{1,0:T(8,128)(2,1)S(1)} %collective-permute-done.13.refs_0_, bf16[1024,256]{1,0:T(8,128)(2,1)S(1)} %bitcast.11, ...), custom_call_target="tpu_custom_call" | custom-call | flops 1073741824 | bytes 16777216 | tf_op jit(solution)/shard_map/pallas_call | solution.py:185
  59.3 2.6 %collective-permute-done.7.block = bf16[128,2176]{1,0:T(8,128)(2,1)S(1)} collective-permute-done((bf16[128,2176]{1,0:T(8,128)(2,1)S(1)}, bf16[128,2176]{1,0:T(8,128)(2,1)S(1)}, u32[]{:S(2)}, u32[]{:S(2)}) %collective-permute-start.7) | collective-permute-done | bytes 557088 | tf_op jit(solution)/shard_map/ppermute | solution.py:248
  61.9 5.1 %collective-permute-start.18 = (bf16[32,48,512]{2,1,0:T(8,128)(2,1)S(1)}, bf16[32,48,512]{2,1,0:T(8,128)(2,1)S(1)}, u32[]{:S(2)}, u32[]{:S(2)}) collective-permute-start(bf16[32,48,512]{2,1,0:T(8,128)(2,1)S(1)} %get-tuple-element.55), channel_id=1, source_target_pairs={{0,1},{1,0},{2,3},{3,2},{4,5},{5,4},{6,7},{7,6},{8,9},{9,8},{10,11... | collective-permute-start | bytes 4718600 | tf_op jit(solution)/shard_map/ppermute | solution.py:248
  69.0 2.0 %shard_map.113 = (bf16[128,1152]{1,0:T(8,128)(2,1)S(1)}, bf16[128,512]{1,0:T(8,128)(2,1)S(1)}, bf16[128,256]{1,0:T(8,128)(2,1)S(1)}) custom-call(s32[1]{0:T(128)} %bitcast.1.expert_ref, bf16[128,2176]{1,0:T(8,128)(2,1)S(1)} %collective-permute-done.7.block, bf16[1024,256]{1,0:T(8,128)(2,1)S(1)} %bitcast.12, bf16[1024,256]{1,0:T(8,128)(2,1)S(1)} %bitcast.19, ...), custom_call_target="tpu_custom_call" | custom-call | flops 671088640 | bytes 16777216 | tf_op jit(solution)/shard_map/pallas_call | solution.py:185
  71.7 2.5 %shard_map.122 = bf16[32,48,512]{2,1,0:T(8,128)(2,1)} custom-call(s32[1]{0:T(128)} %bitcast.1.expert_ref, bf16[128,2176]{1,0:T(8,128)(2,1)S(1)} %collective-permute-done.7.block, bf16[128,512]{1,0:T(8,128)(2,1)S(1)} %get-tuple-element.50.pre, bf16[128,256]{1,0:T(8,128)(2,1)S(1)} %get-tuple-element.51.act, ...), custom_call_target="tpu_custom_call" | custom-call | flops 603979776 | bytes 16777216 | tf_op jit(solution)/shard_map/pallas_call | solution.py:185
  74.2 9.7 %all-to-all-start = ((bf16[32,48,512]{2,1,0:T(8,128)(2,1)}), bf16[32,48,512]{2,1,0:T(8,128)(2,1)S(1)}, u32[]{:S(2)}, u32[]{:S(2)}) async-start(bf16[32,48,512]{2,1,0:T(8,128)(2,1)} %shard_map.122), calls=%async_computation | async-start | bytes 3145728 | tf_op jit(solution)/shard_map/all_to_all | solution.py:304
  87.7 5.3 %collective-permute-done.8.p = bf16[128,1152]{1,0:T(8,128)(2,1)S(1)} collective-permute-done((bf16[128,1152]{1,0:T(8,128)(2,1)}, bf16[128,1152]{1,0:T(8,128)(2,1)S(1)}, u32[]{:S(2)}, u32[]{:S(2)}) %collective-permute-start.8) | collective-permute-done | bytes 294944 | tf_op jit(solution)/shard_map/ppermute | solution.py:248
  96.3 1.9 %collective-permute-start.15 = (bf16[128,1152]{1,0:T(8,128)(2,1)S(1)}, bf16[128,1152]{1,0:T(8,128)(2,1)S(1)}, u32[]{:S(2)}, u32[]{:S(2)}) collective-permute-start(bf16[128,1152]{1,0:T(8,128)(2,1)S(1)} %shard_map.119), channel_id=1, source_target_pairs={{2,0},{15,1},{4,2},{1,3},{6,4},{3,5},{8,6},{5,7},{10,8},{7,9},{12,... | collective-permute-start | bytes 884744 | tf_op jit(solution)/shard_map/ppermute | solution.py:248
  98.2 3.9 %collective-permute-done.10.p = bf16[128,1152]{1,0:T(8,128)(2,1)S(1)} collective-permute-done((bf16[128,1152]{1,0:T(8,128)(2,1)S(1)}, bf16[128,1152]{1,0:T(8,128)(2,1)S(1)}, u32[]{:S(2)}, u32[]{:S(2)}) %collective-permute-start.10) | collective-permute-done | bytes 294944 | tf_op jit(solution)/shard_map/ppermute | solution.py:248
  105.4 3.1 %collective-permute-start.16 = (bf16[128,1152]{1,0:T(8,128)(2,1)S(1)}, bf16[128,1152]{1,0:T(8,128)(2,1)S(1)}, u32[]{:S(2)}, u32[]{:S(2)}) collective-permute-start(bf16[128,1152]{1,0:T(8,128)(2,1)S(1)} %shard_map.120), channel_id=1, source_target_pairs={{15,0},{2,1},{1,2},{4,3},{3,4},{6,5},{5,6},{8,7},{7,8},{10,9},{9,1... | collective-permute-start | bytes 884744 | tf_op jit(solution)/shard_map/ppermute | solution.py:248
  108.5 2.7 %collective-permute-done.11.p = bf16[128,1152]{1,0:T(8,128)(2,1)S(1)} collective-permute-done((bf16[128,1152]{1,0:T(8,128)(2,1)S(1)}, bf16[128,1152]{1,0:T(8,128)(2,1)S(1)}, u32[]{:S(2)}, u32[]{:S(2)}) %collective-permute-start.11) | collective-permute-done | bytes 294944 | tf_op jit(solution)/shard_map/ppermute | solution.py:248
  111.2 1.9 %collective-permute-start.12 = (bf16[128,1152]{1,0:T(8,128)(2,1)S(1)}, bf16[128,1152]{1,0:T(8,128)(2,1)S(1)}, u32[]{:S(2)}, u32[]{:S(2)}) collective-permute-start(bf16[128,1152]{1,0:T(8,128)(2,1)S(1)} %shard_map.117), channel_id=1, source_target_pairs={{2,0},{15,1},{4,2},{1,3},{6,4},{3,5},{8,6},{5,7},{10,8},{7,9},{12,... | collective-permute-start | bytes 884744 | tf_op jit(solution)/shard_map/ppermute | solution.py:248
  114.2 6.4 %collective-permute-done.12.p = bf16[128,1152]{1,0:T(8,128)(2,1)S(1)} collective-permute-done((bf16[128,1152]{1,0:T(8,128)(2,1)S(1)}, bf16[128,1152]{1,0:T(8,128)(2,1)S(1)}, u32[]{:S(2)}, u32[]{:S(2)}) %collective-permute-start.12) | collective-permute-done | bytes 294944 | tf_op jit(solution)/shard_map/ppermute | solution.py:248
  (56 shorter events, 28.2 us)
Async XLA Ops:
  2.5 21.4 %collective-permute-start = (bf16[128,2176]{1,0:T(8,128)(2,1)}, bf16[128,2176]{1,0:T(8,128)(2,1)S(1)}, u32[]{:S(2)}, u32[]{:S(2)}) collective-permute-start(bf16[128,2176]{1,0:T(8,128)(2,1)} %shard_map.110.refs_0_), channel_id=1, source_target_pairs={{0,2},{1,15},{2,4},{3,1},{4,6},{5,3},{6,8},{7,5},{8,10},{9,7},{10,... | collective-permute-start | bytes 1671176 | tf_op jit(solution)/shard_map/ppermute | solution.py:248
  14.0 14.8 %collective-permute-start.6 = (bf16[128,2176]{1,0:T(8,128)(2,1)}, bf16[128,2176]{1,0:T(8,128)(2,1)S(1)}, u32[]{:S(2)}, u32[]{:S(2)}) collective-permute-start(bf16[128,2176]{1,0:T(8,128)(2,1)} %shard_map.110.refs_0_), channel_id=1, source_target_pairs={{0,15},{1,2},{2,1},{3,4},{4,3},{5,6},{6,5},{7,8},{8,7},{9,10},{10,... | collective-permute-start | bytes 1671176 | tf_op jit(solution)/shard_map/ppermute | solution.py:248
  16.0 15.7 %collective-permute-start.2 = (bf16[1024,256]{1,0:T(8,128)(2,1)}, bf16[1024,256]{1,0:T(8,128)(2,1)S(1)}, u32[]{:S(2)}, u32[]{:S(2)}) collective-permute-start(bf16[1024,256]{1,0:T(8,128)(2,1)} %bitcast.7), channel_id=1, source_target_pairs={{0,1},{1,0},{2,3},{3,2},{4,5},{5,4},{6,7},{7,6},{8,9},{9,8},{10,11... | collective-permute-start | bytes 1572872 | tf_op jit(solution)/shard_map/ppermute | solution.py:248
  18.5 13.2 %collective-permute-start.3 = (bf16[1024,256]{1,0:T(8,128)(2,1)}, bf16[1024,256]{1,0:T(8,128)(2,1)S(1)}, u32[]{:S(2)}, u32[]{:S(2)}) collective-permute-start(bf16[1024,256]{1,0:T(8,128)(2,1)} %bitcast.14), channel_id=1, source_target_pairs={{0,1},{1,0},{2,3},{3,2},{4,5},{5,4},{6,7},{7,6},{8,9},{9,8},{10,11... | collective-permute-start | bytes 1572872 | tf_op jit(solution)/shard_map/ppermute | solution.py:248
  20.5 11.2 %collective-permute-start.4 = (bf16[256,1024]{1,0:T(8,128)(2,1)}, bf16[256,1024]{1,0:T(8,128)(2,1)S(1)}, u32[]{:S(2)}, u32[]{:S(2)}) collective-permute-start(bf16[256,1024]{1,0:T(8,128)(2,1)} %bitcast.21), channel_id=1, source_target_pairs={{0,1},{1,0},{2,3},{3,2},{4,5},{5,4},{6,7},{7,6},{8,9},{9,8},{10,11... | collective-permute-start | bytes 1572872 | tf_op jit(solution)/shard_map/ppermute | solution.py:248
  23.9 15.5 %collective-permute-start.1 = (bf16[128,2176]{1,0:T(8,128)(2,1)S(1)}, bf16[128,2176]{1,0:T(8,128)(2,1)S(1)}, u32[]{:S(2)}, u32[]{:S(2)}) collective-permute-start(bf16[128,2176]{1,0:T(8,128)(2,1)S(1)} %collective-permute-done.refs_1_), channel_id=1, source_target_pairs={{0,2},{1,15},{2,4},{3,1},{4,6},{5,3},{6,8},{7,5},{8,10},{9,7},{10,... | collective-permute-start | bytes 1671176 | tf_op jit(solution)/shard_map/ppermute | solution.py:248
  28.9 12.5 %collective-permute-start.9 = (bf16[128,2176]{1,0:T(8,128)(2,1)S(1)}, bf16[128,2176]{1,0:T(8,128)(2,1)S(1)}, u32[]{:S(2)}, u32[]{:S(2)}) collective-permute-start(bf16[128,2176]{1,0:T(8,128)(2,1)S(1)} %collective-permute-done.6.refs_0_), channel_id=1, source_target_pairs={{0,2},{1,15},{2,4},{3,1},{4,6},{5,3},{6,8},{7,5},{8,10},{9,7},{10,... | collective-permute-start | bytes 1671176 | tf_op jit(solution)/shard_map/ppermute | solution.py:248
  35.9 10.4 %copy-start.1 = (bf16[1,1024,256]{2,1,0:T(8,128)(2,1)S(1)}, bf16[1,1024,256]{2,1,0:T(8,128)(2,1)}, u32[]{:S(2)}) copy-start(bf16[1,1024,256]{2,1,0:T(8,128)(2,1)} %param.11) | copy-start | bytes 1572868
  35.9 10.4 %copy-start.3 = (bf16[1,1024,256]{2,1,0:T(8,128)(2,1)S(1)}, bf16[1,1024,256]{2,1,0:T(8,128)(2,1)}, u32[]{:S(2)}) copy-start(bf16[1,1024,256]{2,1,0:T(8,128)(2,1)} %param.12) | copy-start | bytes 1572868
  35.9 10.4 %copy-start.5 = (bf16[1,256,1024]{2,1,0:T(8,128)(2,1)S(1)}, bf16[1,256,1024]{2,1,0:T(8,128)(2,1)}, u32[]{:S(2)}) copy-start(bf16[1,256,1024]{2,1,0:T(8,128)(2,1)} %param.13) | copy-start | bytes 1572868
  39.4 11.4 %collective-permute-start.5 = (bf16[128,2176]{1,0:T(8,128)(2,1)S(1)}, bf16[128,2176]{1,0:T(8,128)(2,1)S(1)}, u32[]{:S(2)}, u32[]{:S(2)}) collective-permute-start(bf16[128,2176]{1,0:T(8,128)(2,1)S(1)} %collective-permute-done.1.refs_1_), channel_id=1, source_target_pairs={{0,2},{1,15},{2,4},{3,1},{4,6},{5,3},{6,8},{7,5},{8,10},{9,7},{10,... | collective-permute-start | bytes 1671176 | tf_op jit(solution)/shard_map/ppermute | solution.py:248
  41.4 15.5 %collective-permute-start.13 = (bf16[128,2176]{1,0:T(8,128)(2,1)S(1)}, bf16[128,2176]{1,0:T(8,128)(2,1)S(1)}, u32[]{:S(2)}, u32[]{:S(2)}) collective-permute-start(bf16[128,2176]{1,0:T(8,128)(2,1)S(1)} %collective-permute-done.9.refs_0_), channel_id=1, source_target_pairs={{0,2},{1,15},{2,4},{3,1},{4,6},{5,3},{6,8},{7,5},{8,10},{9,7},{10,... | collective-permute-start | bytes 1671176 | tf_op jit(solution)/shard_map/ppermute | solution.py:248
  50.8 11.1 %collective-permute-start.7 = (bf16[128,2176]{1,0:T(8,128)(2,1)S(1)}, bf16[128,2176]{1,0:T(8,128)(2,1)S(1)}, u32[]{:S(2)}, u32[]{:S(2)}) collective-permute-start(bf16[128,2176]{1,0:T(8,128)(2,1)S(1)} %collective-permute-done.5.refs_1_), channel_id=1, source_target_pairs={{0,2},{1,15},{2,4},{3,1},{4,6},{5,3},{6,8},{7,5},{8,10},{9,7},{10,... | collective-permute-start | bytes 1671176 | tf_op jit(solution)/shard_map/ppermute | solution.py:248
  61.9 9.1 %collective-permute-start.18 = (bf16[32,48,512]{2,1,0:T(8,128)(2,1)S(1)}, bf16[32,48,512]{2,1,0:T(8,128)(2,1)S(1)}, u32[]{:S(2)}, u32[]{:S(2)}) collective-permute-start(bf16[32,48,512]{2,1,0:T(8,128)(2,1)S(1)} %get-tuple-element.55), channel_id=1, source_target_pairs={{0,1},{1,0},{2,3},{3,2},{4,5},{5,4},{6,7},{7,6},{8,9},{9,8},{10,11... | collective-permute-start | bytes 4718600 | tf_op jit(solution)/shard_map/ppermute | solution.py:248
  67.1 3.9 %collective-permute-start.17 = (bf16[128,2176]{1,0:T(8,128)(2,1)S(1)}, bf16[128,2176]{1,0:T(8,128)(2,1)S(1)}, u32[]{:S(2)}, u32[]{:S(2)}) collective-permute-start(bf16[128,2176]{1,0:T(8,128)(2,1)S(1)} %collective-permute-done.7.block), channel_id=1, source_target_pairs={{0,1},{1,0},{2,3},{3,2},{4,5},{5,4},{6,7},{7,6},{8,9},{9,8},{10,11... | collective-permute-start | bytes 1671176 | tf_op jit(solution)/shard_map/ppermute | solution.py:248
  74.2 47.3 %all-to-all-start = ((bf16[32,48,512]{2,1,0:T(8,128)(2,1)}), bf16[32,48,512]{2,1,0:T(8,128)(2,1)S(1)}, u32[]{:S(2)}, u32[]{:S(2)}) async-start(bf16[32,48,512]{2,1,0:T(8,128)(2,1)} %shard_map.122), calls=%async_computation | async-start | bytes 3145728 | tf_op jit(solution)/shard_map/all_to_all | solution.py:304
  83.9 9.2 %collective-permute-start.8 = (bf16[128,1152]{1,0:T(8,128)(2,1)}, bf16[128,1152]{1,0:T(8,128)(2,1)S(1)}, u32[]{:S(2)}, u32[]{:S(2)}) collective-permute-start(bf16[128,1152]{1,0:T(8,128)(2,1)} %copy-done.10), channel_id=1, source_target_pairs={{2,0},{15,1},{4,2},{1,3},{6,4},{3,5},{8,6},{5,7},{10,8},{7,9},{12,... | collective-permute-start | bytes 884744 | tf_op jit(solution)/shard_map/ppermute | solution.py:248
  85.8 10.4 %collective-permute-start.14 = (bf16[128,1152]{1,0:T(8,128)(2,1)S(1)}, bf16[128,1152]{1,0:T(8,128)(2,1)S(1)}, u32[]{:S(2)}, u32[]{:S(2)}) collective-permute-start(bf16[128,1152]{1,0:T(8,128)(2,1)S(1)} %get-tuple-element.44), channel_id=1, source_target_pairs={{2,0},{15,1},{4,2},{1,3},{6,4},{3,5},{8,6},{5,7},{10,8},{7,9},{12,... | collective-permute-start | bytes 884744 | tf_op jit(solution)/shard_map/ppermute | solution.py:248
  93.1 9.0 %collective-permute-start.10 = (bf16[128,1152]{1,0:T(8,128)(2,1)S(1)}, bf16[128,1152]{1,0:T(8,128)(2,1)S(1)}, u32[]{:S(2)}, u32[]{:S(2)}) collective-permute-start(bf16[128,1152]{1,0:T(8,128)(2,1)S(1)} %shard_map.115), channel_id=1, source_target_pairs={{2,0},{15,1},{4,2},{1,3},{6,4},{3,5},{8,6},{5,7},{10,8},{7,9},{12,... | collective-permute-start | bytes 884744 | tf_op jit(solution)/shard_map/ppermute | solution.py:248
  96.3 9.0 %collective-permute-start.15 = (bf16[128,1152]{1,0:T(8,128)(2,1)S(1)}, bf16[128,1152]{1,0:T(8,128)(2,1)S(1)}, u32[]{:S(2)}, u32[]{:S(2)}) collective-permute-start(bf16[128,1152]{1,0:T(8,128)(2,1)S(1)} %shard_map.119), channel_id=1, source_target_pairs={{2,0},{15,1},{4,2},{1,3},{6,4},{3,5},{8,6},{5,7},{10,8},{7,9},{12,... | collective-permute-start | bytes 884744 | tf_op jit(solution)/shard_map/ppermute | solution.py:248
  102.2 9.0 %collective-permute-start.11 = (bf16[128,1152]{1,0:T(8,128)(2,1)S(1)}, bf16[128,1152]{1,0:T(8,128)(2,1)S(1)}, u32[]{:S(2)}, u32[]{:S(2)}) collective-permute-start(bf16[128,1152]{1,0:T(8,128)(2,1)S(1)} %shard_map.116), channel_id=1, source_target_pairs={{2,0},{15,1},{4,2},{1,3},{6,4},{3,5},{8,6},{5,7},{10,8},{7,9},{12,... | collective-permute-start | bytes 884744 | tf_op jit(solution)/shard_map/ppermute | solution.py:248
  105.3 15.2 %copy-start.7 = (s32[128,10]{0,1:T(8,128)S(1)}, s32[128,10]{0,1:T(8,128)}, u32[]{:S(2)}) copy-start(s32[128,10]{0,1:T(8,128)} %param.9) | copy-start | bytes 15364
  105.4 8.8 %collective-permute-start.16 = (bf16[128,1152]{1,0:T(8,128)(2,1)S(1)}, bf16[128,1152]{1,0:T(8,128)(2,1)S(1)}, u32[]{:S(2)}, u32[]{:S(2)}) collective-permute-start(bf16[128,1152]{1,0:T(8,128)(2,1)S(1)} %shard_map.120), channel_id=1, source_target_pairs={{15,0},{2,1},{1,2},{4,3},{3,4},{6,5},{5,6},{8,7},{7,8},{10,9},{9,1... | collective-permute-start | bytes 884744 | tf_op jit(solution)/shard_map/ppermute | solution.py:248
  111.2 9.3 %collective-permute-start.12 = (bf16[128,1152]{1,0:T(8,128)(2,1)S(1)}, bf16[128,1152]{1,0:T(8,128)(2,1)S(1)}, u32[]{:S(2)}, u32[]{:S(2)}) collective-permute-start(bf16[128,1152]{1,0:T(8,128)(2,1)S(1)} %shard_map.117), channel_id=1, source_target_pairs={{2,0},{15,1},{4,2},{1,3},{6,4},{3,5},{8,6},{5,7},{10,8},{7,9},{12,... | collective-permute-start | bytes 884744 | tf_op jit(solution)/shard_map/ppermute | solution.py:248
  (9 other events, 18.1 us)

commit v7 on v6

--- a/solution.py
+++ b/solution.py
@@ -1,4 +1,5 @@
 import functools
+import math
 
 import jax
 import jax.numpy as jnp
@@ -10,8 +11,8 @@
 BF = jnp.bfloat16
 F32 = jnp.float32
 LANES = 128
-HOP_FLOPS = 5_000_000_000
-SIDE_FLOPS = 2_500_000_000
+HOP_FLOPS = 1_000_000_000
+SIDE_FLOPS = 500_000_000
 
 
 def dot(a, b, ca, cb):
@@ -95,17 +96,24 @@
 
 
 def to_parts(out, d_gu, first_row):
-    replicas, rows, wide = out.shape
+    nx, _, rows, wide = out.shape
     n = rows * 2 // 3
-    reps = d_gu.shape[0] // n
-    out[first_row // n : first_row // n + reps, :n, :] = d_gu.astype(BF).reshape(reps, n, wide)
-
-
-def down_to_parts(out, d_down):
-    replicas, rows, half = out.shape
+    y, ys = first_row // (nx * n), d_gu.shape[0] // (nx * n)
+    pieces = d_gu.astype(BF).reshape(ys, nx, n, wide)
+    for x in range(nx):
+        out[x, y : y + ys, :n, :] = pieces[:, x]
+
+
+def down_to_parts(out, d_down, early=None):
+    nx, ny, rows, half = out.shape
     m = rows // 3 // 2
-    pieces = [d_down[:, :half].reshape(replicas, m, half), d_down[:, half:].reshape(replicas, m, half)]
-    out[:, rows - 2 * m :, :] = jnp.concatenate(pieces, axis=1).astype(BF)
+    pieces = [d_down[:, c : c + half].reshape(ny, nx, m, half) for c in (0, half)]
+    pieces = jnp.concatenate(pieces, axis=2)
+    for x in range(nx):
+        piece = pieces[:, x]
+        if early is not None:
+            piece = piece + early[x, :, rows - 2 * m :, :].astype(F32)
+        out[x, :, rows - 2 * m :, :] = piece.astype(BF)
 
 
 def group_kernel(first, swap, n_blocks, expert_ref, *refs):
@@ -138,7 +146,7 @@
 
 
 def steps(outs, swap, width, hidden):
-    step = max(width // outs[2].shape[0], 2 * hidden) if swap else 2 * hidden
+    step = max(width // outs[2].shape[1], 2 * hidden) if swap else 2 * hidden
     return [slice(r, r + step) for r in range(0, width, step)]
 
 
@@ -149,7 +157,7 @@
     out_act[...] = acts[0]
 
 
-def last_kernel(expert_ref, block, pre, act, theirs, w_gate, w_up, w_down, acc_gu, acc_d, early, out):
+def last_kernel(expert_ref, block, pre, act, theirs, w_gate, w_up, w_down, acc_gu, acc_d, early, out, made, sems):
     width, hidden = w_gate.shape
     x, dy, dense = split([theirs], width)
     here = lax.broadcasted_iota(jnp.int32, dense.shape, 1) == expert_ref[0]
@@ -159,15 +167,29 @@
     dy = jnp.concatenate([block[:, width : 2 * width], dy], axis=0)
     grads = jnp.concatenate([pre[...], jnp.concatenate([gate_pre, up_pre], axis=1)], axis=0)
     gated = jnp.concatenate([act[...], gated], axis=0)
-    replicas, rows, wide = out.shape
-    n, m = width // replicas, hidden // replicas
-    step = max(n, 2 * hidden)
+    nx, ny, rows, wide = out.shape
+    n = rows * 2 // 3
+    step = max(nx * n, 2 * hidden)
+    copies = []
+
+    def leave(*where):
+        copies.append(pltpu.make_async_copy(made.at[where], out.at[where], sems.at[len(copies)]))
+        copies[-1].start()
+
     for r in range(0, width, step):
-        partner = early[r // n : (r + step) // n, :n, :].reshape(step, wide).astype(F32)
-        d_gu = dot(x[:, r : r + step], grads, 0, 0) + acc_gu[r : r + step, :] + partner
-        to_parts(out, d_gu, r)
-    down_to_parts(out, dot(gated, dy, 0, 0) + acc_d[...])
-    out[:, n:, :] = (out[:, n:, :].astype(F32) + early[:, n:, :].astype(F32)).astype(BF)
+        y, ys = r // (nx * n), step // (nx * n)
+        partner = jnp.stack([early[p, y : y + ys, :n, :] for p in range(nx)], axis=1)
+        d_gu = dot(x[:, r : r + step], grads, 0, 0) + acc_gu[r : r + step, :]
+        to_parts(made, d_gu + partner.reshape(step, wide).astype(F32), r)
+        leave(slice(None), pl.ds(y, ys), pl.ds(0, n))
+    down_to_parts(made, dot(gated, dy, 0, 0) + acc_d[...], early)
+    leave(slice(None), slice(None), pl.ds(n, rows - n))
+    for copy in copies:
+        copy.wait()
+
+
+def halfway_kernel(parts, out):
+    out[...] = jnp.sum(parts[...].astype(F32), axis=0).astype(BF)
 
 
 def sum_kernel(parts, gate, up, down):
@@ -181,19 +203,20 @@
 VMEM = pl.BlockSpec(memory_space=pltpu.VMEM)
 
 
-def call(kernel, out_shape, expert, operands, aliases, flops):
+def call(kernel, out_shape, expert, operands, aliases, flops, out_specs=VMEM, scratch=()):
     return pl.pallas_call(
         kernel,
         out_shape=out_shape,
         in_specs=[pl.BlockSpec(memory_space=pltpu.SMEM)] + [VMEM] * len(operands),
-        out_specs=[VMEM] * len(out_shape),
+        out_specs=[out_specs] * len(out_shape),
+        scratch_shapes=scratch,
         input_output_aliases=aliases,
         compiler_params=pltpu.CompilerParams(vmem_limit_bytes=26 * 1024 * 1024),
         cost_estimate=pl.CostEstimate(flops=flops, bytes_accessed=16 * 1024 * 1024, transcendentals=0),
     )(expert, *operands)
 
 
-def group(expert, blocks, weights, acc, replicas=0):
+def group(expert, blocks, weights, acc, replicas=()):
     rows = blocks[0].shape[0]
     width, hidden = weights[0].shape
     own = 2 * hidden if replicas else 4 * hidden
@@ -202,7 +225,7 @@
         jax.ShapeDtypeStruct((own // 2, width), F32),
     ]
     if replicas:
-        shapes.append(jax.ShapeDtypeStruct((replicas, (width + 2 * hidden) // replicas, 2 * hidden), BF))
+        shapes.append(jax.ShapeDtypeStruct((*replicas, (width + 2 * hidden) // math.prod(replicas), 2 * hidden), BF))
     n = len(blocks)
     return call(
         functools.partial(group_kernel, not acc, bool(replicas), n),
@@ -236,6 +259,10 @@
 def on_device(tokens, cotangent, routing, gates, gate_weight, up_weight, down_weight):
     groups = lax.axis_size("expert")
     replicas = lax.axis_size("dp")
+    nx = 4 if replicas % 4 == 0 else 1
+    ny = replicas // nx
+    along_x = [[y * nx + x for x in range(nx)] for y in range(ny)]
+    along_y = [[y * nx + x for y in range(ny)] for x in range(nx)]
     rows, width = tokens.shape
     hidden = gate_weight.shape[2]
     out = [(i, (i + 2 if i % 2 == 0 else i - 2) % groups) for i in range(groups)]
@@ -274,7 +301,7 @@
     b3 = send(b2, out)
     a4 = send(after(a3, g_a2), out)
     g_b2, g_a3, *acc = group(expert, (b2, a3), weights, acc)
-    g_b3, *acc, early = group(expert, (b3,), weights, acc, replicas)
+    g_b3, *acc, early = group(expert, (b3,), weights, acc, (nx, ny))
     early = send(after(early, a4), swap)
     theirs = send(a4, swap)
     g_a4, pre, act = call(
@@ -296,12 +323,24 @@
         (a4, pre, act, theirs, *weights[:3], *acc, early),
         {},
         2 * rows * width * hidden * 9,
+        in_hbm,
+        [pltpu.VMEM(early.shape, BF), pltpu.SemaphoreType.DMA((8,))],
     )
 
     b = send(g_b3, home)
     a = send(g_a4, home)
 
-    parts = lax.all_to_all(parts, "dp", split_axis=0, concat_axis=0, tiled=True)
+    if nx > 1:
+        parts = lax.all_to_all(parts, "dp", split_axis=0, concat_axis=0, axis_index_groups=along_x, tiled=True)
+    parts = pl.pallas_call(
+        halfway_kernel,
+        out_shape=jax.ShapeDtypeStruct(parts.shape[1:], BF),
+        in_specs=[VMEM],
+        out_specs=VMEM,
+        compiler_params=pltpu.CompilerParams(vmem_limit_bytes=8 * 1024 * 1024),
+    )(parts)
+    if ny > 1:
+        parts = lax.all_to_all(parts, "dp", split_axis=0, concat_axis=0, axis_index_groups=along_y, tiled=True)
     slab = jax.ShapeDtypeStruct((1, width // replicas, hidden), F32)
     sums = pl.pallas_call(
         sum_kernel,

time: 125 us -> 128 us (1.024)
  starting transfers between devices: 68.4 us -> 71.9 us
  Pallas kernels: 21.4 us -> 23.7 us
  waiting for transfers between devices: 25.2 us -> 23.3 us
    ppermute x19, waiting for transfers between devices: 25.2 us -> 17.7 us  [send(): return lax.ppermute(a, 'expert', pairs)]
    all_to_all x1 -> x2, waiting for transfers between devices: 0.01 us -> 5.67 us  [on_device(): lax.all_to_all(parts, 'dp', split_axis=0, concat_axis=0, axis_index_group...]
    ppermute x19, starting transfers between devices: 58.7 us -> 61.1 us  [send(): return lax.ppermute(a, 'expert', pairs)]
    pallas_call x5, Pallas kernels: 0.36 us -> 2.08 us  [add(): pl.pallas_call(add_kernel, out_shape=jax.ShapeDtypeStruct(p.shape, BF), i...]
    all_to_all x1 -> x2, starting transfers between devices: 9.67 us -> 10.8 us  [on_device(): lax.all_to_all(parts, 'dp', split_axis=0, concat_axis=0, axis_index_group...]
  transfers between devices with their start and end apart: 20 -> 21, of which waited for: 9 -> 8; matrix products, arithmetic and copies ran while one was open for 0% -> 0% of each run, Pallas kernels for 13% -> 15%
where the time goes in v7:
time: 128 us; the launch traced here: 126 us
  starting transfers between devices  71.9 us (56%)
  Pallas kernels  23.7 us (19%)
  waiting for transfers between devices  23.3 us (18%)
  local copies, waits for them, and re-layouts  6.32 us (5%)
    ppermute x19, starting transfers between devices, send(): return lax.ppermute(a, 'expert', pairs)  61.1 us
    ppermute x19, waiting for transfers between devices, send(): return lax.ppermute(a, 'expert', pairs)  17.7 us
    pallas_call x6, Pallas kernels, call(): pl.pallas_call(kernel, out_shape=out_shape, in_specs=[pl.BlockSpec(memory...  17.1 us
    all_to_all x2, starting transfers between devices, on_device(): lax.all_to_all(parts, 'dp', split_axis=0, concat_axis=0, axis_index_group...  10.8 us
    unnamed x26, local copies, waits for them, and re-layouts  6.32 us
    all_to_all x2, waiting for transfers between devices, on_device(): lax.all_to_all(parts, 'dp', split_axis=0, concat_axis=0, axis_index_group...  5.67 us
  transfers between devices with their start and end apart: 21, of which 8 were waited for; matrix products, arithmetic and copies ran while one was open for 0% of the time, Pallas kernels for 15%

profile of v7, /device:TPU:1, one launch (start us, length us, event | category | flops | bytes accessed | tf_op | source)
XLA Modules:
  0.0 126.3 jit_solution(2029669165443313703)
XLA Ops:
  2.5 11.5 %collective-permute-start = (bf16[128,2176]{1,0:T(8,128)(2,1)}, bf16[128,2176]{1,0:T(8,128)(2,1)S(1)}, u32[]{:S(2)}, u32[]{:S(2)}) collective-permute-start(bf16[128,2176]{1,0:T(8,128)(2,1)} %shard_map.110.refs_0_), channel_id=1, source_target_pairs={{0,2},{1,15},{2,4},{3,1},{4,6},{5,3},{6,8},{7,5},{8,10},{9,7},{10,... | collective-permute-start | bytes 1671176 | tf_op jit(solution)/shard_map/ppermute | solution.py:275
  16.0 2.6 %collective-permute-start.2 = (bf16[1024,256]{1,0:T(8,128)(2,1)}, bf16[1024,256]{1,0:T(8,128)(2,1)S(1)}, u32[]{:S(2)}, u32[]{:S(2)}) collective-permute-start(bf16[1024,256]{1,0:T(8,128)(2,1)} %bitcast.7), channel_id=1, source_target_pairs={{0,1},{1,0},{2,3},{3,2},{4,5},{5,4},{6,7},{7,6},{8,9},{9,8},{10,11... | collective-permute-start | bytes 1572872 | tf_op jit(solution)/shard_map/ppermute | solution.py:275
  18.6 1.9 %collective-permute-start.3 = (bf16[1024,256]{1,0:T(8,128)(2,1)}, bf16[1024,256]{1,0:T(8,128)(2,1)S(1)}, u32[]{:S(2)}, u32[]{:S(2)}) collective-permute-start(bf16[1024,256]{1,0:T(8,128)(2,1)} %bitcast.14), channel_id=1, source_target_pairs={{0,1},{1,0},{2,3},{3,2},{4,5},{5,4},{6,7},{7,6},{8,9},{9,8},{10,11... | collective-permute-start | bytes 1572872 | tf_op jit(solution)/shard_map/ppermute | solution.py:275
  20.5 2.4 %collective-permute-start.4 = (bf16[256,1024]{1,0:T(8,128)(2,1)}, bf16[256,1024]{1,0:T(8,128)(2,1)S(1)}, u32[]{:S(2)}, u32[]{:S(2)}) collective-permute-start(bf16[256,1024]{1,0:T(8,128)(2,1)} %bitcast.21), channel_id=1, source_target_pairs={{0,1},{1,0},{2,3},{3,2},{4,5},{5,4},{6,7},{7,6},{8,9},{9,8},{10,11... | collective-permute-start | bytes 1572872 | tf_op jit(solution)/shard_map/ppermute | solution.py:275
  24.0 4.9 %collective-permute-start.1 = (bf16[128,2176]{1,0:T(8,128)(2,1)S(1)}, bf16[128,2176]{1,0:T(8,128)(2,1)S(1)}, u32[]{:S(2)}, u32[]{:S(2)}) collective-permute-start(bf16[128,2176]{1,0:T(8,128)(2,1)S(1)} %collective-permute-done.refs_1_), channel_id=1, source_target_pairs={{0,2},{1,15},{2,4},{3,1},{4,6},{5,3},{6,8},{7,5},{8,10},{9,7},{10,... | collective-permute-start | bytes 1671176 | tf_op jit(solution)/shard_map/ppermute | solution.py:275
  28.9 2.8 %collective-permute-start.9 = (bf16[128,2176]{1,0:T(8,128)(2,1)S(1)}, bf16[128,2176]{1,0:T(8,128)(2,1)S(1)}, u32[]{:S(2)}, u32[]{:S(2)}) collective-permute-start(bf16[128,2176]{1,0:T(8,128)(2,1)S(1)} %collective-permute-done.6.refs_0_), channel_id=1, source_target_pairs={{0,2},{1,15},{2,4},{3,1},{4,6},{5,3},{6,8},{7,5},{8,10},{9,7},{10,... | collective-permute-start | bytes 1671176 | tf_op jit(solution)/shard_map/ppermute | solution.py:275
  35.9 2.8 %shard_map.111 = (bf16[128,1152]{1,0:T(8,128)(2,1)S(1)}, bf16[128,1152]{1,0:T(8,128)(2,1)S(1)}, f32[1024,1024]{1,0:T(8,128)S(1)}, f32[512,1024]{1,0:T(8,128)S(1)}) custom-call(s32[1]{0:T(128)} %bitcast.1.expert_ref, bf16[128,2176]{1,0:T(8,128)(2,1)S(1)} %copy-done.6, bf16[128,2176]{1,0:T(8,128)(2,1)S(1)} %collective-permute-done.refs_1_, ...), custom_call_target="tpu_custom_call" | custom-call | flops 2147483648 | bytes 16777216 | tf_op jit(solution)/shard_map/pallas_call | solution.py:207
  41.4 4.9 %collective-permute-start.13 = (bf16[128,2176]{1,0:T(8,128)(2,1)S(1)}, bf16[128,2176]{1,0:T(8,128)(2,1)S(1)}, u32[]{:S(2)}, u32[]{:S(2)}) collective-permute-start(bf16[128,2176]{1,0:T(8,128)(2,1)S(1)} %collective-permute-done.9.refs_0_), channel_id=1, source_target_pairs={{0,2},{1,15},{2,4},{3,1},{4,6},{5,3},{6,8},{7,5},{8,10},{9,7},{10,... | collective-permute-start | bytes 1671176 | tf_op jit(solution)/shard_map/ppermute | solution.py:275
  46.4 3.8 %shard_map.112 = (bf16[128,1152]{1,0:T(8,128)(2,1)S(1)}, bf16[128,1152]{1,0:T(8,128)(2,1)S(1)}, f32[1024,1024]{1,0:T(8,128)S(1)}, f32[512,1024]{1,0:T(8,128)S(1)}) custom-call(s32[1]{0:T(128)} %bitcast.1.expert_ref, bf16[128,2176]{1,0:T(8,128)(2,1)S(1)} %collective-permute-done.6.refs_0_, ...), custom_call_target="tpu_custom_call", output_to_operand_aliasing={{2}: (9, {}), {3}: (10, {})} | custom-call | flops 2147483648 | bytes 16777216 | tf_op jit(solution)/shard_map/pallas_call | solution.py:207
  50.9 2.2 %collective-permute-start.7 = (bf16[128,2176]{1,0:T(8,128)(2,1)S(1)}, bf16[128,2176]{1,0:T(8,128)(2,1)S(1)}, u32[]{:S(2)}, u32[]{:S(2)}) collective-permute-start(bf16[128,2176]{1,0:T(8,128)(2,1)S(1)} %collective-permute-done.5.refs_1_), channel_id=1, source_target_pairs={{0,2},{1,15},{2,4},{3,1},{4,6},{5,3},{6,8},{7,5},{8,10},{9,7},{10,... | collective-permute-start | bytes 1671176 | tf_op jit(solution)/shard_map/ppermute | solution.py:275
  53.0 3.8 %shard_map.114 = (bf16[128,1152]{1,0:T(8,128)(2,1)S(1)}, bf16[128,1152]{1,0:T(8,128)(2,1)S(1)}, f32[1024,1024]{1,0:T(8,128)S(1)}, f32[512,1024]{1,0:T(8,128)S(1)}) custom-call(s32[1]{0:T(128)} %bitcast.1.expert_ref, bf16[128,2176]{1,0:T(8,128)(2,1)S(1)} %collective-permute-done.9.refs_0_, ...), custom_call_target="tpu_custom_call", output_to_operand_aliasing={{2}: (9, {}), {3}: (10, {})} | custom-call | flops 2147483648 | bytes 16777216 | tf_op jit(solution)/shard_map/pallas_call | solution.py:207
  56.9 2.5 %shard_map.118 = (bf16[128,1152]{1,0:T(8,128)(2,1)S(1)}, f32[1024,512]{1,0:T(8,128)S(1)}, f32[256,1024]{1,0:T(8,128)S(1)}, bf16[4,8,48,512]{3,2,1,0:T(8,128)(2,1)S(1)}) custom-call(s32[1]{0:T(128)} %bitcast.1.expert_ref, bf16[128,2176]{1,0:T(8,128)(2,1)S(1)} %collective-permute-done.13.refs_0_, bf16[1024,256]{1,0:T(8,128)(2,1)S(1)} %bitcast.11, ...), custom_call_target="tpu_custom_call" | custom-call | flops 1073741824 | bytes 16777216 | tf_op jit(solution)/shard_map/pallas_call | solution.py:207
  59.3 2.6 %collective-permute-done.7.block = bf16[128,2176]{1,0:T(8,128)(2,1)S(1)} collective-permute-done((bf16[128,2176]{1,0:T(8,128)(2,1)S(1)}, bf16[128,2176]{1,0:T(8,128)(2,1)S(1)}, u32[]{:S(2)}, u32[]{:S(2)}) %collective-permute-start.7) | collective-permute-done | bytes 557088 | tf_op jit(solution)/shard_map/ppermute | solution.py:275
  61.9 5.1 %collective-permute-start.18 = (bf16[4,8,48,512]{3,2,1,0:T(8,128)(2,1)S(1)}, bf16[4,8,48,512]{3,2,1,0:T(8,128)(2,1)S(1)}, u32[]{:S(2)}, u32[]{:S(2)}) collective-permute-start(bf16[4,8,48,512]{3,2,1,0:T(8,128)(2,1)S(1)} %get-tuple-element.55), channel_id=1, source_target_pairs={{0,1},{1,0},{2,3},{3,2},{4,5},{5,4},{6,7},{7,6},{8,9},{9,8},{10,11... | collective-permute-start | bytes 4718600 | tf_op jit(solution)/shard_map/ppermute | solution.py:275
  69.0 2.0 %shard_map.113 = (bf16[128,1152]{1,0:T(8,128)(2,1)S(1)}, bf16[128,512]{1,0:T(8,128)(2,1)S(1)}, bf16[128,256]{1,0:T(8,128)(2,1)S(1)}) custom-call(s32[1]{0:T(128)} %bitcast.1.expert_ref, bf16[128,2176]{1,0:T(8,128)(2,1)S(1)} %collective-permute-done.7.block, bf16[1024,256]{1,0:T(8,128)(2,1)S(1)} %bitcast.12, bf16[1024,256]{1,0:T(8,128)(2,1)S(1)} %bitcast.19, ...), custom_call_target="tpu_custom_call" | custom-call | flops 671088640 | bytes 16777216 | tf_op jit(solution)/shard_map/pallas_call | solution.py:207
  71.8 2.2 %shard_map.122 = bf16[4,8,48,512]{3,2,1,0:T(8,128)(2,1)} custom-call(s32[1]{0:T(128)} %bitcast.1.expert_ref, bf16[128,2176]{1,0:T(8,128)(2,1)S(1)} %collective-permute-done.7.block, bf16[128,512]{1,0:T(8,128)(2,1)S(1)} %get-tuple-element.50.pre, bf16[128,256]{1,0:T(8,128)(2,1)S(1)} %get-tuple-element.51.act, ...), custom_call_target="tpu_custom_call" | custom-call | flops 603979776 | bytes 16777216 | tf_op jit(solution)/shard_map/pallas_call | solution.py:207
  74.0 4.0 %all-to-all-start = ((bf16[4,8,48,512]{3,2,1,0:T(8,128)(2,1)}), bf16[4,8,48,512]{3,2,1,0:T(8,128)(2,1)S(1)}, u32[]{:S(2)}, u32[]{:S(2)}) async-start(bf16[4,8,48,512]{3,2,1,0:T(8,128)(2,1)} %shard_map.122), calls=%async_computation | async-start | bytes 3145728 | tf_op jit(solution)/shard_map/all_to_all | solution.py:334
  79.9 1.9 %collective-permute-start.14 = (bf16[128,1152]{1,0:T(8,128)(2,1)S(1)}, bf16[128,1152]{1,0:T(8,128)(2,1)S(1)}, u32[]{:S(2)}, u32[]{:S(2)}) collective-permute-start(bf16[128,1152]{1,0:T(8,128)(2,1)S(1)} %get-tuple-element.44), channel_id=1, source_target_pairs={{2,0},{15,1},{4,2},{1,3},{6,4},{3,5},{8,6},{5,7},{10,8},{7,9},{12,... | collective-permute-start | bytes 884744 | tf_op jit(solution)/shard_map/ppermute | solution.py:275
  81.9 5.3 %collective-permute-done.8.p = bf16[128,1152]{1,0:T(8,128)(2,1)S(1)} collective-permute-done((bf16[128,1152]{1,0:T(8,128)(2,1)}, bf16[128,1152]{1,0:T(8,128)(2,1)S(1)}, u32[]{:S(2)}, u32[]{:S(2)}) %collective-permute-start.8) | collective-permute-done | bytes 294944 | tf_op jit(solution)/shard_map/ppermute | solution.py:275
  92.4 5.7 %all-to-all-done.parts = bf16[4,8,48,512]{3,2,1,0:T(8,128)(2,1)S(1)} async-done(((bf16[4,8,48,512]{3,2,1,0:T(8,128)(2,1)}), bf16[4,8,48,512]{3,2,1,0:T(8,128)(2,1)S(1)}, u32[]{:S(2)}, u32[]{:S(2)}) %all-to-all-start) | async-done | bytes 1572896 | tf_op jit(solution)/shard_map/all_to_all | solution.py:334
  99.0 6.8 %all-to-all-start.1 = ((bf16[8,48,512]{2,1,0:T(8,128)(2,1)}), bf16[8,48,512]{2,1,0:T(8,128)(2,1)S(1)}, u32[]{:S(2)}, u32[]{:S(2)}) async-start(bf16[8,48,512]{2,1,0:T(8,128)(2,1)} %shard_map.123), calls=%async_computation.1 | async-start | bytes 786432 | tf_op jit(solution)/shard_map/all_to_all | solution.py:343
  108.9 5.5 %collective-permute-start.16 = (bf16[128,1152]{1,0:T(8,128)(2,1)S(1)}, bf16[128,1152]{1,0:T(8,128)(2,1)S(1)}, u32[]{:S(2)}, u32[]{:S(2)}) collective-permute-start(bf16[128,1152]{1,0:T(8,128)(2,1)S(1)} %shard_map.120), channel_id=1, source_target_pairs={{15,0},{2,1},{1,2},{4,3},{3,4},{6,5},{5,6},{8,7},{7,8},{10,9},{9,1... | collective-permute-start | bytes 884744 | tf_op jit(solution)/shard_map/ppermute | solution.py:275
  117.9 2.4 %collective-permute-done.16.q = bf16[128,1152]{1,0:T(8,128)(2,1)S(1)} collective-permute-done((bf16[128,1152]{1,0:T(8,128)(2,1)S(1)}, bf16[128,1152]{1,0:T(8,128)(2,1)S(1)}, u32[]{:S(2)}, u32[]{:S(2)}) %collective-permute-start.16) | collective-permute-done | bytes 294944 | tf_op jit(solution)/shard_map/ppermute | solution.py:275
  120.2 4.4 %collective-permute-done.12.p = bf16[128,1152]{1,0:T(8,128)(2,1)S(1)} collective-permute-done((bf16[128,1152]{1,0:T(8,128)(2,1)S(1)}, bf16[128,1152]{1,0:T(8,128)(2,1)S(1)}, u32[]{:S(2)}, u32[]{:S(2)}) %collective-permute-start.12) | collective-permute-done | bytes 294944 | tf_op jit(solution)/shard_map/ppermute | solution.py:275
  (59 shorter events, 31.2 us)
Async XLA Ops:
  2.5 21.4 %collective-permute-start = (bf16[128,2176]{1,0:T(8,128)(2,1)}, bf16[128,2176]{1,0:T(8,128)(2,1)S(1)}, u32[]{:S(2)}, u32[]{:S(2)}) collective-permute-start(bf16[128,2176]{1,0:T(8,128)(2,1)} %shard_map.110.refs_0_), channel_id=1, source_target_pairs={{0,2},{1,15},{2,4},{3,1},{4,6},{5,3},{6,8},{7,5},{8,10},{9,7},{10,... | collective-permute-start | bytes 1671176 | tf_op jit(solution)/shard_map/ppermute | solution.py:275
  14.1 14.8 %collective-permute-start.6 = (bf16[128,2176]{1,0:T(8,128)(2,1)}, bf16[128,2176]{1,0:T(8,128)(2,1)S(1)}, u32[]{:S(2)}, u32[]{:S(2)}) collective-permute-start(bf16[128,2176]{1,0:T(8,128)(2,1)} %shard_map.110.refs_0_), channel_id=1, source_target_pairs={{0,15},{1,2},{2,1},{3,4},{4,3},{5,6},{6,5},{7,8},{8,7},{9,10},{10,... | collective-permute-start | bytes 1671176 | tf_op jit(solution)/shard_map/ppermute | solution.py:275
  16.0 15.7 %collective-permute-start.2 = (bf16[1024,256]{1,0:T(8,128)(2,1)}, bf16[1024,256]{1,0:T(8,128)(2,1)S(1)}, u32[]{:S(2)}, u32[]{:S(2)}) collective-permute-start(bf16[1024,256]{1,0:T(8,128)(2,1)} %bitcast.7), channel_id=1, source_target_pairs={{0,1},{1,0},{2,3},{3,2},{4,5},{5,4},{6,7},{7,6},{8,9},{9,8},{10,11... | collective-permute-start | bytes 1572872 | tf_op jit(solution)/shard_map/ppermute | solution.py:275
  18.6 13.2 %collective-permute-start.3 = (bf16[1024,256]{1,0:T(8,128)(2,1)}, bf16[1024,256]{1,0:T(8,128)(2,1)S(1)}, u32[]{:S(2)}, u32[]{:S(2)}) collective-permute-start(bf16[1024,256]{1,0:T(8,128)(2,1)} %bitcast.14), channel_id=1, source_target_pairs={{0,1},{1,0},{2,3},{3,2},{4,5},{5,4},{6,7},{7,6},{8,9},{9,8},{10,11... | collective-permute-start | bytes 1572872 | tf_op jit(solution)/shard_map/ppermute | solution.py:275
  20.5 11.2 %collective-permute-start.4 = (bf16[256,1024]{1,0:T(8,128)(2,1)}, bf16[256,1024]{1,0:T(8,128)(2,1)S(1)}, u32[]{:S(2)}, u32[]{:S(2)}) collective-permute-start(bf16[256,1024]{1,0:T(8,128)(2,1)} %bitcast.21), channel_id=1, source_target_pairs={{0,1},{1,0},{2,3},{3,2},{4,5},{5,4},{6,7},{7,6},{8,9},{9,8},{10,11... | collective-permute-start | bytes 1572872 | tf_op jit(solution)/shard_map/ppermute | solution.py:275
  24.0 15.5 %collective-permute-start.1 = (bf16[128,2176]{1,0:T(8,128)(2,1)S(1)}, bf16[128,2176]{1,0:T(8,128)(2,1)S(1)}, u32[]{:S(2)}, u32[]{:S(2)}) collective-permute-start(bf16[128,2176]{1,0:T(8,128)(2,1)S(1)} %collective-permute-done.refs_1_), channel_id=1, source_target_pairs={{0,2},{1,15},{2,4},{3,1},{4,6},{5,3},{6,8},{7,5},{8,10},{9,7},{10,... | collective-permute-start | bytes 1671176 | tf_op jit(solution)/shard_map/ppermute | solution.py:275
  28.9 12.5 %collective-permute-start.9 = (bf16[128,2176]{1,0:T(8,128)(2,1)S(1)}, bf16[128,2176]{1,0:T(8,128)(2,1)S(1)}, u32[]{:S(2)}, u32[]{:S(2)}) collective-permute-start(bf16[128,2176]{1,0:T(8,128)(2,1)S(1)} %collective-permute-done.6.refs_0_), channel_id=1, source_target_pairs={{0,2},{1,15},{2,4},{3,1},{4,6},{5,3},{6,8},{7,5},{8,10},{9,7},{10,... | collective-permute-start | bytes 1671176 | tf_op jit(solution)/shard_map/ppermute | solution.py:275
  35.9 10.4 %copy-start.5 = (bf16[1,256,1024]{2,1,0:T(8,128)(2,1)S(1)}, bf16[1,256,1024]{2,1,0:T(8,128)(2,1)}, u32[]{:S(2)}) copy-start(bf16[1,256,1024]{2,1,0:T(8,128)(2,1)} %param.13) | copy-start | bytes 1572868
  39.4 11.4 %collective-permute-start.5 = (bf16[128,2176]{1,0:T(8,128)(2,1)S(1)}, bf16[128,2176]{1,0:T(8,128)(2,1)S(1)}, u32[]{:S(2)}, u32[]{:S(2)}) collective-permute-start(bf16[128,2176]{1,0:T(8,128)(2,1)S(1)} %collective-permute-done.1.refs_1_), channel_id=1, source_target_pairs={{0,2},{1,15},{2,4},{3,1},{4,6},{5,3},{6,8},{7,5},{8,10},{9,7},{10,... | collective-permute-start | bytes 1671176 | tf_op jit(solution)/shard_map/ppermute | solution.py:275
  41.4 15.5 %collective-permute-start.13 = (bf16[128,2176]{1,0:T(8,128)(2,1)S(1)}, bf16[128,2176]{1,0:T(8,128)(2,1)S(1)}, u32[]{:S(2)}, u32[]{:S(2)}) collective-permute-start(bf16[128,2176]{1,0:T(8,128)(2,1)S(1)} %collective-permute-done.9.refs_0_), channel_id=1, source_target_pairs={{0,2},{1,15},{2,4},{3,1},{4,6},{5,3},{6,8},{7,5},{8,10},{9,7},{10,... | collective-permute-start | bytes 1671176 | tf_op jit(solution)/shard_map/ppermute | solution.py:275
  50.9 11.1 %collective-permute-start.7 = (bf16[128,2176]{1,0:T(8,128)(2,1)S(1)}, bf16[128,2176]{1,0:T(8,128)(2,1)S(1)}, u32[]{:S(2)}, u32[]{:S(2)}) collective-permute-start(bf16[128,2176]{1,0:T(8,128)(2,1)S(1)} %collective-permute-done.5.refs_1_), channel_id=1, source_target_pairs={{0,2},{1,15},{2,4},{3,1},{4,6},{5,3},{6,8},{7,5},{8,10},{9,7},{10,... | collective-permute-start | bytes 1671176 | tf_op jit(solution)/shard_map/ppermute | solution.py:275
  61.9 9.1 %collective-permute-start.18 = (bf16[4,8,48,512]{3,2,1,0:T(8,128)(2,1)S(1)}, bf16[4,8,48,512]{3,2,1,0:T(8,128)(2,1)S(1)}, u32[]{:S(2)}, u32[]{:S(2)}) collective-permute-start(bf16[4,8,48,512]{3,2,1,0:T(8,128)(2,1)S(1)} %get-tuple-element.55), channel_id=1, source_target_pairs={{0,1},{1,0},{2,3},{3,2},{4,5},{5,4},{6,7},{7,6},{8,9},{9,8},{10,11... | collective-permute-start | bytes 4718600 | tf_op jit(solution)/shard_map/ppermute | solution.py:275
  67.1 3.9 %collective-permute-start.17 = (bf16[128,2176]{1,0:T(8,128)(2,1)S(1)}, bf16[128,2176]{1,0:T(8,128)(2,1)S(1)}, u32[]{:S(2)}, u32[]{:S(2)}) collective-permute-start(bf16[128,2176]{1,0:T(8,128)(2,1)S(1)} %collective-permute-done.7.block), channel_id=1, source_target_pairs={{0,1},{1,0},{2,3},{3,2},{4,5},{5,4},{6,7},{7,6},{8,9},{9,8},{10,11... | collective-permute-start | bytes 1671176 | tf_op jit(solution)/shard_map/ppermute | solution.py:275
  74.0 24.0 %all-to-all-start = ((bf16[4,8,48,512]{3,2,1,0:T(8,128)(2,1)}), bf16[4,8,48,512]{3,2,1,0:T(8,128)(2,1)S(1)}, u32[]{:S(2)}, u32[]{:S(2)}) async-start(bf16[4,8,48,512]{3,2,1,0:T(8,128)(2,1)} %shard_map.122), calls=%async_computation | async-start | bytes 3145728 | tf_op jit(solution)/shard_map/all_to_all | solution.py:334
  78.0 9.2 %collective-permute-start.8 = (bf16[128,1152]{1,0:T(8,128)(2,1)}, bf16[128,1152]{1,0:T(8,128)(2,1)S(1)}, u32[]{:S(2)}, u32[]{:S(2)}) collective-permute-start(bf16[128,1152]{1,0:T(8,128)(2,1)} %copy-done.10), channel_id=1, source_target_pairs={{2,0},{15,1},{4,2},{1,3},{6,4},{3,5},{8,6},{5,7},{10,8},{7,9},{12,... | collective-permute-start | bytes 884744 | tf_op jit(solution)/shard_map/ppermute | solution.py:275
  79.9 10.4 %collective-permute-start.14 = (bf16[128,1152]{1,0:T(8,128)(2,1)S(1)}, bf16[128,1152]{1,0:T(8,128)(2,1)S(1)}, u32[]{:S(2)}, u32[]{:S(2)}) collective-permute-start(bf16[128,1152]{1,0:T(8,128)(2,1)S(1)} %get-tuple-element.44), channel_id=1, source_target_pairs={{2,0},{15,1},{4,2},{1,3},{6,4},{3,5},{8,6},{5,7},{10,8},{7,9},{12,... | collective-permute-start | bytes 884744 | tf_op jit(solution)/shard_map/ppermute | solution.py:275
  88.0 17.8 %collective-permute-start.10 = (bf16[128,1152]{1,0:T(8,128)(2,1)}, bf16[128,1152]{1,0:T(8,128)(2,1)}, u32[]{:S(2)}, u32[]{:S(2)}) collective-permute-start(bf16[128,1152]{1,0:T(8,128)(2,1)} %shard_map.115), channel_id=1, source_target_pairs={{2,0},{15,1},{4,2},{1,3},{6,4},{3,5},{8,6},{5,7},{10,8},{7,9},{12,... | collective-permute-start | bytes 884744 | tf_op jit(solution)/shard_map/ppermute | solution.py:275
  90.4 15.4 %copy-start.9 = (bf16[128,1152]{1,0:T(8,128)(2,1)S(1)}, bf16[128,1152]{1,0:T(8,128)(2,1)}, u32[]{:S(2)}) copy-start(bf16[128,1152]{1,0:T(8,128)(2,1)} %copy-done.8) | copy-start | bytes 884740
  90.4 18.4 %collective-permute-start.15 = (bf16[128,1152]{1,0:T(8,128)(2,1)S(1)}, bf16[128,1152]{1,0:T(8,128)(2,1)S(1)}, u32[]{:S(2)}, u32[]{:S(2)}) collective-permute-start(bf16[128,1152]{1,0:T(8,128)(2,1)S(1)} %shard_map.119), channel_id=1, source_target_pairs={{2,0},{15,1},{4,2},{1,3},{6,4},{3,5},{8,6},{5,7},{10,8},{7,9},{12,... | collective-permute-start | bytes 884744 | tf_op jit(solution)/shard_map/ppermute | solution.py:275
  99.0 26.7 %all-to-all-start.1 = ((bf16[8,48,512]{2,1,0:T(8,128)(2,1)}), bf16[8,48,512]{2,1,0:T(8,128)(2,1)S(1)}, u32[]{:S(2)}, u32[]{:S(2)}) async-start(bf16[8,48,512]{2,1,0:T(8,128)(2,1)} %shard_map.123), calls=%async_computation.1 | async-start | bytes 786432 | tf_op jit(solution)/shard_map/all_to_all | solution.py:343
  106.9 9.0 %collective-permute-start.11 = (bf16[128,1152]{1,0:T(8,128)(2,1)S(1)}, bf16[128,1152]{1,0:T(8,128)(2,1)S(1)}, u32[]{:S(2)}, u32[]{:S(2)}) collective-permute-start(bf16[128,1152]{1,0:T(8,128)(2,1)S(1)} %shard_map.116), channel_id=1, source_target_pairs={{2,0},{15,1},{4,2},{1,3},{6,4},{3,5},{8,6},{5,7},{10,8},{7,9},{12,... | collective-permute-start | bytes 884744 | tf_op jit(solution)/shard_map/ppermute | solution.py:275
  108.9 15.7 %copy-start.7 = (s32[128,10]{0,1:T(8,128)S(1)}, s32[128,10]{0,1:T(8,128)}, u32[]{:S(2)}) copy-start(s32[128,10]{0,1:T(8,128)} %param.9) | copy-start | bytes 15364
  108.9 11.3 %collective-permute-start.16 = (bf16[128,1152]{1,0:T(8,128)(2,1)S(1)}, bf16[128,1152]{1,0:T(8,128)(2,1)S(1)}, u32[]{:S(2)}, u32[]{:S(2)}) collective-permute-start(bf16[128,1152]{1,0:T(8,128)(2,1)S(1)} %shard_map.120), channel_id=1, source_target_pairs={{15,0},{2,1},{1,2},{4,3},{3,4},{6,5},{5,6},{8,7},{7,8},{10,9},{9,1... | collective-permute-start | bytes 884744 | tf_op jit(solution)/shard_map/ppermute | solution.py:275
  115.9 8.7 %collective-permute-start.12 = (bf16[128,1152]{1,0:T(8,128)(2,1)S(1)}, bf16[128,1152]{1,0:T(8,128)(2,1)S(1)}, u32[]{:S(2)}, u32[]{:S(2)}) collective-permute-start(bf16[128,1152]{1,0:T(8,128)(2,1)S(1)} %shard_map.117), channel_id=1, source_target_pairs={{2,0},{15,1},{4,2},{1,3},{6,4},{3,5},{8,6},{5,7},{10,8},{7,9},{12,... | collective-permute-start | bytes 884744 | tf_op jit(solution)/shard_map/ppermute | solution.py:275
  (10 other events, 37.2 us)

commit v8 on v7

--- a/solution.py
+++ b/solution.py
@@ -11,8 +11,8 @@
 BF = jnp.bfloat16
 F32 = jnp.float32
 LANES = 128
-HOP_FLOPS = 1_000_000_000
-SIDE_FLOPS = 500_000_000
+HOP_FLOPS = 4_000_000_000
+SIDE_FLOPS = 2_000_000_000
 
 
 def dot(a, b, ca, cb):
@@ -95,25 +95,33 @@
     return x, dy, grads, acts
 
 
-def to_parts(out, d_gu, first_row):
-    nx, _, rows, wide = out.shape
+def put(outs, where, value):
+    at = 0
+    for out in outs:
+        wide = out.shape[-1]
+        out[where] = value[..., at : at + wide]
+        at += wide
+
+
+def to_parts(outs, d_gu, first_row):
+    nx, _, rows, _ = outs[0].shape
     n = rows * 2 // 3
     y, ys = first_row // (nx * n), d_gu.shape[0] // (nx * n)
-    pieces = d_gu.astype(BF).reshape(ys, nx, n, wide)
+    pieces = d_gu.astype(BF).reshape(ys, nx, n, d_gu.shape[1])
     for x in range(nx):
-        out[x, y : y + ys, :n, :] = pieces[:, x]
-
-
-def down_to_parts(out, d_down, early=None):
-    nx, ny, rows, half = out.shape
-    m = rows // 3 // 2
+        put(outs, (x, slice(y, y + ys), slice(0, n)), pieces[:, x])
+
+
+def down_to_parts(outs, d_down, early=()):
+    nx, ny, rows, _ = outs[0].shape
+    m, half = rows // 3 // 2, d_down.shape[1] // 2
     pieces = [d_down[:, c : c + half].reshape(ny, nx, m, half) for c in (0, half)]
     pieces = jnp.concatenate(pieces, axis=2)
     for x in range(nx):
-        piece = pieces[:, x]
-        if early is not None:
-            piece = piece + early[x, :, rows - 2 * m :, :].astype(F32)
-        out[x, :, rows - 2 * m :, :] = piece.astype(BF)
+        piece, where = pieces[:, x], (x, slice(0, ny), slice(rows - 2 * m, rows))
+        if early:
+            piece = piece + jnp.concatenate([e[where] for e in early], axis=-1).astype(F32)
+        put(outs, where, piece.astype(BF))
 
 
 def group_kernel(first, swap, n_blocks, expert_ref, *refs):
@@ -131,7 +139,7 @@
             d_gu = d_gu + acc_gu[rows, :]
         if swap:
             outs[0][rows, :] = d_gu[:, : 2 * hidden]
-            to_parts(outs[2], d_gu[:, 2 * hidden :], rows.start)
+            to_parts(outs[2:], d_gu[:, 2 * hidden :], rows.start)
         else:
             outs[0][rows, :] = d_gu
     for j, act in enumerate(acts):
@@ -140,7 +148,7 @@
         if not first:
             d_down = d_down + acc_d[rows, :]
         if swap and j == 1:
-            down_to_parts(outs[2], d_down)
+            down_to_parts(outs[2:], d_down)
         else:
             outs[1][rows, :] = d_down
 
@@ -157,7 +165,8 @@
     out_act[...] = acts[0]
 
 
-def last_kernel(expert_ref, block, pre, act, theirs, w_gate, w_up, w_down, acc_gu, acc_d, early, out, made, sems):
+def last_kernel(expert_ref, block, pre, act, theirs, w_gate, w_up, w_down, acc_gu, acc_d, *refs):
+    *early, out, made, sems = refs
     width, hidden = w_gate.shape
     x, dy, dense = split([theirs], width)
     here = lax.broadcasted_iota(jnp.int32, dense.shape, 1) == expert_ref[0]
@@ -178,11 +187,12 @@
 
     for r in range(0, width, step):
         y, ys = r // (nx * n), step // (nx * n)
-        partner = jnp.stack([early[p, y : y + ys, :n, :] for p in range(nx)], axis=1)
+        partner = [jnp.stack([e[p, y : y + ys, :n, :] for p in range(nx)], axis=1) for e in early]
+        partner = jnp.concatenate(partner, axis=-1)
         d_gu = dot(x[:, r : r + step], grads, 0, 0) + acc_gu[r : r + step, :]
-        to_parts(made, d_gu + partner.reshape(step, wide).astype(F32), r)
+        to_parts([made], d_gu + partner.reshape(step, wide).astype(F32), r)
         leave(slice(None), pl.ds(y, ys), pl.ds(0, n))
-    down_to_parts(made, dot(gated, dy, 0, 0) + acc_d[...], early)
+    down_to_parts([made], dot(gated, dy, 0, 0) + acc_d[...], early)
     leave(slice(None), slice(None), pl.ds(n, rows - n))
     for copy in copies:
         copy.wait()
@@ -225,7 +235,7 @@
         jax.ShapeDtypeStruct((own // 2, width), F32),
     ]
     if replicas:
-        shapes.append(jax.ShapeDtypeStruct((*replicas, (width + 2 * hidden) // math.prod(replicas), 2 * hidden), BF))
+        shapes += [jax.ShapeDtypeStruct((*replicas, (width + 2 * hidden) // math.prod(replicas), hidden), BF)] * 2
     n = len(blocks)
     return call(
         functools.partial(group_kernel, not acc, bool(replicas), n),
@@ -301,8 +311,9 @@
     b3 = send(b2, out)
     a4 = send(after(a3, g_a2), out)
     g_b2, g_a3, *acc = group(expert, (b2, a3), weights, acc)
-    g_b3, *acc, early = group(expert, (b3,), weights, acc, (nx, ny))
-    early = send(after(early, a4), swap)
+    g_b3, *acc, early0, early1 = group(expert, (b3,), weights, acc, (nx, ny))
+    early = [send(early0, swap), send(early1, swap)]
+    whole = jax.ShapeDtypeStruct((*early0.shape[:-1], 2 * hidden), BF)
     theirs = send(a4, swap)
     g_a4, pre, act = call(
         far_kernel,
@@ -318,13 +329,13 @@
     )
     (parts,) = call(
         last_kernel,
-        [jax.ShapeDtypeStruct(early.shape, BF)],
+        [whole],
         expert,
-        (a4, pre, act, theirs, *weights[:3], *acc, early),
+        (a4, pre, act, theirs, *weights[:3], *acc, *early),
         {},
         2 * rows * width * hidden * 9,
         in_hbm,
-        [pltpu.VMEM(early.shape, BF), pltpu.SemaphoreType.DMA((8,))],
+        [pltpu.VMEM(whole.shape, BF), pltpu.SemaphoreType.DMA((8,))],
     )
 
     b = send(g_b3, home)

time: 128 us -> 123 us (0.961)
  waiting for transfers between devices: 23.3 us -> 12.4 us
  starting transfers between devices: 71.9 us -> 79.1 us
  local copies, waits for them, and re-layouts: 6.32 us -> 4.92 us
    ppermute x19 -> x20, waiting for transfers between devices: 17.7 us -> 9.8 us  [send(): return lax.ppermute(a, 'expert', pairs)]
    ppermute x19 -> x20, starting transfers between devices: 61.1 us -> 68.3 us  [send(): return lax.ppermute(a, 'expert', pairs)]
    all_to_all x2, waiting for transfers between devices: 5.67 us -> 2.64 us  [on_device(): lax.all_to_all(parts, 'dp', split_axis=0, concat_axis=0, axis_index_group...]
    unnamed x26 -> x28, local copies, waits for them, and re-layouts: 6.32 us -> 4.92 us
  transfers between devices with their start and end apart: 21 -> 22, of which waited for: 8 -> 6; matrix products, arithmetic and copies ran while one was open for 0% -> 0% of each run, Pallas kernels for 15% -> 18%
where the time goes in v8:
time: 123 us; the launch traced here: 122 us
  starting transfers between devices  79.1 us (64%)
  Pallas kernels  24.8 us (20%)
  waiting for transfers between devices  12.4 us (10%)
  local copies, waits for them, and re-layouts  4.92 us (4%)
    ppermute x20, starting transfers between devices, send(): return lax.ppermute(a, 'expert', pairs)  68.3 us
    pallas_call x6, Pallas kernels, call(): pl.pallas_call(kernel, out_shape=out_shape, in_specs=[pl.BlockSpec(memory...  18.3 us
    all_to_all x2, starting transfers between devices, on_device(): lax.all_to_all(parts, 'dp', split_axis=0, concat_axis=0, axis_index_group...  10.8 us
    ppermute x20, waiting for transfers between devices, send(): return lax.ppermute(a, 'expert', pairs)  9.8 us
    unnamed x28, local copies, waits for them, and re-layouts  4.92 us
    all_to_all x2, waiting for transfers between devices, on_device(): lax.all_to_all(parts, 'dp', split_axis=0, concat_axis=0, axis_index_group...  2.64 us
  transfers between devices with their start and end apart: 22, of which 6 were waited for; matrix products, arithmetic and copies ran while one was open for 0% of the time, Pallas kernels for 18%

profile of v8, /device:TPU:1, one launch (start us, length us, event | category | flops | bytes accessed | tf_op | source)
XLA Modules:
  0.0 122.4 jit_solution(15606106747066517329)
XLA Ops:
  2.6 11.5 %collective-permute-start = (bf16[128,2176]{1,0:T(8,128)(2,1)}, bf16[128,2176]{1,0:T(8,128)(2,1)}, u32[]{:S(2)}, u32[]{:S(2)}) collective-permute-start(bf16[128,2176]{1,0:T(8,128)(2,1)} %shard_map.110.refs_0_), channel_id=1, source_target_pairs={{0,2},{1,15},{2,4},{3,1},{4,6},{5,3},{6,8},{7,5},{8,10},{9,7},{10,... | collective-permute-start | bytes 1671176 | tf_op jit(solution)/shard_map/ppermute | solution.py:285
  16.0 2.6 %collective-permute-start.2 = (bf16[1024,256]{1,0:T(8,128)(2,1)}, bf16[1024,256]{1,0:T(8,128)(2,1)S(1)}, u32[]{:S(2)}, u32[]{:S(2)}) collective-permute-start(bf16[1024,256]{1,0:T(8,128)(2,1)} %bitcast.7), channel_id=1, source_target_pairs={{0,1},{1,0},{2,3},{3,2},{4,5},{5,4},{6,7},{7,6},{8,9},{9,8},{10,11... | collective-permute-start | bytes 1572872 | tf_op jit(solution)/shard_map/ppermute | solution.py:285
  20.5 2.4 %collective-permute-start.4 = (bf16[256,1024]{1,0:T(8,128)(2,1)}, bf16[256,1024]{1,0:T(8,128)(2,1)S(1)}, u32[]{:S(2)}, u32[]{:S(2)}) collective-permute-start(bf16[256,1024]{1,0:T(8,128)(2,1)} %bitcast.21), channel_id=1, source_target_pairs={{0,1},{1,0},{2,3},{3,2},{4,5},{5,4},{6,7},{7,6},{8,9},{9,8},{10,11... | collective-permute-start | bytes 1572872 | tf_op jit(solution)/shard_map/ppermute | solution.py:285
  24.0 5.0 %collective-permute-start.1 = (bf16[128,2176]{1,0:T(8,128)(2,1)}, bf16[128,2176]{1,0:T(8,128)(2,1)S(1)}, u32[]{:S(2)}, u32[]{:S(2)}) collective-permute-start(bf16[128,2176]{1,0:T(8,128)(2,1)} %collective-permute-done.refs_1_), channel_id=1, source_target_pairs={{0,2},{1,15},{2,4},{3,1},{4,6},{5,3},{6,8},{7,5},{8,10},{9,7},{10,... | collective-permute-start | bytes 1671176 | tf_op jit(solution)/shard_map/ppermute | solution.py:285
  29.0 2.7 %collective-permute-start.9 = (bf16[128,2176]{1,0:T(8,128)(2,1)S(1)}, bf16[128,2176]{1,0:T(8,128)(2,1)S(1)}, u32[]{:S(2)}, u32[]{:S(2)}) collective-permute-start(bf16[128,2176]{1,0:T(8,128)(2,1)S(1)} %collective-permute-done.6.refs_0_), channel_id=1, source_target_pairs={{0,2},{1,15},{2,4},{3,1},{4,6},{5,3},{6,8},{7,5},{8,10},{9,7},{10,... | collective-permute-start | bytes 1671176 | tf_op jit(solution)/shard_map/ppermute | solution.py:285
  36.0 4.0 %shard_map.111 = (bf16[128,1152]{1,0:T(8,128)(2,1)S(1)}, bf16[128,1152]{1,0:T(8,128)(2,1)S(1)}, f32[1024,1024]{1,0:T(8,128)S(1)}, f32[512,1024]{1,0:T(8,128)S(1)}) custom-call(s32[1]{0:T(128)} %bitcast.1.expert_ref, bf16[128,2176]{1,0:T(8,128)(2,1)S(1)} %copy-done.6, bf16[128,2176]{1,0:T(8,128)(2,1)} %collective-permute-done.refs_1_, ...), custom_call_target="tpu_custom_call" | custom-call | flops 2147483648 | bytes 16777216 | tf_op jit(solution)/shard_map/pallas_call | solution.py:217
  41.9 4.8 %collective-permute-start.13 = (bf16[128,2176]{1,0:T(8,128)(2,1)S(1)}, bf16[128,2176]{1,0:T(8,128)(2,1)S(1)}, u32[]{:S(2)}, u32[]{:S(2)}) collective-permute-start(bf16[128,2176]{1,0:T(8,128)(2,1)S(1)} %collective-permute-done.9.refs_0_), channel_id=1, source_target_pairs={{0,2},{1,15},{2,4},{3,1},{4,6},{5,3},{6,8},{7,5},{8,10},{9,7},{10,... | collective-permute-start | bytes 1671176 | tf_op jit(solution)/shard_map/ppermute | solution.py:285
  46.7 3.8 %shard_map.112 = (bf16[128,1152]{1,0:T(8,128)(2,1)S(1)}, bf16[128,1152]{1,0:T(8,128)(2,1)S(1)}, f32[1024,1024]{1,0:T(8,128)S(1)}, f32[512,1024]{1,0:T(8,128)S(1)}) custom-call(s32[1]{0:T(128)} %bitcast.1.expert_ref, bf16[128,2176]{1,0:T(8,128)(2,1)S(1)} %collective-permute-done.6.refs_0_, ...), custom_call_target="tpu_custom_call", output_to_operand_aliasing={{2}: (9, {}), {3}: (10, {})} | custom-call | flops 2147483648 | bytes 16777216 | tf_op jit(solution)/shard_map/pallas_call | solution.py:217
  51.2 2.3 %collective-permute-start.7 = (bf16[128,2176]{1,0:T(8,128)(2,1)S(1)}, bf16[128,2176]{1,0:T(8,128)(2,1)S(1)}, u32[]{:S(2)}, u32[]{:S(2)}) collective-permute-start(bf16[128,2176]{1,0:T(8,128)(2,1)S(1)} %collective-permute-done.5.refs_1_), channel_id=1, source_target_pairs={{0,2},{1,15},{2,4},{3,1},{4,6},{5,3},{6,8},{7,5},{8,10},{9,7},{10,... | collective-permute-start | bytes 1671176 | tf_op jit(solution)/shard_map/ppermute | solution.py:285
  53.5 3.8 %shard_map.114 = (bf16[128,1152]{1,0:T(8,128)(2,1)S(1)}, bf16[128,1152]{1,0:T(8,128)(2,1)S(1)}, f32[1024,1024]{1,0:T(8,128)S(1)}, f32[512,1024]{1,0:T(8,128)S(1)}) custom-call(s32[1]{0:T(128)} %bitcast.1.expert_ref, bf16[128,2176]{1,0:T(8,128)(2,1)S(1)} %collective-permute-done.9.refs_0_, ...), custom_call_target="tpu_custom_call", output_to_operand_aliasing={{2}: (9, {}), {3}: (10, {})} | custom-call | flops 2147483648 | bytes 16777216 | tf_op jit(solution)/shard_map/pallas_call | solution.py:217
  57.4 2.5 %shard_map.118 = (bf16[128,1152]{1,0:T(8,128)(2,1)S(1)}, f32[1024,512]{1,0:T(8,128)S(1)}, f32[256,1024]{1,0:T(8,128)S(1)}, bf16[4,8,48,256]{3,2,1,0:T(8,128)(2,1)S(1)}, bf16[4,8,48,256]{3,2,1,0:T(8,128)(2,1)S(1)}) custom-call(s32[1]{0:T(128)} %bitcast.1.expert_ref, bf16[128,2176]{1,0:T(8,128)(2,1)S(1)} %collective-permute-done.13.refs_0_, ...), custom_call_target="tpu_custom_call" | custom-call | flops 1073741824 | bytes 16777216 | tf_op jit(solution)/shard_map/pallas_call | solution.py:217
  59.8 3.4 %collective-permute-start.18 = (bf16[4,8,48,256]{3,2,1,0:T(8,128)(2,1)S(1)}, bf16[4,8,48,256]{3,2,1,0:T(8,128)(2,1)S(1)}, u32[]{:S(2)}, u32[]{:S(2)}) collective-permute-start(bf16[4,8,48,256]{3,2,1,0:T(8,128)(2,1)S(1)} %get-tuple-element.54), channel_id=1, source_target_pairs={{0,1},{1,0},{2,3},{3,2},{4,5},{5,4},{6,7},{7,6},{8,9},{9,8},{10,11... | collective-permute-start | bytes 2359304 | tf_op jit(solution)/shard_map/ppermute | solution.py:285
  65.2 2.4 %collective-permute-start.17 = (bf16[128,2176]{1,0:T(8,128)(2,1)S(1)}, bf16[128,2176]{1,0:T(8,128)(2,1)S(1)}, u32[]{:S(2)}, u32[]{:S(2)}) collective-permute-start(bf16[128,2176]{1,0:T(8,128)(2,1)S(1)} %collective-permute-done.7.block), channel_id=1, source_target_pairs={{0,1},{1,0},{2,3},{3,2},{4,5},{5,4},{6,7},{7,6},{8,9},{9,8},{10,11... | collective-permute-start | bytes 1671176 | tf_op jit(solution)/shard_map/ppermute | solution.py:285
  69.6 3.0 %collective-permute-start.8 = (bf16[128,1152]{1,0:T(8,128)(2,1)S(1)}, bf16[128,1152]{1,0:T(8,128)(2,1)}, u32[]{:S(2)}, u32[]{:S(2)}) collective-permute-start(bf16[128,1152]{1,0:T(8,128)(2,1)S(1)} %get-tuple-element.38), channel_id=1, source_target_pairs={{2,0},{15,1},{4,2},{1,3},{6,4},{3,5},{8,6},{5,7},{10,8},{7,9},{12,... | collective-permute-start | bytes 884744 | tf_op jit(solution)/shard_map/ppermute | solution.py:285
  72.6 2.3 %shard_map.122 = bf16[4,8,48,512]{3,2,1,0:T(8,128)(2,1)} custom-call(s32[1]{0:T(128)} %bitcast.1.expert_ref, bf16[128,2176]{1,0:T(8,128)(2,1)S(1)} %collective-permute-done.7.block, bf16[128,512]{1,0:T(8,128)(2,1)S(1)} %get-tuple-element.50.pre, bf16[128,256]{1,0:T(8,128)(2,1)S(1)} %get-tuple-element.51.act, ...), custom_call_target="tpu_custom_call" | custom-call | flops 603979776 | bytes 16777216 | tf_op jit(solution)/shard_map/pallas_call | solution.py:217
  74.9 4.0 %all-to-all-start = ((bf16[4,8,48,512]{3,2,1,0:T(8,128)(2,1)}), bf16[4,8,48,512]{3,2,1,0:T(8,128)(2,1)S(1)}, u32[]{:S(2)}, u32[]{:S(2)}) async-start(bf16[4,8,48,512]{3,2,1,0:T(8,128)(2,1)} %shard_map.122), calls=%async_computation | async-start | bytes 3145728 | tf_op jit(solution)/shard_map/all_to_all | solution.py:345
  78.9 3.4 %collective-permute-start.14 = (bf16[128,1152]{1,0:T(8,128)(2,1)S(1)}, bf16[128,1152]{1,0:T(8,128)(2,1)S(1)}, u32[]{:S(2)}, u32[]{:S(2)}) collective-permute-start(bf16[128,1152]{1,0:T(8,128)(2,1)S(1)} %get-tuple-element.44), channel_id=1, source_target_pairs={{2,0},{15,1},{4,2},{1,3},{6,4},{3,5},{8,6},{5,7},{10,8},{7,9},{12,... | collective-permute-start | bytes 884744 | tf_op jit(solution)/shard_map/ppermute | solution.py:285
  83.4 3.3 %collective-permute-start.10 = (bf16[128,1152]{1,0:T(8,128)(2,1)S(1)}, bf16[128,1152]{1,0:T(8,128)(2,1)S(1)}, u32[]{:S(2)}, u32[]{:S(2)}) collective-permute-start(bf16[128,1152]{1,0:T(8,128)(2,1)S(1)} %shard_map.115), channel_id=1, source_target_pairs={{2,0},{15,1},{4,2},{1,3},{6,4},{3,5},{8,6},{5,7},{10,8},{7,9},{12,... | collective-permute-start | bytes 884744 | tf_op jit(solution)/shard_map/ppermute | solution.py:285
  92.4 2.2 %collective-permute-start.11 = (bf16[128,1152]{1,0:T(8,128)(2,1)S(1)}, bf16[128,1152]{1,0:T(8,128)(2,1)S(1)}, u32[]{:S(2)}, u32[]{:S(2)}) collective-permute-start(bf16[128,1152]{1,0:T(8,128)(2,1)S(1)} %shard_map.116), channel_id=1, source_target_pairs={{2,0},{15,1},{4,2},{1,3},{6,4},{3,5},{8,6},{5,7},{10,8},{7,9},{12,... | collective-permute-start | bytes 884744 | tf_op jit(solution)/shard_map/ppermute | solution.py:285
  94.6 2.6 %all-to-all-done.parts = bf16[4,8,48,512]{3,2,1,0:T(8,128)(2,1)S(1)} async-done(((bf16[4,8,48,512]{3,2,1,0:T(8,128)(2,1)}), bf16[4,8,48,512]{3,2,1,0:T(8,128)(2,1)S(1)}, u32[]{:S(2)}, u32[]{:S(2)}) %all-to-all-start) | async-done | bytes 1572896 | tf_op jit(solution)/shard_map/all_to_all | solution.py:345
  98.2 6.8 %all-to-all-start.1 = ((bf16[8,48,512]{2,1,0:T(8,128)(2,1)}), bf16[8,48,512]{2,1,0:T(8,128)(2,1)S(1)}, u32[]{:S(2)}, u32[]{:S(2)}) async-start(bf16[8,48,512]{2,1,0:T(8,128)(2,1)} %shard_map.123), calls=%async_computation.1 | async-start | bytes 786432 | tf_op jit(solution)/shard_map/all_to_all | solution.py:354
  105.1 6.8 %collective-permute-start.16 = (bf16[128,1152]{1,0:T(8,128)(2,1)S(1)}, bf16[128,1152]{1,0:T(8,128)(2,1)S(1)}, u32[]{:S(2)}, u32[]{:S(2)}) collective-permute-start(bf16[128,1152]{1,0:T(8,128)(2,1)S(1)} %shard_map.120), channel_id=1, source_target_pairs={{15,0},{2,1},{1,2},{4,3},{3,4},{6,5},{5,6},{8,7},{7,8},{10,9},{9,1... | collective-permute-start | bytes 884744 | tf_op jit(solution)/shard_map/ppermute | solution.py:285
  112.0 2.7 %collective-permute-start.12 = (bf16[128,1152]{1,0:T(8,128)(2,1)S(1)}, bf16[128,1152]{1,0:T(8,128)(2,1)S(1)}, u32[]{:S(2)}, u32[]{:S(2)}) collective-permute-start(bf16[128,1152]{1,0:T(8,128)(2,1)S(1)} %shard_map.117), channel_id=1, source_target_pairs={{2,0},{15,1},{4,2},{1,3},{6,4},{3,5},{8,6},{5,7},{10,8},{7,9},{12,... | collective-permute-start | bytes 884744 | tf_op jit(solution)/shard_map/ppermute | solution.py:285
  116.6 4.1 %collective-permute-done.12.p = bf16[128,1152]{1,0:T(8,128)(2,1)S(1)} collective-permute-done((bf16[128,1152]{1,0:T(8,128)(2,1)S(1)}, bf16[128,1152]{1,0:T(8,128)(2,1)S(1)}, u32[]{:S(2)}, u32[]{:S(2)}) %collective-permute-start.12) | collective-permute-done | bytes 294944 | tf_op jit(solution)/shard_map/ppermute | solution.py:285
  (63 shorter events, 29.1 us)
Async XLA Ops:
  2.6 21.4 %collective-permute-start = (bf16[128,2176]{1,0:T(8,128)(2,1)}, bf16[128,2176]{1,0:T(8,128)(2,1)}, u32[]{:S(2)}, u32[]{:S(2)}) collective-permute-start(bf16[128,2176]{1,0:T(8,128)(2,1)} %shard_map.110.refs_0_), channel_id=1, source_target_pairs={{0,2},{1,15},{2,4},{3,1},{4,6},{5,3},{6,8},{7,5},{8,10},{9,7},{10,... | collective-permute-start | bytes 1671176 | tf_op jit(solution)/shard_map/ppermute | solution.py:285
  14.1 14.9 %collective-permute-start.6 = (bf16[128,2176]{1,0:T(8,128)(2,1)}, bf16[128,2176]{1,0:T(8,128)(2,1)S(1)}, u32[]{:S(2)}, u32[]{:S(2)}) collective-permute-start(bf16[128,2176]{1,0:T(8,128)(2,1)} %shard_map.110.refs_0_), channel_id=1, source_target_pairs={{0,15},{1,2},{2,1},{3,4},{4,3},{5,6},{6,5},{7,8},{8,7},{9,10},{10,... | collective-permute-start | bytes 1671176 | tf_op jit(solution)/shard_map/ppermute | solution.py:285
  16.0 15.7 %collective-permute-start.2 = (bf16[1024,256]{1,0:T(8,128)(2,1)}, bf16[1024,256]{1,0:T(8,128)(2,1)S(1)}, u32[]{:S(2)}, u32[]{:S(2)}) collective-permute-start(bf16[1024,256]{1,0:T(8,128)(2,1)} %bitcast.7), channel_id=1, source_target_pairs={{0,1},{1,0},{2,3},{3,2},{4,5},{5,4},{6,7},{7,6},{8,9},{9,8},{10,11... | collective-permute-start | bytes 1572872 | tf_op jit(solution)/shard_map/ppermute | solution.py:285
  18.6 13.2 %collective-permute-start.3 = (bf16[1024,256]{1,0:T(8,128)(2,1)}, bf16[1024,256]{1,0:T(8,128)(2,1)S(1)}, u32[]{:S(2)}, u32[]{:S(2)}) collective-permute-start(bf16[1024,256]{1,0:T(8,128)(2,1)} %bitcast.14), channel_id=1, source_target_pairs={{0,1},{1,0},{2,3},{3,2},{4,5},{5,4},{6,7},{7,6},{8,9},{9,8},{10,11... | collective-permute-start | bytes 1572872 | tf_op jit(solution)/shard_map/ppermute | solution.py:285
  20.5 11.3 %collective-permute-start.4 = (bf16[256,1024]{1,0:T(8,128)(2,1)}, bf16[256,1024]{1,0:T(8,128)(2,1)S(1)}, u32[]{:S(2)}, u32[]{:S(2)}) collective-permute-start(bf16[256,1024]{1,0:T(8,128)(2,1)} %bitcast.21), channel_id=1, source_target_pairs={{0,1},{1,0},{2,3},{3,2},{4,5},{5,4},{6,7},{7,6},{8,9},{9,8},{10,11... | collective-permute-start | bytes 1572872 | tf_op jit(solution)/shard_map/ppermute | solution.py:285
  24.0 16.0 %collective-permute-start.1 = (bf16[128,2176]{1,0:T(8,128)(2,1)}, bf16[128,2176]{1,0:T(8,128)(2,1)S(1)}, u32[]{:S(2)}, u32[]{:S(2)}) collective-permute-start(bf16[128,2176]{1,0:T(8,128)(2,1)} %collective-permute-done.refs_1_), channel_id=1, source_target_pairs={{0,2},{1,15},{2,4},{3,1},{4,6},{5,3},{6,8},{7,5},{8,10},{9,7},{10,... | collective-permute-start | bytes 1671176 | tf_op jit(solution)/shard_map/ppermute | solution.py:285
  29.0 12.9 %collective-permute-start.9 = (bf16[128,2176]{1,0:T(8,128)(2,1)S(1)}, bf16[128,2176]{1,0:T(8,128)(2,1)S(1)}, u32[]{:S(2)}, u32[]{:S(2)}) collective-permute-start(bf16[128,2176]{1,0:T(8,128)(2,1)S(1)} %collective-permute-done.6.refs_0_), channel_id=1, source_target_pairs={{0,2},{1,15},{2,4},{3,1},{4,6},{5,3},{6,8},{7,5},{8,10},{9,7},{10,... | collective-permute-start | bytes 1671176 | tf_op jit(solution)/shard_map/ppermute | solution.py:285
  40.0 11.3 %collective-permute-start.5 = (bf16[128,2176]{1,0:T(8,128)(2,1)S(1)}, bf16[128,2176]{1,0:T(8,128)(2,1)S(1)}, u32[]{:S(2)}, u32[]{:S(2)}) collective-permute-start(bf16[128,2176]{1,0:T(8,128)(2,1)S(1)} %collective-permute-done.1.refs_1_), channel_id=1, source_target_pairs={{0,2},{1,15},{2,4},{3,1},{4,6},{5,3},{6,8},{7,5},{8,10},{9,7},{10,... | collective-permute-start | bytes 1671176 | tf_op jit(solution)/shard_map/ppermute | solution.py:285
  41.9 15.5 %collective-permute-start.13 = (bf16[128,2176]{1,0:T(8,128)(2,1)S(1)}, bf16[128,2176]{1,0:T(8,128)(2,1)S(1)}, u32[]{:S(2)}, u32[]{:S(2)}) collective-permute-start(bf16[128,2176]{1,0:T(8,128)(2,1)S(1)} %collective-permute-done.9.refs_0_), channel_id=1, source_target_pairs={{0,2},{1,15},{2,4},{3,1},{4,6},{5,3},{6,8},{7,5},{8,10},{9,7},{10,... | collective-permute-start | bytes 1671176 | tf_op jit(solution)/shard_map/ppermute | solution.py:285
  51.2 14.0 %collective-permute-start.7 = (bf16[128,2176]{1,0:T(8,128)(2,1)S(1)}, bf16[128,2176]{1,0:T(8,128)(2,1)S(1)}, u32[]{:S(2)}, u32[]{:S(2)}) collective-permute-start(bf16[128,2176]{1,0:T(8,128)(2,1)S(1)} %collective-permute-done.5.refs_1_), channel_id=1, source_target_pairs={{0,2},{1,15},{2,4},{3,1},{4,6},{5,3},{6,8},{7,5},{8,10},{9,7},{10,... | collective-permute-start | bytes 1671176 | tf_op jit(solution)/shard_map/ppermute | solution.py:285
  59.8 12.8 %collective-permute-start.18 = (bf16[4,8,48,256]{3,2,1,0:T(8,128)(2,1)S(1)}, bf16[4,8,48,256]{3,2,1,0:T(8,128)(2,1)S(1)}, u32[]{:S(2)}, u32[]{:S(2)}) collective-permute-start(bf16[4,8,48,256]{3,2,1,0:T(8,128)(2,1)S(1)} %get-tuple-element.54), channel_id=1, source_target_pairs={{0,1},{1,0},{2,3},{3,2},{4,5},{5,4},{6,7},{7,6},{8,9},{9,8},{10,11... | collective-permute-start | bytes 2359304 | tf_op jit(solution)/shard_map/ppermute | solution.py:285
  63.3 9.4 %collective-permute-start.19 = (bf16[4,8,48,256]{3,2,1,0:T(8,128)(2,1)S(1)}, bf16[4,8,48,256]{3,2,1,0:T(8,128)(2,1)S(1)}, u32[]{:S(2)}, u32[]{:S(2)}) collective-permute-start(bf16[4,8,48,256]{3,2,1,0:T(8,128)(2,1)S(1)} %get-tuple-element.55), channel_id=1, source_target_pairs={{0,1},{1,0},{2,3},{3,2},{4,5},{5,4},{6,7},{7,6},{8,9},{9,8},{10,11... | collective-permute-start | bytes 2359304 | tf_op jit(solution)/shard_map/ppermute | solution.py:285
  65.2 7.4 %collective-permute-start.17 = (bf16[128,2176]{1,0:T(8,128)(2,1)S(1)}, bf16[128,2176]{1,0:T(8,128)(2,1)S(1)}, u32[]{:S(2)}, u32[]{:S(2)}) collective-permute-start(bf16[128,2176]{1,0:T(8,128)(2,1)S(1)} %collective-permute-done.7.block), channel_id=1, source_target_pairs={{0,1},{1,0},{2,3},{3,2},{4,5},{5,4},{6,7},{7,6},{8,9},{9,8},{10,11... | collective-permute-start | bytes 1671176 | tf_op jit(solution)/shard_map/ppermute | solution.py:285
  69.6 12.7 %collective-permute-start.8 = (bf16[128,1152]{1,0:T(8,128)(2,1)S(1)}, bf16[128,1152]{1,0:T(8,128)(2,1)}, u32[]{:S(2)}, u32[]{:S(2)}) collective-permute-start(bf16[128,1152]{1,0:T(8,128)(2,1)S(1)} %get-tuple-element.38), channel_id=1, source_target_pairs={{2,0},{15,1},{4,2},{1,3},{6,4},{3,5},{8,6},{5,7},{10,8},{7,9},{12,... | collective-permute-start | bytes 884744 | tf_op jit(solution)/shard_map/ppermute | solution.py:285
  74.9 22.4 %all-to-all-start = ((bf16[4,8,48,512]{3,2,1,0:T(8,128)(2,1)}), bf16[4,8,48,512]{3,2,1,0:T(8,128)(2,1)S(1)}, u32[]{:S(2)}, u32[]{:S(2)}) async-start(bf16[4,8,48,512]{3,2,1,0:T(8,128)(2,1)} %shard_map.122), calls=%async_computation | async-start | bytes 3145728 | tf_op jit(solution)/shard_map/all_to_all | solution.py:345
  78.9 9.0 %collective-permute-start.14 = (bf16[128,1152]{1,0:T(8,128)(2,1)S(1)}, bf16[128,1152]{1,0:T(8,128)(2,1)S(1)}, u32[]{:S(2)}, u32[]{:S(2)}) collective-permute-start(bf16[128,1152]{1,0:T(8,128)(2,1)S(1)} %get-tuple-element.44), channel_id=1, source_target_pairs={{2,0},{15,1},{4,2},{1,3},{6,4},{3,5},{8,6},{5,7},{10,8},{7,9},{12,... | collective-permute-start | bytes 884744 | tf_op jit(solution)/shard_map/ppermute | solution.py:285
  83.4 9.0 %collective-permute-start.10 = (bf16[128,1152]{1,0:T(8,128)(2,1)S(1)}, bf16[128,1152]{1,0:T(8,128)(2,1)S(1)}, u32[]{:S(2)}, u32[]{:S(2)}) collective-permute-start(bf16[128,1152]{1,0:T(8,128)(2,1)S(1)} %shard_map.115), channel_id=1, source_target_pairs={{2,0},{15,1},{4,2},{1,3},{6,4},{3,5},{8,6},{5,7},{10,8},{7,9},{12,... | collective-permute-start | bytes 884744 | tf_op jit(solution)/shard_map/ppermute | solution.py:285
  88.7 16.3 %collective-permute-start.15 = (bf16[128,1152]{1,0:T(8,128)(2,1)}, bf16[128,1152]{1,0:T(8,128)(2,1)S(1)}, u32[]{:S(2)}, u32[]{:S(2)}) collective-permute-start(bf16[128,1152]{1,0:T(8,128)(2,1)} %shard_map.119), channel_id=1, source_target_pairs={{2,0},{15,1},{4,2},{1,3},{6,4},{3,5},{8,6},{5,7},{10,8},{7,9},{12,... | collective-permute-start | bytes 884744 | tf_op jit(solution)/shard_map/ppermute | solution.py:285
  92.4 12.6 %copy-start.9 = (bf16[128,1152]{1,0:T(8,128)(2,1)S(1)}, bf16[128,1152]{1,0:T(8,128)(2,1)}, u32[]{:S(2)}) copy-start(bf16[128,1152]{1,0:T(8,128)(2,1)} %copy-done.8) | copy-start | bytes 884740
  92.4 19.5 %collective-permute-start.11 = (bf16[128,1152]{1,0:T(8,128)(2,1)S(1)}, bf16[128,1152]{1,0:T(8,128)(2,1)S(1)}, u32[]{:S(2)}, u32[]{:S(2)}) collective-permute-start(bf16[128,1152]{1,0:T(8,128)(2,1)S(1)} %shard_map.116), channel_id=1, source_target_pairs={{2,0},{15,1},{4,2},{1,3},{6,4},{3,5},{8,6},{5,7},{10,8},{7,9},{12,... | collective-permute-start | bytes 884744 | tf_op jit(solution)/shard_map/ppermute | solution.py:285
  98.2 23.5 %all-to-all-start.1 = ((bf16[8,48,512]{2,1,0:T(8,128)(2,1)}), bf16[8,48,512]{2,1,0:T(8,128)(2,1)S(1)}, u32[]{:S(2)}, u32[]{:S(2)}) async-start(bf16[8,48,512]{2,1,0:T(8,128)(2,1)} %shard_map.123), calls=%async_computation.1 | async-start | bytes 786432 | tf_op jit(solution)/shard_map/all_to_all | solution.py:354
  105.1 15.6 %copy-start.7 = (s32[128,10]{0,1:T(8,128)S(1)}, s32[128,10]{0,1:T(8,128)}, u32[]{:S(2)}) copy-start(s32[128,10]{0,1:T(8,128)} %param.9) | copy-start | bytes 15364
  105.1 11.5 %collective-permute-start.16 = (bf16[128,1152]{1,0:T(8,128)(2,1)S(1)}, bf16[128,1152]{1,0:T(8,128)(2,1)S(1)}, u32[]{:S(2)}, u32[]{:S(2)}) collective-permute-start(bf16[128,1152]{1,0:T(8,128)(2,1)S(1)} %shard_map.120), channel_id=1, source_target_pairs={{15,0},{2,1},{1,2},{4,3},{3,4},{6,5},{5,6},{8,7},{7,8},{10,9},{9,1... | collective-permute-start | bytes 884744 | tf_op jit(solution)/shard_map/ppermute | solution.py:285
  112.0 8.7 %collective-permute-start.12 = (bf16[128,1152]{1,0:T(8,128)(2,1)S(1)}, bf16[128,1152]{1,0:T(8,128)(2,1)S(1)}, u32[]{:S(2)}, u32[]{:S(2)}) collective-permute-start(bf16[128,1152]{1,0:T(8,128)(2,1)S(1)} %shard_map.117), channel_id=1, source_target_pairs={{2,0},{15,1},{4,2},{1,3},{6,4},{3,5},{8,6},{5,7},{10,8},{7,9},{12,... | collective-permute-start | bytes 884744 | tf_op jit(solution)/shard_map/ppermute | solution.py:285
  (12 other events, 65.1 us)

commit v9 on v8

--- a/solution.py
+++ b/solution.py
@@ -11,8 +11,8 @@
 BF = jnp.bfloat16
 F32 = jnp.float32
 LANES = 128
-HOP_FLOPS = 4_000_000_000
-SIDE_FLOPS = 2_000_000_000
+HOP_FLOPS = 5_000_000_000
+SIDE_FLOPS = 2_500_000_000
 
 
 def dot(a, b, ca, cb):
@@ -198,10 +198,6 @@
         copy.wait()
 
 
-def halfway_kernel(parts, out):
-    out[...] = jnp.sum(parts[...].astype(F32), axis=0).astype(BF)
-
-
 def sum_kernel(parts, gate, up, down):
     n, hidden = gate.shape[1:]
     m = down.shape[1]
@@ -269,10 +265,7 @@
 def on_device(tokens, cotangent, routing, gates, gate_weight, up_weight, down_weight):
     groups = lax.axis_size("expert")
     replicas = lax.axis_size("dp")
-    nx = 4 if replicas % 4 == 0 else 1
-    ny = replicas // nx
-    along_x = [[y * nx + x for x in range(nx)] for y in range(ny)]
-    along_y = [[y * nx + x for y in range(ny)] for x in range(nx)]
+    nx, ny = 1, replicas
     rows, width = tokens.shape
     hidden = gate_weight.shape[2]
     out = [(i, (i + 2 if i % 2 == 0 else i - 2) % groups) for i in range(groups)]
@@ -341,17 +334,7 @@
     b = send(g_b3, home)
     a = send(g_a4, home)
 
-    if nx > 1:
-        parts = lax.all_to_all(parts, "dp", split_axis=0, concat_axis=0, axis_index_groups=along_x, tiled=True)
-    parts = pl.pallas_call(
-        halfway_kernel,
-        out_shape=jax.ShapeDtypeStruct(parts.shape[1:], BF),
-        in_specs=[VMEM],
-        out_specs=VMEM,
-        compiler_params=pltpu.CompilerParams(vmem_limit_bytes=8 * 1024 * 1024),
-    )(parts)
-    if ny > 1:
-        parts = lax.all_to_all(parts, "dp", split_axis=0, concat_axis=0, axis_index_groups=along_y, tiled=True)
+    parts = lax.all_to_all(parts[0], "dp", split_axis=0, concat_axis=0, tiled=True)
     slab = jax.ShapeDtypeStruct((1, width // replicas, hidden), F32)
     sums = pl.pallas_call(
         sum_kernel,

time: 123 us -> 123 us (level); the launches traced: 122 us -> 121 us
  waiting for transfers between devices: 12.4 us -> 20 us
  starting transfers between devices: 79.1 us -> 72.4 us
  Pallas kernels: 24.8 us -> 22.4 us
    ppermute x20, waiting for transfers between devices: 9.8 us -> 20 us  [send(): return lax.ppermute(a, 'expert', pairs)]
    ppermute x20, starting transfers between devices: 68.3 us -> 62.7 us  [send(): return lax.ppermute(a, 'expert', pairs)]
    all_to_all x2 -> x1, waiting for transfers between devices: 2.64 us -> 0.01 us  [on_device(): lax.all_to_all(parts[0], 'dp', split_axis=0, concat_axis=0, tiled=True)]
    pallas_call x5, Pallas kernels: 2.03 us -> 0.36 us  [add(): pl.pallas_call(add_kernel, out_shape=jax.ShapeDtypeStruct(p.shape, BF), i...]
    all_to_all x2 -> x1, starting transfers between devices: 10.8 us -> 9.68 us  [on_device(): lax.all_to_all(parts[0], 'dp', split_axis=0, concat_axis=0, tiled=True)]
  transfers between devices with their start and end apart: 22 -> 21, of which waited for: 6 -> 8; matrix products, arithmetic and copies ran while one was open for 0% -> 0% of each run, Pallas kernels for 18% -> 14%
where the time goes in v9:
time: 123 us; the launch traced here: 121 us
  starting transfers between devices  72.4 us (59%)
  Pallas kernels  22.4 us (18%)
  waiting for transfers between devices  20 us (16%)
  local copies, waits for them, and re-layouts  4.92 us (4%)
    ppermute x20, starting transfers between devices, send(): return lax.ppermute(a, 'expert', pairs)  62.7 us
    ppermute x20, waiting for transfers between devices, send(): return lax.ppermute(a, 'expert', pairs)  20 us
    pallas_call x6, Pallas kernels, call(): pl.pallas_call(kernel, out_shape=out_shape, in_specs=[pl.BlockSpec(memory...  18.3 us
    all_to_all x1, starting transfers between devices, on_device(): lax.all_to_all(parts[0], 'dp', split_axis=0, concat_axis=0, tiled=True)  9.68 us
    unnamed x28, local copies, waits for them, and re-layouts  4.92 us
  transfers between devices with their start and end apart: 21, of which 8 were waited for; matrix products, arithmetic and copies ran while one was open for 0% of the time, Pallas kernels for 14%

profile of v9, /device:TPU:1, one launch (start us, length us, event | category | flops | bytes accessed | tf_op | source)
XLA Modules:
  0.0 120.8 jit_solution(4150236715985271775)
XLA Ops:
  0.6 1.9 %shard_map.110.refs_0_ = bf16[128,2176]{1,0:T(8,128)(2,1)} custom-call(s32[10,128]{1,0:T(8,128)} %bitcast.29, bf16[10,128]{1,0:T(8,128)(2,1)} %bitcast.31, bf16[128,1024]{1,0:T(8,128)(2,1)} %tokens.1, bf16[128,1024]{1,0:T(8,128)(2,1)} %cotangent.1), custom_call_target="tpu_custom_call" | custom-call | tf_op jit(solution)/shard_map/pallas_call | solution.py:281
  2.6 11.5 %collective-permute-start = (bf16[128,2176]{1,0:T(8,128)(2,1)}, bf16[128,2176]{1,0:T(8,128)(2,1)}, u32[]{:S(2)}, u32[]{:S(2)}) collective-permute-start(bf16[128,2176]{1,0:T(8,128)(2,1)} %shard_map.110.refs_0_), channel_id=1, source_target_pairs={{0,2},{1,15},{2,4},{3,1},{4,6},{5,3},{6,8},{7,5},{8,10},{9,7},{10,... | collective-permute-start | bytes 1671176 | tf_op jit(solution)/shard_map/ppermute | solution.py:278
  16.0 2.6 %collective-permute-start.2 = (bf16[1024,256]{1,0:T(8,128)(2,1)}, bf16[1024,256]{1,0:T(8,128)(2,1)S(1)}, u32[]{:S(2)}, u32[]{:S(2)}) collective-permute-start(bf16[1024,256]{1,0:T(8,128)(2,1)} %bitcast.8), channel_id=1, source_target_pairs={{0,1},{1,0},{2,3},{3,2},{4,5},{5,4},{6,7},{7,6},{8,9},{9,8},{10,11... | collective-permute-start | bytes 1572872 | tf_op jit(solution)/shard_map/ppermute | solution.py:278
  20.5 2.4 %collective-permute-start.4 = (bf16[256,1024]{1,0:T(8,128)(2,1)}, bf16[256,1024]{1,0:T(8,128)(2,1)S(1)}, u32[]{:S(2)}, u32[]{:S(2)}) collective-permute-start(bf16[256,1024]{1,0:T(8,128)(2,1)} %bitcast.22), channel_id=1, source_target_pairs={{0,1},{1,0},{2,3},{3,2},{4,5},{5,4},{6,7},{7,6},{8,9},{9,8},{10,11... | collective-permute-start | bytes 1572872 | tf_op jit(solution)/shard_map/ppermute | solution.py:278
  24.0 5.0 %collective-permute-start.1 = (bf16[128,2176]{1,0:T(8,128)(2,1)}, bf16[128,2176]{1,0:T(8,128)(2,1)S(1)}, u32[]{:S(2)}, u32[]{:S(2)}) collective-permute-start(bf16[128,2176]{1,0:T(8,128)(2,1)} %collective-permute-done.refs_1_), channel_id=1, source_target_pairs={{0,2},{1,15},{2,4},{3,1},{4,6},{5,3},{6,8},{7,5},{8,10},{9,7},{10,... | collective-permute-start | bytes 1671176 | tf_op jit(solution)/shard_map/ppermute | solution.py:278
  29.0 2.7 %collective-permute-start.9 = (bf16[128,2176]{1,0:T(8,128)(2,1)S(1)}, bf16[128,2176]{1,0:T(8,128)(2,1)S(1)}, u32[]{:S(2)}, u32[]{:S(2)}) collective-permute-start(bf16[128,2176]{1,0:T(8,128)(2,1)S(1)} %collective-permute-done.6.refs_0_), channel_id=1, source_target_pairs={{0,2},{1,15},{2,4},{3,1},{4,6},{5,3},{6,8},{7,5},{8,10},{9,7},{10,... | collective-permute-start | bytes 1671176 | tf_op jit(solution)/shard_map/ppermute | solution.py:278
  36.0 4.0 %shard_map.111 = (bf16[128,1152]{1,0:T(8,128)(2,1)S(1)}, bf16[128,1152]{1,0:T(8,128)(2,1)S(1)}, f32[1024,1024]{1,0:T(8,128)S(1)}, f32[512,1024]{1,0:T(8,128)S(1)}) custom-call(s32[1]{0:T(128)} %bitcast.1.expert_ref, bf16[128,2176]{1,0:T(8,128)(2,1)S(1)} %copy-done.6, bf16[128,2176]{1,0:T(8,128)(2,1)} %collective-permute-done.refs_1_, ...), custom_call_target="tpu_custom_call" | custom-call | flops 2147483648 | bytes 16777216 | tf_op jit(solution)/shard_map/pallas_call | solution.py:213
  41.9 4.8 %collective-permute-start.13 = (bf16[128,2176]{1,0:T(8,128)(2,1)S(1)}, bf16[128,2176]{1,0:T(8,128)(2,1)S(1)}, u32[]{:S(2)}, u32[]{:S(2)}) collective-permute-start(bf16[128,2176]{1,0:T(8,128)(2,1)S(1)} %collective-permute-done.9.refs_0_), channel_id=1, source_target_pairs={{0,2},{1,15},{2,4},{3,1},{4,6},{5,3},{6,8},{7,5},{8,10},{9,7},{10,... | collective-permute-start | bytes 1671176 | tf_op jit(solution)/shard_map/ppermute | solution.py:278
  46.7 3.8 %shard_map.112 = (bf16[128,1152]{1,0:T(8,128)(2,1)S(1)}, bf16[128,1152]{1,0:T(8,128)(2,1)S(1)}, f32[1024,1024]{1,0:T(8,128)S(1)}, f32[512,1024]{1,0:T(8,128)S(1)}) custom-call(s32[1]{0:T(128)} %bitcast.1.expert_ref, bf16[128,2176]{1,0:T(8,128)(2,1)S(1)} %collective-permute-done.6.refs_0_, ...), custom_call_target="tpu_custom_call", output_to_operand_aliasing={{2}: (9, {}), {3}: (10, {})} | custom-call | flops 2147483648 | bytes 16777216 | tf_op jit(solution)/shard_map/pallas_call | solution.py:213
  51.2 2.3 %collective-permute-start.7 = (bf16[128,2176]{1,0:T(8,128)(2,1)S(1)}, bf16[128,2176]{1,0:T(8,128)(2,1)S(1)}, u32[]{:S(2)}, u32[]{:S(2)}) collective-permute-start(bf16[128,2176]{1,0:T(8,128)(2,1)S(1)} %collective-permute-done.5.refs_1_), channel_id=1, source_target_pairs={{0,2},{1,15},{2,4},{3,1},{4,6},{5,3},{6,8},{7,5},{8,10},{9,7},{10,... | collective-permute-start | bytes 1671176 | tf_op jit(solution)/shard_map/ppermute | solution.py:278
  53.6 3.8 %shard_map.114 = (bf16[128,1152]{1,0:T(8,128)(2,1)S(1)}, bf16[128,1152]{1,0:T(8,128)(2,1)S(1)}, f32[1024,1024]{1,0:T(8,128)S(1)}, f32[512,1024]{1,0:T(8,128)S(1)}) custom-call(s32[1]{0:T(128)} %bitcast.1.expert_ref, bf16[128,2176]{1,0:T(8,128)(2,1)S(1)} %collective-permute-done.9.refs_0_, ...), custom_call_target="tpu_custom_call", output_to_operand_aliasing={{2}: (9, {}), {3}: (10, {})} | custom-call | flops 2147483648 | bytes 16777216 | tf_op jit(solution)/shard_map/pallas_call | solution.py:213
  57.4 2.5 %shard_map.118 = (bf16[128,1152]{1,0:T(8,128)(2,1)S(1)}, f32[1024,512]{1,0:T(8,128)S(1)}, f32[256,1024]{1,0:T(8,128)S(1)}, bf16[1,32,48,256]{3,2,1,0:T(8,128)(2,1)S(1)}, bf16[1,32,48,256]{3,2,1,0:T(8,128)(2,1)S(1)}) custom-call(s32[1]{0:T(128)} %bitcast.1.expert_ref, bf16[128,2176]{1,0:T(8,128)(2,1)S(1)} %collective-permute-done.13.refs_0_, ...), custom_call_target="tpu_custom_call" | custom-call | flops 1073741824 | bytes 16777216 | tf_op jit(solution)/shard_map/pallas_call | solution.py:213
  59.9 3.4 %collective-permute-start.18 = (bf16[1,32,48,256]{3,2,1,0:T(8,128)(2,1)S(1)}, bf16[1,32,48,256]{3,2,1,0:T(8,128)(2,1)S(1)}, u32[]{:S(2)}, u32[]{:S(2)}) collective-permute-start(bf16[1,32,48,256]{3,2,1,0:T(8,128)(2,1)S(1)} %get-tuple-element.54), channel_id=1, source_target_pairs={{0,1},{1,0},{2,3},{3,2},{4,5},{5,4},{6,7},{7,6},{8,9},{9,8},{10,11... | collective-permute-start | bytes 2359304 | tf_op jit(solution)/shard_map/ppermute | solution.py:278
  65.2 2.4 %collective-permute-start.17 = (bf16[128,2176]{1,0:T(8,128)(2,1)S(1)}, bf16[128,2176]{1,0:T(8,128)(2,1)S(1)}, u32[]{:S(2)}, u32[]{:S(2)}) collective-permute-start(bf16[128,2176]{1,0:T(8,128)(2,1)S(1)} %collective-permute-done.7.block), channel_id=1, source_target_pairs={{0,1},{1,0},{2,3},{3,2},{4,5},{5,4},{6,7},{7,6},{8,9},{9,8},{10,11... | collective-permute-start | bytes 1671176 | tf_op jit(solution)/shard_map/ppermute | solution.py:278
  67.6 2.0 %shard_map.113 = (bf16[128,1152]{1,0:T(8,128)(2,1)S(1)}, bf16[128,512]{1,0:T(8,128)(2,1)S(1)}, bf16[128,256]{1,0:T(8,128)(2,1)S(1)}) custom-call(s32[1]{0:T(128)} %bitcast.1.expert_ref, bf16[128,2176]{1,0:T(8,128)(2,1)S(1)} %collective-permute-done.7.block, bf16[1024,256]{1,0:T(8,128)(2,1)S(1)} %bitcast.13, bf16[1024,256]{1,0:T(8,128)(2,1)S(1)} %bitcast.20, ...), custom_call_target="tpu_custom_call" | custom-call | flops 671088640 | bytes 16777216 | tf_op jit(solution)/shard_map/pallas_call | solution.py:213
  69.7 2.3 %shard_map.122 = bf16[1,32,48,512]{3,2,1,0:T(8,128)(2,1)} custom-call(s32[1]{0:T(128)} %bitcast.1.expert_ref, bf16[128,2176]{1,0:T(8,128)(2,1)S(1)} %collective-permute-done.7.block, bf16[128,512]{1,0:T(8,128)(2,1)S(1)} %get-tuple-element.50.pre, bf16[128,256]{1,0:T(8,128)(2,1)S(1)} %get-tuple-element.51.act, ...), custom_call_target="tpu_custom_call" | custom-call | flops 603979776 | bytes 16777216 | tf_op jit(solution)/shard_map/pallas_call | solution.py:213
  71.9 9.7 %all-to-all-start = ((bf16[32,48,512]{2,1,0:T(8,128)(2,1)}), bf16[32,48,512]{2,1,0:T(8,128)(2,1)S(1)}, u32[]{:S(2)}, u32[]{:S(2)}) async-start(bf16[32,48,512]{2,1,0:T(8,128)(2,1)} %bitcast.7), calls=%async_computation | async-start | bytes 3145728 | tf_op jit(solution)/shard_map/all_to_all | solution.py:337
  81.6 3.0 %collective-permute-start.8 = (bf16[128,1152]{1,0:T(8,128)(2,1)S(1)}, bf16[128,1152]{1,0:T(8,128)(2,1)S(1)}, u32[]{:S(2)}, u32[]{:S(2)}) collective-permute-start(bf16[128,1152]{1,0:T(8,128)(2,1)S(1)} %get-tuple-element.38), channel_id=1, source_target_pairs={{2,0},{15,1},{4,2},{1,3},{6,4},{3,5},{8,6},{5,7},{10,8},{7,9},{12,... | collective-permute-start | bytes 884744 | tf_op jit(solution)/shard_map/ppermute | solution.py:278
  84.6 3.4 %collective-permute-start.14 = (bf16[128,1152]{1,0:T(8,128)(2,1)S(1)}, bf16[128,1152]{1,0:T(8,128)(2,1)S(1)}, u32[]{:S(2)}, u32[]{:S(2)}) collective-permute-start(bf16[128,1152]{1,0:T(8,128)(2,1)S(1)} %get-tuple-element.44), channel_id=1, source_target_pairs={{2,0},{15,1},{4,2},{1,3},{6,4},{3,5},{8,6},{5,7},{10,8},{7,9},{12,... | collective-permute-start | bytes 884744 | tf_op jit(solution)/shard_map/ppermute | solution.py:278
  88.0 2.8 %collective-permute-done.8.p = bf16[128,1152]{1,0:T(8,128)(2,1)S(1)} collective-permute-done((bf16[128,1152]{1,0:T(8,128)(2,1)S(1)}, bf16[128,1152]{1,0:T(8,128)(2,1)S(1)}, u32[]{:S(2)}, u32[]{:S(2)}) %collective-permute-start.8) | collective-permute-done | bytes 294944 | tf_op jit(solution)/shard_map/ppermute | solution.py:278
  94.1 2.1 %collective-permute-start.15 = (bf16[128,1152]{1,0:T(8,128)(2,1)S(1)}, bf16[128,1152]{1,0:T(8,128)(2,1)S(1)}, u32[]{:S(2)}, u32[]{:S(2)}) collective-permute-start(bf16[128,1152]{1,0:T(8,128)(2,1)S(1)} %shard_map.119), channel_id=1, source_target_pairs={{2,0},{15,1},{4,2},{1,3},{6,4},{3,5},{8,6},{5,7},{10,8},{7,9},{12,... | collective-permute-start | bytes 884744 | tf_op jit(solution)/shard_map/ppermute | solution.py:278
  96.1 3.7 %collective-permute-done.10.p = bf16[128,1152]{1,0:T(8,128)(2,1)S(1)} collective-permute-done((bf16[128,1152]{1,0:T(8,128)(2,1)S(1)}, bf16[128,1152]{1,0:T(8,128)(2,1)S(1)}, u32[]{:S(2)}, u32[]{:S(2)}) %collective-permute-start.10) | collective-permute-done | bytes 294944 | tf_op jit(solution)/shard_map/ppermute | solution.py:278
  103.3 3.8 %collective-permute-start.16 = (bf16[128,1152]{1,0:T(8,128)(2,1)S(1)}, bf16[128,1152]{1,0:T(8,128)(2,1)S(1)}, u32[]{:S(2)}, u32[]{:S(2)}) collective-permute-start(bf16[128,1152]{1,0:T(8,128)(2,1)S(1)} %shard_map.120), channel_id=1, source_target_pairs={{15,0},{2,1},{1,2},{4,3},{3,4},{6,5},{5,6},{8,7},{7,8},{10,9},{9,1... | collective-permute-start | bytes 884744 | tf_op jit(solution)/shard_map/ppermute | solution.py:278
  112.6 6.4 %collective-permute-done.12.p = bf16[128,1152]{1,0:T(8,128)(2,1)S(1)} collective-permute-done((bf16[128,1152]{1,0:T(8,128)(2,1)S(1)}, bf16[128,1152]{1,0:T(8,128)(2,1)S(1)}, u32[]{:S(2)}, u32[]{:S(2)}) %collective-permute-start.12) | collective-permute-done | bytes 294944 | tf_op jit(solution)/shard_map/ppermute | solution.py:278
  (60 shorter events, 27.6 us)
Async XLA Ops:
  2.6 21.4 %collective-permute-start = (bf16[128,2176]{1,0:T(8,128)(2,1)}, bf16[128,2176]{1,0:T(8,128)(2,1)}, u32[]{:S(2)}, u32[]{:S(2)}) collective-permute-start(bf16[128,2176]{1,0:T(8,128)(2,1)} %shard_map.110.refs_0_), channel_id=1, source_target_pairs={{0,2},{1,15},{2,4},{3,1},{4,6},{5,3},{6,8},{7,5},{8,10},{9,7},{10,... | collective-permute-start | bytes 1671176 | tf_op jit(solution)/shard_map/ppermute | solution.py:278
  14.1 14.9 %collective-permute-start.6 = (bf16[128,2176]{1,0:T(8,128)(2,1)}, bf16[128,2176]{1,0:T(8,128)(2,1)S(1)}, u32[]{:S(2)}, u32[]{:S(2)}) collective-permute-start(bf16[128,2176]{1,0:T(8,128)(2,1)} %shard_map.110.refs_0_), channel_id=1, source_target_pairs={{0,15},{1,2},{2,1},{3,4},{4,3},{5,6},{6,5},{7,8},{8,7},{9,10},{10,... | collective-permute-start | bytes 1671176 | tf_op jit(solution)/shard_map/ppermute | solution.py:278
  16.0 15.7 %collective-permute-start.2 = (bf16[1024,256]{1,0:T(8,128)(2,1)}, bf16[1024,256]{1,0:T(8,128)(2,1)S(1)}, u32[]{:S(2)}, u32[]{:S(2)}) collective-permute-start(bf16[1024,256]{1,0:T(8,128)(2,1)} %bitcast.8), channel_id=1, source_target_pairs={{0,1},{1,0},{2,3},{3,2},{4,5},{5,4},{6,7},{7,6},{8,9},{9,8},{10,11... | collective-permute-start | bytes 1572872 | tf_op jit(solution)/shard_map/ppermute | solution.py:278
  18.6 13.2 %collective-permute-start.3 = (bf16[1024,256]{1,0:T(8,128)(2,1)}, bf16[1024,256]{1,0:T(8,128)(2,1)S(1)}, u32[]{:S(2)}, u32[]{:S(2)}) collective-permute-start(bf16[1024,256]{1,0:T(8,128)(2,1)} %bitcast.15), channel_id=1, source_target_pairs={{0,1},{1,0},{2,3},{3,2},{4,5},{5,4},{6,7},{7,6},{8,9},{9,8},{10,11... | collective-permute-start | bytes 1572872 | tf_op jit(solution)/shard_map/ppermute | solution.py:278
  20.5 11.3 %collective-permute-start.4 = (bf16[256,1024]{1,0:T(8,128)(2,1)}, bf16[256,1024]{1,0:T(8,128)(2,1)S(1)}, u32[]{:S(2)}, u32[]{:S(2)}) collective-permute-start(bf16[256,1024]{1,0:T(8,128)(2,1)} %bitcast.22), channel_id=1, source_target_pairs={{0,1},{1,0},{2,3},{3,2},{4,5},{5,4},{6,7},{7,6},{8,9},{9,8},{10,11... | collective-permute-start | bytes 1572872 | tf_op jit(solution)/shard_map/ppermute | solution.py:278
  24.0 16.0 %collective-permute-start.1 = (bf16[128,2176]{1,0:T(8,128)(2,1)}, bf16[128,2176]{1,0:T(8,128)(2,1)S(1)}, u32[]{:S(2)}, u32[]{:S(2)}) collective-permute-start(bf16[128,2176]{1,0:T(8,128)(2,1)} %collective-permute-done.refs_1_), channel_id=1, source_target_pairs={{0,2},{1,15},{2,4},{3,1},{4,6},{5,3},{6,8},{7,5},{8,10},{9,7},{10,... | collective-permute-start | bytes 1671176 | tf_op jit(solution)/shard_map/ppermute | solution.py:278
  29.0 12.9 %collective-permute-start.9 = (bf16[128,2176]{1,0:T(8,128)(2,1)S(1)}, bf16[128,2176]{1,0:T(8,128)(2,1)S(1)}, u32[]{:S(2)}, u32[]{:S(2)}) collective-permute-start(bf16[128,2176]{1,0:T(8,128)(2,1)S(1)} %collective-permute-done.6.refs_0_), channel_id=1, source_target_pairs={{0,2},{1,15},{2,4},{3,1},{4,6},{5,3},{6,8},{7,5},{8,10},{9,7},{10,... | collective-permute-start | bytes 1671176 | tf_op jit(solution)/shard_map/ppermute | solution.py:278
  36.0 10.7 %copy-start.3 = (bf16[1,1024,256]{2,1,0:T(8,128)(2,1)S(1)}, bf16[1,1024,256]{2,1,0:T(8,128)(2,1)}, u32[]{:S(2)}) copy-start(bf16[1,1024,256]{2,1,0:T(8,128)(2,1)} %param.12) | copy-start | bytes 1572868
  36.0 10.7 %copy-start.5 = (bf16[1,256,1024]{2,1,0:T(8,128)(2,1)S(1)}, bf16[1,256,1024]{2,1,0:T(8,128)(2,1)}, u32[]{:S(2)}) copy-start(bf16[1,256,1024]{2,1,0:T(8,128)(2,1)} %param.13) | copy-start | bytes 1572868
  40.0 11.2 %collective-permute-start.5 = (bf16[128,2176]{1,0:T(8,128)(2,1)S(1)}, bf16[128,2176]{1,0:T(8,128)(2,1)S(1)}, u32[]{:S(2)}, u32[]{:S(2)}) collective-permute-start(bf16[128,2176]{1,0:T(8,128)(2,1)S(1)} %collective-permute-done.1.refs_1_), channel_id=1, source_target_pairs={{0,2},{1,15},{2,4},{3,1},{4,6},{5,3},{6,8},{7,5},{8,10},{9,7},{10,... | collective-permute-start | bytes 1671176 | tf_op jit(solution)/shard_map/ppermute | solution.py:278
  41.9 15.5 %collective-permute-start.13 = (bf16[128,2176]{1,0:T(8,128)(2,1)S(1)}, bf16[128,2176]{1,0:T(8,128)(2,1)S(1)}, u32[]{:S(2)}, u32[]{:S(2)}) collective-permute-start(bf16[128,2176]{1,0:T(8,128)(2,1)S(1)} %collective-permute-done.9.refs_0_), channel_id=1, source_target_pairs={{0,2},{1,15},{2,4},{3,1},{4,6},{5,3},{6,8},{7,5},{8,10},{9,7},{10,... | collective-permute-start | bytes 1671176 | tf_op jit(solution)/shard_map/ppermute | solution.py:278
  51.2 14.0 %collective-permute-start.7 = (bf16[128,2176]{1,0:T(8,128)(2,1)S(1)}, bf16[128,2176]{1,0:T(8,128)(2,1)S(1)}, u32[]{:S(2)}, u32[]{:S(2)}) collective-permute-start(bf16[128,2176]{1,0:T(8,128)(2,1)S(1)} %collective-permute-done.5.refs_1_), channel_id=1, source_target_pairs={{0,2},{1,15},{2,4},{3,1},{4,6},{5,3},{6,8},{7,5},{8,10},{9,7},{10,... | collective-permute-start | bytes 1671176 | tf_op jit(solution)/shard_map/ppermute | solution.py:278
  59.9 9.8 %collective-permute-start.18 = (bf16[1,32,48,256]{3,2,1,0:T(8,128)(2,1)S(1)}, bf16[1,32,48,256]{3,2,1,0:T(8,128)(2,1)S(1)}, u32[]{:S(2)}, u32[]{:S(2)}) collective-permute-start(bf16[1,32,48,256]{3,2,1,0:T(8,128)(2,1)S(1)} %get-tuple-element.54), channel_id=1, source_target_pairs={{0,1},{1,0},{2,3},{3,2},{4,5},{5,4},{6,7},{7,6},{8,9},{9,8},{10,11... | collective-permute-start | bytes 2359304 | tf_op jit(solution)/shard_map/ppermute | solution.py:278
  63.3 6.4 %collective-permute-start.19 = (bf16[1,32,48,256]{3,2,1,0:T(8,128)(2,1)S(1)}, bf16[1,32,48,256]{3,2,1,0:T(8,128)(2,1)S(1)}, u32[]{:S(2)}, u32[]{:S(2)}) collective-permute-start(bf16[1,32,48,256]{3,2,1,0:T(8,128)(2,1)S(1)} %get-tuple-element.55), channel_id=1, source_target_pairs={{0,1},{1,0},{2,3},{3,2},{4,5},{5,4},{6,7},{7,6},{8,9},{9,8},{10,11... | collective-permute-start | bytes 2359304 | tf_op jit(solution)/shard_map/ppermute | solution.py:278
  65.2 4.5 %collective-permute-start.17 = (bf16[128,2176]{1,0:T(8,128)(2,1)S(1)}, bf16[128,2176]{1,0:T(8,128)(2,1)S(1)}, u32[]{:S(2)}, u32[]{:S(2)}) collective-permute-start(bf16[128,2176]{1,0:T(8,128)(2,1)S(1)} %collective-permute-done.7.block), channel_id=1, source_target_pairs={{0,1},{1,0},{2,3},{3,2},{4,5},{5,4},{6,7},{7,6},{8,9},{9,8},{10,11... | collective-permute-start | bytes 1671176 | tf_op jit(solution)/shard_map/ppermute | solution.py:278
  71.9 48.0 %all-to-all-start = ((bf16[32,48,512]{2,1,0:T(8,128)(2,1)}), bf16[32,48,512]{2,1,0:T(8,128)(2,1)S(1)}, u32[]{:S(2)}, u32[]{:S(2)}) async-start(bf16[32,48,512]{2,1,0:T(8,128)(2,1)} %bitcast.7), calls=%async_computation | async-start | bytes 3145728 | tf_op jit(solution)/shard_map/all_to_all | solution.py:337
  81.6 9.2 %collective-permute-start.8 = (bf16[128,1152]{1,0:T(8,128)(2,1)S(1)}, bf16[128,1152]{1,0:T(8,128)(2,1)S(1)}, u32[]{:S(2)}, u32[]{:S(2)}) collective-permute-start(bf16[128,1152]{1,0:T(8,128)(2,1)S(1)} %get-tuple-element.38), channel_id=1, source_target_pairs={{2,0},{15,1},{4,2},{1,3},{6,4},{3,5},{8,6},{5,7},{10,8},{7,9},{12,... | collective-permute-start | bytes 884744 | tf_op jit(solution)/shard_map/ppermute | solution.py:278
  84.6 9.4 %collective-permute-start.14 = (bf16[128,1152]{1,0:T(8,128)(2,1)S(1)}, bf16[128,1152]{1,0:T(8,128)(2,1)S(1)}, u32[]{:S(2)}, u32[]{:S(2)}) collective-permute-start(bf16[128,1152]{1,0:T(8,128)(2,1)S(1)} %get-tuple-element.44), channel_id=1, source_target_pairs={{2,0},{15,1},{4,2},{1,3},{6,4},{3,5},{8,6},{5,7},{10,8},{7,9},{12,... | collective-permute-start | bytes 884744 | tf_op jit(solution)/shard_map/ppermute | solution.py:278
  90.9 9.0 %collective-permute-start.10 = (bf16[128,1152]{1,0:T(8,128)(2,1)S(1)}, bf16[128,1152]{1,0:T(8,128)(2,1)S(1)}, u32[]{:S(2)}, u32[]{:S(2)}) collective-permute-start(bf16[128,1152]{1,0:T(8,128)(2,1)S(1)} %shard_map.115), channel_id=1, source_target_pairs={{2,0},{15,1},{4,2},{1,3},{6,4},{3,5},{8,6},{5,7},{10,8},{7,9},{12,... | collective-permute-start | bytes 884744 | tf_op jit(solution)/shard_map/ppermute | solution.py:278
  94.1 9.1 %collective-permute-start.15 = (bf16[128,1152]{1,0:T(8,128)(2,1)S(1)}, bf16[128,1152]{1,0:T(8,128)(2,1)S(1)}, u32[]{:S(2)}, u32[]{:S(2)}) collective-permute-start(bf16[128,1152]{1,0:T(8,128)(2,1)S(1)} %shard_map.119), channel_id=1, source_target_pairs={{2,0},{15,1},{4,2},{1,3},{6,4},{3,5},{8,6},{5,7},{10,8},{7,9},{12,... | collective-permute-start | bytes 884744 | tf_op jit(solution)/shard_map/ppermute | solution.py:278
  99.9 9.0 %collective-permute-start.11 = (bf16[128,1152]{1,0:T(8,128)(2,1)S(1)}, bf16[128,1152]{1,0:T(8,128)(2,1)S(1)}, u32[]{:S(2)}, u32[]{:S(2)}) collective-permute-start(bf16[128,1152]{1,0:T(8,128)(2,1)S(1)} %shard_map.116), channel_id=1, source_target_pairs={{2,0},{15,1},{4,2},{1,3},{6,4},{3,5},{8,6},{5,7},{10,8},{7,9},{12,... | collective-permute-start | bytes 884744 | tf_op jit(solution)/shard_map/ppermute | solution.py:278
  103.2 15.7 %copy-start.7 = (s32[128,10]{0,1:T(8,128)S(1)}, s32[128,10]{0,1:T(8,128)}, u32[]{:S(2)}) copy-start(s32[128,10]{0,1:T(8,128)} %param.9) | copy-start | bytes 15364
  103.3 9.3 %collective-permute-start.16 = (bf16[128,1152]{1,0:T(8,128)(2,1)S(1)}, bf16[128,1152]{1,0:T(8,128)(2,1)S(1)}, u32[]{:S(2)}, u32[]{:S(2)}) collective-permute-start(bf16[128,1152]{1,0:T(8,128)(2,1)S(1)} %shard_map.120), channel_id=1, source_target_pairs={{15,0},{2,1},{1,2},{4,3},{3,4},{6,5},{5,6},{8,7},{7,8},{10,9},{9,1... | collective-permute-start | bytes 884744 | tf_op jit(solution)/shard_map/ppermute | solution.py:278
  109.0 10.0 %collective-permute-start.12 = (bf16[128,1152]{1,0:T(8,128)(2,1)S(1)}, bf16[128,1152]{1,0:T(8,128)(2,1)S(1)}, u32[]{:S(2)}, u32[]{:S(2)}) collective-permute-start(bf16[128,1152]{1,0:T(8,128)(2,1)S(1)} %shard_map.117), channel_id=1, source_target_pairs={{2,0},{15,1},{4,2},{1,3},{6,4},{3,5},{8,6},{5,7},{10,8},{7,9},{12,... | collective-permute-start | bytes 884744 | tf_op jit(solution)/shard_map/ppermute | solution.py:278
  (11 other events, 53.1 us)

commit v10 on v8

--- a/solution.py
+++ b/solution.py
@@ -11,8 +11,8 @@
 BF = jnp.bfloat16
 F32 = jnp.float32
 LANES = 128
-HOP_FLOPS = 4_000_000_000
-SIDE_FLOPS = 2_000_000_000
+HOP_FLOPS = 3_000_000_000
+SIDE_FLOPS = 500_000_000
 
 
 def dot(a, b, ca, cb):
@@ -362,7 +362,7 @@
     )(parts)
 
     b = send(add(b, g_b2, SIDE_FLOPS), home)
-    a = send(add(a, g_a3), home)
+    a = send(add(a, g_a3, SIDE_FLOPS), home)
     b = send(add(b, g_b1, SIDE_FLOPS), uncross)
     a = send(add(a, g_a2), home)
     a = send(add(a, g_a1), home)

time: 123 us -> 124 us (level)
  waiting for transfers between devices: 12.4 us -> 18.2 us
  starting transfers between devices: 79.1 us -> 75.9 us
  Pallas kernels: 24.8 us -> 23.1 us
    ppermute x20, waiting for transfers between devices: 9.8 us -> 18.1 us  [send(): return lax.ppermute(a, 'expert', pairs)]
    ppermute x20, starting transfers between devices: 68.3 us -> 64.8 us  [send(): return lax.ppermute(a, 'expert', pairs)]
    all_to_all x2, waiting for transfers between devices: 2.64 us -> 0.04 us  [on_device(): lax.all_to_all(parts, 'dp', split_axis=0, concat_axis=0, axis_index_group...]
    pallas_call x5, Pallas kernels: 2.03 us -> 0.36 us  [add(): pl.pallas_call(add_kernel, out_shape=jax.ShapeDtypeStruct(p.shape, BF), i...]
    unnamed x28 -> x32, local copies, waits for them, and re-layouts: 4.92 us -> 4.93 us
  transfers between devices with their start and end apart: 22 -> 22, of which waited for: 6 -> 6; matrix products, arithmetic and copies ran while one was open for 0% -> 0% of each run, Pallas kernels for 18% -> 15%
where the time goes in v10:
time: 124 us; the launch traced here: 123 us
  starting transfers between devices  75.9 us (61%)
  Pallas kernels  23.1 us (19%)
  waiting for transfers between devices  18.2 us (15%)
  local copies, waits for them, and re-layouts  4.93 us (4%)
    ppermute x20, starting transfers between devices, send(): return lax.ppermute(a, 'expert', pairs)  64.8 us
    pallas_call x6, Pallas kernels, call(): pl.pallas_call(kernel, out_shape=out_shape, in_specs=[pl.BlockSpec(memory...  18.2 us
    ppermute x20, waiting for transfers between devices, send(): return lax.ppermute(a, 'expert', pairs)  18.1 us
    all_to_all x2, starting transfers between devices, on_device(): lax.all_to_all(parts, 'dp', split_axis=0, concat_axis=0, axis_index_group...  11.1 us
    unnamed x32, local copies, waits for them, and re-layouts  4.93 us
  transfers between devices with their start and end apart: 22, of which 6 were waited for; matrix products, arithmetic and copies ran while one was open for 0% of the time, Pallas kernels for 15%

profile of v10, /device:TPU:1, one launch (start us, length us, event | category | flops | bytes accessed | tf_op | source)
XLA Modules:
  0.0 123.2 jit_solution(8067915542287431811)
XLA Ops:
  2.6 11.5 %collective-permute-start = (bf16[128,2176]{1,0:T(8,128)(2,1)}, bf16[128,2176]{1,0:T(8,128)(2,1)}, u32[]{:S(2)}, u32[]{:S(2)}) collective-permute-start(bf16[128,2176]{1,0:T(8,128)(2,1)} %shard_map.110.refs_0_), channel_id=1, source_target_pairs={{0,2},{1,15},{2,4},{3,1},{4,6},{5,3},{6,8},{7,5},{8,10},{9,7},{10,... | collective-permute-start | bytes 1671176 | tf_op jit(solution)/shard_map/ppermute | solution.py:285
  16.0 2.6 %collective-permute-start.2 = (bf16[1024,256]{1,0:T(8,128)(2,1)}, bf16[1024,256]{1,0:T(8,128)(2,1)S(1)}, u32[]{:S(2)}, u32[]{:S(2)}) collective-permute-start(bf16[1024,256]{1,0:T(8,128)(2,1)} %bitcast.7), channel_id=1, source_target_pairs={{0,1},{1,0},{2,3},{3,2},{4,5},{5,4},{6,7},{7,6},{8,9},{9,8},{10,11... | collective-permute-start | bytes 1572872 | tf_op jit(solution)/shard_map/ppermute | solution.py:285
  20.5 2.4 %collective-permute-start.4 = (bf16[256,1024]{1,0:T(8,128)(2,1)}, bf16[256,1024]{1,0:T(8,128)(2,1)S(1)}, u32[]{:S(2)}, u32[]{:S(2)}) collective-permute-start(bf16[256,1024]{1,0:T(8,128)(2,1)} %bitcast.21), channel_id=1, source_target_pairs={{0,1},{1,0},{2,3},{3,2},{4,5},{5,4},{6,7},{7,6},{8,9},{9,8},{10,11... | collective-permute-start | bytes 1572872 | tf_op jit(solution)/shard_map/ppermute | solution.py:285
  24.0 5.0 %collective-permute-start.1 = (bf16[128,2176]{1,0:T(8,128)(2,1)}, bf16[128,2176]{1,0:T(8,128)(2,1)S(1)}, u32[]{:S(2)}, u32[]{:S(2)}) collective-permute-start(bf16[128,2176]{1,0:T(8,128)(2,1)} %collective-permute-done.refs_1_), channel_id=1, source_target_pairs={{0,2},{1,15},{2,4},{3,1},{4,6},{5,3},{6,8},{7,5},{8,10},{9,7},{10,... | collective-permute-start | bytes 1671176 | tf_op jit(solution)/shard_map/ppermute | solution.py:285
  29.0 2.7 %collective-permute-start.9 = (bf16[128,2176]{1,0:T(8,128)(2,1)S(1)}, bf16[128,2176]{1,0:T(8,128)(2,1)S(1)}, u32[]{:S(2)}, u32[]{:S(2)}) collective-permute-start(bf16[128,2176]{1,0:T(8,128)(2,1)S(1)} %collective-permute-done.6.refs_0_), channel_id=1, source_target_pairs={{0,2},{1,15},{2,4},{3,1},{4,6},{5,3},{6,8},{7,5},{8,10},{9,7},{10,... | collective-permute-start | bytes 1671176 | tf_op jit(solution)/shard_map/ppermute | solution.py:285
  36.0 4.0 %shard_map.111 = (bf16[128,1152]{1,0:T(8,128)(2,1)S(1)}, bf16[128,1152]{1,0:T(8,128)(2,1)S(1)}, f32[1024,1024]{1,0:T(8,128)S(1)}, f32[512,1024]{1,0:T(8,128)S(1)}) custom-call(s32[1]{0:T(128)} %bitcast.1.expert_ref, bf16[128,2176]{1,0:T(8,128)(2,1)S(1)} %copy-done.6, bf16[128,2176]{1,0:T(8,128)(2,1)} %collective-permute-done.refs_1_, ...), custom_call_target="tpu_custom_call" | custom-call | flops 2147483648 | bytes 16777216 | tf_op jit(solution)/shard_map/pallas_call | solution.py:217
  41.9 4.8 %collective-permute-start.13 = (bf16[128,2176]{1,0:T(8,128)(2,1)S(1)}, bf16[128,2176]{1,0:T(8,128)(2,1)S(1)}, u32[]{:S(2)}, u32[]{:S(2)}) collective-permute-start(bf16[128,2176]{1,0:T(8,128)(2,1)S(1)} %collective-permute-done.9.refs_0_), channel_id=1, source_target_pairs={{0,2},{1,15},{2,4},{3,1},{4,6},{5,3},{6,8},{7,5},{8,10},{9,7},{10,... | collective-permute-start | bytes 1671176 | tf_op jit(solution)/shard_map/ppermute | solution.py:285
  46.7 3.8 %shard_map.112 = (bf16[128,1152]{1,0:T(8,128)(2,1)S(1)}, bf16[128,1152]{1,0:T(8,128)(2,1)S(1)}, f32[1024,1024]{1,0:T(8,128)S(1)}, f32[512,1024]{1,0:T(8,128)S(1)}) custom-call(s32[1]{0:T(128)} %bitcast.1.expert_ref, bf16[128,2176]{1,0:T(8,128)(2,1)S(1)} %collective-permute-done.6.refs_0_, ...), custom_call_target="tpu_custom_call", output_to_operand_aliasing={{2}: (9, {}), {3}: (10, {})} | custom-call | flops 2147483648 | bytes 16777216 | tf_op jit(solution)/shard_map/pallas_call | solution.py:217
  51.2 2.3 %collective-permute-start.7 = (bf16[128,2176]{1,0:T(8,128)(2,1)S(1)}, bf16[128,2176]{1,0:T(8,128)(2,1)S(1)}, u32[]{:S(2)}, u32[]{:S(2)}) collective-permute-start(bf16[128,2176]{1,0:T(8,128)(2,1)S(1)} %collective-permute-done.5.refs_1_), channel_id=1, source_target_pairs={{0,2},{1,15},{2,4},{3,1},{4,6},{5,3},{6,8},{7,5},{8,10},{9,7},{10,... | collective-permute-start | bytes 1671176 | tf_op jit(solution)/shard_map/ppermute | solution.py:285
  53.5 3.8 %shard_map.114 = (bf16[128,1152]{1,0:T(8,128)(2,1)S(1)}, bf16[128,1152]{1,0:T(8,128)(2,1)S(1)}, f32[1024,1024]{1,0:T(8,128)S(1)}, f32[512,1024]{1,0:T(8,128)S(1)}) custom-call(s32[1]{0:T(128)} %bitcast.1.expert_ref, bf16[128,2176]{1,0:T(8,128)(2,1)S(1)} %collective-permute-done.9.refs_0_, ...), custom_call_target="tpu_custom_call", output_to_operand_aliasing={{2}: (9, {}), {3}: (10, {})} | custom-call | flops 2147483648 | bytes 16777216 | tf_op jit(solution)/shard_map/pallas_call | solution.py:217
  57.3 2.5 %shard_map.118 = (bf16[128,1152]{1,0:T(8,128)(2,1)S(1)}, f32[1024,512]{1,0:T(8,128)S(1)}, f32[256,1024]{1,0:T(8,128)S(1)}, bf16[4,8,48,256]{3,2,1,0:T(8,128)(2,1)S(1)}, bf16[4,8,48,256]{3,2,1,0:T(8,128)(2,1)S(1)}) custom-call(s32[1]{0:T(128)} %bitcast.1.expert_ref, bf16[128,2176]{1,0:T(8,128)(2,1)S(1)} %collective-permute-done.13.refs_0_, ...), custom_call_target="tpu_custom_call" | custom-call | flops 1073741824 | bytes 16777216 | tf_op jit(solution)/shard_map/pallas_call | solution.py:217
  59.8 3.4 %collective-permute-start.18 = (bf16[4,8,48,256]{3,2,1,0:T(8,128)(2,1)S(1)}, bf16[4,8,48,256]{3,2,1,0:T(8,128)(2,1)S(1)}, u32[]{:S(2)}, u32[]{:S(2)}) collective-permute-start(bf16[4,8,48,256]{3,2,1,0:T(8,128)(2,1)S(1)} %get-tuple-element.54), channel_id=1, source_target_pairs={{0,1},{1,0},{2,3},{3,2},{4,5},{5,4},{6,7},{7,6},{8,9},{9,8},{10,11... | collective-permute-start | bytes 2359304 | tf_op jit(solution)/shard_map/ppermute | solution.py:285
  65.2 2.4 %collective-permute-start.17 = (bf16[128,2176]{1,0:T(8,128)(2,1)S(1)}, bf16[128,2176]{1,0:T(8,128)(2,1)S(1)}, u32[]{:S(2)}, u32[]{:S(2)}) collective-permute-start(bf16[128,2176]{1,0:T(8,128)(2,1)S(1)} %collective-permute-done.7.block), channel_id=1, source_target_pairs={{0,1},{1,0},{2,3},{3,2},{4,5},{5,4},{6,7},{7,6},{8,9},{9,8},{10,11... | collective-permute-start | bytes 1671176 | tf_op jit(solution)/shard_map/ppermute | solution.py:285
  69.7 2.2 %shard_map.122 = bf16[4,8,48,512]{3,2,1,0:T(8,128)(2,1)} custom-call(s32[1]{0:T(128)} %bitcast.1.expert_ref, bf16[128,2176]{1,0:T(8,128)(2,1)S(1)} %collective-permute-done.7.block, bf16[128,512]{1,0:T(8,128)(2,1)S(1)} %get-tuple-element.50.pre, bf16[128,256]{1,0:T(8,128)(2,1)S(1)} %get-tuple-element.51.act, ...), custom_call_target="tpu_custom_call" | custom-call | flops 603979776 | bytes 16777216 | tf_op jit(solution)/shard_map/pallas_call | solution.py:217
  71.9 4.2 %all-to-all-start = ((bf16[4,8,48,512]{3,2,1,0:T(8,128)(2,1)}), bf16[4,8,48,512]{3,2,1,0:T(8,128)(2,1)S(1)}, u32[]{:S(2)}, u32[]{:S(2)}) async-start(bf16[4,8,48,512]{3,2,1,0:T(8,128)(2,1)} %shard_map.122), calls=%async_computation | async-start | bytes 3145728 | tf_op jit(solution)/shard_map/all_to_all | solution.py:345
  76.1 3.1 %collective-permute-start.8 = (bf16[128,1152]{1,0:T(8,128)(2,1)S(1)}, bf16[128,1152]{1,0:T(8,128)(2,1)S(1)}, u32[]{:S(2)}, u32[]{:S(2)}) collective-permute-start(bf16[128,1152]{1,0:T(8,128)(2,1)S(1)} %get-tuple-element.38), channel_id=1, source_target_pairs={{2,0},{15,1},{4,2},{1,3},{6,4},{3,5},{8,6},{5,7},{10,8},{7,9},{12,... | collective-permute-start | bytes 884744 | tf_op jit(solution)/shard_map/ppermute | solution.py:285
  79.2 3.4 %collective-permute-start.14 = (bf16[128,1152]{1,0:T(8,128)(2,1)S(1)}, bf16[128,1152]{1,0:T(8,128)(2,1)S(1)}, u32[]{:S(2)}, u32[]{:S(2)}) collective-permute-start(bf16[128,1152]{1,0:T(8,128)(2,1)S(1)} %get-tuple-element.44), channel_id=1, source_target_pairs={{2,0},{15,1},{4,2},{1,3},{6,4},{3,5},{8,6},{5,7},{10,8},{7,9},{12,... | collective-permute-start | bytes 884744 | tf_op jit(solution)/shard_map/ppermute | solution.py:285
  82.6 2.8 %collective-permute-done.8.p = bf16[128,1152]{1,0:T(8,128)(2,1)S(1)} collective-permute-done((bf16[128,1152]{1,0:T(8,128)(2,1)S(1)}, bf16[128,1152]{1,0:T(8,128)(2,1)S(1)}, u32[]{:S(2)}, u32[]{:S(2)}) %collective-permute-start.8) | collective-permute-done | bytes 294944 | tf_op jit(solution)/shard_map/ppermute | solution.py:285
  90.6 3.9 %collective-permute-done.10.p = bf16[128,1152]{1,0:T(8,128)(2,1)S(1)} collective-permute-done((bf16[128,1152]{1,0:T(8,128)(2,1)S(1)}, bf16[128,1152]{1,0:T(8,128)(2,1)S(1)}, u32[]{:S(2)}, u32[]{:S(2)}) %collective-permute-start.10) | collective-permute-done | bytes 294944 | tf_op jit(solution)/shard_map/ppermute | solution.py:285
  94.5 2.1 %collective-permute-start.11 = (bf16[128,1152]{1,0:T(8,128)(2,1)S(1)}, bf16[128,1152]{1,0:T(8,128)(2,1)S(1)}, u32[]{:S(2)}, u32[]{:S(2)}) collective-permute-start(bf16[128,1152]{1,0:T(8,128)(2,1)S(1)} %shard_map.116), channel_id=1, source_target_pairs={{2,0},{15,1},{4,2},{1,3},{6,4},{3,5},{8,6},{5,7},{10,8},{7,9},{12,... | collective-permute-start | bytes 884744 | tf_op jit(solution)/shard_map/ppermute | solution.py:285
  97.6 6.9 %all-to-all-start.1 = ((bf16[8,48,512]{2,1,0:T(8,128)(2,1)}), bf16[8,48,512]{2,1,0:T(8,128)(2,1)S(1)}, u32[]{:S(2)}, u32[]{:S(2)}) async-start(bf16[8,48,512]{2,1,0:T(8,128)(2,1)} %shard_map.123), calls=%async_computation.1 | async-start | bytes 786432 | tf_op jit(solution)/shard_map/all_to_all | solution.py:354
  104.6 5.0 %collective-permute-start.16 = (bf16[128,1152]{1,0:T(8,128)(2,1)S(1)}, bf16[128,1152]{1,0:T(8,128)(2,1)S(1)}, u32[]{:S(2)}, u32[]{:S(2)}) collective-permute-start(bf16[128,1152]{1,0:T(8,128)(2,1)S(1)} %shard_map.120), channel_id=1, source_target_pairs={{15,0},{2,1},{1,2},{4,3},{3,4},{6,5},{5,6},{8,7},{7,8},{10,9},{9,1... | collective-permute-start | bytes 884744 | tf_op jit(solution)/shard_map/ppermute | solution.py:285
  109.8 2.6 %collective-permute-start.12 = (bf16[128,1152]{1,0:T(8,128)(2,1)S(1)}, bf16[128,1152]{1,0:T(8,128)(2,1)S(1)}, u32[]{:S(2)}, u32[]{:S(2)}) collective-permute-start(bf16[128,1152]{1,0:T(8,128)(2,1)S(1)} %shard_map.117), channel_id=1, source_target_pairs={{2,0},{15,1},{4,2},{1,3},{6,4},{3,5},{8,6},{5,7},{10,8},{7,9},{12,... | collective-permute-start | bytes 884744 | tf_op jit(solution)/shard_map/ppermute | solution.py:285
  114.1 7.5 %collective-permute-done.12.p = bf16[128,1152]{1,0:T(8,128)(2,1)S(1)} collective-permute-done((bf16[128,1152]{1,0:T(8,128)(2,1)S(1)}, bf16[128,1152]{1,0:T(8,128)(2,1)S(1)}, u32[]{:S(2)}, u32[]{:S(2)}) %collective-permute-start.12) | collective-permute-done | bytes 294944 | tf_op jit(solution)/shard_map/ppermute | solution.py:285
  (67 shorter events, 27.3 us)
Async XLA Ops:
  2.6 21.4 %collective-permute-start = (bf16[128,2176]{1,0:T(8,128)(2,1)}, bf16[128,2176]{1,0:T(8,128)(2,1)}, u32[]{:S(2)}, u32[]{:S(2)}) collective-permute-start(bf16[128,2176]{1,0:T(8,128)(2,1)} %shard_map.110.refs_0_), channel_id=1, source_target_pairs={{0,2},{1,15},{2,4},{3,1},{4,6},{5,3},{6,8},{7,5},{8,10},{9,7},{10,... | collective-permute-start | bytes 1671176 | tf_op jit(solution)/shard_map/ppermute | solution.py:285
  14.1 14.9 %collective-permute-start.6 = (bf16[128,2176]{1,0:T(8,128)(2,1)}, bf16[128,2176]{1,0:T(8,128)(2,1)S(1)}, u32[]{:S(2)}, u32[]{:S(2)}) collective-permute-start(bf16[128,2176]{1,0:T(8,128)(2,1)} %shard_map.110.refs_0_), channel_id=1, source_target_pairs={{0,15},{1,2},{2,1},{3,4},{4,3},{5,6},{6,5},{7,8},{8,7},{9,10},{10,... | collective-permute-start | bytes 1671176 | tf_op jit(solution)/shard_map/ppermute | solution.py:285
  16.0 15.7 %collective-permute-start.2 = (bf16[1024,256]{1,0:T(8,128)(2,1)}, bf16[1024,256]{1,0:T(8,128)(2,1)S(1)}, u32[]{:S(2)}, u32[]{:S(2)}) collective-permute-start(bf16[1024,256]{1,0:T(8,128)(2,1)} %bitcast.7), channel_id=1, source_target_pairs={{0,1},{1,0},{2,3},{3,2},{4,5},{5,4},{6,7},{7,6},{8,9},{9,8},{10,11... | collective-permute-start | bytes 1572872 | tf_op jit(solution)/shard_map/ppermute | solution.py:285
  18.6 13.2 %collective-permute-start.3 = (bf16[1024,256]{1,0:T(8,128)(2,1)}, bf16[1024,256]{1,0:T(8,128)(2,1)S(1)}, u32[]{:S(2)}, u32[]{:S(2)}) collective-permute-start(bf16[1024,256]{1,0:T(8,128)(2,1)} %bitcast.14), channel_id=1, source_target_pairs={{0,1},{1,0},{2,3},{3,2},{4,5},{5,4},{6,7},{7,6},{8,9},{9,8},{10,11... | collective-permute-start | bytes 1572872 | tf_op jit(solution)/shard_map/ppermute | solution.py:285
  20.5 11.3 %collective-permute-start.4 = (bf16[256,1024]{1,0:T(8,128)(2,1)}, bf16[256,1024]{1,0:T(8,128)(2,1)S(1)}, u32[]{:S(2)}, u32[]{:S(2)}) collective-permute-start(bf16[256,1024]{1,0:T(8,128)(2,1)} %bitcast.21), channel_id=1, source_target_pairs={{0,1},{1,0},{2,3},{3,2},{4,5},{5,4},{6,7},{7,6},{8,9},{9,8},{10,11... | collective-permute-start | bytes 1572872 | tf_op jit(solution)/shard_map/ppermute | solution.py:285
  24.0 16.0 %collective-permute-start.1 = (bf16[128,2176]{1,0:T(8,128)(2,1)}, bf16[128,2176]{1,0:T(8,128)(2,1)S(1)}, u32[]{:S(2)}, u32[]{:S(2)}) collective-permute-start(bf16[128,2176]{1,0:T(8,128)(2,1)} %collective-permute-done.refs_1_), channel_id=1, source_target_pairs={{0,2},{1,15},{2,4},{3,1},{4,6},{5,3},{6,8},{7,5},{8,10},{9,7},{10,... | collective-permute-start | bytes 1671176 | tf_op jit(solution)/shard_map/ppermute | solution.py:285
  29.0 12.9 %collective-permute-start.9 = (bf16[128,2176]{1,0:T(8,128)(2,1)S(1)}, bf16[128,2176]{1,0:T(8,128)(2,1)S(1)}, u32[]{:S(2)}, u32[]{:S(2)}) collective-permute-start(bf16[128,2176]{1,0:T(8,128)(2,1)S(1)} %collective-permute-done.6.refs_0_), channel_id=1, source_target_pairs={{0,2},{1,15},{2,4},{3,1},{4,6},{5,3},{6,8},{7,5},{8,10},{9,7},{10,... | collective-permute-start | bytes 1671176 | tf_op jit(solution)/shard_map/ppermute | solution.py:285
  40.0 11.2 %collective-permute-start.5 = (bf16[128,2176]{1,0:T(8,128)(2,1)S(1)}, bf16[128,2176]{1,0:T(8,128)(2,1)S(1)}, u32[]{:S(2)}, u32[]{:S(2)}) collective-permute-start(bf16[128,2176]{1,0:T(8,128)(2,1)S(1)} %collective-permute-done.1.refs_1_), channel_id=1, source_target_pairs={{0,2},{1,15},{2,4},{3,1},{4,6},{5,3},{6,8},{7,5},{8,10},{9,7},{10,... | collective-permute-start | bytes 1671176 | tf_op jit(solution)/shard_map/ppermute | solution.py:285
  41.9 15.4 %collective-permute-start.13 = (bf16[128,2176]{1,0:T(8,128)(2,1)S(1)}, bf16[128,2176]{1,0:T(8,128)(2,1)S(1)}, u32[]{:S(2)}, u32[]{:S(2)}) collective-permute-start(bf16[128,2176]{1,0:T(8,128)(2,1)S(1)} %collective-permute-done.9.refs_0_), channel_id=1, source_target_pairs={{0,2},{1,15},{2,4},{3,1},{4,6},{5,3},{6,8},{7,5},{8,10},{9,7},{10,... | collective-permute-start | bytes 1671176 | tf_op jit(solution)/shard_map/ppermute | solution.py:285
  51.2 14.0 %collective-permute-start.7 = (bf16[128,2176]{1,0:T(8,128)(2,1)S(1)}, bf16[128,2176]{1,0:T(8,128)(2,1)S(1)}, u32[]{:S(2)}, u32[]{:S(2)}) collective-permute-start(bf16[128,2176]{1,0:T(8,128)(2,1)S(1)} %collective-permute-done.5.refs_1_), channel_id=1, source_target_pairs={{0,2},{1,15},{2,4},{3,1},{4,6},{5,3},{6,8},{7,5},{8,10},{9,7},{10,... | collective-permute-start | bytes 1671176 | tf_op jit(solution)/shard_map/ppermute | solution.py:285
  59.8 9.8 %collective-permute-start.18 = (bf16[4,8,48,256]{3,2,1,0:T(8,128)(2,1)S(1)}, bf16[4,8,48,256]{3,2,1,0:T(8,128)(2,1)S(1)}, u32[]{:S(2)}, u32[]{:S(2)}) collective-permute-start(bf16[4,8,48,256]{3,2,1,0:T(8,128)(2,1)S(1)} %get-tuple-element.54), channel_id=1, source_target_pairs={{0,1},{1,0},{2,3},{3,2},{4,5},{5,4},{6,7},{7,6},{8,9},{9,8},{10,11... | collective-permute-start | bytes 2359304 | tf_op jit(solution)/shard_map/ppermute | solution.py:285
  63.3 6.4 %collective-permute-start.19 = (bf16[4,8,48,256]{3,2,1,0:T(8,128)(2,1)S(1)}, bf16[4,8,48,256]{3,2,1,0:T(8,128)(2,1)S(1)}, u32[]{:S(2)}, u32[]{:S(2)}) collective-permute-start(bf16[4,8,48,256]{3,2,1,0:T(8,128)(2,1)S(1)} %get-tuple-element.55), channel_id=1, source_target_pairs={{0,1},{1,0},{2,3},{3,2},{4,5},{5,4},{6,7},{7,6},{8,9},{9,8},{10,11... | collective-permute-start | bytes 2359304 | tf_op jit(solution)/shard_map/ppermute | solution.py:285
  65.2 4.4 %collective-permute-start.17 = (bf16[128,2176]{1,0:T(8,128)(2,1)S(1)}, bf16[128,2176]{1,0:T(8,128)(2,1)S(1)}, u32[]{:S(2)}, u32[]{:S(2)}) collective-permute-start(bf16[128,2176]{1,0:T(8,128)(2,1)S(1)} %collective-permute-done.7.block), channel_id=1, source_target_pairs={{0,1},{1,0},{2,3},{3,2},{4,5},{5,4},{6,7},{7,6},{8,9},{9,8},{10,11... | collective-permute-start | bytes 1671176 | tf_op jit(solution)/shard_map/ppermute | solution.py:285
  71.9 24.7 %all-to-all-start = ((bf16[4,8,48,512]{3,2,1,0:T(8,128)(2,1)}), bf16[4,8,48,512]{3,2,1,0:T(8,128)(2,1)S(1)}, u32[]{:S(2)}, u32[]{:S(2)}) async-start(bf16[4,8,48,512]{3,2,1,0:T(8,128)(2,1)} %shard_map.122), calls=%async_computation | async-start | bytes 3145728 | tf_op jit(solution)/shard_map/all_to_all | solution.py:345
  76.1 18.4 %copy-start.11 = (bf16[128,1152]{1,0:T(8,128)(2,1)S(1)}, bf16[128,1152]{1,0:T(8,128)(2,1)}, u32[]{:S(2)}) copy-start(bf16[128,1152]{1,0:T(8,128)(2,1)} %copy-done.10) | copy-start | bytes 884740
  76.1 9.3 %collective-permute-start.8 = (bf16[128,1152]{1,0:T(8,128)(2,1)S(1)}, bf16[128,1152]{1,0:T(8,128)(2,1)S(1)}, u32[]{:S(2)}, u32[]{:S(2)}) collective-permute-start(bf16[128,1152]{1,0:T(8,128)(2,1)S(1)} %get-tuple-element.38), channel_id=1, source_target_pairs={{2,0},{15,1},{4,2},{1,3},{6,4},{3,5},{8,6},{5,7},{10,8},{7,9},{12,... | collective-permute-start | bytes 884744 | tf_op jit(solution)/shard_map/ppermute | solution.py:285
  79.2 9.4 %collective-permute-start.14 = (bf16[128,1152]{1,0:T(8,128)(2,1)S(1)}, bf16[128,1152]{1,0:T(8,128)(2,1)S(1)}, u32[]{:S(2)}, u32[]{:S(2)}) collective-permute-start(bf16[128,1152]{1,0:T(8,128)(2,1)S(1)} %get-tuple-element.44), channel_id=1, source_target_pairs={{2,0},{15,1},{4,2},{1,3},{6,4},{3,5},{8,6},{5,7},{10,8},{7,9},{12,... | collective-permute-start | bytes 884744 | tf_op jit(solution)/shard_map/ppermute | solution.py:285
  85.5 9.0 %collective-permute-start.10 = (bf16[128,1152]{1,0:T(8,128)(2,1)S(1)}, bf16[128,1152]{1,0:T(8,128)(2,1)S(1)}, u32[]{:S(2)}, u32[]{:S(2)}) collective-permute-start(bf16[128,1152]{1,0:T(8,128)(2,1)S(1)} %shard_map.115), channel_id=1, source_target_pairs={{2,0},{15,1},{4,2},{1,3},{6,4},{3,5},{8,6},{5,7},{10,8},{7,9},{12,... | collective-permute-start | bytes 884744 | tf_op jit(solution)/shard_map/ppermute | solution.py:285
  88.6 15.9 %collective-permute-start.15 = (bf16[128,1152]{1,0:T(8,128)(2,1)S(1)}, bf16[128,1152]{1,0:T(8,128)(2,1)S(1)}, u32[]{:S(2)}, u32[]{:S(2)}) collective-permute-start(bf16[128,1152]{1,0:T(8,128)(2,1)S(1)} %shard_map.119), channel_id=1, source_target_pairs={{2,0},{15,1},{4,2},{1,3},{6,4},{3,5},{8,6},{5,7},{10,8},{7,9},{12,... | collective-permute-start | bytes 884744 | tf_op jit(solution)/shard_map/ppermute | solution.py:285
  94.5 15.1 %collective-permute-start.11 = (bf16[128,1152]{1,0:T(8,128)(2,1)S(1)}, bf16[128,1152]{1,0:T(8,128)(2,1)S(1)}, u32[]{:S(2)}, u32[]{:S(2)}) collective-permute-start(bf16[128,1152]{1,0:T(8,128)(2,1)S(1)} %shard_map.116), channel_id=1, source_target_pairs={{2,0},{15,1},{4,2},{1,3},{6,4},{3,5},{8,6},{5,7},{10,8},{7,9},{12,... | collective-permute-start | bytes 884744 | tf_op jit(solution)/shard_map/ppermute | solution.py:285
  97.6 25.0 %all-to-all-start.1 = ((bf16[8,48,512]{2,1,0:T(8,128)(2,1)}), bf16[8,48,512]{2,1,0:T(8,128)(2,1)S(1)}, u32[]{:S(2)}, u32[]{:S(2)}) async-start(bf16[8,48,512]{2,1,0:T(8,128)(2,1)} %shard_map.123), calls=%async_computation.1 | async-start | bytes 786432 | tf_op jit(solution)/shard_map/all_to_all | solution.py:354
  104.6 16.9 %copy-start.7 = (s32[128,10]{0,1:T(8,128)S(1)}, s32[128,10]{0,1:T(8,128)}, u32[]{:S(2)}) copy-start(s32[128,10]{0,1:T(8,128)} %param.9) | copy-start | bytes 15364
  104.6 9.4 %collective-permute-start.16 = (bf16[128,1152]{1,0:T(8,128)(2,1)S(1)}, bf16[128,1152]{1,0:T(8,128)(2,1)S(1)}, u32[]{:S(2)}, u32[]{:S(2)}) collective-permute-start(bf16[128,1152]{1,0:T(8,128)(2,1)S(1)} %shard_map.120), channel_id=1, source_target_pairs={{15,0},{2,1},{1,2},{4,3},{3,4},{6,5},{5,6},{8,7},{7,8},{10,9},{9,1... | collective-permute-start | bytes 884744 | tf_op jit(solution)/shard_map/ppermute | solution.py:285
  109.8 11.8 %collective-permute-start.12 = (bf16[128,1152]{1,0:T(8,128)(2,1)S(1)}, bf16[128,1152]{1,0:T(8,128)(2,1)S(1)}, u32[]{:S(2)}, u32[]{:S(2)}) collective-permute-start(bf16[128,1152]{1,0:T(8,128)(2,1)S(1)} %shard_map.117), channel_id=1, source_target_pairs={{2,0},{15,1},{4,2},{1,3},{6,4},{3,5},{8,6},{5,7},{10,8},{7,9},{12,... | collective-permute-start | bytes 884744 | tf_op jit(solution)/shard_map/ppermute | solution.py:285
  (14 other events, 91.8 us)

commit v11 on v9

--- a/solution.py
+++ b/solution.py
@@ -13,6 +13,7 @@
 LANES = 128
 HOP_FLOPS = 5_000_000_000
 SIDE_FLOPS = 2_500_000_000
+FAR_FLOPS = 15_000_000_000
 
 
 def dot(a, b, ca, cb):
@@ -40,7 +41,7 @@
         copy.wait()
 
 
-def finish_kernel(routing, p, q, r, token_grad, gate_grad):
+def finish_kernel(parts, routing, p, q, r, token_grad, gate_grad, gate, up, down):
     rows, width = token_grad.shape
     total = p[...].astype(F32) + q[...].astype(F32) + r[...].astype(F32)
     token_grad[...] = total[:, :width].astype(BF)
@@ -52,6 +53,11 @@
         for k in range(routing.shape[0])
     ]
     gate_grad[...] = jnp.concatenate(picked, axis=0).astype(BF)
+    n, hidden = gate.shape[1:]
+    m = down.shape[1]
+    total = jnp.sum(parts[...].astype(F32), axis=0)
+    gate[0], up[0] = total[:n, :hidden], total[:n, hidden:]
+    down[0] = jnp.concatenate([total[n : n + m], total[n + m :]], axis=1)
 
 
 def split(blocks, width):
@@ -198,14 +204,6 @@
         copy.wait()
 
 
-def sum_kernel(parts, gate, up, down):
-    n, hidden = gate.shape[1:]
-    m = down.shape[1]
-    total = jnp.sum(parts[...].astype(F32), axis=0)
-    gate[0], up[0] = total[:n, :hidden], total[:n, hidden:]
-    down[0] = jnp.concatenate([total[n : n + m], total[n + m :]], axis=1)
-
-
 VMEM = pl.BlockSpec(memory_space=pltpu.VMEM)
 
 
@@ -231,7 +229,7 @@
         jax.ShapeDtypeStruct((own // 2, width), F32),
     ]
     if replicas:
-        shapes += [jax.ShapeDtypeStruct((*replicas, (width + 2 * hidden) // math.prod(replicas), hidden), BF)] * 2
+        shapes += [jax.ShapeDtypeStruct((*replicas, (width + 2 * hidden) // math.prod(replicas), 2 * hidden), BF)]
     n = len(blocks)
     return call(
         functools.partial(group_kernel, not acc, bool(replicas), n),
@@ -304,9 +302,9 @@
     b3 = send(b2, out)
     a4 = send(after(a3, g_a2), out)
     g_b2, g_a3, *acc = group(expert, (b2, a3), weights, acc)
-    g_b3, *acc, early0, early1 = group(expert, (b3,), weights, acc, (nx, ny))
-    early = [send(early0, swap), send(early1, swap)]
-    whole = jax.ShapeDtypeStruct((*early0.shape[:-1], 2 * hidden), BF)
+    g_b3, *acc, early = group(expert, (b3,), weights, acc, (nx, ny))
+    early = send(early, swap)
+    whole = jax.ShapeDtypeStruct(early.shape, BF)
     theirs = send(a4, swap)
     g_a4, pre, act = call(
         far_kernel,
@@ -318,13 +316,13 @@
         expert,
         (a4, *weights),
         {},
-        2 * rows * width * hidden * 10,
+        FAR_FLOPS,
     )
     (parts,) = call(
         last_kernel,
         [whole],
         expert,
-        (a4, pre, act, theirs, *weights[:3], *acc, *early),
+        (a4, pre, act, theirs, *weights[:3], *acc, early),
         {},
         2 * rows * width * hidden * 9,
         in_hbm,
@@ -335,27 +333,25 @@
     a = send(g_a4, home)
 
     parts = lax.all_to_all(parts[0], "dp", split_axis=0, concat_axis=0, tiled=True)
-    slab = jax.ShapeDtypeStruct((1, width // replicas, hidden), F32)
-    sums = pl.pallas_call(
-        sum_kernel,
-        out_shape=[slab, slab, jax.ShapeDtypeStruct((1, hidden // replicas, width), F32)],
-        in_specs=[VMEM],
-        out_specs=[VMEM] * 3,
-        compiler_params=pltpu.CompilerParams(vmem_limit_bytes=8 * 1024 * 1024),
-    )(parts)
-
     b = send(add(b, g_b2, SIDE_FLOPS), home)
     a = send(add(a, g_a3), home)
     b = send(add(b, g_b1, SIDE_FLOPS), uncross)
     a = send(add(a, g_a2), home)
     a = send(add(a, g_a1), home)
-    token_grad, gate_grad = pl.pallas_call(
+    slab = jax.ShapeDtypeStruct((1, width // replicas, hidden), F32)
+    token_grad, gate_grad, *sums = pl.pallas_call(
         finish_kernel,
-        out_shape=[jax.ShapeDtypeStruct((rows, width), BF), jax.ShapeDtypeStruct(gates.shape[::-1], BF)],
-        in_specs=[VMEM] * 4,
-        out_specs=[VMEM] * 2,
-        compiler_params=pltpu.CompilerParams(vmem_limit_bytes=8 * 1024 * 1024),
-    )(routing.T, a, b, g_own)
+        out_shape=[
+            jax.ShapeDtypeStruct((rows, width), BF),
+            jax.ShapeDtypeStruct(gates.shape[::-1], BF),
+            slab,
+            slab,
+            jax.ShapeDtypeStruct((1, hidden // replicas, width), F32),
+        ],
+        in_specs=[VMEM] * 5,
+        out_specs=[VMEM] * 5,
+        compiler_params=pltpu.CompilerParams(vmem_limit_bytes=12 * 1024 * 1024),
+    )(parts, routing.T, a, b, g_own)
     return token_grad, gate_grad.T, *sums
 
 

time: 123 us -> 122 us (level)
  starting transfers between devices: 72.4 us -> 68.9 us
  waiting for transfers between devices: 20 us -> 23.5 us
    ppermute x20 -> x19, starting transfers between devices: 62.7 us -> 59.2 us  [send(): return lax.ppermute(a, 'expert', pairs)]
    ppermute x20 -> x19, waiting for transfers between devices: 20 us -> 22.2 us  [send(): return lax.ppermute(a, 'expert', pairs)]
    all_to_all x1, waiting for transfers between devices: 0.01 us -> 1.35 us  [on_device(): lax.all_to_all(parts[0], 'dp', split_axis=0, concat_axis=0, tiled=True)]
  transfers between devices with their start and end apart: 21 -> 20, of which waited for: 8 -> 9; matrix products, arithmetic and copies ran while one was open for 0% -> 0% of each run, Pallas kernels for 14% -> 14%
where the time goes in v11:
time: 122 us; the launch traced here: 120 us
  starting transfers between devices  68.9 us (56%)
  waiting for transfers between devices  23.5 us (19%)
  Pallas kernels  21.8 us (18%)
  local copies, waits for them, and re-layouts  4.91 us (4%)
    ppermute x19, starting transfers between devices, send(): return lax.ppermute(a, 'expert', pairs)  59.2 us
    ppermute x19, waiting for transfers between devices, send(): return lax.ppermute(a, 'expert', pairs)  22.2 us
    pallas_call x6, Pallas kernels, call(): pl.pallas_call(kernel, out_shape=out_shape, in_specs=[pl.BlockSpec(memory...  18.3 us
    all_to_all x1, starting transfers between devices, on_device(): lax.all_to_all(parts[0], 'dp', split_axis=0, concat_axis=0, tiled=True)  9.68 us
    unnamed x28, local copies, waits for them, and re-layouts  4.91 us
  transfers between devices with their start and end apart: 20, of which 9 were waited for; matrix products, arithmetic and copies ran while one was open for 0% of the time, Pallas kernels for 14%

profile of v11, /device:TPU:1, one launch (start us, length us, event | category | flops | bytes accessed | tf_op | source)
XLA Modules:
  0.0 120.1 jit_solution(13600442069154744660)
XLA Ops:
  0.6 1.9 %shard_map.110.refs_0_ = bf16[128,2176]{1,0:T(8,128)(2,1)} custom-call(s32[10,128]{1,0:T(8,128)} %bitcast.29, bf16[10,128]{1,0:T(8,128)(2,1)} %bitcast.31, bf16[128,1024]{1,0:T(8,128)(2,1)} %tokens.1, bf16[128,1024]{1,0:T(8,128)(2,1)} %cotangent.1), custom_call_target="tpu_custom_call" | custom-call | tf_op jit(solution)/shard_map/pallas_call | solution.py:279
  2.6 11.5 %collective-permute-start = (bf16[128,2176]{1,0:T(8,128)(2,1)}, bf16[128,2176]{1,0:T(8,128)(2,1)}, u32[]{:S(2)}, u32[]{:S(2)}) collective-permute-start(bf16[128,2176]{1,0:T(8,128)(2,1)} %shard_map.110.refs_0_), channel_id=1, source_target_pairs={{0,2},{1,15},{2,4},{3,1},{4,6},{5,3},{6,8},{7,5},{8,10},{9,7},{10,... | collective-permute-start | bytes 1671176 | tf_op jit(solution)/shard_map/ppermute | solution.py:276
  16.0 2.6 %collective-permute-start.2 = (bf16[1024,256]{1,0:T(8,128)(2,1)}, bf16[1024,256]{1,0:T(8,128)(2,1)S(1)}, u32[]{:S(2)}, u32[]{:S(2)}) collective-permute-start(bf16[1024,256]{1,0:T(8,128)(2,1)} %bitcast.8), channel_id=1, source_target_pairs={{0,1},{1,0},{2,3},{3,2},{4,5},{5,4},{6,7},{7,6},{8,9},{9,8},{10,11... | collective-permute-start | bytes 1572872 | tf_op jit(solution)/shard_map/ppermute | solution.py:276
  20.5 2.4 %collective-permute-start.4 = (bf16[256,1024]{1,0:T(8,128)(2,1)}, bf16[256,1024]{1,0:T(8,128)(2,1)S(1)}, u32[]{:S(2)}, u32[]{:S(2)}) collective-permute-start(bf16[256,1024]{1,0:T(8,128)(2,1)} %bitcast.22), channel_id=1, source_target_pairs={{0,1},{1,0},{2,3},{3,2},{4,5},{5,4},{6,7},{7,6},{8,9},{9,8},{10,11... | collective-permute-start | bytes 1572872 | tf_op jit(solution)/shard_map/ppermute | solution.py:276
  24.0 5.0 %collective-permute-start.1 = (bf16[128,2176]{1,0:T(8,128)(2,1)}, bf16[128,2176]{1,0:T(8,128)(2,1)S(1)}, u32[]{:S(2)}, u32[]{:S(2)}) collective-permute-start(bf16[128,2176]{1,0:T(8,128)(2,1)} %collective-permute-done.refs_1_), channel_id=1, source_target_pairs={{0,2},{1,15},{2,4},{3,1},{4,6},{5,3},{6,8},{7,5},{8,10},{9,7},{10,... | collective-permute-start | bytes 1671176 | tf_op jit(solution)/shard_map/ppermute | solution.py:276
  29.0 2.7 %collective-permute-start.9 = (bf16[128,2176]{1,0:T(8,128)(2,1)S(1)}, bf16[128,2176]{1,0:T(8,128)(2,1)S(1)}, u32[]{:S(2)}, u32[]{:S(2)}) collective-permute-start(bf16[128,2176]{1,0:T(8,128)(2,1)S(1)} %collective-permute-done.6.refs_0_), channel_id=1, source_target_pairs={{0,2},{1,15},{2,4},{3,1},{4,6},{5,3},{6,8},{7,5},{8,10},{9,7},{10,... | collective-permute-start | bytes 1671176 | tf_op jit(solution)/shard_map/ppermute | solution.py:276
  36.0 4.0 %shard_map.111 = (bf16[128,1152]{1,0:T(8,128)(2,1)S(1)}, bf16[128,1152]{1,0:T(8,128)(2,1)S(1)}, f32[1024,1024]{1,0:T(8,128)S(1)}, f32[512,1024]{1,0:T(8,128)S(1)}) custom-call(s32[1]{0:T(128)} %bitcast.expert_ref, bf16[128,2176]{1,0:T(8,128)(2,1)S(1)} %copy-done.6, bf16[128,2176]{1,0:T(8,128)(2,1)} %collective-permute-done.refs_1_, ...), custom_call_target="tpu_custom_call" | custom-call | flops 2147483648 | bytes 16777216 | tf_op jit(solution)/shard_map/pallas_call | solution.py:211
  41.9 4.8 %collective-permute-start.10 = (bf16[128,2176]{1,0:T(8,128)(2,1)S(1)}, bf16[128,2176]{1,0:T(8,128)(2,1)S(1)}, u32[]{:S(2)}, u32[]{:S(2)}) collective-permute-start(bf16[128,2176]{1,0:T(8,128)(2,1)S(1)} %collective-permute-done.9.refs_0_), channel_id=1, source_target_pairs={{0,2},{1,15},{2,4},{3,1},{4,6},{5,3},{6,8},{7,5},{8,10},{9,7},{10,... | collective-permute-start | bytes 1671176 | tf_op jit(solution)/shard_map/ppermute | solution.py:276
  46.7 3.8 %shard_map.112 = (bf16[128,1152]{1,0:T(8,128)(2,1)S(1)}, bf16[128,1152]{1,0:T(8,128)(2,1)S(1)}, f32[1024,1024]{1,0:T(8,128)S(1)}, f32[512,1024]{1,0:T(8,128)S(1)}) custom-call(s32[1]{0:T(128)} %bitcast.expert_ref, bf16[128,2176]{1,0:T(8,128)(2,1)S(1)} %collective-permute-done.6.refs_0_, ...), custom_call_target="tpu_custom_call", output_to_operand_aliasing={{2}: (9, {}), {3}: (10, {})} | custom-call | flops 2147483648 | bytes 16777216 | tf_op jit(solution)/shard_map/pallas_call | solution.py:211
  51.2 2.3 %collective-permute-start.7 = (bf16[128,2176]{1,0:T(8,128)(2,1)S(1)}, bf16[128,2176]{1,0:T(8,128)(2,1)S(1)}, u32[]{:S(2)}, u32[]{:S(2)}) collective-permute-start(bf16[128,2176]{1,0:T(8,128)(2,1)S(1)} %collective-permute-done.5.refs_1_), channel_id=1, source_target_pairs={{0,2},{1,15},{2,4},{3,1},{4,6},{5,3},{6,8},{7,5},{8,10},{9,7},{10,... | collective-permute-start | bytes 1671176 | tf_op jit(solution)/shard_map/ppermute | solution.py:276
  53.5 3.8 %shard_map.114 = (bf16[128,1152]{1,0:T(8,128)(2,1)S(1)}, bf16[128,1152]{1,0:T(8,128)(2,1)S(1)}, f32[1024,1024]{1,0:T(8,128)S(1)}, f32[512,1024]{1,0:T(8,128)S(1)}) custom-call(s32[1]{0:T(128)} %bitcast.expert_ref, bf16[128,2176]{1,0:T(8,128)(2,1)S(1)} %collective-permute-done.9.refs_0_, ...), custom_call_target="tpu_custom_call", output_to_operand_aliasing={{2}: (9, {}), {3}: (10, {})} | custom-call | flops 2147483648 | bytes 16777216 | tf_op jit(solution)/shard_map/pallas_call | solution.py:211
  57.4 2.5 %shard_map.115 = (bf16[128,1152]{1,0:T(8,128)(2,1)S(1)}, f32[1024,512]{1,0:T(8,128)S(1)}, f32[256,1024]{1,0:T(8,128)S(1)}, bf16[1,32,48,512]{3,2,1,0:T(8,128)(2,1)S(1)}) custom-call(s32[1]{0:T(128)} %bitcast.expert_ref, bf16[128,2176]{1,0:T(8,128)(2,1)S(1)} %collective-permute-done.10.refs_0_, bf16[1024,256]{1,0:T(8,128)(2,1)S(1)} %bitcast.12, ...), custom_call_target="tpu_custom_call" | custom-call | flops 1073741824 | bytes 16777216 | tf_op jit(solution)/shard_map/pallas_call | solution.py:211
  59.9 3.4 %collective-permute-start.11 = (bf16[1,32,48,512]{3,2,1,0:T(8,128)(2,1)S(1)}, bf16[1,32,48,512]{3,2,1,0:T(8,128)(2,1)S(1)}, u32[]{:S(2)}, u32[]{:S(2)}) collective-permute-start(bf16[1,32,48,512]{3,2,1,0:T(8,128)(2,1)S(1)} %get-tuple-element.45), channel_id=1, source_target_pairs={{0,1},{1,0},{2,3},{3,2},{4,5},{5,4},{6,7},{7,6},{8,9},{9,8},{10,11... | collective-permute-start | bytes 4718600 | tf_op jit(solution)/shard_map/ppermute | solution.py:276
  63.3 4.1 %collective-permute-start.8 = (bf16[128,2176]{1,0:T(8,128)(2,1)S(1)}, bf16[128,2176]{1,0:T(8,128)(2,1)S(1)}, u32[]{:S(2)}, u32[]{:S(2)}) collective-permute-start(bf16[128,2176]{1,0:T(8,128)(2,1)S(1)} %collective-permute-done.7.block), channel_id=1, source_target_pairs={{0,1},{1,0},{2,3},{3,2},{4,5},{5,4},{6,7},{7,6},{8,9},{9,8},{10,11... | collective-permute-start | bytes 1671176 | tf_op jit(solution)/shard_map/ppermute | solution.py:276
  67.4 2.0 %shard_map.113 = (bf16[128,1152]{1,0:T(8,128)(2,1)S(1)}, bf16[128,512]{1,0:T(8,128)(2,1)S(1)}, bf16[128,256]{1,0:T(8,128)(2,1)S(1)}) custom-call(s32[1]{0:T(128)} %bitcast.expert_ref, bf16[128,2176]{1,0:T(8,128)(2,1)S(1)} %collective-permute-done.7.block, bf16[1024,256]{1,0:T(8,128)(2,1)S(1)} %bitcast.13, bf16[1024,256]{1,0:T(8,128)(2,1)S(1)} %bitcast.20, ...), custom_call_target="tpu_custom_call" | custom-call | flops 15000000512 | bytes 16777216 | tf_op jit(solution)/shard_map/pallas_call | solution.py:211
  69.5 2.2 %shard_map.116 = bf16[1,32,48,512]{3,2,1,0:T(8,128)(2,1)} custom-call(s32[1]{0:T(128)} %bitcast.expert_ref, bf16[128,2176]{1,0:T(8,128)(2,1)S(1)} %collective-permute-done.7.block, bf16[128,512]{1,0:T(8,128)(2,1)S(1)} %get-tuple-element.37.pre, bf16[128,256]{1,0:T(8,128)(2,1)S(1)} %get-tuple-element.38.act, ...), custom_call_target="tpu_custom_call" | custom-call | flops 603979776 | bytes 16777216 | tf_op jit(solution)/shard_map/pallas_call | solution.py:211
  71.7 9.7 %all-to-all-start = ((bf16[32,48,512]{2,1,0:T(8,128)(2,1)}), bf16[32,48,512]{2,1,0:T(8,128)(2,1)S(1)}, u32[]{:S(2)}, u32[]{:S(2)}) async-start(bf16[32,48,512]{2,1,0:T(8,128)(2,1)} %bitcast.6), calls=%async_computation | async-start | bytes 3145728 | tf_op jit(solution)/shard_map/all_to_all | solution.py:335
  83.3 2.2 %collective-permute-start.16 = (bf16[128,1152]{1,0:T(8,128)(2,1)S(1)}, bf16[128,1152]{1,0:T(8,128)(2,1)S(1)}, u32[]{:S(2)}, u32[]{:S(2)}) collective-permute-start(bf16[128,1152]{1,0:T(8,128)(2,1)S(1)} %get-tuple-element.48), channel_id=1, source_target_pairs={{2,0},{15,1},{4,2},{1,3},{6,4},{3,5},{8,6},{5,7},{10,8},{7,9},{12,... | collective-permute-start | bytes 884744 | tf_op jit(solution)/shard_map/ppermute | solution.py:276
  85.5 4.8 %collective-permute-done.12.p = bf16[128,1152]{1,0:T(8,128)(2,1)S(1)} collective-permute-done((bf16[128,1152]{1,0:T(8,128)(2,1)S(1)}, bf16[128,1152]{1,0:T(8,128)(2,1)S(1)}, u32[]{:S(2)}, u32[]{:S(2)}) %collective-permute-start.12) | collective-permute-done | bytes 294944 | tf_op jit(solution)/shard_map/ppermute | solution.py:276
  93.6 2.1 %collective-permute-start.17 = (bf16[128,1152]{1,0:T(8,128)(2,1)S(1)}, bf16[128,1152]{1,0:T(8,128)(2,1)S(1)}, u32[]{:S(2)}, u32[]{:S(2)}) collective-permute-start(bf16[128,1152]{1,0:T(8,128)(2,1)S(1)} %shard_map.120), channel_id=1, source_target_pairs={{2,0},{15,1},{4,2},{1,3},{6,4},{3,5},{8,6},{5,7},{10,8},{7,9},{12,... | collective-permute-start | bytes 884744 | tf_op jit(solution)/shard_map/ppermute | solution.py:276
  95.7 3.7 %collective-permute-done.13.p = bf16[128,1152]{1,0:T(8,128)(2,1)S(1)} collective-permute-done((bf16[128,1152]{1,0:T(8,128)(2,1)S(1)}, bf16[128,1152]{1,0:T(8,128)(2,1)S(1)}, u32[]{:S(2)}, u32[]{:S(2)}) %collective-permute-start.13) | collective-permute-done | bytes 294944 | tf_op jit(solution)/shard_map/ppermute | solution.py:276
  102.8 2.6 %collective-permute-start.18 = (bf16[128,1152]{1,0:T(8,128)(2,1)S(1)}, bf16[128,1152]{1,0:T(8,128)(2,1)S(1)}, u32[]{:S(2)}, u32[]{:S(2)}) collective-permute-start(bf16[128,1152]{1,0:T(8,128)(2,1)S(1)} %shard_map.121), channel_id=1, source_target_pairs={{15,0},{2,1},{1,2},{4,3},{3,4},{6,5},{5,6},{8,7},{7,8},{10,9},{9,1... | collective-permute-start | bytes 884744 | tf_op jit(solution)/shard_map/ppermute | solution.py:276
  105.5 3.0 %collective-permute-done.14.p = bf16[128,1152]{1,0:T(8,128)(2,1)S(1)} collective-permute-done((bf16[128,1152]{1,0:T(8,128)(2,1)S(1)}, bf16[128,1152]{1,0:T(8,128)(2,1)S(1)}, u32[]{:S(2)}, u32[]{:S(2)}) %collective-permute-start.14) | collective-permute-done | bytes 294944 | tf_op jit(solution)/shard_map/ppermute | solution.py:276
  111.3 6.2 %collective-permute-done.15.p = bf16[128,1152]{1,0:T(8,128)(2,1)S(1)} collective-permute-done((bf16[128,1152]{1,0:T(8,128)(2,1)S(1)}, bf16[128,1152]{1,0:T(8,128)(2,1)S(1)}, u32[]{:S(2)}, u32[]{:S(2)}) %collective-permute-start.15) | collective-permute-done | bytes 294944 | tf_op jit(solution)/shard_map/ppermute | solution.py:276
  (57 shorter events, 25.6 us)
Async XLA Ops:
  2.6 21.4 %collective-permute-start = (bf16[128,2176]{1,0:T(8,128)(2,1)}, bf16[128,2176]{1,0:T(8,128)(2,1)}, u32[]{:S(2)}, u32[]{:S(2)}) collective-permute-start(bf16[128,2176]{1,0:T(8,128)(2,1)} %shard_map.110.refs_0_), channel_id=1, source_target_pairs={{0,2},{1,15},{2,4},{3,1},{4,6},{5,3},{6,8},{7,5},{8,10},{9,7},{10,... | collective-permute-start | bytes 1671176 | tf_op jit(solution)/shard_map/ppermute | solution.py:276
  14.1 14.9 %collective-permute-start.6 = (bf16[128,2176]{1,0:T(8,128)(2,1)}, bf16[128,2176]{1,0:T(8,128)(2,1)S(1)}, u32[]{:S(2)}, u32[]{:S(2)}) collective-permute-start(bf16[128,2176]{1,0:T(8,128)(2,1)} %shard_map.110.refs_0_), channel_id=1, source_target_pairs={{0,15},{1,2},{2,1},{3,4},{4,3},{5,6},{6,5},{7,8},{8,7},{9,10},{10,... | collective-permute-start | bytes 1671176 | tf_op jit(solution)/shard_map/ppermute | solution.py:276
  16.0 15.7 %collective-permute-start.2 = (bf16[1024,256]{1,0:T(8,128)(2,1)}, bf16[1024,256]{1,0:T(8,128)(2,1)S(1)}, u32[]{:S(2)}, u32[]{:S(2)}) collective-permute-start(bf16[1024,256]{1,0:T(8,128)(2,1)} %bitcast.8), channel_id=1, source_target_pairs={{0,1},{1,0},{2,3},{3,2},{4,5},{5,4},{6,7},{7,6},{8,9},{9,8},{10,11... | collective-permute-start | bytes 1572872 | tf_op jit(solution)/shard_map/ppermute | solution.py:276
  18.6 13.2 %collective-permute-start.3 = (bf16[1024,256]{1,0:T(8,128)(2,1)}, bf16[1024,256]{1,0:T(8,128)(2,1)S(1)}, u32[]{:S(2)}, u32[]{:S(2)}) collective-permute-start(bf16[1024,256]{1,0:T(8,128)(2,1)} %bitcast.15), channel_id=1, source_target_pairs={{0,1},{1,0},{2,3},{3,2},{4,5},{5,4},{6,7},{7,6},{8,9},{9,8},{10,11... | collective-permute-start | bytes 1572872 | tf_op jit(solution)/shard_map/ppermute | solution.py:276
  20.5 11.3 %collective-permute-start.4 = (bf16[256,1024]{1,0:T(8,128)(2,1)}, bf16[256,1024]{1,0:T(8,128)(2,1)S(1)}, u32[]{:S(2)}, u32[]{:S(2)}) collective-permute-start(bf16[256,1024]{1,0:T(8,128)(2,1)} %bitcast.22), channel_id=1, source_target_pairs={{0,1},{1,0},{2,3},{3,2},{4,5},{5,4},{6,7},{7,6},{8,9},{9,8},{10,11... | collective-permute-start | bytes 1572872 | tf_op jit(solution)/shard_map/ppermute | solution.py:276
  24.0 16.0 %collective-permute-start.1 = (bf16[128,2176]{1,0:T(8,128)(2,1)}, bf16[128,2176]{1,0:T(8,128)(2,1)S(1)}, u32[]{:S(2)}, u32[]{:S(2)}) collective-permute-start(bf16[128,2176]{1,0:T(8,128)(2,1)} %collective-permute-done.refs_1_), channel_id=1, source_target_pairs={{0,2},{1,15},{2,4},{3,1},{4,6},{5,3},{6,8},{7,5},{8,10},{9,7},{10,... | collective-permute-start | bytes 1671176 | tf_op jit(solution)/shard_map/ppermute | solution.py:276
  29.0 12.9 %collective-permute-start.9 = (bf16[128,2176]{1,0:T(8,128)(2,1)S(1)}, bf16[128,2176]{1,0:T(8,128)(2,1)S(1)}, u32[]{:S(2)}, u32[]{:S(2)}) collective-permute-start(bf16[128,2176]{1,0:T(8,128)(2,1)S(1)} %collective-permute-done.6.refs_0_), channel_id=1, source_target_pairs={{0,2},{1,15},{2,4},{3,1},{4,6},{5,3},{6,8},{7,5},{8,10},{9,7},{10,... | collective-permute-start | bytes 1671176 | tf_op jit(solution)/shard_map/ppermute | solution.py:276
  36.0 10.7 %copy-start.1 = (bf16[1,1024,256]{2,1,0:T(8,128)(2,1)S(1)}, bf16[1,1024,256]{2,1,0:T(8,128)(2,1)}, u32[]{:S(2)}) copy-start(bf16[1,1024,256]{2,1,0:T(8,128)(2,1)} %param.11) | copy-start | bytes 1572868
  36.0 10.7 %copy-start.3 = (bf16[1,1024,256]{2,1,0:T(8,128)(2,1)S(1)}, bf16[1,1024,256]{2,1,0:T(8,128)(2,1)}, u32[]{:S(2)}) copy-start(bf16[1,1024,256]{2,1,0:T(8,128)(2,1)} %param.12) | copy-start | bytes 1572868
  36.0 10.7 %copy-start.5 = (bf16[1,256,1024]{2,1,0:T(8,128)(2,1)S(1)}, bf16[1,256,1024]{2,1,0:T(8,128)(2,1)}, u32[]{:S(2)}) copy-start(bf16[1,256,1024]{2,1,0:T(8,128)(2,1)} %param.13) | copy-start | bytes 1572868
  40.0 11.2 %collective-permute-start.5 = (bf16[128,2176]{1,0:T(8,128)(2,1)S(1)}, bf16[128,2176]{1,0:T(8,128)(2,1)S(1)}, u32[]{:S(2)}, u32[]{:S(2)}) collective-permute-start(bf16[128,2176]{1,0:T(8,128)(2,1)S(1)} %collective-permute-done.1.refs_1_), channel_id=1, source_target_pairs={{0,2},{1,15},{2,4},{3,1},{4,6},{5,3},{6,8},{7,5},{8,10},{9,7},{10,... | collective-permute-start | bytes 1671176 | tf_op jit(solution)/shard_map/ppermute | solution.py:276
  41.9 15.5 %collective-permute-start.10 = (bf16[128,2176]{1,0:T(8,128)(2,1)S(1)}, bf16[128,2176]{1,0:T(8,128)(2,1)S(1)}, u32[]{:S(2)}, u32[]{:S(2)}) collective-permute-start(bf16[128,2176]{1,0:T(8,128)(2,1)S(1)} %collective-permute-done.9.refs_0_), channel_id=1, source_target_pairs={{0,2},{1,15},{2,4},{3,1},{4,6},{5,3},{6,8},{7,5},{8,10},{9,7},{10,... | collective-permute-start | bytes 1671176 | tf_op jit(solution)/shard_map/ppermute | solution.py:276
  51.2 12.1 %collective-permute-start.7 = (bf16[128,2176]{1,0:T(8,128)(2,1)S(1)}, bf16[128,2176]{1,0:T(8,128)(2,1)S(1)}, u32[]{:S(2)}, u32[]{:S(2)}) collective-permute-start(bf16[128,2176]{1,0:T(8,128)(2,1)S(1)} %collective-permute-done.5.refs_1_), channel_id=1, source_target_pairs={{0,2},{1,15},{2,4},{3,1},{4,6},{5,3},{6,8},{7,5},{8,10},{9,7},{10,... | collective-permute-start | bytes 1671176 | tf_op jit(solution)/shard_map/ppermute | solution.py:276
  59.9 9.6 %collective-permute-start.11 = (bf16[1,32,48,512]{3,2,1,0:T(8,128)(2,1)S(1)}, bf16[1,32,48,512]{3,2,1,0:T(8,128)(2,1)S(1)}, u32[]{:S(2)}, u32[]{:S(2)}) collective-permute-start(bf16[1,32,48,512]{3,2,1,0:T(8,128)(2,1)S(1)} %get-tuple-element.45), channel_id=1, source_target_pairs={{0,1},{1,0},{2,3},{3,2},{4,5},{5,4},{6,7},{7,6},{8,9},{9,8},{10,11... | collective-permute-start | bytes 4718600 | tf_op jit(solution)/shard_map/ppermute | solution.py:276
  63.3 6.2 %collective-permute-start.8 = (bf16[128,2176]{1,0:T(8,128)(2,1)S(1)}, bf16[128,2176]{1,0:T(8,128)(2,1)S(1)}, u32[]{:S(2)}, u32[]{:S(2)}) collective-permute-start(bf16[128,2176]{1,0:T(8,128)(2,1)S(1)} %collective-permute-done.7.block), channel_id=1, source_target_pairs={{0,1},{1,0},{2,3},{3,2},{4,5},{5,4},{6,7},{7,6},{8,9},{9,8},{10,11... | collective-permute-start | bytes 1671176 | tf_op jit(solution)/shard_map/ppermute | solution.py:276
  71.7 47.2 %all-to-all-start = ((bf16[32,48,512]{2,1,0:T(8,128)(2,1)}), bf16[32,48,512]{2,1,0:T(8,128)(2,1)S(1)}, u32[]{:S(2)}, u32[]{:S(2)}) async-start(bf16[32,48,512]{2,1,0:T(8,128)(2,1)} %bitcast.6), calls=%async_computation | async-start | bytes 3145728 | tf_op jit(solution)/shard_map/all_to_all | solution.py:335
  81.4 9.0 %collective-permute-start.12 = (bf16[128,1152]{1,0:T(8,128)(2,1)S(1)}, bf16[128,1152]{1,0:T(8,128)(2,1)S(1)}, u32[]{:S(2)}, u32[]{:S(2)}) collective-permute-start(bf16[128,1152]{1,0:T(8,128)(2,1)S(1)} %get-tuple-element.46), channel_id=1, source_target_pairs={{2,0},{15,1},{4,2},{1,3},{6,4},{3,5},{8,6},{5,7},{10,8},{7,9},{12,... | collective-permute-start | bytes 884744 | tf_op jit(solution)/shard_map/ppermute | solution.py:276
  83.3 10.2 %collective-permute-start.16 = (bf16[128,1152]{1,0:T(8,128)(2,1)S(1)}, bf16[128,1152]{1,0:T(8,128)(2,1)S(1)}, u32[]{:S(2)}, u32[]{:S(2)}) collective-permute-start(bf16[128,1152]{1,0:T(8,128)(2,1)S(1)} %get-tuple-element.48), channel_id=1, source_target_pairs={{2,0},{15,1},{4,2},{1,3},{6,4},{3,5},{8,6},{5,7},{10,8},{7,9},{12,... | collective-permute-start | bytes 884744 | tf_op jit(solution)/shard_map/ppermute | solution.py:276
  90.4 9.0 %collective-permute-start.13 = (bf16[128,1152]{1,0:T(8,128)(2,1)S(1)}, bf16[128,1152]{1,0:T(8,128)(2,1)S(1)}, u32[]{:S(2)}, u32[]{:S(2)}) collective-permute-start(bf16[128,1152]{1,0:T(8,128)(2,1)S(1)} %shard_map.117), channel_id=1, source_target_pairs={{2,0},{15,1},{4,2},{1,3},{6,4},{3,5},{8,6},{5,7},{10,8},{7,9},{12,... | collective-permute-start | bytes 884744 | tf_op jit(solution)/shard_map/ppermute | solution.py:276
  93.6 9.1 %collective-permute-start.17 = (bf16[128,1152]{1,0:T(8,128)(2,1)S(1)}, bf16[128,1152]{1,0:T(8,128)(2,1)S(1)}, u32[]{:S(2)}, u32[]{:S(2)}) collective-permute-start(bf16[128,1152]{1,0:T(8,128)(2,1)S(1)} %shard_map.120), channel_id=1, source_target_pairs={{2,0},{15,1},{4,2},{1,3},{6,4},{3,5},{8,6},{5,7},{10,8},{7,9},{12,... | collective-permute-start | bytes 884744 | tf_op jit(solution)/shard_map/ppermute | solution.py:276
  99.5 9.0 %collective-permute-start.14 = (bf16[128,1152]{1,0:T(8,128)(2,1)S(1)}, bf16[128,1152]{1,0:T(8,128)(2,1)S(1)}, u32[]{:S(2)}, u32[]{:S(2)}) collective-permute-start(bf16[128,1152]{1,0:T(8,128)(2,1)S(1)} %shard_map.118), channel_id=1, source_target_pairs={{2,0},{15,1},{4,2},{1,3},{6,4},{3,5},{8,6},{5,7},{10,8},{7,9},{12,... | collective-permute-start | bytes 884744 | tf_op jit(solution)/shard_map/ppermute | solution.py:276
  102.8 16.1 %copy-start.7 = (s32[128,10]{0,1:T(8,128)S(1)}, s32[128,10]{0,1:T(8,128)}, u32[]{:S(2)}) copy-start(s32[128,10]{0,1:T(8,128)} %param.9) | copy-start | bytes 15364
  102.8 8.5 %collective-permute-start.18 = (bf16[128,1152]{1,0:T(8,128)(2,1)S(1)}, bf16[128,1152]{1,0:T(8,128)(2,1)S(1)}, u32[]{:S(2)}, u32[]{:S(2)}) collective-permute-start(bf16[128,1152]{1,0:T(8,128)(2,1)S(1)} %shard_map.121), channel_id=1, source_target_pairs={{15,0},{2,1},{1,2},{4,3},{3,4},{6,5},{5,6},{8,7},{7,8},{10,9},{9,1... | collective-permute-start | bytes 884744 | tf_op jit(solution)/shard_map/ppermute | solution.py:276
  108.6 9.0 %collective-permute-start.15 = (bf16[128,1152]{1,0:T(8,128)(2,1)S(1)}, bf16[128,1152]{1,0:T(8,128)(2,1)S(1)}, u32[]{:S(2)}, u32[]{:S(2)}) collective-permute-start(bf16[128,1152]{1,0:T(8,128)(2,1)S(1)} %shard_map.119), channel_id=1, source_target_pairs={{2,0},{15,1},{4,2},{1,3},{6,4},{3,5},{8,6},{5,7},{10,8},{7,9},{12,... | collective-permute-start | bytes 884744 | tf_op jit(solution)/shard_map/ppermute | solution.py:276
  (10 other events, 42.3 us)

commit v12 on v11

--- a/solution.py
+++ b/solution.py
@@ -184,13 +184,15 @@
     gated = jnp.concatenate([act[...], gated], axis=0)
     nx, ny, rows, wide = out.shape
     n = rows * 2 // 3
-    step = max(nx * n, 2 * hidden)
+    step = max(nx * n, hidden)
     copies = []
 
     def leave(*where):
         copies.append(pltpu.make_async_copy(made.at[where], out.at[where], sems.at[len(copies)]))
         copies[-1].start()
 
+    down_to_parts([made], dot(gated, dy, 0, 0) + acc_d[...], early)
+    leave(slice(None), slice(None), pl.ds(n, rows - n))
     for r in range(0, width, step):
         y, ys = r // (nx * n), step // (nx * n)
         partner = [jnp.stack([e[p, y : y + ys, :n, :] for p in range(nx)], axis=1) for e in early]
@@ -198,8 +200,6 @@
         d_gu = dot(x[:, r : r + step], grads, 0, 0) + acc_gu[r : r + step, :]
         to_parts([made], d_gu + partner.reshape(step, wide).astype(F32), r)
         leave(slice(None), pl.ds(y, ys), pl.ds(0, n))
-    down_to_parts([made], dot(gated, dy, 0, 0) + acc_d[...], early)
-    leave(slice(None), slice(None), pl.ds(n, rows - n))
     for copy in copies:
         copy.wait()
 

time: 122 us -> 122 us (level)
  no operation moved by 1% of the time
where the time goes in v12:
time: 122 us; the launch traced here: 120 us
  starting transfers between devices  68.8 us (56%)
  waiting for transfers between devices  23.5 us (19%)
  Pallas kernels  21.6 us (18%)
  local copies, waits for them, and re-layouts  4.91 us (4%)
    ppermute x19, starting transfers between devices, send(): return lax.ppermute(a, 'expert', pairs)  59.2 us
    ppermute x19, waiting for transfers between devices, send(): return lax.ppermute(a, 'expert', pairs)  22.2 us
    pallas_call x6, Pallas kernels, call(): pl.pallas_call(kernel, out_shape=out_shape, in_specs=[pl.BlockSpec(memory...  18.1 us
    all_to_all x1, starting transfers between devices, on_device(): lax.all_to_all(parts[0], 'dp', split_axis=0, concat_axis=0, tiled=True)  9.68 us
    unnamed x28, local copies, waits for them, and re-layouts  4.91 us
  transfers between devices with their start and end apart: 20, of which 9 were waited for; matrix products, arithmetic and copies ran while one was open for 0% of the time, Pallas kernels for 14%

profile of v12, /device:TPU:1, one launch (start us, length us, event | category | flops | bytes accessed | tf_op | source)
XLA Modules:
  0.0 119.9 jit_solution(12778954476515640015)
XLA Ops:
  0.6 1.9 %shard_map.110.refs_0_ = bf16[128,2176]{1,0:T(8,128)(2,1)} custom-call(s32[10,128]{1,0:T(8,128)} %bitcast.29, bf16[10,128]{1,0:T(8,128)(2,1)} %bitcast.31, bf16[128,1024]{1,0:T(8,128)(2,1)} %tokens.1, bf16[128,1024]{1,0:T(8,128)(2,1)} %cotangent.1), custom_call_target="tpu_custom_call" | custom-call | tf_op jit(solution)/shard_map/pallas_call | solution.py:279
  2.6 11.5 %collective-permute-start = (bf16[128,2176]{1,0:T(8,128)(2,1)}, bf16[128,2176]{1,0:T(8,128)(2,1)}, u32[]{:S(2)}, u32[]{:S(2)}) collective-permute-start(bf16[128,2176]{1,0:T(8,128)(2,1)} %shard_map.110.refs_0_), channel_id=1, source_target_pairs={{0,2},{1,15},{2,4},{3,1},{4,6},{5,3},{6,8},{7,5},{8,10},{9,7},{10,... | collective-permute-start | bytes 1671176 | tf_op jit(solution)/shard_map/ppermute | solution.py:276
  16.0 2.6 %collective-permute-start.2 = (bf16[1024,256]{1,0:T(8,128)(2,1)}, bf16[1024,256]{1,0:T(8,128)(2,1)S(1)}, u32[]{:S(2)}, u32[]{:S(2)}) collective-permute-start(bf16[1024,256]{1,0:T(8,128)(2,1)} %bitcast.8), channel_id=1, source_target_pairs={{0,1},{1,0},{2,3},{3,2},{4,5},{5,4},{6,7},{7,6},{8,9},{9,8},{10,11... | collective-permute-start | bytes 1572872 | tf_op jit(solution)/shard_map/ppermute | solution.py:276
  20.5 2.4 %collective-permute-start.4 = (bf16[256,1024]{1,0:T(8,128)(2,1)}, bf16[256,1024]{1,0:T(8,128)(2,1)S(1)}, u32[]{:S(2)}, u32[]{:S(2)}) collective-permute-start(bf16[256,1024]{1,0:T(8,128)(2,1)} %bitcast.22), channel_id=1, source_target_pairs={{0,1},{1,0},{2,3},{3,2},{4,5},{5,4},{6,7},{7,6},{8,9},{9,8},{10,11... | collective-permute-start | bytes 1572872 | tf_op jit(solution)/shard_map/ppermute | solution.py:276
  24.0 5.0 %collective-permute-start.1 = (bf16[128,2176]{1,0:T(8,128)(2,1)}, bf16[128,2176]{1,0:T(8,128)(2,1)S(1)}, u32[]{:S(2)}, u32[]{:S(2)}) collective-permute-start(bf16[128,2176]{1,0:T(8,128)(2,1)} %collective-permute-done.refs_1_), channel_id=1, source_target_pairs={{0,2},{1,15},{2,4},{3,1},{4,6},{5,3},{6,8},{7,5},{8,10},{9,7},{10,... | collective-permute-start | bytes 1671176 | tf_op jit(solution)/shard_map/ppermute | solution.py:276
  29.0 2.7 %collective-permute-start.9 = (bf16[128,2176]{1,0:T(8,128)(2,1)S(1)}, bf16[128,2176]{1,0:T(8,128)(2,1)S(1)}, u32[]{:S(2)}, u32[]{:S(2)}) collective-permute-start(bf16[128,2176]{1,0:T(8,128)(2,1)S(1)} %collective-permute-done.6.refs_0_), channel_id=1, source_target_pairs={{0,2},{1,15},{2,4},{3,1},{4,6},{5,3},{6,8},{7,5},{8,10},{9,7},{10,... | collective-permute-start | bytes 1671176 | tf_op jit(solution)/shard_map/ppermute | solution.py:276
  36.0 4.0 %shard_map.111 = (bf16[128,1152]{1,0:T(8,128)(2,1)S(1)}, bf16[128,1152]{1,0:T(8,128)(2,1)S(1)}, f32[1024,1024]{1,0:T(8,128)S(1)}, f32[512,1024]{1,0:T(8,128)S(1)}) custom-call(s32[1]{0:T(128)} %bitcast.expert_ref, bf16[128,2176]{1,0:T(8,128)(2,1)S(1)} %copy-done.6, bf16[128,2176]{1,0:T(8,128)(2,1)} %collective-permute-done.refs_1_, ...), custom_call_target="tpu_custom_call" | custom-call | flops 2147483648 | bytes 16777216 | tf_op jit(solution)/shard_map/pallas_call | solution.py:211
  41.9 4.8 %collective-permute-start.10 = (bf16[128,2176]{1,0:T(8,128)(2,1)S(1)}, bf16[128,2176]{1,0:T(8,128)(2,1)S(1)}, u32[]{:S(2)}, u32[]{:S(2)}) collective-permute-start(bf16[128,2176]{1,0:T(8,128)(2,1)S(1)} %collective-permute-done.9.refs_0_), channel_id=1, source_target_pairs={{0,2},{1,15},{2,4},{3,1},{4,6},{5,3},{6,8},{7,5},{8,10},{9,7},{10,... | collective-permute-start | bytes 1671176 | tf_op jit(solution)/shard_map/ppermute | solution.py:276
  46.7 3.8 %shard_map.112 = (bf16[128,1152]{1,0:T(8,128)(2,1)S(1)}, bf16[128,1152]{1,0:T(8,128)(2,1)S(1)}, f32[1024,1024]{1,0:T(8,128)S(1)}, f32[512,1024]{1,0:T(8,128)S(1)}) custom-call(s32[1]{0:T(128)} %bitcast.expert_ref, bf16[128,2176]{1,0:T(8,128)(2,1)S(1)} %collective-permute-done.6.refs_0_, ...), custom_call_target="tpu_custom_call", output_to_operand_aliasing={{2}: (9, {}), {3}: (10, {})} | custom-call | flops 2147483648 | bytes 16777216 | tf_op jit(solution)/shard_map/pallas_call | solution.py:211
  51.2 2.3 %collective-permute-start.7 = (bf16[128,2176]{1,0:T(8,128)(2,1)S(1)}, bf16[128,2176]{1,0:T(8,128)(2,1)S(1)}, u32[]{:S(2)}, u32[]{:S(2)}) collective-permute-start(bf16[128,2176]{1,0:T(8,128)(2,1)S(1)} %collective-permute-done.5.refs_1_), channel_id=1, source_target_pairs={{0,2},{1,15},{2,4},{3,1},{4,6},{5,3},{6,8},{7,5},{8,10},{9,7},{10,... | collective-permute-start | bytes 1671176 | tf_op jit(solution)/shard_map/ppermute | solution.py:276
  53.5 3.8 %shard_map.114 = (bf16[128,1152]{1,0:T(8,128)(2,1)S(1)}, bf16[128,1152]{1,0:T(8,128)(2,1)S(1)}, f32[1024,1024]{1,0:T(8,128)S(1)}, f32[512,1024]{1,0:T(8,128)S(1)}) custom-call(s32[1]{0:T(128)} %bitcast.expert_ref, bf16[128,2176]{1,0:T(8,128)(2,1)S(1)} %collective-permute-done.9.refs_0_, ...), custom_call_target="tpu_custom_call", output_to_operand_aliasing={{2}: (9, {}), {3}: (10, {})} | custom-call | flops 2147483648 | bytes 16777216 | tf_op jit(solution)/shard_map/pallas_call | solution.py:211
  57.4 2.5 %shard_map.115 = (bf16[128,1152]{1,0:T(8,128)(2,1)S(1)}, f32[1024,512]{1,0:T(8,128)S(1)}, f32[256,1024]{1,0:T(8,128)S(1)}, bf16[1,32,48,512]{3,2,1,0:T(8,128)(2,1)S(1)}) custom-call(s32[1]{0:T(128)} %bitcast.expert_ref, bf16[128,2176]{1,0:T(8,128)(2,1)S(1)} %collective-permute-done.10.refs_0_, bf16[1024,256]{1,0:T(8,128)(2,1)S(1)} %bitcast.12, ...), custom_call_target="tpu_custom_call" | custom-call | flops 1073741824 | bytes 16777216 | tf_op jit(solution)/shard_map/pallas_call | solution.py:211
  59.9 3.4 %collective-permute-start.11 = (bf16[1,32,48,512]{3,2,1,0:T(8,128)(2,1)S(1)}, bf16[1,32,48,512]{3,2,1,0:T(8,128)(2,1)S(1)}, u32[]{:S(2)}, u32[]{:S(2)}) collective-permute-start(bf16[1,32,48,512]{3,2,1,0:T(8,128)(2,1)S(1)} %get-tuple-element.45), channel_id=1, source_target_pairs={{0,1},{1,0},{2,3},{3,2},{4,5},{5,4},{6,7},{7,6},{8,9},{9,8},{10,11... | collective-permute-start | bytes 4718600 | tf_op jit(solution)/shard_map/ppermute | solution.py:276
  63.3 4.1 %collective-permute-start.8 = (bf16[128,2176]{1,0:T(8,128)(2,1)S(1)}, bf16[128,2176]{1,0:T(8,128)(2,1)S(1)}, u32[]{:S(2)}, u32[]{:S(2)}) collective-permute-start(bf16[128,2176]{1,0:T(8,128)(2,1)S(1)} %collective-permute-done.7.block), channel_id=1, source_target_pairs={{0,1},{1,0},{2,3},{3,2},{4,5},{5,4},{6,7},{7,6},{8,9},{9,8},{10,11... | collective-permute-start | bytes 1671176 | tf_op jit(solution)/shard_map/ppermute | solution.py:276
  67.4 2.0 %shard_map.113 = (bf16[128,1152]{1,0:T(8,128)(2,1)S(1)}, bf16[128,512]{1,0:T(8,128)(2,1)S(1)}, bf16[128,256]{1,0:T(8,128)(2,1)S(1)}) custom-call(s32[1]{0:T(128)} %bitcast.expert_ref, bf16[128,2176]{1,0:T(8,128)(2,1)S(1)} %collective-permute-done.7.block, bf16[1024,256]{1,0:T(8,128)(2,1)S(1)} %bitcast.13, bf16[1024,256]{1,0:T(8,128)(2,1)S(1)} %bitcast.20, ...), custom_call_target="tpu_custom_call" | custom-call | flops 15000000512 | bytes 16777216 | tf_op jit(solution)/shard_map/pallas_call | solution.py:211
  69.5 2.1 %shard_map.116 = bf16[1,32,48,512]{3,2,1,0:T(8,128)(2,1)} custom-call(s32[1]{0:T(128)} %bitcast.expert_ref, bf16[128,2176]{1,0:T(8,128)(2,1)S(1)} %collective-permute-done.7.block, bf16[128,512]{1,0:T(8,128)(2,1)S(1)} %get-tuple-element.37.pre, bf16[128,256]{1,0:T(8,128)(2,1)S(1)} %get-tuple-element.38.act, ...), custom_call_target="tpu_custom_call" | custom-call | flops 603979776 | bytes 16777216 | tf_op jit(solution)/shard_map/pallas_call | solution.py:211
  71.5 9.7 %all-to-all-start = ((bf16[32,48,512]{2,1,0:T(8,128)(2,1)}), bf16[32,48,512]{2,1,0:T(8,128)(2,1)S(1)}, u32[]{:S(2)}, u32[]{:S(2)}) async-start(bf16[32,48,512]{2,1,0:T(8,128)(2,1)} %bitcast.6), calls=%async_computation | async-start | bytes 3145728 | tf_op jit(solution)/shard_map/all_to_all | solution.py:335
  83.2 2.2 %collective-permute-start.16 = (bf16[128,1152]{1,0:T(8,128)(2,1)S(1)}, bf16[128,1152]{1,0:T(8,128)(2,1)S(1)}, u32[]{:S(2)}, u32[]{:S(2)}) collective-permute-start(bf16[128,1152]{1,0:T(8,128)(2,1)S(1)} %get-tuple-element.48), channel_id=1, source_target_pairs={{2,0},{15,1},{4,2},{1,3},{6,4},{3,5},{8,6},{5,7},{10,8},{7,9},{12,... | collective-permute-start | bytes 884744 | tf_op jit(solution)/shard_map/ppermute | solution.py:276
  85.4 4.8 %collective-permute-done.12.p = bf16[128,1152]{1,0:T(8,128)(2,1)S(1)} collective-permute-done((bf16[128,1152]{1,0:T(8,128)(2,1)S(1)}, bf16[128,1152]{1,0:T(8,128)(2,1)S(1)}, u32[]{:S(2)}, u32[]{:S(2)}) %collective-permute-start.12) | collective-permute-done | bytes 294944 | tf_op jit(solution)/shard_map/ppermute | solution.py:276
  93.4 2.1 %collective-permute-start.17 = (bf16[128,1152]{1,0:T(8,128)(2,1)S(1)}, bf16[128,1152]{1,0:T(8,128)(2,1)S(1)}, u32[]{:S(2)}, u32[]{:S(2)}) collective-permute-start(bf16[128,1152]{1,0:T(8,128)(2,1)S(1)} %shard_map.120), channel_id=1, source_target_pairs={{2,0},{15,1},{4,2},{1,3},{6,4},{3,5},{8,6},{5,7},{10,8},{7,9},{12,... | collective-permute-start | bytes 884744 | tf_op jit(solution)/shard_map/ppermute | solution.py:276
  95.5 3.7 %collective-permute-done.13.p = bf16[128,1152]{1,0:T(8,128)(2,1)S(1)} collective-permute-done((bf16[128,1152]{1,0:T(8,128)(2,1)S(1)}, bf16[128,1152]{1,0:T(8,128)(2,1)S(1)}, u32[]{:S(2)}, u32[]{:S(2)}) %collective-permute-start.13) | collective-permute-done | bytes 294944 | tf_op jit(solution)/shard_map/ppermute | solution.py:276
  102.6 2.6 %collective-permute-start.18 = (bf16[128,1152]{1,0:T(8,128)(2,1)S(1)}, bf16[128,1152]{1,0:T(8,128)(2,1)S(1)}, u32[]{:S(2)}, u32[]{:S(2)}) collective-permute-start(bf16[128,1152]{1,0:T(8,128)(2,1)S(1)} %shard_map.121), channel_id=1, source_target_pairs={{15,0},{2,1},{1,2},{4,3},{3,4},{6,5},{5,6},{8,7},{7,8},{10,9},{9,1... | collective-permute-start | bytes 884744 | tf_op jit(solution)/shard_map/ppermute | solution.py:276
  105.3 3.0 %collective-permute-done.14.p = bf16[128,1152]{1,0:T(8,128)(2,1)S(1)} collective-permute-done((bf16[128,1152]{1,0:T(8,128)(2,1)S(1)}, bf16[128,1152]{1,0:T(8,128)(2,1)S(1)}, u32[]{:S(2)}, u32[]{:S(2)}) %collective-permute-start.14) | collective-permute-done | bytes 294944 | tf_op jit(solution)/shard_map/ppermute | solution.py:276
  111.1 6.2 %collective-permute-done.15.p = bf16[128,1152]{1,0:T(8,128)(2,1)S(1)} collective-permute-done((bf16[128,1152]{1,0:T(8,128)(2,1)S(1)}, bf16[128,1152]{1,0:T(8,128)(2,1)S(1)}, u32[]{:S(2)}, u32[]{:S(2)}) %collective-permute-start.15) | collective-permute-done | bytes 294944 | tf_op jit(solution)/shard_map/ppermute | solution.py:276
  (57 shorter events, 25.6 us)
Async XLA Ops:
  2.6 21.4 %collective-permute-start = (bf16[128,2176]{1,0:T(8,128)(2,1)}, bf16[128,2176]{1,0:T(8,128)(2,1)}, u32[]{:S(2)}, u32[]{:S(2)}) collective-permute-start(bf16[128,2176]{1,0:T(8,128)(2,1)} %shard_map.110.refs_0_), channel_id=1, source_target_pairs={{0,2},{1,15},{2,4},{3,1},{4,6},{5,3},{6,8},{7,5},{8,10},{9,7},{10,... | collective-permute-start | bytes 1671176 | tf_op jit(solution)/shard_map/ppermute | solution.py:276
  14.1 14.9 %collective-permute-start.6 = (bf16[128,2176]{1,0:T(8,128)(2,1)}, bf16[128,2176]{1,0:T(8,128)(2,1)S(1)}, u32[]{:S(2)}, u32[]{:S(2)}) collective-permute-start(bf16[128,2176]{1,0:T(8,128)(2,1)} %shard_map.110.refs_0_), channel_id=1, source_target_pairs={{0,15},{1,2},{2,1},{3,4},{4,3},{5,6},{6,5},{7,8},{8,7},{9,10},{10,... | collective-permute-start | bytes 1671176 | tf_op jit(solution)/shard_map/ppermute | solution.py:276
  16.0 15.7 %collective-permute-start.2 = (bf16[1024,256]{1,0:T(8,128)(2,1)}, bf16[1024,256]{1,0:T(8,128)(2,1)S(1)}, u32[]{:S(2)}, u32[]{:S(2)}) collective-permute-start(bf16[1024,256]{1,0:T(8,128)(2,1)} %bitcast.8), channel_id=1, source_target_pairs={{0,1},{1,0},{2,3},{3,2},{4,5},{5,4},{6,7},{7,6},{8,9},{9,8},{10,11... | collective-permute-start | bytes 1572872 | tf_op jit(solution)/shard_map/ppermute | solution.py:276
  18.6 13.2 %collective-permute-start.3 = (bf16[1024,256]{1,0:T(8,128)(2,1)}, bf16[1024,256]{1,0:T(8,128)(2,1)S(1)}, u32[]{:S(2)}, u32[]{:S(2)}) collective-permute-start(bf16[1024,256]{1,0:T(8,128)(2,1)} %bitcast.15), channel_id=1, source_target_pairs={{0,1},{1,0},{2,3},{3,2},{4,5},{5,4},{6,7},{7,6},{8,9},{9,8},{10,11... | collective-permute-start | bytes 1572872 | tf_op jit(solution)/shard_map/ppermute | solution.py:276
  20.5 11.3 %collective-permute-start.4 = (bf16[256,1024]{1,0:T(8,128)(2,1)}, bf16[256,1024]{1,0:T(8,128)(2,1)S(1)}, u32[]{:S(2)}, u32[]{:S(2)}) collective-permute-start(bf16[256,1024]{1,0:T(8,128)(2,1)} %bitcast.22), channel_id=1, source_target_pairs={{0,1},{1,0},{2,3},{3,2},{4,5},{5,4},{6,7},{7,6},{8,9},{9,8},{10,11... | collective-permute-start | bytes 1572872 | tf_op jit(solution)/shard_map/ppermute | solution.py:276
  24.0 16.0 %collective-permute-start.1 = (bf16[128,2176]{1,0:T(8,128)(2,1)}, bf16[128,2176]{1,0:T(8,128)(2,1)S(1)}, u32[]{:S(2)}, u32[]{:S(2)}) collective-permute-start(bf16[128,2176]{1,0:T(8,128)(2,1)} %collective-permute-done.refs_1_), channel_id=1, source_target_pairs={{0,2},{1,15},{2,4},{3,1},{4,6},{5,3},{6,8},{7,5},{8,10},{9,7},{10,... | collective-permute-start | bytes 1671176 | tf_op jit(solution)/shard_map/ppermute | solution.py:276
  29.0 12.9 %collective-permute-start.9 = (bf16[128,2176]{1,0:T(8,128)(2,1)S(1)}, bf16[128,2176]{1,0:T(8,128)(2,1)S(1)}, u32[]{:S(2)}, u32[]{:S(2)}) collective-permute-start(bf16[128,2176]{1,0:T(8,128)(2,1)S(1)} %collective-permute-done.6.refs_0_), channel_id=1, source_target_pairs={{0,2},{1,15},{2,4},{3,1},{4,6},{5,3},{6,8},{7,5},{8,10},{9,7},{10,... | collective-permute-start | bytes 1671176 | tf_op jit(solution)/shard_map/ppermute | solution.py:276
  36.0 10.7 %copy-start.1 = (bf16[1,1024,256]{2,1,0:T(8,128)(2,1)S(1)}, bf16[1,1024,256]{2,1,0:T(8,128)(2,1)}, u32[]{:S(2)}) copy-start(bf16[1,1024,256]{2,1,0:T(8,128)(2,1)} %param.11) | copy-start | bytes 1572868
  36.0 10.7 %copy-start.3 = (bf16[1,1024,256]{2,1,0:T(8,128)(2,1)S(1)}, bf16[1,1024,256]{2,1,0:T(8,128)(2,1)}, u32[]{:S(2)}) copy-start(bf16[1,1024,256]{2,1,0:T(8,128)(2,1)} %param.12) | copy-start | bytes 1572868
  36.0 10.7 %copy-start.5 = (bf16[1,256,1024]{2,1,0:T(8,128)(2,1)S(1)}, bf16[1,256,1024]{2,1,0:T(8,128)(2,1)}, u32[]{:S(2)}) copy-start(bf16[1,256,1024]{2,1,0:T(8,128)(2,1)} %param.13) | copy-start | bytes 1572868
  40.0 11.2 %collective-permute-start.5 = (bf16[128,2176]{1,0:T(8,128)(2,1)S(1)}, bf16[128,2176]{1,0:T(8,128)(2,1)S(1)}, u32[]{:S(2)}, u32[]{:S(2)}) collective-permute-start(bf16[128,2176]{1,0:T(8,128)(2,1)S(1)} %collective-permute-done.1.refs_1_), channel_id=1, source_target_pairs={{0,2},{1,15},{2,4},{3,1},{4,6},{5,3},{6,8},{7,5},{8,10},{9,7},{10,... | collective-permute-start | bytes 1671176 | tf_op jit(solution)/shard_map/ppermute | solution.py:276
  41.9 15.5 %collective-permute-start.10 = (bf16[128,2176]{1,0:T(8,128)(2,1)S(1)}, bf16[128,2176]{1,0:T(8,128)(2,1)S(1)}, u32[]{:S(2)}, u32[]{:S(2)}) collective-permute-start(bf16[128,2176]{1,0:T(8,128)(2,1)S(1)} %collective-permute-done.9.refs_0_), channel_id=1, source_target_pairs={{0,2},{1,15},{2,4},{3,1},{4,6},{5,3},{6,8},{7,5},{8,10},{9,7},{10,... | collective-permute-start | bytes 1671176 | tf_op jit(solution)/shard_map/ppermute | solution.py:276
  51.2 12.1 %collective-permute-start.7 = (bf16[128,2176]{1,0:T(8,128)(2,1)S(1)}, bf16[128,2176]{1,0:T(8,128)(2,1)S(1)}, u32[]{:S(2)}, u32[]{:S(2)}) collective-permute-start(bf16[128,2176]{1,0:T(8,128)(2,1)S(1)} %collective-permute-done.5.refs_1_), channel_id=1, source_target_pairs={{0,2},{1,15},{2,4},{3,1},{4,6},{5,3},{6,8},{7,5},{8,10},{9,7},{10,... | collective-permute-start | bytes 1671176 | tf_op jit(solution)/shard_map/ppermute | solution.py:276
  59.9 9.6 %collective-permute-start.11 = (bf16[1,32,48,512]{3,2,1,0:T(8,128)(2,1)S(1)}, bf16[1,32,48,512]{3,2,1,0:T(8,128)(2,1)S(1)}, u32[]{:S(2)}, u32[]{:S(2)}) collective-permute-start(bf16[1,32,48,512]{3,2,1,0:T(8,128)(2,1)S(1)} %get-tuple-element.45), channel_id=1, source_target_pairs={{0,1},{1,0},{2,3},{3,2},{4,5},{5,4},{6,7},{7,6},{8,9},{9,8},{10,11... | collective-permute-start | bytes 4718600 | tf_op jit(solution)/shard_map/ppermute | solution.py:276
  63.3 6.2 %collective-permute-start.8 = (bf16[128,2176]{1,0:T(8,128)(2,1)S(1)}, bf16[128,2176]{1,0:T(8,128)(2,1)S(1)}, u32[]{:S(2)}, u32[]{:S(2)}) collective-permute-start(bf16[128,2176]{1,0:T(8,128)(2,1)S(1)} %collective-permute-done.7.block), channel_id=1, source_target_pairs={{0,1},{1,0},{2,3},{3,2},{4,5},{5,4},{6,7},{7,6},{8,9},{9,8},{10,11... | collective-permute-start | bytes 1671176 | tf_op jit(solution)/shard_map/ppermute | solution.py:276
  71.5 47.2 %all-to-all-start = ((bf16[32,48,512]{2,1,0:T(8,128)(2,1)}), bf16[32,48,512]{2,1,0:T(8,128)(2,1)S(1)}, u32[]{:S(2)}, u32[]{:S(2)}) async-start(bf16[32,48,512]{2,1,0:T(8,128)(2,1)} %bitcast.6), calls=%async_computation | async-start | bytes 3145728 | tf_op jit(solution)/shard_map/all_to_all | solution.py:335
  81.2 9.0 %collective-permute-start.12 = (bf16[128,1152]{1,0:T(8,128)(2,1)S(1)}, bf16[128,1152]{1,0:T(8,128)(2,1)S(1)}, u32[]{:S(2)}, u32[]{:S(2)}) collective-permute-start(bf16[128,1152]{1,0:T(8,128)(2,1)S(1)} %get-tuple-element.46), channel_id=1, source_target_pairs={{2,0},{15,1},{4,2},{1,3},{6,4},{3,5},{8,6},{5,7},{10,8},{7,9},{12,... | collective-permute-start | bytes 884744 | tf_op jit(solution)/shard_map/ppermute | solution.py:276
  83.2 10.2 %collective-permute-start.16 = (bf16[128,1152]{1,0:T(8,128)(2,1)S(1)}, bf16[128,1152]{1,0:T(8,128)(2,1)S(1)}, u32[]{:S(2)}, u32[]{:S(2)}) collective-permute-start(bf16[128,1152]{1,0:T(8,128)(2,1)S(1)} %get-tuple-element.48), channel_id=1, source_target_pairs={{2,0},{15,1},{4,2},{1,3},{6,4},{3,5},{8,6},{5,7},{10,8},{7,9},{12,... | collective-permute-start | bytes 884744 | tf_op jit(solution)/shard_map/ppermute | solution.py:276
  90.3 9.0 %collective-permute-start.13 = (bf16[128,1152]{1,0:T(8,128)(2,1)S(1)}, bf16[128,1152]{1,0:T(8,128)(2,1)S(1)}, u32[]{:S(2)}, u32[]{:S(2)}) collective-permute-start(bf16[128,1152]{1,0:T(8,128)(2,1)S(1)} %shard_map.117), channel_id=1, source_target_pairs={{2,0},{15,1},{4,2},{1,3},{6,4},{3,5},{8,6},{5,7},{10,8},{7,9},{12,... | collective-permute-start | bytes 884744 | tf_op jit(solution)/shard_map/ppermute | solution.py:276
  93.4 9.1 %collective-permute-start.17 = (bf16[128,1152]{1,0:T(8,128)(2,1)S(1)}, bf16[128,1152]{1,0:T(8,128)(2,1)S(1)}, u32[]{:S(2)}, u32[]{:S(2)}) collective-permute-start(bf16[128,1152]{1,0:T(8,128)(2,1)S(1)} %shard_map.120), channel_id=1, source_target_pairs={{2,0},{15,1},{4,2},{1,3},{6,4},{3,5},{8,6},{5,7},{10,8},{7,9},{12,... | collective-permute-start | bytes 884744 | tf_op jit(solution)/shard_map/ppermute | solution.py:276
  99.3 9.0 %collective-permute-start.14 = (bf16[128,1152]{1,0:T(8,128)(2,1)S(1)}, bf16[128,1152]{1,0:T(8,128)(2,1)S(1)}, u32[]{:S(2)}, u32[]{:S(2)}) collective-permute-start(bf16[128,1152]{1,0:T(8,128)(2,1)S(1)} %shard_map.118), channel_id=1, source_target_pairs={{2,0},{15,1},{4,2},{1,3},{6,4},{3,5},{8,6},{5,7},{10,8},{7,9},{12,... | collective-permute-start | bytes 884744 | tf_op jit(solution)/shard_map/ppermute | solution.py:276
  102.6 16.1 %copy-start.7 = (s32[128,10]{0,1:T(8,128)S(1)}, s32[128,10]{0,1:T(8,128)}, u32[]{:S(2)}) copy-start(s32[128,10]{0,1:T(8,128)} %param.9) | copy-start | bytes 15364
  102.6 8.5 %collective-permute-start.18 = (bf16[128,1152]{1,0:T(8,128)(2,1)S(1)}, bf16[128,1152]{1,0:T(8,128)(2,1)S(1)}, u32[]{:S(2)}, u32[]{:S(2)}) collective-permute-start(bf16[128,1152]{1,0:T(8,128)(2,1)S(1)} %shard_map.121), channel_id=1, source_target_pairs={{15,0},{2,1},{1,2},{4,3},{3,4},{6,5},{5,6},{8,7},{7,8},{10,9},{9,1... | collective-permute-start | bytes 884744 | tf_op jit(solution)/shard_map/ppermute | solution.py:276
  108.4 9.0 %collective-permute-start.15 = (bf16[128,1152]{1,0:T(8,128)(2,1)S(1)}, bf16[128,1152]{1,0:T(8,128)(2,1)S(1)}, u32[]{:S(2)}, u32[]{:S(2)}) collective-permute-start(bf16[128,1152]{1,0:T(8,128)(2,1)S(1)} %shard_map.119), channel_id=1, source_target_pairs={{2,0},{15,1},{4,2},{1,3},{6,4},{3,5},{8,6},{5,7},{10,8},{7,9},{12,... | collective-permute-start | bytes 884744 | tf_op jit(solution)/shard_map/ppermute | solution.py:276
  (10 other events, 42.3 us)
